TPU v7x, 32 devices: a whole 2x2x4 slice. The times are simulated.
32 devices in a mesh: dp: 8 (over y, x, core), tensor: 4 (over z).
Axes of the slice: x: 2, y: 2, z: 4, core: 2. Of those that a mesh axis runs over, the one named last changes fastest.
Arguments:
- tokens: bfloat16 [16384, 1536], P(('dp', 'tensor')), may hold values from -6 to 6
- positions: int32 [16384], P('dp'), may hold values from 0 to 2047, as said below
- norm1_gain: bfloat16 [1536], P('dp'), may hold values from 0.5 to 1.5
- w_query: bfloat16 [1536, 1536], P('dp', 'tensor'), may hold values from -0.3125 to 0.3125
- key_weight: bfloat16 [1536, 768], P('dp', 'tensor'), may hold values from -0.3125 to 0.3125
- value_weight: bfloat16 [1536, 768], P('dp', 'tensor'), may hold values from -0.15625 to 0.15625
- w_out: bfloat16 [1536, 1536], P('dp', 'tensor'), may hold values from -0.625 to 0.625
- norm2_gain: bfloat16 [1536], P('dp'), may hold values from 0.5 to 1.5
- w_gate: bfloat16 [1536, 4096], P('dp', 'tensor'), may hold values from -0.15625 to 0.15625
- w_up: bfloat16 [1536, 4096], P('dp', 'tensor'), may hold values from -0.15625 to 0.15625
- w_down: bfloat16 [1536, 4096], P('dp', 'tensor'), may hold values from -0.09375 to 0.09375
- cotangent: bfloat16 [16384, 1536], P(('dp', 'tensor')), may hold values from -6 to 6
Outputs:
- mixed: bfloat16 [16384, 1536], P(('dp', 'tensor'))
- grad_tokens: float32 [16384, 1536], P(('dp', 'tensor'))
- grad_norm1: float32 [1536], P('dp')
- grad_query: float32 [1536, 1536], P('dp', 'tensor')
- grad_key: float32 [1536, 768], P('dp', 'tensor')
- grad_value: float32 [1536, 768], P('dp', 'tensor')
- grad_output: float32 [1536, 1536], P('dp', 'tensor')
- grad_norm2: float32 [1536], P('dp')
- grad_gate: float32 [1536, 4096], P('dp', 'tensor')
- grad_up: float32 [1536, 4096], P('dp', 'tensor')
- grad_down: float32 [1536, 4096], P('dp', 'tensor')
Inputs may be any that keep to these rules, and one draw needn't show every extreme that they name: Each aligned block of 2048 tokens is one sequence holding one or three packed documents; positions count 0, 1, 2, ... from each document's first token, and every sequence starts a document at its first token.
All inputs are finite; a program needn't handle non-finite values.
Results may differ from a plain program's by a relative error of at most 0.02.
Values may be sent and summed in bfloat16 or wider, within the bound.
No kernel may reach another device: no remote copies, remote signals or barrier semaphores. Data moves between devices by JAX's collectives and lax.ppermute only.
A program may use at most 192 MiB of HBM per device.

v0:
```python
import jax
import jax.numpy as jnp
from jax import lax
from jax.sharding import PartitionSpec as P

HEAD_SIZE = 96
SEQUENCE_LENGTH = 2048


epsilon = 1e-05
rope_base = 100000.0
masked_score = -1e30
contract_rows = (((0,), (0,)), ((), ()))
contract_cols = (((1,), (1,)), ((), ()))


def spin_tables(places):
    inverse = rope_base ** (-(2.0 / HEAD_SIZE) * jnp.arange(HEAD_SIZE // 2, dtype=jnp.float32))
    angles = places.astype(jnp.float32)[:, None] * inverse[None, :]
    return (jnp.cos(angles), jnp.sin(angles))


def apply_rotation(values, cosine_table, sine_table):
    middle = values.shape[-1] // 2
    leading = values[..., :middle]
    trailing = values[..., middle:]
    cos_part = cosine_table[:, None, :]
    sin_part = sine_table[:, None, :]
    return jnp.concatenate(
        [leading * cos_part - trailing * sin_part, trailing * cos_part + leading * sin_part], -1
    )


def visible(query_index, places, length):
    key_index = jnp.arange(length, dtype=jnp.int32)[None, :]
    return (key_index <= query_index[:, None]) & (key_index >= (query_index - places)[:, None])


def block_scores(query_block, every_key, row_start, place_block, length):
    block_rows = query_block.shape[0]
    query_index = row_start + jnp.arange(block_rows, dtype=jnp.int32)
    scores = jnp.einsum(
        "bkgd,tkd->kgbt", query_block, every_key, preferred_element_type=jnp.float32
    ) * HEAD_SIZE ** (-0.5)
    shown = visible(query_index, place_block, length)
    return (jnp.where(shown, scores, masked_score), shown)


def attend_forward(sequence_item):
    query_rows, every_key, every_value, places = sequence_item
    length = query_rows.shape[0]
    block_rows = min(512, length)
    starts = jnp.arange(length // block_rows, dtype=jnp.int32) * block_rows

    def one_block(row_start):
        query_block = lax.dynamic_slice_in_dim(query_rows, row_start, block_rows, 0)
        place_block = lax.dynamic_slice_in_dim(places, row_start, block_rows, 0)
        scores, shown = block_scores(query_block, every_key, row_start, place_block, length)
        largest = jnp.max(scores, -1, keepdims=True)
        weights = jnp.exp(scores - largest)
        totals = jnp.sum(weights, -1, keepdims=True)
        shares = (weights / totals).astype(jnp.bfloat16)
        mixed_block = jnp.einsum(
            "kgbt,tkd->bkgd", shares, every_value, preferred_element_type=jnp.float32
        )
        return (mixed_block.astype(jnp.bfloat16), (largest + jnp.log(totals))[..., 0])

    blocks, log_sums = lax.map(one_block, starts)
    return (blocks.reshape(query_rows.shape), log_sums)


def attend_backward(sequence_item):
    query_rows, every_key, every_value, places, head_grads, log_sums = sequence_item
    length = query_rows.shape[0]
    block_rows = min(512, length)
    starts = jnp.arange(length // block_rows, dtype=jnp.int32) * block_rows
    scale = HEAD_SIZE ** (-0.5)

    def one_block(carried, block_item):
        key_total, value_total = carried
        row_start, log_block = block_item
        query_block = lax.dynamic_slice_in_dim(query_rows, row_start, block_rows, 0)
        place_block = lax.dynamic_slice_in_dim(places, row_start, block_rows, 0)
        grad_block = lax.dynamic_slice_in_dim(head_grads, row_start, block_rows, 0)
        scores, shown = block_scores(query_block, every_key, row_start, place_block, length)
        shares = jnp.where(shown, jnp.exp(scores - log_block[..., None]), 0.0)
        value_total = value_total + jnp.einsum(
            "kgbt,bkgd->tkd",
            shares.astype(jnp.bfloat16),
            grad_block,
            preferred_element_type=jnp.float32,
        )
        share_grads = jnp.einsum(
            "bkgd,tkd->kgbt", grad_block, every_value, preferred_element_type=jnp.float32
        )
        inner = jnp.sum(shares * share_grads, -1, keepdims=True)
        score_grads = (shares * (share_grads - inner)).astype(jnp.bfloat16)
        query_part = (
            jnp.einsum("kgbt,tkd->bkgd", score_grads, every_key, preferred_element_type=jnp.float32)
            * scale
        )
        key_total = (
            key_total
            + jnp.einsum(
                "kgbt,bkgd->tkd", score_grads, query_block, preferred_element_type=jnp.float32
            )
            * scale
        )
        return ((key_total, value_total), query_part)

    zeros_kv = jnp.zeros(every_key.shape, jnp.float32)
    (key_total, value_total), query_parts = lax.scan(
        one_block, (zeros_kv, zeros_kv), (starts, log_sums)
    )
    return (query_parts.reshape(query_rows.shape), key_total, value_total)


def norm_back(normed_grad, values, inverse_root, gain):
    scaled = normed_grad * gain.astype(jnp.float32)
    gain_grad = jnp.sum(normed_grad * values * inverse_root, 0)
    value_grad = inverse_root * scaled - values * inverse_root**3 * jnp.mean(
        scaled * values, -1, keepdims=True
    )
    return (value_grad, gain_grad)


def per_device(
    tokens,
    positions,
    norm1_gain,
    w_query,
    key_weight,
    value_weight,
    w_out,
    norm2_gain,
    w_gate,
    w_up,
    w_down,
    cotangent,
):
    gathered = (
        lax.all_gather(norm1_gain, "dp", axis=0, tiled=True),
        lax.all_gather(norm2_gain, "dp", axis=0, tiled=True),
        lax.all_gather(w_query, "dp", axis=0, tiled=True),
        lax.all_gather(key_weight, "dp", axis=0, tiled=True),
        lax.all_gather(value_weight, "dp", axis=0, tiled=True),
        lax.all_gather(w_out, "dp", axis=0, tiled=True),
        lax.all_gather(w_gate, "dp", axis=0, tiled=True),
        lax.all_gather(w_up, "dp", axis=0, tiled=True),
        lax.all_gather(w_down, "dp", axis=0, tiled=True),
    )
    gain_first, gain_second, wq_full, wk_full, wv_full, wo_full, wg_full, wu_full, wd_full = (
        gathered
    )
    group_rows = positions.shape[0]
    seq_count = group_rows // SEQUENCE_LENGTH
    qheads = wq_full.shape[1] // HEAD_SIZE
    kvheads = wk_full.shape[1] // HEAD_SIZE
    share_heads = qheads // kvheads
    cosine_table, sine_table = spin_tables(positions)
    stream = tokens.astype(jnp.float32)
    inverse_first = lax.rsqrt(jnp.mean(stream * stream, -1, keepdims=True) + epsilon)
    first_normed = (stream * inverse_first * gain_first.astype(jnp.float32)).astype(jnp.bfloat16)
    attn_whole = lax.all_gather(first_normed, "tensor", axis=0, tiled=True)
    query_proj = jnp.dot(attn_whole, wq_full, preferred_element_type=jnp.float32).reshape(
        group_rows, qheads, HEAD_SIZE
    )
    key_proj = jnp.dot(attn_whole, wk_full, preferred_element_type=jnp.float32).reshape(
        group_rows, kvheads, HEAD_SIZE
    )
    query_rows = apply_rotation(query_proj, cosine_table, sine_table).astype(jnp.bfloat16)
    every_key = apply_rotation(key_proj, cosine_table, sine_table).astype(jnp.bfloat16)
    every_value = jnp.dot(attn_whole, wv_full, preferred_element_type=jnp.float32).astype(
        jnp.bfloat16
    )
    query_seqs = query_rows.reshape(seq_count, SEQUENCE_LENGTH, kvheads, share_heads, HEAD_SIZE)
    key_seqs = every_key.reshape(seq_count, SEQUENCE_LENGTH, kvheads, HEAD_SIZE)
    value_seqs = every_value.reshape(seq_count, SEQUENCE_LENGTH, kvheads, HEAD_SIZE)
    place_seqs = positions.reshape(seq_count, SEQUENCE_LENGTH)
    attended, log_sums = lax.map(attend_forward, (query_seqs, key_seqs, value_seqs, place_seqs))
    heads_out = attended.reshape(group_rows, qheads * HEAD_SIZE)
    piece = heads_out
    middle_stream = stream + lax.psum_scatter(
        lax.dot_general(piece, wo_full, contract_cols, preferred_element_type=jnp.float32),
        "tensor",
        scatter_dimension=0,
        tiled=True,
    )
    inverse_second = lax.rsqrt(jnp.mean(middle_stream * middle_stream, -1, keepdims=True) + epsilon)
    second_normed = (middle_stream * inverse_second * gain_second.astype(jnp.float32)).astype(
        jnp.bfloat16
    )
    ff_whole = lax.all_gather(second_normed, "tensor", axis=0, tiled=True)
    gate_value = jnp.dot(ff_whole, wg_full, preferred_element_type=jnp.float32)
    up_value = jnp.dot(ff_whole, wu_full, preferred_element_type=jnp.float32)
    sigmoid_gate = jax.nn.sigmoid(gate_value)
    silu_gate = gate_value * sigmoid_gate
    hidden = (silu_gate * up_value).astype(jnp.bfloat16)
    piece = hidden
    mixed = (
        middle_stream
        + lax.psum_scatter(
            lax.dot_general(
                piece, wd_full, contract_cols, preferred_element_type=jnp.float32
            ).astype(jnp.bfloat16),
            "tensor",
            scatter_dimension=0,
            tiled=True,
        ).astype(jnp.float32)
    ).astype(jnp.bfloat16)
    backward_set = (
        lax.all_gather(norm1_gain, "dp", axis=0, tiled=True),
        lax.all_gather(norm2_gain, "dp", axis=0, tiled=True),
        lax.all_gather(w_query, "dp", axis=0, tiled=True),
        lax.all_gather(key_weight, "dp", axis=0, tiled=True),
        lax.all_gather(value_weight, "dp", axis=0, tiled=True),
        lax.all_gather(w_out, "dp", axis=0, tiled=True),
        lax.all_gather(w_gate, "dp", axis=0, tiled=True),
        lax.all_gather(w_up, "dp", axis=0, tiled=True),
        lax.all_gather(w_down, "dp", axis=0, tiled=True),
    )
    gain_first, gain_second, wq_full, wk_full, wv_full, wo_full, wg_full, wu_full, wd_full = (
        backward_set
    )
    out_whole = lax.all_gather(cotangent, "tensor", axis=0, tiled=True)
    hidden_grad = jnp.dot(out_whole, wd_full, preferred_element_type=jnp.float32)
    gate_grad = (hidden_grad * up_value * (sigmoid_gate + silu_gate * (1.0 - sigmoid_gate))).astype(
        jnp.bfloat16
    )
    up_grad = (hidden_grad * silu_gate).astype(jnp.bfloat16)
    down_wgrad = lax.dot_general(
        out_whole, hidden, contract_rows, preferred_element_type=jnp.float32
    )
    gate_wgrad = lax.dot_general(
        ff_whole, gate_grad, contract_rows, preferred_element_type=jnp.float32
    )
    up_wgrad = lax.dot_general(ff_whole, up_grad, contract_rows, preferred_element_type=jnp.float32)
    second_grad = lax.psum_scatter(
        lax.dot_general(gate_grad, wg_full, contract_cols, preferred_element_type=jnp.float32)
        + lax.dot_general(up_grad, wu_full, contract_cols, preferred_element_type=jnp.float32),
        "tensor",
        scatter_dimension=0,
        tiled=True,
    )
    middle_part, gain_second_grad = norm_back(
        second_grad, middle_stream, inverse_second, gain_second
    )
    middle_grad = cotangent.astype(jnp.float32) + middle_part
    branch_whole = lax.all_gather(middle_grad.astype(jnp.bfloat16), "tensor", axis=0, tiled=True)
    out_wgrad = lax.dot_general(
        branch_whole, heads_out, contract_rows, preferred_element_type=jnp.float32
    )
    heads_grad = jnp.dot(branch_whole, wo_full, preferred_element_type=jnp.float32).astype(
        jnp.bfloat16
    )
    grad_seqs = heads_grad.reshape(seq_count, SEQUENCE_LENGTH, kvheads, share_heads, HEAD_SIZE)
    query_parts, key_parts, value_parts = lax.map(
        attend_backward, (query_seqs, key_seqs, value_seqs, place_seqs, grad_seqs, log_sums)
    )
    query_grad = (
        apply_rotation(
            query_parts.reshape(group_rows, qheads, HEAD_SIZE), cosine_table, -sine_table
        )
        .reshape(group_rows, qheads * HEAD_SIZE)
        .astype(jnp.bfloat16)
    )
    key_grad = (
        apply_rotation(key_parts.reshape(group_rows, kvheads, HEAD_SIZE), cosine_table, -sine_table)
        .reshape(group_rows, kvheads * HEAD_SIZE)
        .astype(jnp.bfloat16)
    )
    value_grad = value_parts.reshape(group_rows, kvheads * HEAD_SIZE).astype(jnp.bfloat16)
    query_wgrad = lax.dot_general(
        attn_whole, query_grad, contract_rows, preferred_element_type=jnp.float32
    )
    key_wgrad = lax.dot_general(
        attn_whole, key_grad, contract_rows, preferred_element_type=jnp.float32
    )
    value_wgrad = lax.dot_general(
        attn_whole, value_grad, contract_rows, preferred_element_type=jnp.float32
    )
    first_grad = lax.psum_scatter(
        (
            lax.dot_general(query_grad, wq_full, contract_cols, preferred_element_type=jnp.float32)
            + lax.dot_general(key_grad, wk_full, contract_cols, preferred_element_type=jnp.float32)
            + lax.dot_general(
                value_grad, wv_full, contract_cols, preferred_element_type=jnp.float32
            )
        ).astype(jnp.bfloat16),
        "tensor",
        scatter_dimension=0,
        tiled=True,
    ).astype(jnp.float32)
    first_part, gain_first_grad = norm_back(first_grad, stream, inverse_first, gain_first)
    input_grad = middle_grad + first_part
    owned = (
        lax.psum_scatter(
            gain_first_grad.astype(jnp.bfloat16), "dp", scatter_dimension=0, tiled=True
        ).astype(jnp.float32),
        lax.psum_scatter(
            gain_second_grad.astype(jnp.bfloat16), "dp", scatter_dimension=0, tiled=True
        ).astype(jnp.float32),
        lax.psum_scatter(
            query_wgrad.astype(jnp.bfloat16), "dp", scatter_dimension=0, tiled=True
        ).astype(jnp.float32),
        lax.psum_scatter(
            key_wgrad.astype(jnp.bfloat16), "dp", scatter_dimension=0, tiled=True
        ).astype(jnp.float32),
        lax.psum_scatter(
            value_wgrad.astype(jnp.bfloat16), "dp", scatter_dimension=0, tiled=True
        ).astype(jnp.float32),
        lax.psum_scatter(
            out_wgrad.astype(jnp.bfloat16), "dp", scatter_dimension=0, tiled=True
        ).astype(jnp.float32),
        lax.psum_scatter(
            gate_wgrad.astype(jnp.bfloat16), "dp", scatter_dimension=0, tiled=True
        ).astype(jnp.float32),
        lax.psum_scatter(
            up_wgrad.astype(jnp.bfloat16), "dp", scatter_dimension=0, tiled=True
        ).astype(jnp.float32),
        lax.psum_scatter(
            down_wgrad.astype(jnp.bfloat16), "dp", scatter_dimension=0, tiled=True
        ).astype(jnp.float32),
    )
    gain_totals = lax.psum((owned[0], owned[1]), "tensor")
    return (
        mixed,
        input_grad,
        gain_totals[0],
        owned[2],
        owned[3],
        owned[4],
        owned[5],
        gain_totals[1],
        owned[6],
        owned[7],
        owned[8],
    )


def solution(mesh):
    in_specs = (
        P(("dp", "tensor"), None),
        P("dp"),
        P("dp"),
        P("dp", "tensor"),
        P("dp", "tensor"),
        P("dp", "tensor"),
        P("dp", "tensor"),
        P("dp"),
        P("dp", "tensor"),
        P("dp", "tensor"),
        P("dp", "tensor"),
        P(("dp", "tensor"), None),
    )
    out_specs = (
        P(("dp", "tensor"), None),
        P(("dp", "tensor"), None),
        P("dp"),
        P("dp", "tensor"),
        P("dp", "tensor"),
        P("dp", "tensor"),
        P("dp", "tensor"),
        P("dp"),
        P("dp", "tensor"),
        P("dp", "tensor"),
        P("dp", "tensor"),
    )
    return jax.shard_map(
        per_device, mesh=mesh, in_specs=in_specs, out_specs=out_specs, check_vma=False
    )
```

profile of v0, /device:TPU:0, one launch (start us, length us, event | category | flops | bytes accessed | tf_op | source)
XLA Modules:
  0.0 1921.7 jit_solution(11328033324999990522)
XLA Ops:
  13.4 16.0 all-reduce.6
  44.0 10.4 all_gather.52
  56.6 91.2 %all-gather.10.cloned.1.call-done = bf16[2048,1536]{1,0:T(8,128)(2,1)} async-done(((bf16[512,1536]{1,0:T(8,128)(2,1)}), bf16[2048,1536]{1,0:T(8,128)(2,1)}) %all-gather.10.cloned.1.call-update) | async-done | bytes 6291472 | tf_op jit(solution)/shard_map/all_gather | solution.py:164
  153.1 19.0 all-gather.12.cloned.1.call-done
  183.8 79.5 %while.47 = (s32[]{:T(128)}, bf16[4,512,2,2,96]{1,4,3,2,0:T(8,128)(2,1)}, f32[4,2,2,512]{3,2,1,0:T(2,128)}, s32[4]{0:T(128)S(1)}, s32[2048]{0:T(1024)S(1)}, /*in...) while((s32[]{:T(128)}, ...), condition=%wide.region_4.5_spmd, body=%wide.region_1.4_spmd.sunk | while | flops 1664285696 | bytes 56961208 | solution.py:68
  268.6 9.8 fusion.61
  279.1 211.3 %reduce-scatter.14.cloned.1.call-done = f32[512,1536]{1,0:T(8,128)} async-done(((f32[2048,1536]{1,0:T(8,128)}), f32[512,1536]{1,0:T(8,128)}) %reduce-scatter.14.cloned.1.call-update) | async-done | bytes 3145744 | tf_op jit(solution)/shard_map/reduce_scatter | solution.py:183
  497.0 28.5 %all-gather.20.cloned.1.call-done = bf16[1536,1024]{1,0:T(8,128)(2,1)} async-done(((bf16[192,1024]{1,0:T(8,128)(2,1)}), bf16[1536,1024]{1,0:T(8,128)(2,1)}) %all-gather.20.cloned.1.call-update) | async-done | bytes 3145744 | tf_op jit(solution)/shard_map/all_gather | solution.py:149
  525.5 117.4 %all-gather.16.cloned.1.call-done = bf16[2048,1536]{1,0:T(8,128)(2,1)} async-done(((bf16[512,1536]{1,0:T(8,128)(2,1)}), bf16[2048,1536]{1,0:T(8,128)(2,1)}) %all-gather.16.cloned.1.call-update) | async-done | bytes 6291472 | tf_op jit(solution)/shard_map/all_gather | solution.py:193
  642.9 12.0 fusion.63
  654.9 20.5 %all-gather.18.cloned.1.call-done = bf16[1536,1024]{1,0:T(8,128)(2,1)} async-done(((bf16[192,1024]{1,0:T(8,128)(2,1)}), bf16[1536,1024]{1,0:T(8,128)(2,1)}) %all-gather.18.cloned.1.call-update) | async-done | bytes 3145744 | tf_op jit(solution)/shard_map/all_gather | solution.py:148
  675.4 11.7 fusion.62
  687.1 22.5 %all-gather.22.cloned.1.call-done = bf16[1536,1024]{1,0:T(8,128)(2,1)} async-done(((bf16[192,1024]{1,0:T(8,128)(2,1)}), bf16[1536,1024]{1,0:T(8,128)(2,1)}) %all-gather.22.cloned.1.call-update) | async-done | bytes 3145744 | tf_op jit(solution)/shard_map/all_gather | solution.py:150
  709.6 117.0 %all-gather.24.cloned.1.call-done = bf16[2048,1536]{1,0:T(8,128)(2,1)} async-done(((bf16[512,1536]{1,0:T(8,128)(2,1)}), bf16[2048,1536]{1,0:T(8,128)(2,1)}) %all-gather.24.cloned.1.call-update) | async-done | bytes 6291472 | tf_op jit(solution)/shard_map/all_gather | solution.py:225
  826.6 18.0 multiply_convert_fusion
  844.6 9.7 fusion.64
  854.3 12.9 convolution_add_fusion
  867.2 11.4 convolution_convert_fusion
  878.8 198.7 %reduce-scatter.18.cloned.1.call-done = f32[512,1536]{1,0:T(8,128)} async-done(((f32[2048,1536]{1,0:T(8,128)}), f32[512,1536]{1,0:T(8,128)}) %reduce-scatter.18.cloned.1.call-update) | async-done | bytes 3145744 | tf_op jit(solution)/shard_map/reduce_scatter | solution.py:238
  1080.7 110.9 %reduce-scatter.16.cloned.1.call-done = bf16[512,1536]{1,0:T(8,128)(2,1)} async-done(((bf16[2048,1536]{1,0:T(8,128)(2,1)}), bf16[512,1536]{1,0:T(8,128)(2,1)}) %reduce-scatter.16.cloned.1.call-update) | async-done | bytes 1572880 | tf_op jit(solution)/shard_map/reduce_scatter | solution.py:202
  1196.8 10.3 fusion.46
  1210.0 11.5 convolution_convert_fusion.2
  1221.6 11.3 convolution_convert_fusion.3
  1233.0 79.8 %all-gather.26.cloned.1.call-done = bf16[2048,1536]{1,0:T(8,128)(2,1)} async-done(((bf16[512,1536]{1,0:T(8,128)(2,1)}), bf16[2048,1536]{1,0:T(8,128)(2,1)}) %all-gather.26.cloned.1.call-update) | async-done | bytes 6291472 | tf_op jit(solution)/shard_map/all_gather | solution.py:249
  1319.7 289.6 %while.48 = (s32[]{:T(128)}, f32[2048,2,96]{0,2,1:T(8,128)S(1)}, f32[2048,2,96]{0,2,1:T(8,128)}, f32[4,512,2,2,96]{1,0,4,3,2:T(4,128)}, s32[4]{0:T(128)S(1)}, /*...) while((s32[]{:T(128)}, f32[2048,2,96]{0,2,1:T(8,128)S(1)}, ...), condition=%wide.region_12.13_spmd.clone, body=%wide.region_10.12_spmd.clone.sunk | while | flops 4073782272 | bytes 149473536 | solution.py:112
  1326.1 10.0 fusion.142
  1336.1 14.4 fusion.144
  1350.4 11.7 fusion.145
  1376.2 16.1 dynamic_update_slice.34
  1398.3 9.7 fusion.142
  1408.1 14.6 fusion.144
  1422.6 12.1 fusion.145
  1449.6 16.1 dynamic_update_slice.34
  1471.7 9.7 fusion.142
  1481.3 14.3 fusion.144
  1495.6 11.3 fusion.145
  1521.4 16.0 dynamic_update_slice.34
  1543.4 9.6 fusion.142
  1553.0 14.3 fusion.144
  1567.3 11.3 fusion.145
  1593.1 16.0 dynamic_update_slice.34
  1646.1 9.9 fusion.65
  1662.5 12.5 add_convert_fusion
  1690.0 38.6 %reduce-scatter.28.cloned.1.call-done = bf16[192,384]{1,0:T(8,128)(2,1)} async-done(((bf16[1536,384]{1,0:T(8,128)(2,1)}), bf16[192,384]{1,0:T(8,128)(2,1)}) %reduce-scatter.28.cloned.1.call-update) | async-done | bytes 147472 | tf_op jit(solution)/shard_map/reduce_scatter | solution.py:312
  1730.3 38.4 %reduce-scatter.22.cloned.1.call-done = bf16[192,384]{1,0:T(8,128)(2,1)} async-done(((bf16[1536,384]{1,0:T(8,128)(2,1)}), bf16[192,384]{1,0:T(8,128)(2,1)}) %reduce-scatter.22.cloned.1.call-update) | async-done | bytes 147472 | tf_op jit(solution)/shard_map/reduce_scatter | solution.py:303
  1770.3 111.4 %reduce-scatter.20.cloned.1.call-done = bf16[512,1536]{1,0:T(8,128)(2,1)} async-done(((bf16[2048,1536]{1,0:T(8,128)(2,1)}), bf16[512,1536]{1,0:T(8,128)(2,1)}) %reduce-scatter.20.cloned.1.call-update) | async-done | bytes 1572880 | tf_op jit(solution)/shard_map/reduce_scatter | solution.py:282
  1884.4 13.9 all-reduce.5
  1898.5 11.7 all-reduce.4
  (241 shorter events, 283.1 us)
Async XLA Ops:
  7.2 140.7 %all-gather.10.cloned.1.call-start = ((), (), s32[]{:S(2)}) async-start(), calls=%async_computation.11 | async-start | bytes 7864320 | tf_op jit(solution)/shard_map/all_gather | solution.py:164
  7.2 27.3 %copy-start.18 = (s32[2048]{0:T(1024)S(1)}, s32[2048]{0:T(1024)}, u32[]{:S(2)}) copy-start(s32[2048]{0:T(1024)} %param.17) | copy-start | bytes 24580
  7.2 27.3 %copy-start.19 = (bf16[192,192]{1,0:T(8,128)(2,1)S(1)}, bf16[192,192]{1,0:T(8,128)(2,1)}, u32[]{:S(2)}) copy-start(bf16[192,192]{1,0:T(8,128)(2,1)} %param.20) | copy-start | bytes 221188
  9.1 34.9 %copy-start.20 = (bf16[192,192]{1,0:T(8,128)(2,1)S(1)}, bf16[192,192]{1,0:T(8,128)(2,1)}, u32[]{:S(2)}) copy-start(bf16[192,192]{1,0:T(8,128)(2,1)} %param.21) | copy-start | bytes 221188
  9.7 34.3 %copy-start.21 = (f32[512]{0:T(512)}, f32[512]{0:T(512)S(1)}, u32[]{:S(2)}) copy-start(f32[512]{0:T(512)S(1)} %get-tuple-element.314) | copy-start | bytes 6148
  33.0 139.1 %all-gather.12.cloned.1.call-start = ((), (), s32[]{:S(2)}) async-start(), calls=%async_computation.12 | async-start | bytes 1327104 | tf_op jit(solution)/shard_map/all_gather | solution.py:144
  33.7 234.8 %all-gather.14.cloned.1.call-start = ((), (), s32[]{:S(2)}) async-start(), calls=%async_computation.13 | async-start | bytes 1327104 | tf_op jit(solution)/shard_map/all_gather | solution.py:147
  34.5 455.9 %reduce-scatter.14.cloned.1.call-start = ((), (), s32[]{:S(2)}) async-start(), calls=%async_computation.14 | async-start | bytes 15728640 | tf_op jit(solution)/shard_map/reduce_scatter | solution.py:183
  44.0 108.9 %copy-start.7 = (bf16[1536,192]{1,0:T(8,128)(2,1)}, bf16[1536,192]{1,0:T(8,128)(2,1)S(1)}, u32[]{:S(2)}) copy-start(bf16[1536,192]{1,0:T(8,128)(2,1)S(1)} %all_gather.51) | copy-start | bytes 1769476
  54.4 123.5 %copy-start.12 = (bf16[1536,192]{1,0:T(8,128)(2,1)}, bf16[1536,192]{1,0:T(8,128)(2,1)S(1)}, u32[]{:S(2)}) copy-start(bf16[1536,192]{1,0:T(8,128)(2,1)S(1)} %all_gather.52) | copy-start | bytes 1769476
  56.6 120.5 %copy-start.3 = (f32[2048,48]{0,1:T(8,128)}, f32[2048,48]{0,1:T(8,128)S(1)}, u32[]{:S(2)}) copy-start(f32[2048,48]{0,1:T(8,128)S(1)} %get-tuple-element.312) | copy-start | bytes 1179652
  278.4 247.1 %all-gather.20.cloned.1.call-start = ((), (), s32[]{:S(2)}) async-start(), calls=%async_computation.17 | async-start | bytes 3538944 | tf_op jit(solution)/shard_map/all_gather | solution.py:149
  279.0 363.9 %all-gather.16.cloned.1.call-start = ((), (), s32[]{:S(2)}) async-start(), calls=%async_computation.15 | async-start | bytes 7864320 | tf_op jit(solution)/shard_map/all_gather | solution.py:193
  494.7 180.6 %all-gather.18.cloned.1.call-start = ((), (), s32[]{:S(2)}) async-start(), calls=%async_computation.16 | async-start | bytes 3538944 | tf_op jit(solution)/shard_map/all_gather | solution.py:148
  495.5 214.1 %all-gather.22.cloned.1.call-start = ((), (), s32[]{:S(2)}) async-start(), calls=%async_computation.18 | async-start | bytes 3538944 | tf_op jit(solution)/shard_map/all_gather | solution.py:150
  496.2 330.3 %all-gather.24.cloned.1.call-start = ((), (), s32[]{:S(2)}) async-start(), calls=%async_computation.20 | async-start | bytes 7864320 | tf_op jit(solution)/shard_map/all_gather | solution.py:225
  497.0 580.4 %reduce-scatter.18.cloned.1.call-start = ((), (), s32[]{:S(2)}) async-start(), calls=%async_computation.21 | async-start | bytes 15728640 | tf_op jit(solution)/shard_map/reduce_scatter | solution.py:238
  826.6 18.0 copy-start.27
  844.6 9.7 copy-start.30
  844.6 9.7 copy-start.26
  844.6 9.7 copy-start.31
  867.2 324.4 %reduce-scatter.16.cloned.1.call-start = ((), (), s32[]{:S(2)}) async-start(), calls=%async_computation.19 | async-start | bytes 7864320 | tf_op jit(solution)/shard_map/reduce_scatter | solution.py:202
  878.7 434.1 %all-gather.26.cloned.1.call-start = ((), (), s32[]{:S(2)}) async-start(), calls=%async_computation.22 | async-start | bytes 7864320 | tf_op jit(solution)/shard_map/all_gather | solution.py:249
  1196.7 479.1 %reduce-scatter.34.cloned.1.call-start = ((), (), s32[]{:S(2)}) async-start(), calls=%async_computation.30 | async-start | bytes 3538944
  1210.0 468.1 %reduce-scatter.32.cloned.1.call-start = ((), (), s32[]{:S(2)}) async-start(), calls=%async_computation.29 | async-start | bytes 3538944 | tf_op jit(solution)/shard_map/reduce_scatter | solution.py:318
  1221.5 458.5 %reduce-scatter.30.cloned.1.call-start = ((), (), s32[]{:S(2)}) async-start(), calls=%async_computation.28 | async-start | bytes 3538944 | tf_op jit(solution)/shard_map/reduce_scatter | solution.py:315
  1232.9 86.8 %copy-start.2 = (bf16[2048,2,96]{0,2,1:T(8,128)(2,1)S(1)}, bf16[2048,2,96]{0,2,1:T(8,128)(2,1)}, u32[]{:S(2)}) copy-start(bf16[2048,2,96]{0,2,1:T(8,128)(2,1)} %copy-done.1) | copy-start | bytes 2359300
  1232.9 86.7 %copy-start.29 = (s32[4]{0:T(128)S(1)}, s32[4]{0:T(128)}, u32[]{:S(2)}) copy-start(s32[4]{0:T(128)} %copy-done.28) | copy-start | bytes 52
  1233.0 449.1 %reduce-scatter.24.cloned.1.call-start = ((), (), s32[]{:S(2)}) async-start(), calls=%async_computation.25 | async-start | bytes 884736 | tf_op jit(solution)/shard_map/reduce_scatter | solution.py:306
  1319.7 289.6 %copy-start.4 = (f32[2048,48]{0,1:T(8,128)S(1)}, f32[2048,48]{0,1:T(8,128)}, u32[]{:S(2)}) copy-start(f32[2048,48]{0,1:T(8,128)} %copy-done.3) | copy-start | bytes 1179652
  1326.1 10.0 copy-start.6
  1398.3 9.7 copy-start.6
  1471.6 9.7 copy-start.6
  1543.4 9.6 copy-start.6
  1616.1 72.3 %reduce-scatter.26.cloned.1.call-start = ((), (), s32[]{:S(2)}) async-start(), calls=%async_computation.26 | async-start | bytes 884736 | tf_op jit(solution)/shard_map/reduce_scatter | solution.py:309
  1624.3 104.3 %reduce-scatter.28.cloned.1.call-start = ((), (), s32[]{:S(2)}) async-start(), calls=%async_computation.27 | async-start | bytes 1327104 | tf_op jit(solution)/shard_map/reduce_scatter | solution.py:312
  1631.8 136.8 %reduce-scatter.22.cloned.1.call-start = ((), (), s32[]{:S(2)}) async-start(), calls=%async_computation.24 | async-start | bytes 1327104 | tf_op jit(solution)/shard_map/reduce_scatter | solution.py:303
  1631.9 9.6 slice-start
  1646.1 9.9 copy-start.8
  1646.1 235.6 %reduce-scatter.20.cloned.1.call-start = ((), (), s32[]{:S(2)}) async-start(), calls=%async_computation.23 | async-start | bytes 7864320 | tf_op jit(solution)/shard_map/reduce_scatter | solution.py:282
  1656.0 6.4 copy-start.13
  1656.0 6.4 copy-start.15
  1675.0 206.7 %copy-start = (bf16[512,1536]{1,0:T(8,128)(2,1)S(1)}, bf16[512,1536]{1,0:T(8,128)(2,1)}, u32[]{:S(2)}) copy-start(bf16[512,1536]{1,0:T(8,128)(2,1)} %param.16) | copy-start | bytes 4718596
  1675.0 206.7 %copy-start.17 = (f32[1536]{0:T(1024)S(1)}, f32[1536]{0:T(1024)}, u32[]{:S(2)}) copy-start(f32[1536]{0:T(1024)} %copy-done.16) | copy-start | bytes 18436
  1675.0 206.7 %copy-start.22 = (f32[512]{0:T(512)S(1)}, f32[512]{0:T(512)}, u32[]{:S(2)}) copy-start(f32[512]{0:T(512)} %copy-done.21) | copy-start | bytes 6148
  1680.1 204.4 %copy-start.23 = (bf16[1536]{0:T(1024)(128)(2,1)S(1)}, bf16[1536]{0:T(1024)(128)(2,1)}, u32[]{:S(2)}) copy-start(bf16[1536]{0:T(1024)(128)(2,1)} %get-tuple-element.238) | copy-start | bytes 9220
  1680.1 230.1 %copy-start.24 = (f32[512]{0:T(512)S(1)}, f32[512]{0:T(512)}, u32[]{:S(2)}) copy-start(f32[512]{0:T(512)} %get-tuple-element.313) | copy-start | bytes 6148
  1881.7 28.5 %copy-start.11 = (bf16[512,1536]{1,0:T(8,128)(2,1)S(1)}, bf16[512,1536]{1,0:T(8,128)(2,1)}, u32[]{:S(2)}) copy-start(bf16[512,1536]{1,0:T(8,128)(2,1)} %reduce-scatter.20.cloned.1.call-done) | copy-start | bytes 4718596
  (9 other events, 28.6 us)
Sparse Core Ops, SparseCore 0:
  33.1 114.7 all-gather.9
  149.7 22.2 all-gather.11
  173.9 24.0 all-gather.13
  278.5 211.8 reduce-scatter.13
  492.1 33.3 all-gather.19
  527.5 115.3 all-gather.15
  644.8 30.5 all-gather.17
  677.2 32.3 all-gather.21
  711.2 115.3 all-gather.23
  867.3 210.0 reduce-scatter.17
  1079.7 111.7 reduce-scatter.15
  1196.8 115.8 all-gather.25
  1316.1 44.4 reduce-scatter.33
  1364.2 46.2 reduce-scatter.31
  1413.8 46.1 reduce-scatter.29
  1616.2 33.8 reduce-scatter.23
  1653.4 34.9 reduce-scatter.25
  1691.8 36.7 reduce-scatter.27
  1731.8 36.7 reduce-scatter.21
  1770.9 110.7 reduce-scatter.19
where the time goes:
time: 1930 us; the launch traced here: 1920 us
  waiting for transfers between devices  1210 us (63%)
  matrix products  385 us (20%)
  other arithmetic  130 us (7%)
  local copies, waits for them, and re-layouts  96.8 us (5%)
  blocking collectives  61.5 us (3%)
    reduce_scatter x1, waiting for transfers between devices, per_device(): lax.psum_scatter(lax.dot_general(piece, wo_full, contract_cols, preferred...  211 us
    reduce_scatter x1, waiting for transfers between devices, per_device(): lax.psum_scatter(lax.dot_general(gate_grad, wg_full, contract_cols, prefe...  199 us
    all_gather x1, waiting for transfers between devices, per_device(): ff_whole = lax.all_gather(second_normed, 'tensor', axis=0, tiled=True)  117 us
    all_gather x1, waiting for transfers between devices, per_device(): out_whole = lax.all_gather(cotangent, 'tensor', axis=0, tiled=True)  117 us
    reduce_scatter x1, waiting for transfers between devices, per_device(): lax.psum_scatter((lax.dot_general(query_grad, wq_full, contract_cols, pre...  111 us
    reduce_scatter x1, waiting for transfers between devices, per_device(): lax.psum_scatter(lax.dot_general(piece, wd_full, contract_cols, preferred...  111 us
    all_gather x1, waiting for transfers between devices, per_device(): attn_whole = lax.all_gather(first_normed, 'tensor', axis=0, tiled=True)  91.2 us
    all_gather x1, waiting for transfers between devices, per_device(): lax.all_gather(middle_grad.astype(jnp.bfloat16), 'tensor', axis=0, tiled=...  79.8 us
  transfers between devices with their start and end apart: 20, of which 15 were waited for; matrix products, arithmetic and copies ran while one was open for 28% of the time, Pallas kernels for 0%

commit v1 on v0

v1 whole, which is shorter than its diff:
```python
import functools
import math

import jax
import jax.numpy as jnp
from jax import lax
from jax.experimental import pallas as pl
from jax.experimental.pallas import tpu as pltpu
from jax.sharding import Mesh
from jax.sharding import PartitionSpec as P

HEAD_SIZE = 96
SEQUENCE_LENGTH = 2048
LANES = 128

epsilon = 1e-05
rope_base = 100000.0
masked_score = -1e30
query_scale = math.log2(math.e) * HEAD_SIZE ** (-0.5)
rows_both = (((0,), (0,)), ((), ()))
cols_both = (((1,), (1,)), ((), ()))
f32 = jnp.float32
bf16 = jnp.bfloat16


def local_block(g, place_ref, ring):
    other = lax.rem(g // ring + place_ref[0], 2)
    step = lax.rem(lax.rem(g, ring) - place_ref[1] + ring, ring)
    return 2 * step + other


def attend_kernel(ring, block, place_ref, q_ref, k_ref, v_ref, start_ref, o_ref, lse_ref):
    g = pl.program_id(1)
    share = q_ref.shape[1] // LANES
    start = start_ref[...]
    row = lax.broadcasted_iota(jnp.int32, (block, block), 0)
    col = lax.broadcasted_iota(jnp.int32, (block, block), 1)
    queries = [q_ref[:, h * LANES : (h + 1) * LANES] for h in range(share)]

    def step(kb, carry, diagonal):
        offset = pl.multiple_of(local_block(kb, place_ref, ring) * block, block)
        keys = k_ref[pl.ds(offset, block), :]
        values = v_ref[pl.ds(offset, block), :]
        shown = row >= start - kb * block
        if diagonal:
            shown = shown & (row <= col)
        out = []
        for h in range(share):
            largest, total, acc = carry[h]
            s = lax.dot_general(keys, queries[h], cols_both, preferred_element_type=f32)
            s = jnp.where(shown, s, masked_score)
            newest = jnp.maximum(largest, jnp.max(s, 0, keepdims=True))
            fade = jnp.exp2(largest - newest)
            p = jnp.exp2(s - newest)
            total = total * fade + jnp.sum(p, 0, keepdims=True)
            acc = acc * fade + lax.dot_general(
                values, p.astype(bf16), rows_both, preferred_element_type=f32
            )
            out.append((newest, total, acc))
        return tuple(out)

    carry = tuple(
        (
            jnp.full((1, block), masked_score, f32),
            jnp.zeros((1, block), f32),
            jnp.zeros((LANES, block), f32),
        )
        for _ in range(share)
    )
    carry = step(g, carry, True)
    carry = lax.fori_loop(0, g, lambda kb, c: step(kb, c, False), carry)
    for h in range(share):
        largest, total, acc = carry[h]
        o_ref[:, h * LANES : (h + 1) * LANES] = jnp.transpose(acc / total).astype(bf16)
        lse_ref[0, h : h + 1, :] = largest + jnp.log2(total)


def attend(place, q, k, v, start, ring):
    length = q.shape[0]
    block = length // (2 * ring)
    kv = k.shape[1] // LANES
    share = q.shape[1] // k.shape[1]

    def at(g, place_ref):
        return local_block(g, place_ref, ring)

    return pl.pallas_call(
        functools.partial(attend_kernel, ring, block),
        grid_spec=pltpu.PrefetchScalarGridSpec(
            num_scalar_prefetch=1,
            grid=(kv, 2 * ring),
            in_specs=[
                pl.BlockSpec((block, share * LANES), lambda h, g, z: (at(g, z), h)),
                pl.BlockSpec((length, LANES), lambda h, g, z: (0, h)),
                pl.BlockSpec((length, LANES), lambda h, g, z: (0, h)),
                pl.BlockSpec((1, block), lambda h, g, z: (0, at(g, z))),
            ],
            out_specs=[
                pl.BlockSpec((block, share * LANES), lambda h, g, z: (at(g, z), h)),
                pl.BlockSpec((1, share, block), lambda h, g, z: (h, 0, at(g, z))),
            ],
        ),
        out_shape=[
            jax.ShapeDtypeStruct(q.shape, bf16),
            jax.ShapeDtypeStruct((kv, share, length), f32),
        ],
        compiler_params=pltpu.CompilerParams(
            vmem_limit_bytes=40 * 2**20, dimension_semantics=("arbitrary", "arbitrary")
        ),
        cost_estimate=pl.CostEstimate(
            flops=10 * length * length * q.shape[1], bytes_accessed=8 * length * q.shape[1], transcendentals=0
        ),
        name="attend",
    )(place, q, k, v, start)


def attend_back_kernel(
    ring,
    block,
    place_ref,
    q_ref,
    k_ref,
    v_ref,
    o_ref,
    do_ref,
    lse_ref,
    start_ref,
    cosq_ref,
    sinq_ref,
    cosk_ref,
    sink_ref,
    dq_ref,
    dk_ref,
    dv_ref,
    dk_acc,
    dv_acc,
):
    g = pl.program_id(1)
    share = q_ref.shape[1] // LANES

    @pl.when(g == 0)
    def _():
        dk_acc[...] = jnp.zeros_like(dk_acc)
        dv_acc[...] = jnp.zeros_like(dv_acc)

    start = start_ref[...]
    row = lax.broadcasted_iota(jnp.int32, (block, block), 0)
    col = lax.broadcasted_iota(jnp.int32, (block, block), 1)
    heads = [slice(h * LANES, (h + 1) * LANES) for h in range(share)]
    queries = [q_ref[:, h] for h in heads]
    grads = [do_ref[:, h] for h in heads]
    lses = [lse_ref[0, h : h + 1, :] for h in range(share)]
    inner = [
        jnp.sum(
            jnp.transpose(do_ref[:, h].astype(f32) * o_ref[:, h].astype(f32)), 0, keepdims=True
        )
        for h in heads
    ]

    def step(kb, carry, diagonal):
        offset = pl.multiple_of(local_block(kb, place_ref, ring) * block, block)
        keys = k_ref[pl.ds(offset, block), :]
        values = v_ref[pl.ds(offset, block), :]
        shown = row >= start - kb * block
        if diagonal:
            shown = shown & (row <= col)
        out = []
        dk = jnp.zeros((block, LANES), f32)
        dv = jnp.zeros((block, LANES), f32)
        for h in range(share):
            s = lax.dot_general(keys, queries[h], cols_both, preferred_element_type=f32)
            p = jnp.where(shown, jnp.exp2(s - lses[h]), 0.0)
            dp = lax.dot_general(values, grads[h], cols_both, preferred_element_type=f32)
            ds = (p * (dp - inner[h])).astype(bf16)
            dv += jnp.dot(p.astype(bf16), grads[h], preferred_element_type=f32)
            dk += jnp.dot(ds, queries[h], preferred_element_type=f32)
            out.append(carry[h] + lax.dot_general(keys, ds, rows_both, preferred_element_type=f32))
        dk_acc[pl.ds(offset, block), :] += dk
        dv_acc[pl.ds(offset, block), :] += dv
        return tuple(out)

    carry = step(g, tuple(jnp.zeros((LANES, block), f32) for _ in range(share)), True)
    carry = lax.fori_loop(0, g, lambda kb, c: step(kb, c, False), carry)
    for h in range(share):
        u = jnp.transpose(carry[h]) * HEAD_SIZE ** (-0.5)
        turned = u * cosq_ref[...] - pltpu.roll(u, LANES // 2, 1) * sinq_ref[...]
        dq_ref[:, heads[h]] = turned.astype(bf16)

    @pl.when(g == pl.num_programs(1) - 1)
    def _():
        def finish(i, _):
            r = pl.ds(pl.multiple_of(i * block, block), block)
            u = dk_acc[r, :] * math.log(2.0)
            turned = u * cosk_ref[r, :] - pltpu.roll(u, LANES // 2, 1) * sink_ref[r, :]
            dk_ref[r, :] = turned.astype(bf16)
            dv_ref[r, :] = dv_acc[r, :].astype(bf16)
            return 0

        lax.fori_loop(0, 2 * ring, finish, 0)


def attend_back(place, q, k, v, o, do, lse, start, cos, sin, ring):
    length = q.shape[0]
    block = length // (2 * ring)
    kv = k.shape[1] // LANES
    share = q.shape[1] // k.shape[1]

    def at(g, place_ref):
        return local_block(g, place_ref, ring)

    qspec = pl.BlockSpec((block, share * LANES), lambda h, g, z: (at(g, z), h))
    kspec = pl.BlockSpec((length, LANES), lambda h, g, z: (0, h))
    tableq = pl.BlockSpec((block, LANES), lambda h, g, z: (at(g, z), 0))
    tablek = pl.BlockSpec((length, LANES), lambda h, g, z: (0, 0))
    return pl.pallas_call(
        functools.partial(attend_back_kernel, ring, block),
        grid_spec=pltpu.PrefetchScalarGridSpec(
            num_scalar_prefetch=1,
            grid=(kv, 2 * ring),
            in_specs=[
                qspec,
                kspec,
                kspec,
                qspec,
                qspec,
                pl.BlockSpec((1, share, block), lambda h, g, z: (h, 0, at(g, z))),
                pl.BlockSpec((1, block), lambda h, g, z: (0, at(g, z))),
                tableq,
                tableq,
                tablek,
                tablek,
            ],
            out_specs=[qspec, kspec, kspec],
            scratch_shapes=[pltpu.VMEM((length, LANES), f32), pltpu.VMEM((length, LANES), f32)],
        ),
        out_shape=[
            jax.ShapeDtypeStruct(q.shape, bf16),
            jax.ShapeDtypeStruct(k.shape, bf16),
            jax.ShapeDtypeStruct(k.shape, bf16),
        ],
        compiler_params=pltpu.CompilerParams(
            vmem_limit_bytes=40 * 2**20, dimension_semantics=("arbitrary", "arbitrary")
        ),
        cost_estimate=pl.CostEstimate(
            flops=20 * length * length * q.shape[1], bytes_accessed=16 * length * q.shape[1], transcendentals=0
        ),
        name="attend_back",
    )(place, q, k, v, o, do, lse, start, cos, sin, cos, sin)


def project_kernel(
    widths, x_ref, gain_ref, w_ref, cos_ref, sin_ref, a_ref, q_ref, k_ref, v_ref
):
    x = x_ref[...].astype(f32)
    root = lax.rsqrt(jnp.mean(x * x, -1, keepdims=True) + epsilon)
    a = (x * root * gain_ref[...]).astype(bf16)
    a_ref[...] = a
    cos = cos_ref[...]
    sin = sin_ref[...]
    whole = jnp.dot(a, w_ref[...], preferred_element_type=f32)
    qw, kw = widths
    for h in range((qw + kw) // LANES):
        u = whole[:, h * LANES : (h + 1) * LANES]
        turned = u * cos + pltpu.roll(u, LANES // 2, 1) * sin
        if h < qw // LANES:
            q_ref[:, h * LANES : (h + 1) * LANES] = (turned * query_scale).astype(bf16)
        else:
            j = h - qw // LANES
            k_ref[:, j * LANES : (j + 1) * LANES] = turned.astype(bf16)
    v_ref[...] = whole[:, qw + kw :].astype(bf16)


def project(x, gain, w, cos, sin, qw, kw):
    rows, width = x.shape
    block = min(256, rows)

    def row(n):
        return pl.BlockSpec((block, n), lambda i: (i, 0))

    def whole(a):
        return pl.BlockSpec(a.shape, lambda i: (0, 0))

    return pl.pallas_call(
        functools.partial(project_kernel, (qw, kw)),
        grid=(rows // block,),
        in_specs=[row(width), whole(gain), whole(w), row(LANES), row(LANES)],
        out_specs=[row(width), row(qw), row(kw), row(kw)],
        out_shape=[jax.ShapeDtypeStruct((rows, n), bf16) for n in (width, qw, kw, kw)],
        compiler_params=pltpu.CompilerParams(
            vmem_limit_bytes=40 * 2**20, dimension_semantics=("arbitrary",)
        ),
        cost_estimate=pl.CostEstimate(
            flops=2 * rows * width * w.shape[1], bytes_accessed=8 * rows * width, transcendentals=0
        ),
        name="project",
    )(x, gain, w, cos, sin)


def hidden_kernel(chunk, a_ref, dy_ref, wg_ref, wu_ref, wd_ref, hid_ref, dg_ref, du_ref):
    a = a_ref[...]
    dy = dy_ref[...]
    for j in range(wg_ref.shape[1] // chunk):
        at = slice(j * chunk, (j + 1) * chunk)
        g = jnp.dot(a, wg_ref[:, at], preferred_element_type=f32)
        u = jnp.dot(a, wu_ref[:, at], preferred_element_type=f32)
        dh = jnp.dot(dy, wd_ref[:, at], preferred_element_type=f32)
        sig = jax.nn.sigmoid(g)
        silu = g * sig
        hid_ref[:, at] = (silu * u).astype(bf16)
        dg_ref[:, at] = (dh * u * (sig + silu * (1.0 - sig))).astype(bf16)
        du_ref[:, at] = (dh * silu).astype(bf16)


def hidden_pass(a, dy, wg, wu, wd):
    rows, width = a.shape
    units = wg.shape[1]
    block = min(256, rows)
    row = pl.BlockSpec((block, width), lambda i: (i, 0))
    out = pl.BlockSpec((block, units), lambda i: (i, 0))
    whole = pl.BlockSpec((width, units), lambda i: (0, 0))
    return pl.pallas_call(
        functools.partial(hidden_kernel, min(256, units)),
        grid=(rows // block,),
        in_specs=[row, row, whole, whole, whole],
        out_specs=[out, out, out],
        out_shape=[jax.ShapeDtypeStruct((rows, units), bf16)] * 3,
        compiler_params=pltpu.CompilerParams(
            vmem_limit_bytes=48 * 2**20, dimension_semantics=("arbitrary",)
        ),
        cost_estimate=pl.CostEstimate(
            flops=6 * rows * width * units, bytes_accessed=4 * rows * width, transcendentals=0
        ),
        name="hidden",
    )(a, dy, wg, wu, wd)


def pad_heads(w):
    half = HEAD_SIZE // 2
    parts = w.reshape(w.shape[0], -1, half)
    return jnp.pad(parts, ((0, 0), (0, 0), (0, LANES // 2 - half))).reshape(w.shape[0], -1)


def cut_heads(w):
    half = HEAD_SIZE // 2
    parts = w.reshape(w.shape[0], -1, LANES // 2)
    return parts[:, :, :half].reshape(w.shape[0], -1)


swap_two = [(0, 1), (1, 0)]
cross_pairs = [(0, 0), (1, 2), (2, 1), (3, 3)]
slant_pairs = [(2 * c + zh, 2 * zh + (1 - c)) for c in range(2) for zh in range(2)]
slant_back = [(b, a) for a, b in slant_pairs]


def relay(a):
    return lax.ppermute(a, ("c", "zh"), cross_pairs)


def other_core(a):
    return lax.ppermute(a, "c", swap_two)


def from_neighbour(a, k, ring):
    return lax.ppermute(a, "zl", [(i, (i - k) % ring) for i in range(ring)])


def both_cores(a):
    return jnp.concatenate([a, other_core(a)], 0)


def gather_weight(w):
    straight = lax.ppermute(w, ("c", "zh"), cross_pairs)
    slanted = lax.ppermute(w, ("c", "zh"), slant_pairs)
    first = lax.axis_index("zh") == 0
    both = jnp.concatenate(
        [jnp.where(first, straight, slanted), jnp.where(first, slanted, straight)], 0
    )
    return lax.all_gather(both, "d", axis=0, tiled=True)


def settle_weight(grad):
    part = lax.psum_scatter(grad.astype(bf16), "d", scatter_dimension=0, tiled=True)
    rows = part.shape[0] // 2
    first = lax.axis_index("zh") == 0
    upper, lower = part[:rows], part[rows:]
    straight = lax.ppermute(jnp.where(first, upper, lower), ("c", "zh"), cross_pairs)
    slanted = lax.ppermute(jnp.where(first, lower, upper), ("c", "zh"), slant_back)
    return straight.astype(f32) + slanted.astype(f32)


def dot(a, b):
    return jnp.dot(a, b, preferred_element_type=f32)


def dot_cols(a, b):
    return lax.dot_general(a, b, cols_both, preferred_element_type=f32)


def dot_rows(a, b):
    return lax.dot_general(a, b, rows_both, preferred_element_type=f32)


def sum_steps(first, second):
    out = first
    for item in second:
        out = out + item
    return out


def per_device(
    ring,
    tokens,
    positions,
    norm1_gain,
    w_query,
    key_weight,
    value_weight,
    w_out,
    norm2_gain,
    w_gate,
    w_up,
    w_down,
    cotangent,
):
    steps = range(ring)
    core = lax.axis_index("c")
    column = lax.axis_index("zl")
    place = jnp.stack([core, column]).astype(jnp.int32)
    rows = tokens.shape[0]
    length = 2 * ring * rows

    def gather_chip(own):
        return [both_cores(own if k == 0 else from_neighbour(own, k, ring)) for k in steps]

    def scatter_sum(partials, kind):
        kept = []
        for k in reversed(steps):
            p = partials[k]
            joined = p[:rows].astype(f32) + other_core(p[rows:].astype(kind)).astype(f32)
            if k:
                moved = lax.ppermute(
                    joined.astype(kind), "zl", [(i, (i + k) % ring) for i in steps]
                )
                joined = moved.astype(f32)
            kept.append(joined)
        return sum_steps(kept[-1], kept[:-1])

    stream_own = relay(tokens)
    attn_shard = jnp.concatenate([w_query, key_weight, value_weight, w_out], 1)
    gains = lax.all_gather(
        jnp.stack([norm1_gain, norm2_gain]), ("d", "c"), axis=1, tiled=True
    ).astype(f32)
    attn_full = gather_weight(attn_shard)
    places = relay(positions).reshape(2, ring, rows)
    chips = gather_chip(stream_own)

    ordered = [
        lax.dynamic_index_in_dim(
            lax.dynamic_index_in_dim(places, (core + j) % 2, 0, keepdims=False),
            (column + k) % ring,
            0,
            keepdims=False,
        )
        for k in steps
        for j in range(2)
    ]
    firsts = [
        ((core + j) % 2 * ring + (column + k) % ring) * rows for k in steps for j in range(2)
    ]
    start = jnp.concatenate(
        [f + jnp.arange(rows, dtype=jnp.int32) - o for f, o in zip(firsts, ordered)]
    )[None, :]
    spots = jnp.concatenate(ordered).astype(f32)
    inverse = rope_base ** (-(2.0 / HEAD_SIZE) * jnp.arange(HEAD_SIZE // 2, dtype=f32))
    angles = spots[:, None] * inverse[None, :]
    gap = jnp.zeros((length, LANES // 2 - HEAD_SIZE // 2), f32)
    cos_half, sin_half = jnp.cos(angles), jnp.sin(angles)
    cos = jnp.concatenate([cos_half, gap, cos_half, gap], 1)
    sin = jnp.concatenate([-sin_half, gap, sin_half, gap], 1)

    qcols, kcols = w_query.shape[1], key_weight.shape[1]
    padded = pad_heads(attn_full)
    qw = qcols // HEAD_SIZE * LANES
    kw = kcols // HEAD_SIZE * LANES
    w_qkv = padded[:, : qw + 2 * kw]
    w_o = padded[:, qw + 2 * kw :]
    gain_first, gain_second = gains[0:1], gains[1:2]

    pieces = [
        project(
            x,
            gain_first,
            w_qkv,
            cos[2 * rows * k : 2 * rows * (k + 1)],
            sin[2 * rows * k : 2 * rows * (k + 1)],
            qw,
            kw,
        )
        for k, x in enumerate(chips)
    ]
    normed_first = [p[0] for p in pieces]
    q, k, v = (jnp.concatenate([p[i] for p in pieces], 0) for i in (1, 2, 3))
    o, lse = attend(place, q, k, v, start, ring)

    stream = stream_own.astype(f32)
    chip_rows = [slice(2 * rows * i, 2 * rows * (i + 1)) for i in steps]
    middle = stream + scatter_sum([dot_cols(o[r], w_o) for r in chip_rows], bf16)
    root_second = lax.rsqrt(jnp.mean(middle * middle, -1, keepdims=True) + epsilon)
    normed_second = (middle * root_second * gain_second).astype(bf16)

    wg_full = gather_weight(w_gate)
    wu_full = gather_weight(w_up)
    wd_full = gather_weight(w_down)
    cot_own = relay(cotangent)
    out_grads = gather_chip(cot_own)
    ff_in = gather_chip(normed_second)

    hidden = [
        hidden_pass(a, dy, wg_full, wu_full, wd_full) for a, dy in zip(ff_in, out_grads)
    ]
    second_grad = scatter_sum(
        [dot_cols(h[1], wg_full) + dot_cols(h[2], wu_full) for h in hidden], bf16
    )
    mixed = middle + scatter_sum([dot_cols(h[0], wd_full) for h in hidden], bf16)
    mixed = relay(mixed.astype(bf16))

    down_wgrad = sum_steps(0.0, [dot_rows(dy, h[0]) for dy, h in zip(out_grads, hidden)])
    gate_wgrad = sum_steps(0.0, [dot_rows(a, h[1]) for a, h in zip(ff_in, hidden)])
    up_wgrad = sum_steps(0.0, [dot_rows(a, h[2]) for a, h in zip(ff_in, hidden)])

    scaled = second_grad * gain_second
    middle_grad = (
        cot_own.astype(f32)
        + root_second * scaled
        - middle * root_second**3 * jnp.mean(scaled * middle, -1, keepdims=True)
    )
    branch = gather_chip(middle_grad.astype(bf16))
    do = jnp.concatenate([dot(b, w_o).astype(bf16) for b in branch], 0)
    out_wgrad = sum_steps(0.0, [dot_rows(b, o[r]) for b, r in zip(branch, chip_rows)])
    dq, dk, dv = attend_back(place, q, k, v, o, do, lse, start, cos, sin, ring)
    dqkv = jnp.concatenate([dq, dk, dv], 1)
    first_grad = scatter_sum([dot_cols(dqkv[r], w_qkv) for r in chip_rows], bf16)
    qkv_wgrad = sum_steps(0.0, [dot_rows(a, dqkv[r]) for a, r in zip(normed_first, chip_rows)])

    root_first = lax.rsqrt(jnp.mean(stream * stream, -1, keepdims=True) + epsilon)
    scaled = first_grad * gain_first
    input_grad = (
        middle_grad
        + root_first * scaled
        - stream * root_first**3 * jnp.mean(scaled * stream, -1, keepdims=True)
    )
    input_grad = relay(input_grad.astype(bf16)).astype(f32)

    grad_down = settle_weight(down_wgrad)
    grad_gate = settle_weight(gate_wgrad)
    grad_up = settle_weight(up_wgrad)
    grad_attn = settle_weight(cut_heads(jnp.concatenate([qkv_wgrad, out_wgrad], 1)))
    grad_query = grad_attn[:, :qcols]
    grad_key = grad_attn[:, qcols : qcols + kcols]
    grad_value = grad_attn[:, qcols + kcols : qcols + 2 * kcols]
    grad_output = grad_attn[:, qcols + 2 * kcols :]

    def weighed(*pairs):
        return sum_steps(0.0, [jnp.sum(w.astype(f32) * g, 1) for w, g in pairs])

    gain_grads = lax.psum(
        jnp.stack(
            [
                weighed((w_query, grad_query), (key_weight, grad_key), (value_weight, grad_value)),
                weighed((w_gate, grad_gate), (w_up, grad_up)),
            ]
        ),
        ("zh", "zl"),
    )
    return (
        mixed,
        input_grad,
        gain_grads[0] / norm1_gain.astype(f32),
        grad_query,
        grad_key,
        grad_value,
        grad_output,
        gain_grads[1] / norm2_gain.astype(f32),
        grad_gate,
        grad_up,
        grad_down,
    )


def solution(mesh):
    dp, tensor = mesh.devices.shape
    ring = tensor // 2
    regrouped = Mesh(mesh.devices.reshape(dp // 2, 2, 2, ring), ("d", "c", "zh", "zl"))
    data, parts = ("d", "c"), ("zh", "zl")
    tokens_spec = P(data + parts, None)
    weight_spec = P(data, parts)
    in_specs = (
        tokens_spec,
        P(data),
        P(data),
        weight_spec,
        weight_spec,
        weight_spec,
        weight_spec,
        P(data),
        weight_spec,
        weight_spec,
        weight_spec,
        tokens_spec,
    )
    out_specs = (
        tokens_spec,
        tokens_spec,
        P(data),
        weight_spec,
        weight_spec,
        weight_spec,
        weight_spec,
        P(data),
        weight_spec,
        weight_spec,
        weight_spec,
    )
    return jax.shard_map(
        functools.partial(per_device, ring),
        mesh=regrouped,
        in_specs=in_specs,
        out_specs=out_specs,
        check_vma=False,
    )
```

time: 1930 us -> 835 us (0.43)
  waiting for transfers between devices: 1210 us -> 257 us
  matrix products: 385 us -> 96.1 us
  starting transfers between devices: 0.81 us -> 157 us
  Pallas kernels: 0 us -> 112 us
  other arithmetic: 130 us -> 67.9 us
  local copies, waits for them, and re-layouts: 96.8 us -> 71.7 us
    reduce_scatter x10 -> x3, waiting for transfers between devices: 714 us -> 0.01 us  [settle_weight(): lax.psum_scatter(grad.astype(bf16), 'd', scatter_dimension=0, tiled=True)]
    all_gather x9 -> x4, waiting for transfers between devices: 496 us -> 0.03 us  [gather_weight(): return lax.all_gather(both, 'd', axis=0, tiled=True)]
    dot_general x49 -> x22, matrix products: 385 us -> 96.1 us  [the longest x10 52.2 us: dot_rows(): return lax.dot_general(a, b, rows_both, preferred_element_type=f32)]
    ppermute x0 -> x45, waiting for transfers between devices: none -> 257 us  [the longest x4 98.4 us: scatter_sum(): lax.ppermute(joined.astype(kind), 'zl', [(i, (i + k) % ring) for i in ste...]
    ppermute x0 -> x45, starting transfers between devices: none -> 155 us  [the longest x4 31.9 us: settle_weight(): lax.ppermute(jnp.where(first, lower, upper), ('c', 'zh'), slant_back)]
    pallas_call x0 -> x6, Pallas kernels: none -> 112 us  [the longest x1 42.8 us: attend_back(): pl.pallas_call(functools.partial(attend_back_kernel, ring, block), grid_s...]
    dynamic_update_slice x8 -> x0, local copies, waits for them, and re-layouts: 67.6 us -> none  [attend_backward(): lax.scan(one_block, (zeros_kv, zeros_kv), (starts, log_sums))]
    convert_element_type x18 -> x10, other arithmetic: 68 us -> 23.1 us  [the longest x4 10.2 us: scatter_sum(): joined.astype(kind)]
  transfers between devices with their start and end apart: 20 -> 53, of which waited for: 15 -> 13; matrix products, arithmetic and copies ran while one was open for 28% -> 23% of each run, Pallas kernels for 0% -> 12%
where the time goes in v1:
time: 835 us; the launch traced here: 825 us
  waiting for transfers between devices  257 us (31%)
  starting transfers between devices  157 us (19%)
  Pallas kernels  112 us (13%)
  matrix products  96.1 us (12%)
  local copies, waits for them, and re-layouts  71.7 us (9%)
  other arithmetic  67.9 us (8%)
  blocking collectives  47.9 us (6%)
  between operations  15.7 us (2%)
    ppermute x4, waiting for transfers between devices, scatter_sum(): lax.ppermute(joined.astype(kind), 'zl', [(i, (i + k) % ring) for i in ste...  98.4 us
    ppermute x4, waiting for transfers between devices, from_neighbour(): return lax.ppermute(a, 'zl', [(i, (i - k) % ring) for i in range(ring)])  88.8 us
    unnamed x203, local copies, waits for them, and re-layouts  52.3 us
    dot_general x10, matrix products, dot_rows(): return lax.dot_general(a, b, rows_both, preferred_element_type=f32)  52.2 us
    ppermute x4, waiting for transfers between devices, settle_weight(): lax.ppermute(jnp.where(first, lower, upper), ('c', 'zh'), slant_back)  45.2 us
    pallas_call x1, Pallas kernels, attend_back(): pl.pallas_call(functools.partial(attend_back_kernel, ring, block), grid_s...  42.8 us
    all_gather x1, blocking collectives, per_device(): lax.all_gather(jnp.stack([norm1_gain, norm2_gain]), ('d', 'c'), axis=1, t...  39.5 us
    dot_general x10, matrix products, dot_cols(): return lax.dot_general(a, b, cols_both, preferred_element_type=f32)  38.4 us
  transfers between devices with their start and end apart: 53, of which 13 were waited for; matrix products, arithmetic and copies ran while one was open for 23% of the time, Pallas kernels for 12%

profile of v1, /device:TPU:0, one launch (start us, length us, event | category | flops | bytes accessed | tf_op | source)
XLA Modules:
  0.0 825.0 jit_solution(3119329578653912902)
XLA Ops:
  9.1 5.3 collective-permute-start.3
  14.7 9.7 %collective-permute-done.3 = bf16[192,1152]{1,0:T(8,128)(2,1)S(1)} collective-permute-done((bf16[192,1152]{1,0:T(8,128)(2,1)S(1)}, bf16[192,1152]{1,0:T(8,128)(2,1)S(1)}, u32[]{:S(2)}, u32[]{:S(2)}) %collective-permute-start.3) | collective-permute-done | bytes 442400 | tf_op jit(solution)/shard_map/ppermute | solution.py:373
  26.8 14.1 %collective-permute-start.16 = (bf16[192,1024]{1,0:T(8,128)(2,1)S(1)}, bf16[192,1024]{1,0:T(8,128)(2,1)S(1)}, u32[]{:S(2)}, u32[]{:S(2)}) collective-permute-start(bf16[192,1024]{1,0:T(8,128)(2,1)S(1)} %copy-done.65), channel_id=1, source_target_pairs={{0,2},{2,6},{4,0},{6,4},{1,3},{3,7},{5,1},{7,5},{8,10},{10,14},{12... | collective-permute-start | bytes 1179656 | tf_op jit(solution)/shard_map/ppermute | solution.py:373
  42.9 7.6 collective-permute-done.16
  50.5 5.1 collective-permute-done.18
  59.7 18.3 %collective-permute-start.5 = (bf16[512,1536]{1,0:T(8,128)(2,1)S(1)}, bf16[512,1536]{1,0:T(8,128)(2,1)S(1)}, u32[]{:S(2)}, u32[]{:S(2)}) collective-permute-start(bf16[512,1536]{1,0:T(8,128)(2,1)S(1)} %collective-permute-done), channel_id=1, source_target_pairs={{0,1},{1,0},{2,3},{3,2},{4,5},{5,4},{6,7},{7,6},{8,9},{9,8},{10,11... | collective-permute-start | bytes 4718600 | tf_op jit(solution)/shard_map/ppermute | solution.py:364
  78.6 13.3 %collective-permute-start.11 = (bf16[512,1536]{1,0:T(8,128)(2,1)}, bf16[512,1536]{1,0:T(8,128)(2,1)}, u32[]{:S(2)}, u32[]{:S(2)}) collective-permute-start(bf16[512,1536]{1,0:T(8,128)(2,1)} %param.23), channel_id=1, source_target_pairs={{0,0},{2,4},{4,2},{6,6},{1,1},{3,5},{5,3},{7,7},{8,8},{10,12},{12,... | collective-permute-start | bytes 4718600 | tf_op jit(solution)/shard_map/ppermute | solution.py:356
  92.0 39.5 %all-gather = bf16[8,192,2]{1,2,0:T(2,128)(2,1)S(1)} all-gather(bf16[1,192,2]{1,2,0:T(2,128)(2,1)S(1)} %maximum_bitcast_fusion), channel_id=1, replica_groups=mesh['d'=4,'c'=2,'zh'=2,'zl'=2] {'d','c'}, dimensions={0}, use_global_device_ids=true | all-gather | bytes 6912 | tf_op jit(solution)/shard_map/all_gather | solution.py:450
  134.2 11.5 %collective-permute-start.6 = (bf16[512,1536]{1,0:T(8,128)(2,1)S(1)}, bf16[512,1536]{1,0:T(8,128)(2,1)}, u32[]{:S(2)}, u32[]{:S(2)}) collective-permute-start(bf16[512,1536]{1,0:T(8,128)(2,1)S(1)} %collective-permute-done.5), channel_id=1, source_target_pairs={{0,4},{4,0},{1,5},{5,1},{2,6},{6,2},{3,7},{7,3},{8,12},{12,8},{9,1... | collective-permute-start | bytes 4718600 | tf_op jit(solution)/shard_map/ppermute | solution.py:360
  145.6 3.7 fusion.40
  166.3 4.7 copy.55.w_ref
  176.8 5.2 project.2
  184.0 5.2 project.3
  189.4 26.7 %attend.1 = (bf16[2048,512]{1,0:T(8,128)(2,1)S(1)}, f32[2,2,2048]{2,1,0:T(2,128)S(1)}) custom-call(s32[2]{0:T(128)S(1)} %pad_add_fusion.1.place_ref, bf16[2048,512]{1,0:T(8,128)(2,1)S(1)} %constant_dynamic-update-slice_fusion.q_ref, bf16[2048,256]{1,0:T(8,128)(2,1)S(1)} %constant_dynamic-update-slice_fusion.2.k_ref, ...), custom_call_target="tpu_custom_call" | custom-call | flops 21474836480 | bytes 8388608 | tf_op jit(solution)/shard_map/attend/pallas_call | solution.py:87
  219.6 3.8 collective-permute-start.14
  234.6 8.7 %collective-permute-start.12 = (bf16[512,1536]{1,0:T(8,128)(2,1)}, bf16[512,1536]{1,0:T(8,128)(2,1)S(1)}, u32[]{:S(2)}, u32[]{:S(2)}) collective-permute-start(bf16[512,1536]{1,0:T(8,128)(2,1)} %collective-permute-done.11), channel_id=1, source_target_pairs={{0,4},{4,0},{1,5},{5,1},{2,6},{6,2},{3,7},{7,3},{8,12},{12,8},{9,1... | collective-permute-start | bytes 4718600 | tf_op jit(solution)/shard_map/ppermute | solution.py:360
  243.2 25.7 %collective-permute-done.22 = bf16[512,1536]{1,0:T(8,128)(2,1)} collective-permute-done((bf16[512,1536]{1,0:T(8,128)(2,1)}, bf16[512,1536]{1,0:T(8,128)(2,1)}, u32[]{:S(2)}, u32[]{:S(2)}) %collective-permute-start.22) | collective-permute-done | bytes 1572896 | tf_op jit(solution)/shard_map/ppermute | solution.py:364
  268.9 32.2 %collective-permute-done.9 = bf16[512,1536]{1,0:T(8,128)(2,1)} collective-permute-done((bf16[512,1536]{1,0:T(8,128)(2,1)}, bf16[512,1536]{1,0:T(8,128)(2,1)}, u32[]{:S(2)}, u32[]{:S(2)}) %collective-permute-start.9) | collective-permute-done | bytes 1572896 | tf_op jit(solution)/shard_map/ppermute | solution.py:441
  301.1 4.2 multiply_reduce_fusion.1
  310.3 30.5 %collective-permute-done.20 = bf16[512,1536]{1,0:T(8,128)(2,1)} collective-permute-done((bf16[512,1536]{1,0:T(8,128)(2,1)S(1)}, bf16[512,1536]{1,0:T(8,128)(2,1)}, u32[]{:S(2)}, u32[]{:S(2)}) %collective-permute-start.20) | collective-permute-done | bytes 1572896 | tf_op jit(solution)/shard_map/ppermute | solution.py:364
  346.5 16.1 %hidden.2 = (bf16[1024,1024]{1,0:T(8,128)(2,1)S(1)}, bf16[1024,1024]{1,0:T(8,128)(2,1)S(1)}, bf16[1024,1024]{1,0:T(8,128)(2,1)}) custom-call(bf16[1024,1536]{1,0:T(8,128)(2,1)} %pad_maximum_fusion.3.a_ref, bf16[1024,1536]{1,0:T(8,128)(2,1)} %copy-done.62, bf16[1536,1024]{1,0:T(8,128)(2,1)} %all-gather.8.cloned.1.call-done.wg_ref, ...), custom_call_target="tpu_custom_call" | custom-call | flops 9663676416 | bytes 6291456 | tf_op jit(solution)/shard_map/hidden/pallas_call | solution.py:321
  362.7 8.5 %fusion.45 = f32[1536,1024]{1,0:T(8,128)} fusion(bf16[1024,1024]{1,0:T(8,128)(2,1)} %get-tuple-element.40, bf16[512,1536]{1,0:T(8,128)(2,1)S(1)} %copy-done.51, bf16[512,1536]{1,0:T(8,128)(2,1)S(1)} %copy-done.41), kind=kOutput, calls=%fused_computation.161 | convolution fusion | flops 3227516928 | bytes 11534336 | tf_op jit(solution)/shard_map/dot_general | solution.py:400
  374.4 15.9 %hidden.3 = (bf16[1024,1024]{1,0:T(8,128)(2,1)S(1)}, bf16[1024,1024]{1,0:T(8,128)(2,1)S(1)}, bf16[1024,1024]{1,0:T(8,128)(2,1)}) custom-call(bf16[1024,1536]{1,0:T(8,128)(2,1)} %copy-done.58, bf16[1024,1536]{1,0:T(8,128)(2,1)} %copy-done.60, bf16[1536,1024]{1,0:T(8,128)(2,1)} %all-gather.8.cloned.1.call-done.wg_ref, ...), custom_call_target="tpu_custom_call" | custom-call | flops 9663676416 | bytes 6291456 | tf_op jit(solution)/shard_map/hidden/pallas_call | solution.py:321
  393.0 9.4 %add_convert_fusion.1 = bf16[1536,1024]{1,0:T(8,128)(2,1)} fusion(f32[1536,1024]{1,0:T(8,128)} %fusion.45, bf16[1024,1536]{1,0:T(8,128)(2,1)} %copy-done.58, bf16[1024,1024]{1,0:T(8,128)(2,1)} %get-tuple-element.42), kind=kOutput, calls=%fused_computation.1 | convolution fusion | flops 3224371200 | bytes 14680064 | tf_op jit(solution)/shard_map/dot_general | solution.py:400
  402.8 6.1 fusion.54
  415.5 5.5 fusion.56
  439.7 5.1 add_convert_fusion
  457.9 27.7 %collective-permute-done.29 = bf16[512,1536]{1,0:T(8,128)(2,1)S(1)} collective-permute-done((bf16[512,1536]{1,0:T(8,128)(2,1)S(1)}, bf16[512,1536]{1,0:T(8,128)(2,1)S(1)}, u32[]{:S(2)}, u32[]{:S(2)}) %collective-permute-start.29) | collective-permute-done | bytes 1572896 | tf_op jit(solution)/shard_map/ppermute | solution.py:441
  488.0 31.1 %collective-permute-done.25 = bf16[512,1536]{1,0:T(8,128)(2,1)S(1)} collective-permute-done((bf16[512,1536]{1,0:T(8,128)(2,1)}, bf16[512,1536]{1,0:T(8,128)(2,1)S(1)}, u32[]{:S(2)}, u32[]{:S(2)}) %collective-permute-start.25) | collective-permute-done | bytes 1572896 | tf_op jit(solution)/shard_map/ppermute | solution.py:441
  519.1 5.6 fusion.47
  528.6 32.7 %collective-permute-done.31 = bf16[512,1536]{1,0:T(8,128)(2,1)} collective-permute-done((bf16[512,1536]{1,0:T(8,128)(2,1)}, bf16[512,1536]{1,0:T(8,128)(2,1)}, u32[]{:S(2)}, u32[]{:S(2)}) %collective-permute-start.31) | collective-permute-done | bytes 1572896 | tf_op jit(solution)/shard_map/ppermute | solution.py:364
  561.2 5.1 add_convert_fusion.2
  568.1 5.5 fusion.18
  583.8 42.8 %attend_back.1 = (bf16[2048,512]{1,0:T(8,128)(2,1)S(1)}, bf16[2048,256]{1,0:T(8,128)(2,1)S(1)}, bf16[2048,256]{1,0:T(8,128)(2,1)S(1)}) custom-call(s32[2]{0:T(128)S(1)} %pad_add_fusion.1.place_ref, bf16[2048,512]{1,0:T(8,128)(2,1)S(1)} %copy-done.7, bf16[2048,256]{1,0:T(8,128)(2,1)S(1)} %copy-done.13, bf16[2048,256]{1,0:T(8,128)(2,1)S(1)} %copy-done.15, ...), custom_call_target="tpu_custom_call" | custom-call | flops 42949672960 | bytes 16777216 | tf_op jit(solution)/shard_map/attend_back/pallas_call | solution.py:215
  635.9 3.9 add_convert_fusion.3
  640.4 4.1 copy.53
  644.5 6.1 fusion.21
  654.0 5.3 fusion.25
  668.1 4.5 collective-permute-start.41
  672.6 23.9 %collective-permute-start.42 = (bf16[192,1024]{1,0:T(8,128)(2,1)}, bf16[192,1024]{1,0:T(8,128)(2,1)}, u32[]{:S(2)}, u32[]{:S(2)}) collective-permute-start(bf16[192,1024]{1,0:T(8,128)(2,1)} %get-tuple-element.97), channel_id=1, source_target_pairs={{2,0},{6,2},{0,4},{4,6},{3,1},{7,3},{1,5},{5,7},{10,8},{14,10},{8,... | collective-permute-start | bytes 1179656 | tf_op jit(solution)/shard_map/ppermute | solution.py:387
  698.5 4.5 collective-permute-start.43
  705.1 6.4 collective-permute-start.44
  711.5 4.5 collective-permute-start.39
  719.9 7.4 collective-permute-done.35
  734.6 13.3 %collective-permute-start.36 = (bf16[512,1536]{1,0:T(8,128)(2,1)}, bf16[512,1536]{1,0:T(8,128)(2,1)}, u32[]{:S(2)}, u32[]{:S(2)}) collective-permute-start(bf16[512,1536]{1,0:T(8,128)(2,1)} %fusion.3), channel_id=1, source_target_pairs={{0,0},{2,4},{4,2},{6,6},{1,1},{3,5},{5,3},{7,7},{8,8},{10,12},{12,... | collective-permute-start | bytes 4718600 | tf_op jit(solution)/shard_map/ppermute | solution.py:356
  751.0 17.1 %collective-permute-done.40 = bf16[192,1024]{1,0:T(8,128)(2,1)S(1)} collective-permute-done((bf16[192,1024]{1,0:T(8,128)(2,1)}, bf16[192,1024]{1,0:T(8,128)(2,1)S(1)}, u32[]{:S(2)}, u32[]{:S(2)}) %collective-permute-start.40) | collective-permute-done | bytes 393248 | tf_op jit(solution)/shard_map/ppermute | solution.py:387
  775.8 28.1 %collective-permute-done.38 = bf16[192,1152]{1,0:T(8,128)(2,1)S(1)} collective-permute-done((bf16[192,1152]{1,0:T(8,128)(2,1)S(1)}, bf16[192,1152]{1,0:T(8,128)(2,1)S(1)}, u32[]{:S(2)}, u32[]{:S(2)}) %collective-permute-start.38) | collective-permute-done | bytes 442400 | tf_op jit(solution)/shard_map/ppermute | solution.py:387
  805.8 8.4 %psum.7 = f32[2,192]{1,0:T(2,128)S(1)} all-reduce(f32[2,192]{1,0:T(2,128)S(1)} %pad_maximum_fusion.18), channel_id=1, replica_groups=mesh['d'=4,'c'=2,'zh'=2,'zl'=2] {'zh','zl'}, use_global_device_ids=true, to_apply=%region_12.13 | all-reduce | flops 384 | bytes 3072 | tf_op jit(solution)/shard_map/psum | solution.py:566
  (389 shorter events, 180.0 us)
Async XLA Ops:
  7.2 152.4 %all-gather.6.cloned.1.call-start = ((), (), s32[]{:S(2)}) async-start(), calls=%async_computation.4 | async-start | bytes 4423680 | tf_op jit(solution)/shard_map/all_gather | solution.py:378
  9.1 15.3 %collective-permute-start.3 = (bf16[192,1152]{1,0:T(8,128)(2,1)S(1)}, bf16[192,1152]{1,0:T(8,128)(2,1)S(1)}, u32[]{:S(2)}, u32[]{:S(2)}) collective-permute-start(bf16[192,1152]{1,0:T(8,128)(2,1)S(1)} %concatenate.83), channel_id=1, source_target_pairs={{0,2},{2,6},{4,0},{6,4},{1,3},{3,7},{5,1},{7,5},{8,10},{10,14},{12... | collective-permute-start | bytes 1327112 | tf_op jit(solution)/shard_map/ppermute | solution.py:373
  26.0 320.5 %all-gather.10.cloned.1.call-start = ((), (), s32[]{:S(2)}) async-start(), calls=%async_computation.6 | async-start | bytes 3932160 | tf_op jit(solution)/shard_map/all_gather | solution.py:378
  26.1 16.8 %collective-permute-start.15 = (bf16[192,1024]{1,0:T(8,128)(2,1)S(1)}, bf16[192,1024]{1,0:T(8,128)(2,1)S(1)}, u32[]{:S(2)}, u32[]{:S(2)}) collective-permute-start(bf16[192,1024]{1,0:T(8,128)(2,1)S(1)} %copy-done.65), channel_id=1, source_target_pairs={{0,0},{2,4},{4,2},{6,6},{1,1},{3,5},{5,3},{7,7},{8,8},{10,12},{12,... | collective-permute-start | bytes 1179656 | tf_op jit(solution)/shard_map/ppermute | solution.py:372
  26.8 23.7 %collective-permute-start.16 = (bf16[192,1024]{1,0:T(8,128)(2,1)S(1)}, bf16[192,1024]{1,0:T(8,128)(2,1)S(1)}, u32[]{:S(2)}, u32[]{:S(2)}) collective-permute-start(bf16[192,1024]{1,0:T(8,128)(2,1)S(1)} %copy-done.65), channel_id=1, source_target_pairs={{0,2},{2,6},{4,0},{6,4},{1,3},{3,7},{5,1},{7,5},{8,10},{10,14},{12... | collective-permute-start | bytes 1179656 | tf_op jit(solution)/shard_map/ppermute | solution.py:373
  41.6 14.0 %collective-permute-start.18 = (bf16[192,1024]{1,0:T(8,128)(2,1)S(1)}, bf16[192,1024]{1,0:T(8,128)(2,1)S(1)}, u32[]{:S(2)}, u32[]{:S(2)}) collective-permute-start(bf16[192,1024]{1,0:T(8,128)(2,1)S(1)} %copy-done.80), channel_id=1, source_target_pairs={{0,2},{2,6},{4,0},{6,4},{1,3},{3,7},{5,1},{7,5},{8,10},{10,14},{12... | collective-permute-start | bytes 1179656 | tf_op jit(solution)/shard_map/ppermute | solution.py:373
  57.5 289.0 %all-gather.12.cloned.1.call-start = ((), (), s32[]{:S(2)}) async-start(), calls=%async_computation.7 | async-start | bytes 3932160 | tf_op jit(solution)/shard_map/all_gather | solution.py:378
  59.7 74.5 %collective-permute-start.5 = (bf16[512,1536]{1,0:T(8,128)(2,1)S(1)}, bf16[512,1536]{1,0:T(8,128)(2,1)S(1)}, u32[]{:S(2)}, u32[]{:S(2)}) collective-permute-start(bf16[512,1536]{1,0:T(8,128)(2,1)S(1)} %collective-permute-done), channel_id=1, source_target_pairs={{0,1},{1,0},{2,3},{3,2},{4,5},{5,4},{6,7},{7,6},{8,9},{9,8},{10,11... | collective-permute-start | bytes 4718600 | tf_op jit(solution)/shard_map/ppermute | solution.py:364
  77.9 54.4 %collective-permute-start.4 = (s32[2048]{0:T(1024)S(1)}, s32[2048]{0:T(1024)S(1)}, u32[]{:S(2)}, u32[]{:S(2)}) collective-permute-start(s32[2048]{0:T(1024)S(1)} %copy-done.81), channel_id=1, source_target_pairs={{0,0},{2,4},{4,2},{6,6},{1,1},{3,5},{5,3},{7,7},{8,8},{10,12},{12,... | collective-permute-start | bytes 24584 | tf_op jit(solution)/shard_map/ppermute | solution.py:356
  78.6 144.9 %collective-permute-start.11 = (bf16[512,1536]{1,0:T(8,128)(2,1)}, bf16[512,1536]{1,0:T(8,128)(2,1)}, u32[]{:S(2)}, u32[]{:S(2)}) collective-permute-start(bf16[512,1536]{1,0:T(8,128)(2,1)} %param.23), channel_id=1, source_target_pairs={{0,0},{2,4},{4,2},{6,6},{1,1},{3,5},{5,3},{7,7},{8,8},{10,12},{12,... | collective-permute-start | bytes 4718600 | tf_op jit(solution)/shard_map/ppermute | solution.py:356
  132.4 22.2 %collective-permute-start.1 = (bf16[512,1536]{1,0:T(8,128)(2,1)S(1)}, bf16[512,1536]{1,0:T(8,128)(2,1)}, u32[]{:S(2)}, u32[]{:S(2)}) collective-permute-start(bf16[512,1536]{1,0:T(8,128)(2,1)S(1)} %collective-permute-done), channel_id=1, source_target_pairs={{0,4},{4,0},{1,5},{5,1},{2,6},{6,2},{3,7},{7,3},{8,12},{12,8},{9,1... | collective-permute-start | bytes 4718600 | tf_op jit(solution)/shard_map/ppermute | solution.py:360
  134.2 23.8 %collective-permute-start.6 = (bf16[512,1536]{1,0:T(8,128)(2,1)S(1)}, bf16[512,1536]{1,0:T(8,128)(2,1)}, u32[]{:S(2)}, u32[]{:S(2)}) collective-permute-start(bf16[512,1536]{1,0:T(8,128)(2,1)S(1)} %collective-permute-done.5), channel_id=1, source_target_pairs={{0,4},{4,0},{1,5},{5,1},{2,6},{6,2},{3,7},{7,3},{8,12},{12,8},{9,1... | collective-permute-start | bytes 4718600 | tf_op jit(solution)/shard_map/ppermute | solution.py:360
  154.3 192.2 %all-gather.8.cloned.1.call-start = ((), (), s32[]{:S(2)}) async-start(), calls=%async_computation.5 | async-start | bytes 3932160 | tf_op jit(solution)/shard_map/all_gather | solution.py:378
  219.6 13.4 %collective-permute-start.14 = (bf16[192,1024]{1,0:T(8,128)(2,1)S(1)}, bf16[192,1024]{1,0:T(8,128)(2,1)S(1)}, u32[]{:S(2)}, u32[]{:S(2)}) collective-permute-start(bf16[192,1024]{1,0:T(8,128)(2,1)S(1)} %copy-done.67), channel_id=1, source_target_pairs={{0,2},{2,6},{4,0},{6,4},{1,3},{3,7},{5,1},{7,5},{8,10},{10,14},{12... | collective-permute-start | bytes 1179656 | tf_op jit(solution)/shard_map/ppermute | solution.py:373
  223.5 45.5 %collective-permute-start.22 = (bf16[512,1536]{1,0:T(8,128)(2,1)}, bf16[512,1536]{1,0:T(8,128)(2,1)}, u32[]{:S(2)}, u32[]{:S(2)}) collective-permute-start(bf16[512,1536]{1,0:T(8,128)(2,1)} %collective-permute-done.11), channel_id=1, source_target_pairs={{0,1},{1,0},{2,3},{3,2},{4,5},{5,4},{6,7},{7,6},{8,9},{9,8},{10,11... | collective-permute-start | bytes 4718600 | tf_op jit(solution)/shard_map/ppermute | solution.py:364
  227.9 41.1 %collective-permute-start.7 = (bf16[512,1536]{1,0:T(8,128)(2,1)}, bf16[512,1536]{1,0:T(8,128)(2,1)}, u32[]{:S(2)}, u32[]{:S(2)}) collective-permute-start(bf16[512,1536]{1,0:T(8,128)(2,1)} %slice.325), channel_id=1, source_target_pairs={{0,4},{4,0},{1,5},{5,1},{2,6},{6,2},{3,7},{7,3},{8,12},{12,8},{9,1... | collective-permute-start | bytes 4718600 | tf_op jit(solution)/shard_map/ppermute | solution.py:360
  230.0 71.1 %collective-permute-start.9 = (bf16[512,1536]{1,0:T(8,128)(2,1)}, bf16[512,1536]{1,0:T(8,128)(2,1)}, u32[]{:S(2)}, u32[]{:S(2)}) collective-permute-start(bf16[512,1536]{1,0:T(8,128)(2,1)} %fusion.15), channel_id=1, source_target_pairs={{0,1},{1,0},{2,3},{3,2},{4,5},{5,4},{6,7},{7,6},{8,9},{9,8},{10,11... | collective-permute-start | bytes 4718600 | tf_op jit(solution)/shard_map/ppermute | solution.py:441
  234.1 431.9 %reduce-scatter.9.cloned.1.call-start = ((), (), s32[]{:S(2)}) async-start(), calls=%async_computation.9 | async-start | bytes 3932160 | tf_op jit(solution)/shard_map/reduce_scatter | solution.py:382
  234.6 75.4 %collective-permute-start.12 = (bf16[512,1536]{1,0:T(8,128)(2,1)}, bf16[512,1536]{1,0:T(8,128)(2,1)S(1)}, u32[]{:S(2)}, u32[]{:S(2)}) collective-permute-start(bf16[512,1536]{1,0:T(8,128)(2,1)} %collective-permute-done.11), channel_id=1, source_target_pairs={{0,4},{4,0},{1,5},{5,1},{2,6},{6,2},{3,7},{7,3},{8,12},{12,8},{9,1... | collective-permute-start | bytes 4718600 | tf_op jit(solution)/shard_map/ppermute | solution.py:360
  268.9 41.2 %collective-permute-start.23 = (bf16[512,1536]{1,0:T(8,128)(2,1)}, bf16[512,1536]{1,0:T(8,128)(2,1)S(1)}, u32[]{:S(2)}, u32[]{:S(2)}) collective-permute-start(bf16[512,1536]{1,0:T(8,128)(2,1)} %collective-permute-done.22), channel_id=1, source_target_pairs={{0,4},{4,0},{1,5},{5,1},{2,6},{6,2},{3,7},{7,3},{8,12},{12,8},{9,1... | collective-permute-start | bytes 4718600 | tf_op jit(solution)/shard_map/ppermute | solution.py:360
  305.7 35.1 %collective-permute-start.20 = (bf16[512,1536]{1,0:T(8,128)(2,1)S(1)}, bf16[512,1536]{1,0:T(8,128)(2,1)}, u32[]{:S(2)}, u32[]{:S(2)}) collective-permute-start(bf16[512,1536]{1,0:T(8,128)(2,1)S(1)} %multiply_convert_fusion), channel_id=1, source_target_pairs={{0,1},{1,0},{2,3},{3,2},{4,5},{5,4},{6,7},{7,6},{8,9},{9,8},{10,11... | collective-permute-start | bytes 4718600 | tf_op jit(solution)/shard_map/ppermute | solution.py:364
  305.7 37.7 %collective-permute-start.10 = (bf16[512,1536]{1,0:T(8,128)(2,1)S(1)}, bf16[512,1536]{1,0:T(8,128)(2,1)S(1)}, u32[]{:S(2)}, u32[]{:S(2)}) collective-permute-start(bf16[512,1536]{1,0:T(8,128)(2,1)S(1)} %multiply_convert_fusion), channel_id=1, source_target_pairs={{0,4},{4,0},{1,5},{5,1},{2,6},{6,2},{3,7},{7,3},{8,12},{12,8},{9,1... | collective-permute-start | bytes 4718600 | tf_op jit(solution)/shard_map/ppermute | solution.py:360
  340.7 30.5 %collective-permute-start.21 = (bf16[512,1536]{1,0:T(8,128)(2,1)}, bf16[512,1536]{1,0:T(8,128)(2,1)}, u32[]{:S(2)}, u32[]{:S(2)}) collective-permute-start(bf16[512,1536]{1,0:T(8,128)(2,1)} %collective-permute-done.20), channel_id=1, source_target_pairs={{0,4},{4,0},{1,5},{5,1},{2,6},{6,2},{3,7},{7,3},{8,12},{12,8},{9,1... | collective-permute-start | bytes 4718600 | tf_op jit(solution)/shard_map/ppermute | solution.py:360
  402.5 294.0 %reduce-scatter.11.cloned.1.call-start = ((), (), s32[]{:S(2)}) async-start(), calls=%async_computation.10 | async-start | bytes 3932160 | tf_op jit(solution)/shard_map/reduce_scatter | solution.py:382
  413.7 44.2 %collective-permute-start.27 = (bf16[512,1536]{1,0:T(8,128)(2,1)}, bf16[512,1536]{1,0:T(8,128)(2,1)}, u32[]{:S(2)}, u32[]{:S(2)}) collective-permute-start(bf16[512,1536]{1,0:T(8,128)(2,1)} %slice.321), channel_id=1, source_target_pairs={{0,4},{4,0},{1,5},{5,1},{2,6},{6,2},{3,7},{7,3},{8,12},{12,8},{9,1... | collective-permute-start | bytes 4718600 | tf_op jit(solution)/shard_map/ppermute | solution.py:360
  429.4 15.9 %collective-permute-start.28 = (bf16[512,1536]{1,0:T(8,128)(2,1)}, bf16[512,1536]{1,0:T(8,128)(2,1)}, u32[]{:S(2)}, u32[]{:S(2)}) collective-permute-start(bf16[512,1536]{1,0:T(8,128)(2,1)} %slice.320), channel_id=1, source_target_pairs={{0,4},{4,0},{1,5},{5,1},{2,6},{6,2},{3,7},{7,3},{8,12},{12,8},{9,1... | collective-permute-start | bytes 4718600 | tf_op jit(solution)/shard_map/ppermute | solution.py:360
  438.6 15.0 %collective-permute-start.24 = (bf16[512,1536]{1,0:T(8,128)(2,1)}, bf16[512,1536]{1,0:T(8,128)(2,1)}, u32[]{:S(2)}, u32[]{:S(2)}) collective-permute-start(bf16[512,1536]{1,0:T(8,128)(2,1)} %slice.322), channel_id=1, source_target_pairs={{0,4},{4,0},{1,5},{5,1},{2,6},{6,2},{3,7},{7,3},{8,12},{12,8},{9,1... | collective-permute-start | bytes 4718600 | tf_op jit(solution)/shard_map/ppermute | solution.py:360
  444.8 258.2 %reduce-scatter.7.cloned.1.call-start = ((), (), s32[]{:S(2)}) async-start(), calls=%async_computation.8 | async-start | bytes 3932160 | tf_op jit(solution)/shard_map/reduce_scatter | solution.py:382
  448.4 37.2 %collective-permute-start.29 = (bf16[512,1536]{1,0:T(8,128)(2,1)S(1)}, bf16[512,1536]{1,0:T(8,128)(2,1)S(1)}, u32[]{:S(2)}, u32[]{:S(2)}) collective-permute-start(bf16[512,1536]{1,0:T(8,128)(2,1)S(1)} %fusion.8), channel_id=1, source_target_pairs={{0,1},{1,0},{2,3},{3,2},{4,5},{5,4},{6,7},{7,6},{8,9},{9,8},{10,11... | collective-permute-start | bytes 4718600 | tf_op jit(solution)/shard_map/ppermute | solution.py:441
  453.0 35.0 %collective-permute-start.19 = (bf16[512,1536]{1,0:T(8,128)(2,1)S(1)}, bf16[512,1536]{1,0:T(8,128)(2,1)S(1)}, u32[]{:S(2)}, u32[]{:S(2)}) collective-permute-start(bf16[512,1536]{1,0:T(8,128)(2,1)S(1)} %slice.323), channel_id=1, source_target_pairs={{0,4},{4,0},{1,5},{5,1},{2,6},{6,2},{3,7},{7,3},{8,12},{12,8},{9,1... | collective-permute-start | bytes 4718600 | tf_op jit(solution)/shard_map/ppermute | solution.py:360
  457.0 62.1 %collective-permute-start.25 = (bf16[512,1536]{1,0:T(8,128)(2,1)}, bf16[512,1536]{1,0:T(8,128)(2,1)S(1)}, u32[]{:S(2)}, u32[]{:S(2)}) collective-permute-start(bf16[512,1536]{1,0:T(8,128)(2,1)} %fusion.11), channel_id=1, source_target_pairs={{0,1},{1,0},{2,3},{3,2},{4,5},{5,4},{6,7},{7,6},{8,9},{9,8},{10,11... | collective-permute-start | bytes 4718600 | tf_op jit(solution)/shard_map/ppermute | solution.py:441
  524.7 36.5 %collective-permute-start.31 = (bf16[512,1536]{1,0:T(8,128)(2,1)}, bf16[512,1536]{1,0:T(8,128)(2,1)}, u32[]{:S(2)}, u32[]{:S(2)}) collective-permute-start(bf16[512,1536]{1,0:T(8,128)(2,1)} %get-tuple-element.74), channel_id=1, source_target_pairs={{0,1},{1,0},{2,3},{3,2},{4,5},{5,4},{6,7},{7,6},{8,9},{9,8},{10,11... | collective-permute-start | bytes 4718600 | tf_op jit(solution)/shard_map/ppermute | solution.py:364
  525.0 43.1 %collective-permute-start.30 = (bf16[512,1536]{1,0:T(8,128)(2,1)}, bf16[512,1536]{1,0:T(8,128)(2,1)}, u32[]{:S(2)}, u32[]{:S(2)}) collective-permute-start(bf16[512,1536]{1,0:T(8,128)(2,1)} %get-tuple-element.74), channel_id=1, source_target_pairs={{0,4},{4,0},{1,5},{5,1},{2,6},{6,2},{3,7},{7,3},{8,12},{12,8},{9,1... | collective-permute-start | bytes 4718600 | tf_op jit(solution)/shard_map/ppermute | solution.py:360
  561.2 16.1 %collective-permute-start.32 = (bf16[512,1536]{1,0:T(8,128)(2,1)}, bf16[512,1536]{1,0:T(8,128)(2,1)}, u32[]{:S(2)}, u32[]{:S(2)}) collective-permute-start(bf16[512,1536]{1,0:T(8,128)(2,1)} %collective-permute-done.31), channel_id=1, source_target_pairs={{0,4},{4,0},{1,5},{5,1},{2,6},{6,2},{3,7},{7,3},{8,12},{12,8},{9,1... | collective-permute-start | bytes 4718600 | tf_op jit(solution)/shard_map/ppermute | solution.py:360
  566.4 181.6 %reduce-scatter.13.cloned.1.call-start = ((), (), s32[]{:S(2)}) async-start(), calls=%async_computation.11 | async-start | bytes 4423680
  650.8 12.2 %collective-permute-start.34 = (bf16[512,1536]{1,0:T(8,128)(2,1)S(1)}, bf16[512,1536]{1,0:T(8,128)(2,1)S(1)}, u32[]{:S(2)}, u32[]{:S(2)}) collective-permute-start(bf16[512,1536]{1,0:T(8,128)(2,1)S(1)} %slice.318), channel_id=1, source_target_pairs={{0,4},{4,0},{1,5},{5,1},{2,6},{6,2},{3,7},{7,3},{8,12},{12,8},{9,1... | collective-permute-start | bytes 4718600 | tf_op jit(solution)/shard_map/ppermute | solution.py:360
  652.3 13.8 %collective-permute-start.26 = (bf16[512,1536]{1,0:T(8,128)(2,1)S(1)}, bf16[512,1536]{1,0:T(8,128)(2,1)}, u32[]{:S(2)}, u32[]{:S(2)}) collective-permute-start(bf16[512,1536]{1,0:T(8,128)(2,1)S(1)} %copy-done.46), channel_id=1, source_target_pairs={{0,0},{2,4},{4,2},{6,6},{1,1},{3,5},{5,3},{7,7},{8,8},{10,12},{12,... | collective-permute-start | bytes 4718600 | tf_op jit(solution)/shard_map/ppermute | solution.py:356
  660.8 57.5 %collective-permute-start.33 = (bf16[512,1536]{1,0:T(8,128)(2,1)}, bf16[512,1536]{1,0:T(8,128)(2,1)S(1)}, u32[]{:S(2)}, u32[]{:S(2)}) collective-permute-start(bf16[512,1536]{1,0:T(8,128)(2,1)} %slice.319), channel_id=1, source_target_pairs={{0,4},{4,0},{1,5},{5,1},{2,6},{6,2},{3,7},{7,3},{8,12},{12,8},{9,1... | collective-permute-start | bytes 4718600 | tf_op jit(solution)/shard_map/ppermute | solution.py:360
  664.6 62.8 %collective-permute-start.35 = (bf16[512,1536]{1,0:T(8,128)(2,1)}, bf16[512,1536]{1,0:T(8,128)(2,1)}, u32[]{:S(2)}, u32[]{:S(2)}) collective-permute-start(bf16[512,1536]{1,0:T(8,128)(2,1)} %fusion.5), channel_id=1, source_target_pairs={{0,1},{1,0},{2,3},{3,2},{4,5},{5,4},{6,7},{7,6},{8,9},{9,8},{10,11... | collective-permute-start | bytes 4718600 | tf_op jit(solution)/shard_map/ppermute | solution.py:441
  668.1 37.0 %collective-permute-start.41 = (bf16[192,1024]{1,0:T(8,128)(2,1)}, bf16[192,1024]{1,0:T(8,128)(2,1)}, u32[]{:S(2)}, u32[]{:S(2)}) collective-permute-start(bf16[192,1024]{1,0:T(8,128)(2,1)} %get-tuple-element.96), channel_id=1, source_target_pairs={{0,0},{2,4},{4,2},{6,6},{1,1},{3,5},{5,3},{7,7},{8,8},{10,12},{12,... | collective-permute-start | bytes 1179656 | tf_op jit(solution)/shard_map/ppermute | solution.py:386
  672.6 38.9 %collective-permute-start.42 = (bf16[192,1024]{1,0:T(8,128)(2,1)}, bf16[192,1024]{1,0:T(8,128)(2,1)}, u32[]{:S(2)}, u32[]{:S(2)}) collective-permute-start(bf16[192,1024]{1,0:T(8,128)(2,1)} %get-tuple-element.97), channel_id=1, source_target_pairs={{2,0},{6,2},{0,4},{4,6},{3,1},{7,3},{1,5},{5,7},{10,8},{14,10},{8,... | collective-permute-start | bytes 1179656 | tf_op jit(solution)/shard_map/ppermute | solution.py:387
  698.5 71.6 %collective-permute-start.43 = (bf16[192,1024]{1,0:T(8,128)(2,1)}, bf16[192,1024]{1,0:T(8,128)(2,1)}, u32[]{:S(2)}, u32[]{:S(2)}) collective-permute-start(bf16[192,1024]{1,0:T(8,128)(2,1)} %get-tuple-element.94), channel_id=1, source_target_pairs={{0,0},{2,4},{4,2},{6,6},{1,1},{3,5},{5,3},{7,7},{8,8},{10,12},{12,... | collective-permute-start | bytes 1179656 | tf_op jit(solution)/shard_map/ppermute | solution.py:386
  705.1 65.1 %collective-permute-start.44 = (bf16[192,1024]{1,0:T(8,128)(2,1)}, bf16[192,1024]{1,0:T(8,128)(2,1)}, u32[]{:S(2)}, u32[]{:S(2)}) collective-permute-start(bf16[192,1024]{1,0:T(8,128)(2,1)} %get-tuple-element.95), channel_id=1, source_target_pairs={{2,0},{6,2},{0,4},{4,6},{3,1},{7,3},{1,5},{5,7},{10,8},{14,10},{8,... | collective-permute-start | bytes 1179656 | tf_op jit(solution)/shard_map/ppermute | solution.py:387
  711.5 38.8 %collective-permute-start.39 = (bf16[192,1024]{1,0:T(8,128)(2,1)}, bf16[192,1024]{1,0:T(8,128)(2,1)}, u32[]{:S(2)}, u32[]{:S(2)}) collective-permute-start(bf16[192,1024]{1,0:T(8,128)(2,1)} %get-tuple-element.98), channel_id=1, source_target_pairs={{0,0},{2,4},{4,2},{6,6},{1,1},{3,5},{5,3},{7,7},{8,8},{10,12},{12,... | collective-permute-start | bytes 1179656 | tf_op jit(solution)/shard_map/ppermute | solution.py:386
  718.3 49.8 %collective-permute-start.40 = (bf16[192,1024]{1,0:T(8,128)(2,1)}, bf16[192,1024]{1,0:T(8,128)(2,1)S(1)}, u32[]{:S(2)}, u32[]{:S(2)}) collective-permute-start(bf16[192,1024]{1,0:T(8,128)(2,1)} %get-tuple-element.99), channel_id=1, source_target_pairs={{2,0},{6,2},{0,4},{4,6},{3,1},{7,3},{1,5},{5,7},{10,8},{14,10},{8,... | collective-permute-start | bytes 1179656 | tf_op jit(solution)/shard_map/ppermute | solution.py:387
  734.6 37.7 %collective-permute-start.36 = (bf16[512,1536]{1,0:T(8,128)(2,1)}, bf16[512,1536]{1,0:T(8,128)(2,1)}, u32[]{:S(2)}, u32[]{:S(2)}) collective-permute-start(bf16[512,1536]{1,0:T(8,128)(2,1)} %fusion.3), channel_id=1, source_target_pairs={{0,0},{2,4},{4,2},{6,6},{1,1},{3,5},{5,3},{7,7},{8,8},{10,12},{12,... | collective-permute-start | bytes 4718600 | tf_op jit(solution)/shard_map/ppermute | solution.py:356
  750.3 25.5 %collective-permute-start.37 = (bf16[192,1152]{1,0:T(8,128)(2,1)S(1)}, bf16[192,1152]{1,0:T(8,128)(2,1)S(1)}, u32[]{:S(2)}, u32[]{:S(2)}) collective-permute-start(bf16[192,1152]{1,0:T(8,128)(2,1)S(1)} %copy.51), channel_id=1, source_target_pairs={{0,0},{2,4},{4,2},{6,6},{1,1},{3,5},{5,3},{7,7},{8,8},{10,12},{12,... | collective-permute-start | bytes 1327112 | tf_op jit(solution)/shard_map/ppermute | solution.py:386
  768.1 35.8 %collective-permute-start.38 = (bf16[192,1152]{1,0:T(8,128)(2,1)S(1)}, bf16[192,1152]{1,0:T(8,128)(2,1)S(1)}, u32[]{:S(2)}, u32[]{:S(2)}) collective-permute-start(bf16[192,1152]{1,0:T(8,128)(2,1)S(1)} %copy.52), channel_id=1, source_target_pairs={{2,0},{6,2},{0,4},{4,6},{3,1},{7,3},{1,5},{5,7},{10,8},{14,10},{8,... | collective-permute-start | bytes 1327112 | tf_op jit(solution)/shard_map/ppermute | solution.py:387
  (99 other events, 1515.9 us)
Sparse Core Ops, SparseCore 0:
  26.2 58.6 all-gather.5
  87.3 44.0 all-gather.9
  154.4 44.7 all-gather.11
  234.2 52.2 all-gather.7
  402.6 44.7 reduce-scatter.8
  450.3 43.9 reduce-scatter.10
  566.5 44.1 reduce-scatter.6
  644.6 47.7 reduce-scatter.12

commit v2 on v1

--- a/solution.py
+++ b/solution.py
@@ -19,7 +19,9 @@
 query_scale = math.log2(math.e) * HEAD_SIZE ** (-0.5)
 rows_both = (((0,), (0,)), ((), ()))
 cols_both = (((1,), (1,)), ((), ()))
+plain = (((1,), (0,)), ((), ()))
 f32 = jnp.float32
+light = pl.CostEstimate(flops=1, bytes_accessed=1, transcendentals=0)
 bf16 = jnp.bfloat16
 
 
@@ -107,9 +109,7 @@
         compiler_params=pltpu.CompilerParams(
             vmem_limit_bytes=40 * 2**20, dimension_semantics=("arbitrary", "arbitrary")
         ),
-        cost_estimate=pl.CostEstimate(
-            flops=10 * length * length * q.shape[1], bytes_accessed=8 * length * q.shape[1], transcendentals=0
-        ),
+        cost_estimate=light,
         name="attend",
     )(place, q, k, v, start)
 
@@ -199,59 +199,70 @@
         lax.fori_loop(0, 2 * ring, finish, 0)
 
 
-def attend_back(place, q, k, v, o, do, lse, start, cos, sin, ring):
+def attend_back(place, q, k, v, o, do, lse, start, cos, sin, ring, head):
     length = q.shape[0]
     block = length // (2 * ring)
-    kv = k.shape[1] // LANES
     share = q.shape[1] // k.shape[1]
 
     def at(g, place_ref):
         return local_block(g, place_ref, ring)
 
-    qspec = pl.BlockSpec((block, share * LANES), lambda h, g, z: (at(g, z), h))
-    kspec = pl.BlockSpec((length, LANES), lambda h, g, z: (0, h))
+    qspec = pl.BlockSpec((block, share * LANES), lambda h, g, z: (at(g, z), head))
+    kspec = pl.BlockSpec((length, LANES), lambda h, g, z: (0, head))
+    qout = pl.BlockSpec((block, share * LANES), lambda h, g, z: (at(g, z), 0))
+    kout = pl.BlockSpec((length, LANES), lambda h, g, z: (0, 0))
     tableq = pl.BlockSpec((block, LANES), lambda h, g, z: (at(g, z), 0))
     tablek = pl.BlockSpec((length, LANES), lambda h, g, z: (0, 0))
     return pl.pallas_call(
         functools.partial(attend_back_kernel, ring, block),
         grid_spec=pltpu.PrefetchScalarGridSpec(
             num_scalar_prefetch=1,
-            grid=(kv, 2 * ring),
+            grid=(1, 2 * ring),
             in_specs=[
                 qspec,
                 kspec,
                 kspec,
                 qspec,
                 qspec,
-                pl.BlockSpec((1, share, block), lambda h, g, z: (h, 0, at(g, z))),
+                pl.BlockSpec((1, share, block), lambda h, g, z: (head, 0, at(g, z))),
                 pl.BlockSpec((1, block), lambda h, g, z: (0, at(g, z))),
                 tableq,
                 tableq,
                 tablek,
                 tablek,
             ],
-            out_specs=[qspec, kspec, kspec],
+            out_specs=[qout, kout, kout],
             scratch_shapes=[pltpu.VMEM((length, LANES), f32), pltpu.VMEM((length, LANES), f32)],
         ),
         out_shape=[
-            jax.ShapeDtypeStruct(q.shape, bf16),
-            jax.ShapeDtypeStruct(k.shape, bf16),
-            jax.ShapeDtypeStruct(k.shape, bf16),
+            jax.ShapeDtypeStruct((length, share * LANES), bf16),
+            jax.ShapeDtypeStruct((length, LANES), bf16),
+            jax.ShapeDtypeStruct((length, LANES), bf16),
         ],
         compiler_params=pltpu.CompilerParams(
             vmem_limit_bytes=40 * 2**20, dimension_semantics=("arbitrary", "arbitrary")
         ),
-        cost_estimate=pl.CostEstimate(
-            flops=20 * length * length * q.shape[1], bytes_accessed=16 * length * q.shape[1], transcendentals=0
-        ),
+        cost_estimate=light,
         name="attend_back",
     )(place, q, k, v, o, do, lse, start, cos, sin, cos, sin)
 
 
+def pieces_spec(block, width, count):
+    return [
+        pl.BlockSpec((block, width), lambda i: (jnp.minimum(i, count - 1), 0)),
+        pl.BlockSpec((block, width), lambda i: (jnp.maximum(i - count, 0), 0)),
+    ]
+
+
+def picked(count, first_ref, second_ref):
+    return jnp.where(pl.program_id(0) < count, first_ref[...], second_ref[...])
+
+
 def project_kernel(
-    widths, x_ref, gain_ref, w_ref, cos_ref, sin_ref, a_ref, q_ref, k_ref, v_ref
+    widths, count, x_ref, y_ref, gain_ref, w_ref, cos_ref, sin_ref, *refs
 ):
-    x = x_ref[...].astype(f32)
+    a_ref, q_ref, k_ref, v_ref = refs[-4:]
+    x = picked(count, x_ref, y_ref).astype(f32)
     root = lax.rsqrt(jnp.mean(x * x, -1, keepdims=True) + epsilon)
     a = (x * root * gain_ref[...]).astype(bf16)
     a_ref[...] = a
@@ -270,68 +281,229 @@
     v_ref[...] = whole[:, qw + kw :].astype(bf16)
 
 
-def project(x, gain, w, cos, sin, qw, kw):
-    rows, width = x.shape
+def project(pair, gain, w, cos, sin, qw, kw, step, before):
+    rows, width = pair[0].shape
+    length = cos.shape[0]
     block = min(256, rows)
+    count = rows // block
+    base = step * 2 * count
+    widths = (width, qw, kw, kw)
 
     def row(n):
-        return pl.BlockSpec((block, n), lambda i: (i, 0))
-
-    def whole(a):
-        return pl.BlockSpec(a.shape, lambda i: (0, 0))
+        return pl.BlockSpec((block, n), lambda i: (base + i, 0))
+
+    def whole(shape):
+        return pl.BlockSpec(shape, lambda i: (0, 0))
 
     return pl.pallas_call(
-        functools.partial(project_kernel, (qw, kw)),
-        grid=(rows // block,),
-        in_specs=[row(width), whole(gain), whole(w), row(LANES), row(LANES)],
-        out_specs=[row(width), row(qw), row(kw), row(kw)],
-        out_shape=[jax.ShapeDtypeStruct((rows, n), bf16) for n in (width, qw, kw, kw)],
+        functools.partial(project_kernel, (qw, kw), count),
+        grid=(2 * count,),
+        in_specs=pieces_spec(block, width, count)
+        + [whole(gain.shape), whole((width, qw + 2 * kw)), row(LANES), row(LANES)]
+        + [pl.BlockSpec(memory_space=pl.ANY)] * len(before),
+        out_specs=[row(n) for n in widths],
+        out_shape=[jax.ShapeDtypeStruct((length, n), bf16) for n in widths],
+        input_output_aliases={6 + i: i for i in range(len(before))},
         compiler_params=pltpu.CompilerParams(
             vmem_limit_bytes=40 * 2**20, dimension_semantics=("arbitrary",)
         ),
-        cost_estimate=pl.CostEstimate(
-            flops=2 * rows * width * w.shape[1], bytes_accessed=8 * rows * width, transcendentals=0
-        ),
+        cost_estimate=light,
         name="project",
-    )(x, gain, w, cos, sin)
-
-
-def hidden_kernel(chunk, a_ref, dy_ref, wg_ref, wu_ref, wd_ref, hid_ref, dg_ref, du_ref):
-    a = a_ref[...]
-    dy = dy_ref[...]
-    for j in range(wg_ref.shape[1] // chunk):
+    )(*pair, gain, w, cos, sin, *before)
+
+
+def hidden_kernel(
+    chunk, count, a_ref, b_ref, dy_ref, dz_ref, w_ref, hid_ref, dgu_ref, da_ref, mixed_ref
+):
+    a = picked(count, a_ref, b_ref)
+    dy = picked(count, dy_ref, dz_ref)
+    units = hid_ref.shape[1]
+    for j in range(units // chunk):
         at = slice(j * chunk, (j + 1) * chunk)
-        g = jnp.dot(a, wg_ref[:, at], preferred_element_type=f32)
-        u = jnp.dot(a, wu_ref[:, at], preferred_element_type=f32)
-        dh = jnp.dot(dy, wd_ref[:, at], preferred_element_type=f32)
+        up = slice(units + j * chunk, units + (j + 1) * chunk)
+        down = slice(2 * units + j * chunk, 2 * units + (j + 1) * chunk)
+        g = jnp.dot(a, w_ref[:, at], preferred_element_type=f32)
+        u = jnp.dot(a, w_ref[:, up], preferred_element_type=f32)
+        dh = jnp.dot(dy, w_ref[:, down], preferred_element_type=f32)
         sig = jax.nn.sigmoid(g)
         silu = g * sig
         hid_ref[:, at] = (silu * u).astype(bf16)
-        dg_ref[:, at] = (dh * u * (sig + silu * (1.0 - sig))).astype(bf16)
-        du_ref[:, at] = (dh * silu).astype(bf16)
-
-
-def hidden_pass(a, dy, wg, wu, wd):
-    rows, width = a.shape
-    units = wg.shape[1]
+        dgu_ref[:, at] = (dh * u * (sig + silu * (1.0 - sig))).astype(bf16)
+        dgu_ref[:, up] = (dh * silu).astype(bf16)
+    da_ref[...] = lax.dot_general(
+        dgu_ref[...], w_ref[:, : 2 * units], cols_both, preferred_element_type=f32
+    ).astype(bf16)
+    mixed_ref[...] = lax.dot_general(
+        hid_ref[...], w_ref[:, 2 * units :], cols_both, preferred_element_type=f32
+    ).astype(bf16)
+
+
+def hidden_pass(a, dy, w):
+    rows, width = a[0].shape
+    units = w.shape[1] // 3
     block = min(256, rows)
-    row = pl.BlockSpec((block, width), lambda i: (i, 0))
-    out = pl.BlockSpec((block, units), lambda i: (i, 0))
-    whole = pl.BlockSpec((width, units), lambda i: (0, 0))
+    count = rows // block
+    widths = [units, 2 * units, width, width]
+
+    def row(n):
+        return pl.BlockSpec((block, n), lambda i: (i, 0))
+
     return pl.pallas_call(
-        functools.partial(hidden_kernel, min(256, units)),
+        functools.partial(hidden_kernel, min(256, units), count),
+        grid=(2 * count,),
+        in_specs=pieces_spec(block, width, count)
+        + pieces_spec(block, width, count)
+        + [pl.BlockSpec(w.shape, lambda i: (0, 0), pipeline_mode=pl.Buffered(1))],
+        out_specs=[row(n) for n in widths],
+        out_shape=[jax.ShapeDtypeStruct((2 * rows, n), bf16) for n in widths],
+        compiler_params=pltpu.CompilerParams(
+            vmem_limit_bytes=40 * 2**20, dimension_semantics=("arbitrary",)
+        ),
+        cost_estimate=light,
+        name="hidden",
+    )(*a, *dy, w)
+
+
+def product_kernel(dims, x_ref, w_ref, *refs):
+    p = lax.dot_general(x_ref[...], w_ref[...], dims, preferred_element_type=f32)
+    out_ref = refs[-1]
+    for ref in refs[:-1]:
+        p = p + ref[...].astype(f32)
+    out_ref[...] = p.astype(out_ref.dtype)
+
+
+def product(x, w, dims, kind=bf16, rows=None, columns=(0, 1), add=None):
+    first, last = (0, x.shape[0]) if rows is None else (rows.start, rows.stop)
+    block = min(256, last - first)
+    wide = w.shape[1] // columns[1]
+    out = w.shape[0] if dims == cols_both else wide
+    row = pl.BlockSpec((block, out), lambda i: (i, 0))
+    extra = [] if add is None else [add]
+    return pl.pallas_call(
+        functools.partial(product_kernel, dims),
+        grid=((last - first) // block,),
+        in_specs=[
+            pl.BlockSpec((block, x.shape[1]), lambda i: (first // block + i, 0)),
+            pl.BlockSpec((w.shape[0], wide), lambda i: (0, columns[0])),
+        ]
+        + [row] * len(extra),
+        out_specs=row,
+        out_shape=jax.ShapeDtypeStruct((last - first, out), kind),
+        compiler_params=pltpu.CompilerParams(
+            vmem_limit_bytes=40 * 2**20, dimension_semantics=("arbitrary",)
+        ),
+        cost_estimate=light,
+        name="product",
+    )(x, w, *extra)
+
+
+def wgrad_kernel(counts, *refs):
+    out_ref = refs[-1]
+    j = pl.program_id(0)
+    first = 0
+    refs = refs[:-1]
+    for pieces, blocks in counts:
+        lefts, rights, refs = refs[:pieces], refs[pieces : 2 * pieces], refs[2 * pieces :]
+
+        @pl.when((j >= first) & (j < first + blocks))
+        def _():
+            total = None
+            for a, b in zip(lefts, rights):
+                p = lax.dot_general(a[...], b[...], rows_both, preferred_element_type=f32)
+                total = p if total is None else total + p
+            out_ref[...] = total.astype(bf16)
+
+        first += blocks
+
+
+def wgrad(groups, rows):
+    width = groups[0][0][0].shape[1]
+    block = min([512] + [group[0][2].shape[1] for group in groups])
+    counts, specs, args = [], [], []
+    first = 0
+    for group in groups:
+        blocks = group[0][2].shape[1] // block
+        counts.append((len(group), blocks))
+        for a, at, _, _ in group:
+            specs.append(
+                pl.BlockSpec(
+                    (rows, width), lambda j, at=at: (at, 0), pipeline_mode=pl.Buffered(1)
+                )
+            )
+            args.append(a)
+        for _, _, b, at in group:
+
+            def spot(j, at=at, first=first, blocks=blocks):
+                return (at, jnp.clip(j - first, 0, blocks - 1))
+
+            specs.append(pl.BlockSpec((rows, block), spot))
+            args.append(b)
+        first += blocks
+    return pl.pallas_call(
+        functools.partial(wgrad_kernel, counts),
+        grid=(first,),
+        in_specs=specs,
+        out_specs=pl.BlockSpec((width, block), lambda j: (0, j)),
+        out_shape=jax.ShapeDtypeStruct((width, first * block), bf16),
+        compiler_params=pltpu.CompilerParams(
+            vmem_limit_bytes=40 * 2**20, dimension_semantics=("arbitrary",)
+        ),
+        cost_estimate=light,
+        name="wgrad",
+    )(*args)
+
+
+def row_pass(body, name, inputs, whole, kinds):
+    width = inputs[0][0].shape[1]
+    rows = min(a.shape[0] - first for a, first in inputs)
+    block = min(256, rows)
+
+    def kernel(*refs):
+        count = len(inputs) + len(whole)
+        values = [ref[...].astype(f32) for ref in refs[:count]]
+        for ref, value in zip(refs[count:], body(*values)):
+            ref[...] = value.astype(ref.dtype)
+
+    return pl.pallas_call(
+        kernel,
         grid=(rows // block,),
-        in_specs=[row, row, whole, whole, whole],
-        out_specs=[out, out, out],
-        out_shape=[jax.ShapeDtypeStruct((rows, units), bf16)] * 3,
-        compiler_params=pltpu.CompilerParams(
-            vmem_limit_bytes=48 * 2**20, dimension_semantics=("arbitrary",)
-        ),
-        cost_estimate=pl.CostEstimate(
-            flops=6 * rows * width * units, bytes_accessed=4 * rows * width, transcendentals=0
-        ),
-        name="hidden",
-    )(a, dy, wg, wu, wd)
+        in_specs=[
+            pl.BlockSpec((block, width), lambda i, first=first: (first // block + i, 0))
+            for _, first in inputs
+        ]
+        + [pl.BlockSpec(a.shape, lambda i: (0, 0)) for a in whole],
+        out_specs=[pl.BlockSpec((block, width), lambda i: (i, 0)) for _ in kinds],
+        out_shape=[jax.ShapeDtypeStruct((rows, width), kind) for kind in kinds],
+        compiler_params=pltpu.CompilerParams(dimension_semantics=("arbitrary",)),
+        cost_estimate=light,
+        name=name,
+    )(*[a for a, _ in inputs], *whole)
+
+
+def inverse_root(x):
+    return lax.rsqrt(jnp.mean(x * x, -1, keepdims=True) + epsilon)
+
+
+def add_rows(*items):
+    return (sum_steps(items[0], items[1:]),)
+
+
+def norm_forward(stream, *rest):
+    *terms, gain = rest
+    middle = sum_steps(stream, terms)
+    return middle, middle * inverse_root(middle) * gain
+
+
+def norm_back(residual, values, *rest):
+    *terms, gain = rest
+    root = inverse_root(values)
+    scaled = sum_steps(terms[0], terms[1:]) * gain
+    out = (
+        residual
+        + root * scaled
+        - values * root**3 * jnp.mean(scaled * values, -1, keepdims=True)
+    )
+    return out, out
 
 
 def pad_heads(w):
@@ -347,13 +519,21 @@
 
 
 swap_two = [(0, 1), (1, 0)]
-cross_pairs = [(0, 0), (1, 2), (2, 1), (3, 3)]
+cross_pairs = [(1, 2), (2, 1)]
 slant_pairs = [(2 * c + zh, 2 * zh + (1 - c)) for c in range(2) for zh in range(2)]
 slant_back = [(b, a) for a, b in slant_pairs]
 
 
+def stays():
+    return lax.axis_index("c") == lax.axis_index("zh")
+
+
+def cross(a):
+    return lax.ppermute(a, ("c", "zh"), cross_pairs)
+
+
 def relay(a):
-    return lax.ppermute(a, ("c", "zh"), cross_pairs)
+    return jnp.where(stays(), a, cross(a))
 
 
 def other_core(a):
@@ -368,24 +548,46 @@
     return jnp.concatenate([a, other_core(a)], 0)
 
 
-def gather_weight(w):
-    straight = lax.ppermute(w, ("c", "zh"), cross_pairs)
-    slanted = lax.ppermute(w, ("c", "zh"), slant_pairs)
+def spread_pair(w):
+    return w, cross(w), lax.ppermute(w, ("c", "zh"), slant_pairs)
+
+
+def arrange(own, crossed, slanted):
     first = lax.axis_index("zh") == 0
-    both = jnp.concatenate(
+    straight = jnp.where(stays(), own, crossed)
+    return jnp.concatenate(
         [jnp.where(first, straight, slanted), jnp.where(first, slanted, straight)], 0
     )
-    return lax.all_gather(both, "d", axis=0, tiled=True)
-
-
-def settle_weight(grad):
-    part = lax.psum_scatter(grad.astype(bf16), "d", scatter_dimension=0, tiled=True)
+
+
+def gather_rows(w):
+    return lax.all_gather(w, "d", axis=0, tiled=True)
+
+
+def send_blocks(part):
     rows = part.shape[0] // 2
     first = lax.axis_index("zh") == 0
     upper, lower = part[:rows], part[rows:]
-    straight = lax.ppermute(jnp.where(first, upper, lower), ("c", "zh"), cross_pairs)
+    straight = jnp.where(first, upper, lower)
     slanted = lax.ppermute(jnp.where(first, lower, upper), ("c", "zh"), slant_back)
-    return straight.astype(f32) + slanted.astype(f32)
+    return straight, cross(straight), slanted
+
+
+def add_blocks(blocks):
+    straight, crossed, slanted = blocks
+    return jnp.where(stays(), straight, crossed).astype(f32) + slanted.astype(f32)
+
+
+def sum_rows(grad):
+    return lax.psum_scatter(grad.astype(bf16), "d", scatter_dimension=0, tiled=True)
+
+
+def after(first, then):
+    return lax.optimization_barrier((first, then))[1]
+
+
+def together(a, b):
+    return lax.optimization_barrier((a, b))
 
 
 def dot(a, b):
@@ -429,30 +631,67 @@
     rows = tokens.shape[0]
     length = 2 * ring * rows
 
-    def gather_chip(own):
-        return [both_cores(own if k == 0 else from_neighbour(own, k, ring)) for k in steps]
-
-    def scatter_sum(partials, kind):
-        kept = []
-        for k in reversed(steps):
-            p = partials[k]
-            joined = p[:rows].astype(f32) + other_core(p[rows:].astype(kind)).astype(f32)
-            if k:
-                moved = lax.ppermute(
-                    joined.astype(kind), "zl", [(i, (i + k) % ring) for i in steps]
-                )
-                joined = moved.astype(f32)
-            kept.append(joined)
-        return sum_steps(kept[-1], kept[:-1])
-
-    stream_own = relay(tokens)
-    attn_shard = jnp.concatenate([w_query, key_weight, value_weight, w_out], 1)
-    gains = lax.all_gather(
-        jnp.stack([norm1_gain, norm2_gain]), ("d", "c"), axis=1, tiled=True
-    ).astype(f32)
-    attn_full = gather_weight(attn_shard)
-    places = relay(positions).reshape(2, ring, rows)
-    chips = gather_chip(stream_own)
+    def swap_chips(own):
+        return [from_neighbour(own, k, ring) for k in steps[1:]]
+
+    def join_cores(partial, kind=bf16):
+        theirs = other_core(partial(slice(rows, 2 * rows), bf16))
+        return partial(slice(0, rows), kind, theirs)
+
+    def join(mine, theirs):
+        return row_pass(add_rows, "join", [(mine, 0), (theirs, 0)], [], [bf16])[0]
+
+    def chip_slice(k, r):
+        return slice(2 * rows * k + r.start, 2 * rows * k + r.stop)
+
+    def send_chips(joined):
+        return [
+            lax.ppermute(p.astype(bf16), "zl", [(i, (i + k) % ring) for i in steps])
+            for k, p in zip(steps[1:], joined)
+        ]
+
+    def pairs_of(kept, k):
+        out = []
+        for c in range(2):
+            for zh in range(2):
+                if (c == zh) == kept:
+                    base = (2 * c + zh) * ring
+                    out += [(base + i, base + (i - k) % ring) for i in steps]
+        return out
+
+    def early_neighbours(original):
+        return [
+            lax.ppermute(original, ("c", "zh", "zl"), pairs_of(True, k)) for k in steps if k
+        ]
+
+    def late_neighbours(moved):
+        return [lax.ppermute(moved, ("c", "zh", "zl"), pairs_of(False, k)) for k in steps[1:]]
+
+    def choose(early, late):
+        return [jnp.where(stays(), e, l) for e, l in zip(early, late)]
+
+    qcols, kcols = w_query.shape[1], key_weight.shape[1]
+    qw = qcols // HEAD_SIZE * LANES
+    kw = kcols // HEAD_SIZE * LANES
+    half = HEAD_SIZE // 2
+    attn_shard = pad_heads(jnp.concatenate([w_query, key_weight, value_weight, w_out], 1))
+    attn_shard = jnp.concatenate(
+        [
+            attn_shard[:, :half],
+            norm1_gain[:, None],
+            norm2_gain[:, None],
+            attn_shard[:, half + 2 :],
+        ],
+        1,
+    )
+    places = jnp.where(stays(), positions, other_core(positions)).reshape(2, ring, rows)
+    attn_shard = after(places, attn_shard)
+    attn_pair = spread_pair(attn_shard)
+    attn_rows = arrange(*attn_pair)
+    tokens = after(attn_rows, tokens)
+    attn_full = gather_rows(attn_rows)
+    stream_raw = cross(tokens)
+    tokens_early = early_neighbours(tokens)
 
     ordered = [
         lax.dynamic_index_in_dim(
@@ -471,107 +710,186 @@
         [f + jnp.arange(rows, dtype=jnp.int32) - o for f, o in zip(firsts, ordered)]
     )[None, :]
     spots = jnp.concatenate(ordered).astype(f32)
-    inverse = rope_base ** (-(2.0 / HEAD_SIZE) * jnp.arange(HEAD_SIZE // 2, dtype=f32))
+    inverse = rope_base ** (-(2.0 / HEAD_SIZE) * jnp.arange(half, dtype=f32))
     angles = spots[:, None] * inverse[None, :]
-    gap = jnp.zeros((length, LANES // 2 - HEAD_SIZE // 2), f32)
+    gap = jnp.zeros((length, LANES // 2 - half), f32)
     cos_half, sin_half = jnp.cos(angles), jnp.sin(angles)
     cos = jnp.concatenate([cos_half, gap, cos_half, gap], 1)
     sin = jnp.concatenate([-sin_half, gap, sin_half, gap], 1)
 
-    qcols, kcols = w_query.shape[1], key_weight.shape[1]
-    padded = pad_heads(attn_full)
-    qw = qcols // HEAD_SIZE * LANES
-    kw = kcols // HEAD_SIZE * LANES
-    w_qkv = padded[:, : qw + 2 * kw]
-    w_o = padded[:, qw + 2 * kw :]
-    gain_first, gain_second = gains[0:1], gains[1:2]
-
-    pieces = [
-        project(
-            x,
-            gain_first,
-            w_qkv,
-            cos[2 * rows * k : 2 * rows * (k + 1)],
-            sin[2 * rows * k : 2 * rows * (k + 1)],
-            qw,
-            kw,
+    stream_raw, tokens_early = after((cos, sin, start), (stream_raw, tokens_early))
+    ff_cols = after((stream_raw, tokens_early), jnp.concatenate([w_gate, w_up, w_down], 1))
+    stream_own = jnp.where(stays(), tokens, stream_raw)
+    tokens_late = late_neighbours(stream_raw)
+    ff_pair = spread_pair(ff_cols)
+
+    out_columns = ((qw + 2 * kw) // qw, (qw + 2 * kw) // qw + 1)
+    gain_first = attn_full[:, half].astype(f32)[None, :]
+    gain_second = attn_full[:, half + 1].astype(f32)[None, :]
+
+    projected = project(
+        (stream_own, other_core(stream_own)), gain_first, attn_full, cos, sin, qw, kw, 0, ()
+    )
+    (tokens_late, ff_pair), projected = together((tokens_late, ff_pair), projected)
+    others = [(x, other_core(x)) for x in choose(tokens_early, tokens_late)]
+    others, ff_pair = together(others, ff_pair)
+    ff_rows = arrange(*ff_pair)
+    ff_full = gather_rows(ff_rows)
+    cot_sent = after(others, cotangent)
+    cot_raw = cross(cot_sent)
+    cot_early = early_neighbours(cot_sent)
+    for k, pair in enumerate(others, 1):
+        projected = project(pair, gain_first, attn_full, cos, sin, qw, kw, k, projected)
+    normed_first, q, k, v = projected
+    o, lse = attend(place, q, k, v, start, ring)
+    o, (cot_raw, cot_early) = together(o, (cot_raw, cot_early))
+
+    def out_product(k):
+        return lambda r, kind, add=None: product(
+            o, attn_full, cols_both, kind, chip_slice(k, r), out_columns, add
         )
-        for k, x in enumerate(chips)
-    ]
-    normed_first = [p[0] for p in pieces]
-    q, k, v = (jnp.concatenate([p[i] for p in pieces], 0) for i in (1, 2, 3))
-    o, lse = attend(place, q, k, v, start, ring)
-
-    stream = stream_own.astype(f32)
-    chip_rows = [slice(2 * rows * i, 2 * rows * (i + 1)) for i in steps]
-    middle = stream + scatter_sum([dot_cols(o[r], w_o) for r in chip_rows], bf16)
-    root_second = lax.rsqrt(jnp.mean(middle * middle, -1, keepdims=True) + epsilon)
-    normed_second = (middle * root_second * gain_second).astype(bf16)
-
-    wg_full = gather_weight(w_gate)
-    wu_full = gather_weight(w_up)
-    wd_full = gather_weight(w_down)
-    cot_own = relay(cotangent)
-    out_grads = gather_chip(cot_own)
-    ff_in = gather_chip(normed_second)
-
-    hidden = [
-        hidden_pass(a, dy, wg_full, wu_full, wd_full) for a, dy in zip(ff_in, out_grads)
-    ]
-    second_grad = scatter_sum(
-        [dot_cols(h[1], wg_full) + dot_cols(h[2], wu_full) for h in hidden], bf16
-    )
-    mixed = middle + scatter_sum([dot_cols(h[0], wd_full) for h in hidden], bf16)
-    mixed = relay(mixed.astype(bf16))
-
-    down_wgrad = sum_steps(0.0, [dot_rows(dy, h[0]) for dy, h in zip(out_grads, hidden)])
-    gate_wgrad = sum_steps(0.0, [dot_rows(a, h[1]) for a, h in zip(ff_in, hidden)])
-    up_wgrad = sum_steps(0.0, [dot_rows(a, h[2]) for a, h in zip(ff_in, hidden)])
-
-    scaled = second_grad * gain_second
-    middle_grad = (
-        cot_own.astype(f32)
-        + root_second * scaled
-        - middle * root_second**3 * jnp.mean(scaled * middle, -1, keepdims=True)
-    )
-    branch = gather_chip(middle_grad.astype(bf16))
-    do = jnp.concatenate([dot(b, w_o).astype(bf16) for b in branch], 0)
-    out_wgrad = sum_steps(0.0, [dot_rows(b, o[r]) for b, r in zip(branch, chip_rows)])
-    dq, dk, dv = attend_back(place, q, k, v, o, do, lse, start, cos, sin, ring)
-    dqkv = jnp.concatenate([dq, dk, dv], 1)
-    first_grad = scatter_sum([dot_cols(dqkv[r], w_qkv) for r in chip_rows], bf16)
-    qkv_wgrad = sum_steps(0.0, [dot_rows(a, dqkv[r]) for a, r in zip(normed_first, chip_rows)])
-
-    root_first = lax.rsqrt(jnp.mean(stream * stream, -1, keepdims=True) + epsilon)
-    scaled = first_grad * gain_first
-    input_grad = (
-        middle_grad
-        + root_first * scaled
-        - stream * root_first**3 * jnp.mean(scaled * stream, -1, keepdims=True)
-    )
-    input_grad = relay(input_grad.astype(bf16)).astype(f32)
-
-    grad_down = settle_weight(down_wgrad)
-    grad_gate = settle_weight(gate_wgrad)
-    grad_up = settle_weight(up_wgrad)
-    grad_attn = settle_weight(cut_heads(jnp.concatenate([qkv_wgrad, out_wgrad], 1)))
+
+    def whole_rows(*arrays):
+        return [(a, 0) for a in arrays]
+
+    sent = send_chips([join_cores(out_product(k)) for k in steps[1:]])
+    joined = join_cores(out_product(0))
+    cot_own = after(joined, jnp.where(stays(), cotangent, cot_raw))
+    sent = after((joined, cot_own), sent)
+    middle, normed_second = row_pass(
+        norm_forward,
+        "norm_forward",
+        whole_rows(stream_own, joined, *sent),
+        [gain_second],
+        [f32, bf16],
+    )
+
+    ff_others = swap_chips(normed_second)
+    cot_late = late_neighbours(after(normed_second, cot_own))
+    ff_in = [(normed_second, other_core(normed_second))]
+    out_grads = [(cot_own, other_core(cot_own))]
+    hidden = [hidden_pass(ff_in[0], out_grads[0], ff_full)]
+    hidden[0], (ff_others, cot_late) = together(hidden[0], (ff_others, cot_late))
+
+    def halves(array):
+        return [array, other_core(array[rows:])]
+
+    second_own = halves(hidden[0][2])
+    mixed_own = halves(hidden[0][3])
+    for a, dy in zip(ff_others, choose(cot_early, cot_late)):
+        ff_in.append((a, other_core(a)))
+        out_grads.append((dy, other_core(dy)))
+        hidden.append(hidden_pass(ff_in[-1], out_grads[-1], ff_full))
+
+    def pieces(pairs, hidden, i):
+        return [(a, 0, h[i], j) for pair, h in zip(pairs, hidden) for j, a in enumerate(pair)]
+
+    joined = [join(*halves(h[2])) for h in hidden[1:]]
+    mixed_joined = [join(*halves(h[3])) for h in hidden[1:]]
+    sent = send_chips(joined)
+    (mixed_joined, second_own, mixed_own), hidden = after(
+        joined, ((mixed_joined, second_own, mixed_own), hidden)
+    )
+    down_wgrad = wgrad([pieces(out_grads, hidden, 0)], rows)
+    sent = after((mixed_joined, down_wgrad), sent)
+    down_part = sum_rows(after(sent, down_wgrad))
+    middle_grad, db = row_pass(
+        norm_back,
+        "norm_back",
+        whole_rows(cot_own, middle, *second_own, *sent),
+        [gain_second],
+        [f32, bf16],
+    )
+    branch_others = swap_chips(db)
+    branch = [(db, other_core(db))]
+    do = [product(b, attn_full, plain, columns=out_columns) for b in branch[0]]
+    gate_up_wgrad = wgrad([pieces(ff_in, after(do, hidden), 1)], rows)
+    branch_others = after(gate_up_wgrad, branch_others)
+    gate_up_part = sum_rows(after(branch_others, gate_up_wgrad))
+    mixed_joined, down_part = after(branch_others, (mixed_joined, down_part))
+    mixed_sent = send_chips(mixed_joined)
+    down_blocks = send_blocks(down_part)
+    for b in branch_others:
+        branch.append((b, other_core(b)))
+        do += [product(b, attn_full, plain, columns=out_columns) for b in branch[-1]]
+    do = jnp.concatenate(do, 0)
+    heads = []
+    kvheads = kw // LANES
+    for h in range(kvheads):
+        part = attend_back(place, q, k, v, o, do, lse, start, cos, sin, ring, h)
+        if h == 0:
+            (mixed_sent, down_blocks), (part, do) = together(
+                (mixed_sent, down_blocks), (part, do)
+            )
+            mixed = row_pass(
+                add_rows, "mixed", whole_rows(middle, *mixed_own, *mixed_sent), [], [bf16]
+            )[0]
+            mixed_raw = cross(mixed)
+        heads.append(part)
+    mixed_raw, heads = together(mixed_raw, heads)
+    mixed = jnp.where(stays(), mixed, mixed_raw)
+    gate_up_blocks = send_blocks(after(heads, gate_up_part))
+    dqkv = jnp.concatenate([h[i] for i in range(3) for h in heads], 1)
+    grad_down = add_blocks(down_blocks)
+
+    def first_product(k, dqkv):
+        return lambda r, kind, add=None: product(
+            dqkv, w_qkv, cols_both, kind, chip_slice(k, r), add=add
+        )
+
+    w_qkv = attn_full[:, : qw + 2 * kw]
+    blocks = range(2 * ring)
+    attn_wgrad = wgrad(
+        [
+            [(normed_first, i, dqkv, i) for i in blocks],
+            [(b, 0, o, i) for i, b in zip(blocks, sum(branch, ()))],
+        ],
+        rows,
+    )
+    attn_part = sum_rows(after(gate_up_part, attn_wgrad))
+    dqkv = after(attn_wgrad, dqkv)
+    joined = [join_cores(first_product(k, dqkv)) for k in steps[1:]]
+    sent = send_chips(joined)
+    dqkv = after(joined, dqkv)
+    first_own = join_cores(first_product(0, dqkv))
+    sent, (first_own, gate_up_blocks) = together(sent, (first_own, gate_up_blocks))
+    input_grad = row_pass(
+        norm_back,
+        "norm_back",
+        whole_rows(middle_grad, stream_own, first_own, *sent),
+        [gain_first],
+        [bf16, bf16],
+    )[0]
+    input_raw = cross(input_grad)
+    attn_blocks = send_blocks(attn_part)
+
+    def weighed(weights, part):
+        weights = weights[:, : part.shape[1]]
+        return jnp.sum(weights.astype(f32) * part.astype(f32), 1).reshape(2, -1)
+
+    gain_parts = jnp.stack(
+        [
+            weighed(attn_rows, attn_part[:, : qw + 2 * kw]),
+            weighed(ff_rows, gate_up_part),
+        ]
+    )
+    gain_parts = jnp.where(core == 0, gain_parts, gain_parts[:, ::-1])
+    gain_grads = gain_parts[:, 0] + other_core(gain_parts[:, 1])
+    for k in steps[1:]:
+        gain_parts = from_neighbour(gain_grads, k, ring) + (gain_parts if k > 1 else gain_grads)
+    gain_grads = gain_parts if ring > 1 else gain_grads
+    gain_grads = gain_grads + lax.ppermute(gain_grads, "zh", swap_two)
+    (input_raw, attn_blocks), gain_grads = together((input_raw, attn_blocks), gain_grads)
+    input_grad = jnp.where(stays(), input_grad, input_raw).astype(f32)
+    grad_gate_up = add_blocks(gate_up_blocks)
+    grad_attn = cut_heads(add_blocks(attn_blocks))
     grad_query = grad_attn[:, :qcols]
     grad_key = grad_attn[:, qcols : qcols + kcols]
     grad_value = grad_attn[:, qcols + kcols : qcols + 2 * kcols]
     grad_output = grad_attn[:, qcols + 2 * kcols :]
-
-    def weighed(*pairs):
-        return sum_steps(0.0, [jnp.sum(w.astype(f32) * g, 1) for w, g in pairs])
-
-    gain_grads = lax.psum(
-        jnp.stack(
-            [
-                weighed((w_query, grad_query), (key_weight, grad_key), (value_weight, grad_value)),
-                weighed((w_gate, grad_gate), (w_up, grad_up)),
-            ]
-        ),
-        ("zh", "zl"),
-    )
+    grad_gate = grad_gate_up[:, : w_gate.shape[1]]
+    grad_up = grad_gate_up[:, w_gate.shape[1] :]
+
     return (
         mixed,
         input_grad,

time: 835 us -> 708 us (0.85)
  Pallas kernels: 112 us -> 227 us
  matrix products: 96.1 us -> 0 us
  waiting for transfers between devices: 257 us -> 195 us
  blocking collectives: 47.9 us -> 0 us
  other arithmetic: 67.9 us -> 31.3 us
  local copies, waits for them, and re-layouts: 71.7 us -> 83.4 us
  starting transfers between devices: 157 us -> 146 us
    pallas_call x4 -> x25, Pallas kernels: 42.3 us -> 158 us  [the longest x2 52.1 us: hidden_pass(): pl.pallas_call(functools.partial(hidden_kernel, min(256, units), count),...]
    dot_general x22 -> x0, matrix products: 96.1 us -> none  [the longest x10 52.2 us: dot_rows(): return lax.dot_general(a, b, rows_both, preferred_element_type=f32)]
    ppermute x4 -> x3, waiting for transfers between devices: 88.8 us -> 13.4 us  [from_neighbour(): return lax.ppermute(a, 'zl', [(i, (i - k) % ring) for i in range(ring)])]
    all_gather x1 -> x0, blocking collectives: 39.5 us -> none  [per_device(): lax.all_gather(jnp.stack([norm1_gain, norm2_gain]), ('d', 'c'), axis=1, t...]
    ppermute x16 -> x18, starting transfers between devices: 27.2 us -> 59.5 us  [other_core(): return lax.ppermute(a, 'c', swap_two)]
    ppermute x25 -> x23, starting transfers between devices: 108 us -> 81.4 us  [the longest x1 25.2 us: per_device(): gain_grads = gain_grads + lax.ppermute(gain_grads, 'zh', swap_two)]
    unnamed x203 -> x211, local copies, waits for them, and re-layouts: 52.3 us -> 72.8 us
    convert_element_type x9 -> x2, other arithmetic: 23.1 us -> 3.66 us  [the longest x1 1.88 us: per_device(): input_grad = jnp.where(stays(), input_grad, input_raw).astype(f32)]
  transfers between devices with their start and end apart: 53 -> 49, of which waited for: 13 -> 18; matrix products, arithmetic and copies ran while one was open for 23% -> 5% of each run, Pallas kernels for 12% -> 29%
where the time goes in v2:
time: 708 us; the launch traced here: 698 us
  Pallas kernels  227 us (32%)
  waiting for transfers between devices  195 us (28%)
  starting transfers between devices  146 us (21%)
  local copies, waits for them, and re-layouts  83.4 us (12%)
  other arithmetic  31.3 us (4%)
  between operations  15.6 us (2%)
    ppermute x4, waiting for transfers between devices, send_chips(): lax.ppermute(p.astype(bf16), 'zl', [(i, (i + k) % ring) for i in steps])  87.7 us
    unnamed x211, local copies, waits for them, and re-layouts  72.8 us
    ppermute x18, starting transfers between devices, other_core(): return lax.ppermute(a, 'c', swap_two)  59.5 us
    pallas_call x2, Pallas kernels, hidden_pass(): pl.pallas_call(functools.partial(hidden_kernel, min(256, units), count),...  52.1 us
    pallas_call x3, Pallas kernels, wgrad(): pl.pallas_call(functools.partial(wgrad_kernel, counts), grid=(first,), in...  42.5 us
    pallas_call x2, Pallas kernels, attend_back(): pl.pallas_call(functools.partial(attend_back_kernel, ring, block), grid_s...  41.8 us
    ppermute x2, waiting for transfers between devices, early_neighbours(): lax.ppermute(original, ('c', 'zh', 'zl'), pairs_of(True, k))  28.3 us
    pallas_call x6, Pallas kernels, row_pass(): pl.pallas_call(kernel, grid=(rows // block,), in_specs=[pl.BlockSpec((blo...  26.9 us
  transfers between devices with their start and end apart: 49, of which 18 were waited for; matrix products, arithmetic and copies ran while one was open for 5% of the time, Pallas kernels for 29%

profile of v2, /device:TPU:0, one launch (start us, length us, event | category | flops | bytes accessed | tf_op | source)
XLA Modules:
  0.0 698.3 jit_solution(12205733539883300338)
XLA Ops:
  13.8 3.7 collective-permute-start.2
  18.2 11.2 %collective-permute-done.2 = bf16[192,1536]{1,0:T(8,128)(2,1)S(1)} collective-permute-done((bf16[192,1536]{1,0:T(8,128)(2,1)S(1)}, bf16[192,1536]{1,0:T(8,128)(2,1)S(1)}, u32[]{:S(2)}, u32[]{:S(2)}) %collective-permute-start.2) | collective-permute-done | bytes 589856 | tf_op jit(solution)/shard_map/ppermute | solution.py:552
  33.6 17.7 %collective-permute-start.4 = (bf16[512,1536]{1,0:T(8,128)(2,1)}, bf16[512,1536]{1,0:T(8,128)(2,1)S(1)}, u32[]{:S(2)}, u32[]{:S(2)}) collective-permute-start(bf16[512,1536]{1,0:T(8,128)(2,1)} %param.12), channel_id=1, source_target_pairs={{0,1},{1,0},{6,7},{7,6},{8,9},{9,8},{14,15},{15,14},{16,17},{17,16... | collective-permute-start | bytes 4718600 | tf_op jit(solution)/shard_map/ppermute | solution.py:664
  51.4 3.7 fusion.4
  56.4 28.3 %collective-permute-done.4 = bf16[512,1536]{1,0:T(8,128)(2,1)S(1)} collective-permute-done((bf16[512,1536]{1,0:T(8,128)(2,1)}, bf16[512,1536]{1,0:T(8,128)(2,1)S(1)}, u32[]{:S(2)}, u32[]{:S(2)}) %collective-permute-start.4) | collective-permute-done | bytes 1572896 | tf_op jit(solution)/shard_map/ppermute | solution.py:664
  84.7 3.3 broadcast_select_fusion.4.x_ref.refs_0_.refs_1_
  94.1 2.9 collective-permute-start.7
  97.0 8.2 %all-gather.3.cloned.1.call-done.w_ref = bf16[1536,1536]{1,0:T(8,128)(2,1)} async-done(((bf16[384,1536]{1,0:T(8,128)(2,1)}), bf16[1536,1536]{1,0:T(8,128)(2,1)}) %all-gather.3.cloned.1.call-update) | async-done | bytes 4718608 | tf_op jit(solution)/shard_map/all_gather | solution.py:564
  109.4 7.5 %project.2 = (bf16[2048,1536]{1,0:T(8,128)(2,1)}, bf16[2048,512]{1,0:T(8,128)(2,1)S(1)}, bf16[2048,256]{1,0:T(8,128)(2,1)S(1)}, bf16[2048,256]{1,0:T(8,128)(2,1)S(1)}) custom-call(bf16[512,1536]{1,0:T(8,128)(2,1)} %broadcast_select_fusion.4.x_ref.refs_0_.refs_1_, bf16[512,1536]{1,0:T(8,128)(2,1)} %collective-permute-done.8.y_ref, ...), custom_call_target="tpu_custom_call" | custom-call | flops 1 | bytes 1 | tf_op jit(solution)/shard_map/project/pallas_call | solution.py:298
  116.9 6.9 collective-permute-done.7
  124.0 26.8 %collective-permute-start.9 = (bf16[512,1536]{1,0:T(8,128)(2,1)S(1)}, bf16[512,1536]{1,0:T(8,128)(2,1)S(1)}, u32[]{:S(2)}, u32[]{:S(2)}) collective-permute-start(bf16[512,1536]{1,0:T(8,128)(2,1)S(1)} %broadcast_select_fusion.3.x_ref), channel_id=1, source_target_pairs={{0,4},{4,0},{1,5},{5,1},{2,6},{6,2},{3,7},{7,3},{8,12},{12,8},{9,1... | collective-permute-start | bytes 4718600 | tf_op jit(solution)/shard_map/ppermute | solution.py:540
  150.8 3.0 collective-permute-done.9.y_ref
  153.9 2.4 broadcast_select_fusion.7
  172.8 6.2 project.3
  180.3 2.3 copy-done.16
  182.6 26.6 %attend.1 = (bf16[2048,512]{1,0:T(8,128)(2,1)S(1)}, f32[2,2,2048]{2,1,0:T(2,128)S(1)}) custom-call(s32[2]{0:T(128)S(1)} %pad_add_fusion.1.place_ref, bf16[2048,512]{1,0:T(8,128)(2,1)S(1)} %copy-done.16, bf16[2048,256]{1,0:T(8,128)(2,1)S(1)} %get-tuple-element.137.k_ref, bf16[2048,256]{1,0:T(8,128)(2,1)S(1)} %get-tuple-element.138.v_ref, s32[1,2048]{1,0:T(1,128)S(1)} %bitcast.22), custom_call_target="tpu_custom_call" | custom-call | flops 1 | bytes 1 | tf_op jit(solution)/shard_map/attend/pallas_call | solution.py:89
  222.0 30.5 %collective-permute-done.14.refs_2_ = bf16[512,1536]{1,0:T(8,128)(2,1)} collective-permute-done((bf16[512,1536]{1,0:T(8,128)(2,1)S(1)}, bf16[512,1536]{1,0:T(8,128)(2,1)}, u32[]{:S(2)}, u32[]{:S(2)}) %collective-permute-start.14) | collective-permute-done | bytes 1572896 | tf_op jit(solution)/shard_map/ppermute | solution.py:649
  252.5 4.6 norm_forward.1
  265.0 26.0 %hidden.2 = (bf16[1024,1024]{1,0:T(8,128)(2,1)S(1)}, bf16[1024,2048]{1,0:T(8,128)(2,1)}, bf16[1024,1536]{1,0:T(8,128)(2,1)S(1)}, bf16[1024,1536]{1,0:T(8,128)(2,1)}) custom-call(bf16[512,1536]{1,0:T(8,128)(2,1)S(1)} %copy-done.41, bf16[512,1536]{1,0:T(8,128)(2,1)S(1)} %copy-done.44, bf16[512,1536]{1,0:T(8,128)(2,1)} %broadcast_select_fusion.2.dy_ref.refs_0_, ...), custom_call_target="tpu_custom_call" | custom-call | flops 1 | bytes 1 | tf_op jit(solution)/shard_map/hidden/pallas_call | solution.py:351
  291.0 3.6 collective-permute-done.17.a_ref.refs_2_
  294.6 16.3 %collective-permute-start.19 = (bf16[512,1536]{1,0:T(8,128)(2,1)}, bf16[512,1536]{1,0:T(8,128)(2,1)S(1)}, u32[]{:S(2)}, u32[]{:S(2)}) collective-permute-start(bf16[512,1536]{1,0:T(8,128)(2,1)} %collective-permute-done.17.a_ref.refs_2_), channel_id=1, source_target_pairs={{0,4},{4,0},{1,5},{5,1},{2,6},{6,2},{3,7},{7,3},{8,12},{12,8},{9,1... | collective-permute-start | bytes 4718600 | tf_op jit(solution)/shard_map/ppermute | solution.py:540
  316.2 26.2 %hidden.3 = (bf16[1024,1024]{1,0:T(8,128)(2,1)S(1)}, bf16[1024,2048]{1,0:T(8,128)(2,1)}, bf16[1024,1536]{1,0:T(8,128)(2,1)S(1)}, bf16[1024,1536]{1,0:T(8,128)(2,1)}) custom-call(bf16[512,1536]{1,0:T(8,128)(2,1)} %collective-permute-done.17.a_ref.refs_2_, bf16[512,1536]{1,0:T(8,128)(2,1)S(1)} %collective-permute-done.19.b_ref.refs_3_, ...), custom_call_target="tpu_custom_call" | custom-call | flops 1 | bytes 1 | tf_op jit(solution)/shard_map/hidden/pallas_call | solution.py:351
  350.7 2.9 join.2
  355.3 2.9 join.3
  364.3 9.4 %wgrad.3 = bf16[1536,1024]{1,0:T(8,128)(2,1)S(1)} custom-call(bf16[512,1536]{1,0:T(8,128)(2,1)} %broadcast_select_fusion.2.dy_ref.refs_0_, bf16[512,1536]{1,0:T(8,128)(2,1)} %collective-permute-done.16.dz_ref.refs_1_, bf16[512,1536]{1,0:T(8,128)(2,1)S(1)} %copy-done.33, bf16[512,1536]{1,0:T(8,128)(2,1)S(1)} %copy-done.53, bf16[1024,1024]{1,0:T(8,128)(2,1)S(1)} %copy-done.36, ...), custom_call_target="tpu_custom_call" | custom-call | flops 1 | bytes 1 | tf_op jit(solution)/shard_map/wgrad/pallas_call | solution.py:442
  375.4 15.0 %collective-permute-done.25.refs_4_ = bf16[512,1536]{1,0:T(8,128)(2,1)} collective-permute-done((bf16[512,1536]{1,0:T(8,128)(2,1)}, bf16[512,1536]{1,0:T(8,128)(2,1)}, u32[]{:S(2)}, u32[]{:S(2)}) %collective-permute-start.25) | collective-permute-done | bytes 1572896 | tf_op jit(solution)/shard_map/ppermute | solution.py:649
  390.4 6.3 norm_back.2
  407.0 17.3 %wgrad.4 = bf16[1536,2048]{1,0:T(8,128)(2,1)} custom-call(bf16[512,1536]{1,0:T(8,128)(2,1)S(1)} %copy-done.42, bf16[512,1536]{1,0:T(8,128)(2,1)S(1)} %copy-done.45, bf16[512,1536]{1,0:T(8,128)(2,1)} %collective-permute-done.17.a_ref.refs_2_, bf16[512,1536]{1,0:T(8,128)(2,1)S(1)} %copy-done.47, bf16[1024,2048]{1,0:T(8,128)(2,1)S(1)} %copy-done.21, ...), custom_call_target="tpu_custom_call" | custom-call | flops 1 | bytes 1 | tf_op jit(solution)/shard_map/wgrad/pallas_call | solution.py:442
  424.4 9.5 %collective-permute-done.27.x_ref.refs_10_ = bf16[512,1536]{1,0:T(8,128)(2,1)} collective-permute-done((bf16[512,1536]{1,0:T(8,128)(2,1)}, bf16[512,1536]{1,0:T(8,128)(2,1)}, u32[]{:S(2)}, u32[]{:S(2)}) %collective-permute-start.27) | collective-permute-done | bytes 1572896 | tf_op jit(solution)/shard_map/ppermute | solution.py:544
  438.6 3.8 collective-permute-start.30
  442.4 2.5 copy-done.3
  445.0 2.4 product.18
  447.4 2.5 product.19
  452.8 20.8 %attend_back.2 = (bf16[2048,256]{1,0:T(8,128)(2,1)S(1)}, bf16[2048,128]{1,0:T(8,128)(2,1)S(1)}, bf16[2048,128]{1,0:T(8,128)(2,1)S(1)}) custom-call(s32[2]{0:T(128)S(1)} %pad_add_fusion.1.place_ref, bf16[2048,512]{1,0:T(8,128)(2,1)S(1)} %copy-done.17, bf16[2048,256]{1,0:T(8,128)(2,1)S(1)} %copy-done.25, bf16[2048,256]{1,0:T(8,128)(2,1)S(1)} %copy-done.30, ...), custom_call_target="tpu_custom_call" | custom-call | flops 1 | bytes 1 | tf_op jit(solution)/shard_map/attend_back/pallas_call | solution.py:216
  476.1 4.0 collective-permute-done.28.refs_3_
  480.1 4.6 mixed.1
  493.9 21.0 %attend_back.3 = (bf16[2048,256]{1,0:T(8,128)(2,1)S(1)}, bf16[2048,128]{1,0:T(8,128)(2,1)S(1)}, bf16[2048,128]{1,0:T(8,128)(2,1)S(1)}) custom-call(s32[2]{0:T(128)S(1)} %pad_add_fusion.1.place_ref, bf16[2048,512]{1,0:T(8,128)(2,1)S(1)} %copy-done.18, bf16[2048,256]{1,0:T(8,128)(2,1)S(1)} %copy-done.26, bf16[2048,256]{1,0:T(8,128)(2,1)S(1)} %copy-done.31, ...), custom_call_target="tpu_custom_call" | custom-call | flops 1 | bytes 1 | tf_op jit(solution)/shard_map/attend_back/pallas_call | solution.py:216
  518.1 15.7 %wgrad.5 = bf16[1536,1536]{1,0:T(8,128)(2,1)} custom-call(bf16[2048,1536]{1,0:T(8,128)(2,1)} %get-tuple-element.197.refs_0_.refs_1_.refs_2_.refs_3_, bf16[2048,1536]{1,0:T(8,128)(2,1)} %get-tuple-element.197.refs_0_.refs_1_.refs_2_.refs_3_, bf16[2048,1536]{1,0:T(8,128)(2,1)} %get-tuple-element.197.refs_0_.refs_1_.refs_2_.refs_3_, ...), custom_call_target="tpu_custom_call" | custom-call | flops 1 | bytes 1 | tf_op jit(solution)/shard_map/wgrad/pallas_call | solution.py:442
  535.9 2.4 slice.120.w_ref
  541.1 9.3 %collective-permute-start.33 = (bf16[512,1536]{1,0:T(8,128)(2,1)S(1)}, bf16[512,1536]{1,0:T(8,128)(2,1)S(1)}, u32[]{:S(2)}, u32[]{:S(2)}) collective-permute-start(bf16[512,1536]{1,0:T(8,128)(2,1)S(1)} %product.20), channel_id=1, source_target_pairs={{0,4},{4,0},{1,5},{5,1},{2,6},{6,2},{3,7},{7,3},{8,12},{12,8},{9,1... | collective-permute-start | bytes 4718600 | tf_op jit(solution)/shard_map/ppermute | solution.py:540
  550.3 3.0 collective-permute-done.33.refs_0_
  555.7 3.0 product.22
  564.2 3.7 collective-permute-start.37
  569.2 3.4 product.23.refs_2_
  574.3 38.3 %collective-permute-done.34.refs_3_ = bf16[512,1536]{1,0:T(8,128)(2,1)} collective-permute-done((bf16[512,1536]{1,0:T(8,128)(2,1)}, bf16[512,1536]{1,0:T(8,128)(2,1)}, u32[]{:S(2)}, u32[]{:S(2)}) %collective-permute-start.34) | collective-permute-done | bytes 1572896 | tf_op jit(solution)/shard_map/ppermute | solution.py:649
  612.7 5.5 norm_back.3
  629.6 25.2 %collective-permute-start.43 = (f32[2,192]{1,0:T(2,128)S(1)}, f32[2,192]{1,0:T(2,128)S(1)}, u32[]{:S(2)}, u32[]{:S(2)}) collective-permute-start(f32[2,192]{1,0:T(2,128)S(1)} %add.152), channel_id=1, source_target_pairs={{0,2},{2,0},{1,3},{3,1},{4,6},{6,4},{5,7},{7,5},{8,10},{10,8},{9,1... | collective-permute-start | bytes 4616 | tf_op jit(solution)/shard_map/ppermute | solution.py:881
  656.1 26.6 %collective-permute-done.43 = f32[2,192]{1,0:T(2,128)S(1)} collective-permute-done((f32[2,192]{1,0:T(2,128)S(1)}, f32[2,192]{1,0:T(2,128)S(1)}, u32[]{:S(2)}, u32[]{:S(2)}) %collective-permute-start.43) | collective-permute-done | bytes 1568 | tf_op jit(solution)/shard_map/ppermute | solution.py:881
  (360 shorter events, 153.8 us)
Async XLA Ops:
  7.2 98.1 %all-gather.3.cloned.1.call-start = ((), (), s32[]{:S(2)}) async-start(), calls=%async_computation.3 | async-start | bytes 5898240 | tf_op jit(solution)/shard_map/all_gather | solution.py:564
  7.2 6.5 collective-permute-start
  13.8 15.6 %collective-permute-start.2 = (bf16[192,1536]{1,0:T(8,128)(2,1)S(1)}, bf16[192,1536]{1,0:T(8,128)(2,1)S(1)}, u32[]{:S(2)}, u32[]{:S(2)}) collective-permute-start(bf16[192,1536]{1,0:T(8,128)(2,1)S(1)} %concatenate.46), channel_id=1, source_target_pairs={{0,2},{2,6},{4,0},{6,4},{1,3},{3,7},{5,1},{7,5},{8,10},{10,14},{12... | collective-permute-start | bytes 1769480 | tf_op jit(solution)/shard_map/ppermute | solution.py:552
  17.5 11.9 %collective-permute-start.1 = (bf16[192,1536]{1,0:T(8,128)(2,1)S(1)}, bf16[192,1536]{1,0:T(8,128)(2,1)S(1)}, u32[]{:S(2)}, u32[]{:S(2)}) collective-permute-start(bf16[192,1536]{1,0:T(8,128)(2,1)S(1)} %concatenate.46), channel_id=1, source_target_pairs={{2,4},{4,2},{3,5},{5,3},{10,12},{12,10},{11,13},{13,11},{18,20},{2... | collective-permute-start | bytes 1769480 | tf_op jit(solution)/shard_map/ppermute | solution.py:532
  31.6 230.6 %all-gather.5.cloned.1.call-start = ((), (), s32[]{:S(2)}) async-start(), calls=%async_computation.4 | async-start | bytes 11796480 | tf_op jit(solution)/shard_map/all_gather | solution.py:564
  31.8 24.6 %collective-permute-start.3 = (bf16[512,1536]{1,0:T(8,128)(2,1)}, bf16[512,1536]{1,0:T(8,128)(2,1)}, u32[]{:S(2)}, u32[]{:S(2)}) collective-permute-start(bf16[512,1536]{1,0:T(8,128)(2,1)} %param.12), channel_id=1, source_target_pairs={{2,4},{4,2},{3,5},{5,3},{10,12},{12,10},{11,13},{13,11},{18,20},{2... | collective-permute-start | bytes 4718600 | tf_op jit(solution)/shard_map/ppermute | solution.py:532
  33.6 51.1 %collective-permute-start.4 = (bf16[512,1536]{1,0:T(8,128)(2,1)}, bf16[512,1536]{1,0:T(8,128)(2,1)S(1)}, u32[]{:S(2)}, u32[]{:S(2)}) collective-permute-start(bf16[512,1536]{1,0:T(8,128)(2,1)} %param.12), channel_id=1, source_target_pairs={{0,1},{1,0},{6,7},{7,6},{8,9},{9,8},{14,15},{15,14},{16,17},{17,16... | collective-permute-start | bytes 4718600 | tf_op jit(solution)/shard_map/ppermute | solution.py:664
  88.0 19.1 %collective-permute-start.8 = (bf16[512,1536]{1,0:T(8,128)(2,1)}, bf16[512,1536]{1,0:T(8,128)(2,1)}, u32[]{:S(2)}, u32[]{:S(2)}) collective-permute-start(bf16[512,1536]{1,0:T(8,128)(2,1)} %broadcast_select_fusion.4.x_ref.refs_0_.refs_1_), channel_id=1, source_target_pairs={{0,4},{4,0},{1,5},{5,1},{2,6},{6,2},{3,7},{7,3},{8,12},{12,8},{9,1... | collective-permute-start | bytes 4718600 | tf_op jit(solution)/shard_map/ppermute | solution.py:540
  89.4 34.4 %collective-permute-start.5 = (bf16[512,1536]{1,0:T(8,128)(2,1)}, bf16[512,1536]{1,0:T(8,128)(2,1)}, u32[]{:S(2)}, u32[]{:S(2)}) collective-permute-start(bf16[512,1536]{1,0:T(8,128)(2,1)} %collective-permute-done.3), channel_id=1, source_target_pairs={{2,3},{3,2},{4,5},{5,4},{10,11},{11,10},{12,13},{13,12},{18,19},{1... | collective-permute-start | bytes 4718600 | tf_op jit(solution)/shard_map/ppermute | solution.py:668
  92.4 24.5 %collective-permute-start.6 = (bf16[192,3072]{1,0:T(8,128)(2,1)}, bf16[192,3072]{1,0:T(8,128)(2,1)}, u32[]{:S(2)}, u32[]{:S(2)}) collective-permute-start(bf16[192,3072]{1,0:T(8,128)(2,1)} %pad_maximum_fusion.7), channel_id=1, source_target_pairs={{2,4},{4,2},{3,5},{5,3},{10,12},{12,10},{11,13},{13,11},{18,20},{2... | collective-permute-start | bytes 3538952 | tf_op jit(solution)/shard_map/ppermute | solution.py:532
  94.1 29.7 %collective-permute-start.7 = (bf16[192,3072]{1,0:T(8,128)(2,1)}, bf16[192,3072]{1,0:T(8,128)(2,1)}, u32[]{:S(2)}, u32[]{:S(2)}) collective-permute-start(bf16[192,3072]{1,0:T(8,128)(2,1)} %pad_maximum_fusion.7), channel_id=1, source_target_pairs={{0,2},{2,6},{4,0},{6,4},{1,3},{3,7},{5,1},{7,5},{8,10},{10,14},{12... | collective-permute-start | bytes 3538952 | tf_op jit(solution)/shard_map/ppermute | solution.py:552
  124.0 29.9 %collective-permute-start.9 = (bf16[512,1536]{1,0:T(8,128)(2,1)S(1)}, bf16[512,1536]{1,0:T(8,128)(2,1)S(1)}, u32[]{:S(2)}, u32[]{:S(2)}) collective-permute-start(bf16[512,1536]{1,0:T(8,128)(2,1)S(1)} %broadcast_select_fusion.3.x_ref), channel_id=1, source_target_pairs={{0,4},{4,0},{1,5},{5,1},{2,6},{6,2},{3,7},{7,3},{8,12},{12,8},{9,1... | collective-permute-start | bytes 4718600 | tf_op jit(solution)/shard_map/ppermute | solution.py:540
  159.4 275.9 %reduce-scatter.4.cloned.1.call-start = ((), (), s32[]{:S(2)}) async-start(), calls=%async_computation.5 | async-start | bytes 3932160 | tf_op jit(solution)/shard_map/reduce_scatter | solution.py:582
  159.4 49.9 %collective-permute-start.10 = (bf16[512,1536]{1,0:T(8,128)(2,1)}, bf16[512,1536]{1,0:T(8,128)(2,1)S(1)}, u32[]{:S(2)}, u32[]{:S(2)}) collective-permute-start(bf16[512,1536]{1,0:T(8,128)(2,1)} %param.23), channel_id=1, source_target_pairs={{2,4},{4,2},{3,5},{5,3},{10,12},{12,10},{11,13},{13,11},{18,20},{2... | collective-permute-start | bytes 4718600 | tf_op jit(solution)/shard_map/ppermute | solution.py:532
  160.3 49.0 %collective-permute-start.11 = (bf16[512,1536]{1,0:T(8,128)(2,1)}, bf16[512,1536]{1,0:T(8,128)(2,1)S(1)}, u32[]{:S(2)}, u32[]{:S(2)}) collective-permute-start(bf16[512,1536]{1,0:T(8,128)(2,1)} %param.23), channel_id=1, source_target_pairs={{0,1},{1,0},{6,7},{7,6},{8,9},{9,8},{14,15},{15,14},{16,17},{17,16... | collective-permute-start | bytes 4718600 | tf_op jit(solution)/shard_map/ppermute | solution.py:664
  212.5 7.0 %collective-permute-start.12 = (bf16[512,1536]{1,0:T(8,128)(2,1)S(1)}, bf16[512,1536]{1,0:T(8,128)(2,1)S(1)}, u32[]{:S(2)}, u32[]{:S(2)}) collective-permute-start(bf16[512,1536]{1,0:T(8,128)(2,1)S(1)} %product.12), channel_id=1, source_target_pairs={{0,4},{4,0},{1,5},{5,1},{2,6},{6,2},{3,7},{7,3},{8,12},{12,8},{9,1... | collective-permute-start | bytes 4718600 | tf_op jit(solution)/shard_map/ppermute | solution.py:540
  215.5 37.0 %collective-permute-start.14 = (bf16[512,1536]{1,0:T(8,128)(2,1)S(1)}, bf16[512,1536]{1,0:T(8,128)(2,1)}, u32[]{:S(2)}, u32[]{:S(2)}) collective-permute-start(bf16[512,1536]{1,0:T(8,128)(2,1)S(1)} %product.15), channel_id=1, source_target_pairs={{0,1},{1,0},{2,3},{3,2},{4,5},{5,4},{6,7},{7,6},{8,9},{9,8},{10,11... | collective-permute-start | bytes 4718600 | tf_op jit(solution)/shard_map/ppermute | solution.py:649
  222.0 39.0 %collective-permute-start.16 = (bf16[512,1536]{1,0:T(8,128)(2,1)}, bf16[512,1536]{1,0:T(8,128)(2,1)}, u32[]{:S(2)}, u32[]{:S(2)}) collective-permute-start(bf16[512,1536]{1,0:T(8,128)(2,1)} %broadcast_select_fusion.2.dy_ref.refs_0_), channel_id=1, source_target_pairs={{0,4},{4,0},{1,5},{5,1},{2,6},{6,2},{3,7},{7,3},{8,12},{12,8},{9,1... | collective-permute-start | bytes 4718600 | tf_op jit(solution)/shard_map/ppermute | solution.py:540
  257.1 4.0 collective-permute-start.15
  257.1 37.5 %collective-permute-start.17 = (bf16[512,1536]{1,0:T(8,128)(2,1)}, bf16[512,1536]{1,0:T(8,128)(2,1)}, u32[]{:S(2)}, u32[]{:S(2)}) collective-permute-start(bf16[512,1536]{1,0:T(8,128)(2,1)} %get-tuple-element.146.a_ref.refs_0_), channel_id=1, source_target_pairs={{0,1},{1,0},{2,3},{3,2},{4,5},{5,4},{6,7},{7,6},{8,9},{9,8},{10,11... | collective-permute-start | bytes 4718600 | tf_op jit(solution)/shard_map/ppermute | solution.py:544
  258.8 35.8 %collective-permute-start.18 = (bf16[512,1536]{1,0:T(8,128)(2,1)}, bf16[512,1536]{1,0:T(8,128)(2,1)}, u32[]{:S(2)}, u32[]{:S(2)}) collective-permute-start(bf16[512,1536]{1,0:T(8,128)(2,1)} %broadcast_select_fusion.2.dy_ref.refs_0_), channel_id=1, source_target_pairs={{2,3},{3,2},{4,5},{5,4},{10,11},{11,10},{12,13},{13,12},{18,19},{1... | collective-permute-start | bytes 4718600 | tf_op jit(solution)/shard_map/ppermute | solution.py:668
  294.6 19.5 %collective-permute-start.19 = (bf16[512,1536]{1,0:T(8,128)(2,1)}, bf16[512,1536]{1,0:T(8,128)(2,1)S(1)}, u32[]{:S(2)}, u32[]{:S(2)}) collective-permute-start(bf16[512,1536]{1,0:T(8,128)(2,1)} %collective-permute-done.17.a_ref.refs_2_), channel_id=1, source_target_pairs={{0,4},{4,0},{1,5},{5,1},{2,6},{6,2},{3,7},{7,3},{8,12},{12,8},{9,1... | collective-permute-start | bytes 4718600 | tf_op jit(solution)/shard_map/ppermute | solution.py:540
  311.1 5.1 collective-permute-start.20
  343.7 7.0 %collective-permute-start.21 = (bf16[512,1536]{1,0:T(8,128)(2,1)S(1)}, bf16[512,1536]{1,0:T(8,128)(2,1)}, u32[]{:S(2)}, u32[]{:S(2)}) collective-permute-start(bf16[512,1536]{1,0:T(8,128)(2,1)S(1)} %slice.91), channel_id=1, source_target_pairs={{0,4},{4,0},{1,5},{5,1},{2,6},{6,2},{3,7},{7,3},{8,12},{12,8},{9,1... | collective-permute-start | bytes 4718600 | tf_op jit(solution)/shard_map/ppermute | solution.py:540
  345.4 12.9 %collective-permute-start.23 = (bf16[512,1536]{1,0:T(8,128)(2,1)}, bf16[512,1536]{1,0:T(8,128)(2,1)}, u32[]{:S(2)}, u32[]{:S(2)}) collective-permute-start(bf16[512,1536]{1,0:T(8,128)(2,1)} %slice.93), channel_id=1, source_target_pairs={{0,4},{4,0},{1,5},{5,1},{2,6},{6,2},{3,7},{7,3},{8,12},{12,8},{9,1... | collective-permute-start | bytes 4718600 | tf_op jit(solution)/shard_map/ppermute | solution.py:540
  347.8 7.5 %collective-permute-start.22 = (bf16[512,1536]{1,0:T(8,128)(2,1)}, bf16[512,1536]{1,0:T(8,128)(2,1)}, u32[]{:S(2)}, u32[]{:S(2)}) collective-permute-start(bf16[512,1536]{1,0:T(8,128)(2,1)} %slice.92), channel_id=1, source_target_pairs={{0,4},{4,0},{1,5},{5,1},{2,6},{6,2},{3,7},{7,3},{8,12},{12,8},{9,1... | collective-permute-start | bytes 4718600 | tf_op jit(solution)/shard_map/ppermute | solution.py:540
  350.3 8.0 %collective-permute-start.24 = (bf16[512,1536]{1,0:T(8,128)(2,1)}, bf16[512,1536]{1,0:T(8,128)(2,1)}, u32[]{:S(2)}, u32[]{:S(2)}) collective-permute-start(bf16[512,1536]{1,0:T(8,128)(2,1)} %slice.94), channel_id=1, source_target_pairs={{0,4},{4,0},{1,5},{5,1},{2,6},{6,2},{3,7},{7,3},{8,12},{12,8},{9,1... | collective-permute-start | bytes 4718600 | tf_op jit(solution)/shard_map/ppermute | solution.py:540
  353.6 36.7 %collective-permute-start.25 = (bf16[512,1536]{1,0:T(8,128)(2,1)}, bf16[512,1536]{1,0:T(8,128)(2,1)}, u32[]{:S(2)}, u32[]{:S(2)}) collective-permute-start(bf16[512,1536]{1,0:T(8,128)(2,1)} %join.2), channel_id=1, source_target_pairs={{0,1},{1,0},{2,3},{3,2},{4,5},{5,4},{6,7},{7,6},{8,9},{9,8},{10,11... | collective-permute-start | bytes 4718600 | tf_op jit(solution)/shard_map/ppermute | solution.py:649
  390.4 145.5 %reduce-scatter.6.cloned.1.call-start = ((), (), s32[]{:S(2)}) async-start(), calls=%async_computation.6 | async-start | bytes 7864320 | tf_op jit(solution)/shard_map/reduce_scatter | solution.py:582
  396.8 6.8 collective-permute-start.26
  396.8 37.1 %collective-permute-start.27 = (bf16[512,1536]{1,0:T(8,128)(2,1)}, bf16[512,1536]{1,0:T(8,128)(2,1)}, u32[]{:S(2)}, u32[]{:S(2)}) collective-permute-start(bf16[512,1536]{1,0:T(8,128)(2,1)} %get-tuple-element.174.x_ref.refs_8_), channel_id=1, source_target_pairs={{0,1},{1,0},{2,3},{3,2},{4,5},{5,4},{6,7},{7,6},{8,9},{9,8},{10,11... | collective-permute-start | bytes 4718600 | tf_op jit(solution)/shard_map/ppermute | solution.py:544
  433.9 186.1 %reduce-scatter.8.cloned.1.call-start = ((), (), s32[]{:S(2)}) async-start(), calls=%async_computation.7 | async-start | bytes 5898240 | tf_op jit(solution)/shard_map/reduce_scatter | solution.py:582
  434.0 13.4 %collective-permute-start.31 = (bf16[512,1536]{1,0:T(8,128)(2,1)}, bf16[512,1536]{1,0:T(8,128)(2,1)}, u32[]{:S(2)}, u32[]{:S(2)}) collective-permute-start(bf16[512,1536]{1,0:T(8,128)(2,1)} %collective-permute-done.27.x_ref.refs_10_), channel_id=1, source_target_pairs={{0,4},{4,0},{1,5},{5,1},{2,6},{6,2},{3,7},{7,3},{8,12},{12,8},{9,1... | collective-permute-start | bytes 4718600 | tf_op jit(solution)/shard_map/ppermute | solution.py:540
  435.2 44.9 %collective-permute-start.28 = (bf16[512,1536]{1,0:T(8,128)(2,1)}, bf16[512,1536]{1,0:T(8,128)(2,1)}, u32[]{:S(2)}, u32[]{:S(2)}) collective-permute-start(bf16[512,1536]{1,0:T(8,128)(2,1)} %join.3), channel_id=1, source_target_pairs={{0,1},{1,0},{2,3},{3,2},{4,5},{5,4},{6,7},{7,6},{8,9},{9,8},{10,11... | collective-permute-start | bytes 4718600 | tf_op jit(solution)/shard_map/ppermute | solution.py:649
  437.9 36.7 %collective-permute-start.29 = (bf16[192,1024]{1,0:T(8,128)(2,1)S(1)}, bf16[192,1024]{1,0:T(8,128)(2,1)S(1)}, u32[]{:S(2)}, u32[]{:S(2)}) collective-permute-start(bf16[192,1024]{1,0:T(8,128)(2,1)S(1)} %get-tuple-element.220), channel_id=1, source_target_pairs={{2,4},{4,2},{3,5},{5,3},{10,12},{12,10},{11,13},{13,11},{18,20},{2... | collective-permute-start | bytes 1179656 | tf_op jit(solution)/shard_map/ppermute | solution.py:532
  438.6 36.8 %collective-permute-start.30 = (bf16[192,1024]{1,0:T(8,128)(2,1)S(1)}, bf16[192,1024]{1,0:T(8,128)(2,1)S(1)}, u32[]{:S(2)}, u32[]{:S(2)}) collective-permute-start(bf16[192,1024]{1,0:T(8,128)(2,1)S(1)} %get-tuple-element.252), channel_id=1, source_target_pairs={{2,0},{6,2},{0,4},{4,6},{3,1},{7,3},{1,5},{5,7},{10,8},{14,10},{8,... | collective-permute-start | bytes 1179656 | tf_op jit(solution)/shard_map/ppermute | solution.py:572
  484.7 30.2 %collective-permute-start.32 = (bf16[512,1536]{1,0:T(8,128)(2,1)}, bf16[512,1536]{1,0:T(8,128)(2,1)S(1)}, u32[]{:S(2)}, u32[]{:S(2)}) collective-permute-start(bf16[512,1536]{1,0:T(8,128)(2,1)} %mixed.1), channel_id=1, source_target_pairs={{2,4},{4,2},{3,5},{5,3},{10,12},{12,10},{11,13},{13,11},{18,20},{2... | collective-permute-start | bytes 4718600 | tf_op jit(solution)/shard_map/ppermute | solution.py:532
  541.1 12.3 %collective-permute-start.33 = (bf16[512,1536]{1,0:T(8,128)(2,1)S(1)}, bf16[512,1536]{1,0:T(8,128)(2,1)S(1)}, u32[]{:S(2)}, u32[]{:S(2)}) collective-permute-start(bf16[512,1536]{1,0:T(8,128)(2,1)S(1)} %product.20), channel_id=1, source_target_pairs={{0,4},{4,0},{1,5},{5,1},{2,6},{6,2},{3,7},{7,3},{8,12},{12,8},{9,1... | collective-permute-start | bytes 4718600 | tf_op jit(solution)/shard_map/ppermute | solution.py:540
  558.7 10.5 %collective-permute-start.35 = (bf16[512,1536]{1,0:T(8,128)(2,1)}, bf16[512,1536]{1,0:T(8,128)(2,1)}, u32[]{:S(2)}, u32[]{:S(2)}) collective-permute-start(bf16[512,1536]{1,0:T(8,128)(2,1)} %product.22), channel_id=1, source_target_pairs={{0,4},{4,0},{1,5},{5,1},{2,6},{6,2},{3,7},{7,3},{8,12},{12,8},{9,1... | collective-permute-start | bytes 4718600 | tf_op jit(solution)/shard_map/ppermute | solution.py:540
  559.0 53.6 %collective-permute-start.34 = (bf16[512,1536]{1,0:T(8,128)(2,1)}, bf16[512,1536]{1,0:T(8,128)(2,1)}, u32[]{:S(2)}, u32[]{:S(2)}) collective-permute-start(bf16[512,1536]{1,0:T(8,128)(2,1)} %copy-done.58), channel_id=1, source_target_pairs={{0,1},{1,0},{2,3},{3,2},{4,5},{5,4},{6,7},{7,6},{8,9},{9,8},{10,11... | collective-permute-start | bytes 4718600 | tf_op jit(solution)/shard_map/ppermute | solution.py:649
  562.5 50.2 %collective-permute-start.36 = (bf16[192,2048]{1,0:T(8,128)(2,1)}, bf16[192,2048]{1,0:T(8,128)(2,1)}, u32[]{:S(2)}, u32[]{:S(2)}) collective-permute-start(bf16[192,2048]{1,0:T(8,128)(2,1)} %get-tuple-element.217), channel_id=1, source_target_pairs={{2,4},{4,2},{3,5},{5,3},{10,12},{12,10},{11,13},{13,11},{18,20},{2... | collective-permute-start | bytes 2359304 | tf_op jit(solution)/shard_map/ppermute | solution.py:532
  564.2 48.4 %collective-permute-start.37 = (bf16[192,2048]{1,0:T(8,128)(2,1)}, bf16[192,2048]{1,0:T(8,128)(2,1)}, u32[]{:S(2)}, u32[]{:S(2)}) collective-permute-start(bf16[192,2048]{1,0:T(8,128)(2,1)} %get-tuple-element.242), channel_id=1, source_target_pairs={{2,0},{6,2},{0,4},{4,6},{3,1},{7,3},{1,5},{5,7},{10,8},{14,10},{8,... | collective-permute-start | bytes 2359304 | tf_op jit(solution)/shard_map/ppermute | solution.py:572
  618.2 64.5 %collective-permute-start.38 = (bf16[512,1536]{1,0:T(8,128)(2,1)}, bf16[512,1536]{1,0:T(8,128)(2,1)}, u32[]{:S(2)}, u32[]{:S(2)}) collective-permute-start(bf16[512,1536]{1,0:T(8,128)(2,1)} %get-tuple-element.210), channel_id=1, source_target_pairs={{2,4},{4,2},{3,5},{5,3},{10,12},{12,10},{11,13},{13,11},{18,20},{2... | collective-permute-start | bytes 4718600 | tf_op jit(solution)/shard_map/ppermute | solution.py:532
  621.7 4.2 collective-permute-start.41
  623.1 59.7 %collective-permute-start.39 = (bf16[192,1536]{1,0:T(8,128)(2,1)S(1)}, bf16[192,1536]{1,0:T(8,128)(2,1)S(1)}, u32[]{:S(2)}, u32[]{:S(2)}) collective-permute-start(bf16[192,1536]{1,0:T(8,128)(2,1)S(1)} %get-tuple-element.214), channel_id=1, source_target_pairs={{2,4},{4,2},{3,5},{5,3},{10,12},{12,10},{11,13},{13,11},{18,20},{2... | collective-permute-start | bytes 1769480 | tf_op jit(solution)/shard_map/ppermute | solution.py:532
  623.8 59.0 %collective-permute-start.40 = (bf16[192,1536]{1,0:T(8,128)(2,1)S(1)}, bf16[192,1536]{1,0:T(8,128)(2,1)S(1)}, u32[]{:S(2)}, u32[]{:S(2)}) collective-permute-start(bf16[192,1536]{1,0:T(8,128)(2,1)S(1)} %get-tuple-element.248), channel_id=1, source_target_pairs={{2,0},{6,2},{0,4},{4,6},{3,1},{7,3},{1,5},{5,7},{10,8},{14,10},{8,... | collective-permute-start | bytes 1769480 | tf_op jit(solution)/shard_map/ppermute | solution.py:572
  626.0 3.6 collective-permute-start.42
  629.6 53.1 %collective-permute-start.43 = (f32[2,192]{1,0:T(2,128)S(1)}, f32[2,192]{1,0:T(2,128)S(1)}, u32[]{:S(2)}, u32[]{:S(2)}) collective-permute-start(f32[2,192]{1,0:T(2,128)S(1)} %add.152), channel_id=1, source_target_pairs={{0,2},{2,0},{1,3},{3,1},{4,6},{6,4},{5,7},{7,5},{8,10},{10,8},{9,1... | collective-permute-start | bytes 4616 | tf_op jit(solution)/shard_map/ppermute | solution.py:881
  (98 other events, 933.3 us)
Sparse Core Ops, SparseCore 0:
  31.8 73.4 all-gather.2
  159.5 95.6 all-gather.4
  390.5 44.7 reduce-scatter.3
  438.1 70.2 reduce-scatter.5
  536.0 65.4 reduce-scatter.7

commit v3 on v2

--- a/solution.py
+++ b/solution.py
@@ -25,14 +25,29 @@
 bf16 = jnp.bfloat16
 
 
-def local_block(g, place_ref, ring):
-    other = lax.rem(g // ring + place_ref[0], 2)
-    step = lax.rem(lax.rem(g, ring) - place_ref[1] + ring, ring)
-    return 2 * step + other
-
-
-def attend_kernel(ring, block, place_ref, q_ref, k_ref, v_ref, start_ref, o_ref, lse_ref):
-    g = pl.program_id(1)
+def flipped(core, column, place, ring):
+    return jnp.where(core == place[2], column, ring - 1 - column)
+
+
+def local_block(g, place, ring):
+    core = g // ring
+    column = flipped(core, lax.rem(g, ring), place, ring)
+    step = lax.rem(column - place[1] + ring, ring)
+    return 2 * step + lax.rem(core + place[0], 2)
+
+
+def global_block(l, place, ring):
+    core = lax.rem(lax.rem(l, 2) + place[0], 2)
+    column = lax.rem(l // 2 + place[1], ring)
+    return core * ring + flipped(core, column, place, ring)
+
+
+def in_hbm(*arrays):
+    return [pltpu.with_memory_space_constraint(a, pltpu.HBM) for a in arrays]
+
+
+def attend_kernel(ring, block, chip, place_ref, q_ref, k_ref, v_ref, start_ref, o_ref, lse_ref):
+    g = global_block(2 * chip + pl.program_id(1), place_ref, ring)
     share = q_ref.shape[1] // LANES
     start = start_ref[...]
     row = lax.broadcasted_iota(jnp.int32, (block, block), 0)
@@ -69,7 +84,7 @@
         )
         for _ in range(share)
     )
-    carry = step(g, carry, True)
+    carry = step(g, carry, 8)
     carry = lax.fori_loop(0, g, lambda kb, c: step(kb, c, False), carry)
     for h in range(share):
         largest, total, acc = carry[h]
@@ -77,34 +92,30 @@
         lse_ref[0, h : h + 1, :] = largest + jnp.log2(total)
 
 
-def attend(place, q, k, v, start, ring):
+def attend(chip, place, q, k, v, start, ring):
     length = q.shape[0]
     block = length // (2 * ring)
     kv = k.shape[1] // LANES
     share = q.shape[1] // k.shape[1]
-
-    def at(g, place_ref):
-        return local_block(g, place_ref, ring)
-
     return pl.pallas_call(
-        functools.partial(attend_kernel, ring, block),
+        functools.partial(attend_kernel, ring, block, chip),
         grid_spec=pltpu.PrefetchScalarGridSpec(
             num_scalar_prefetch=1,
-            grid=(kv, 2 * ring),
+            grid=(kv, 2),
             in_specs=[
-                pl.BlockSpec((block, share * LANES), lambda h, g, z: (at(g, z), h)),
-                pl.BlockSpec((length, LANES), lambda h, g, z: (0, h)),
-                pl.BlockSpec((length, LANES), lambda h, g, z: (0, h)),
-                pl.BlockSpec((1, block), lambda h, g, z: (0, at(g, z))),
+                pl.BlockSpec((block, share * LANES), lambda h, j, z: (2 * chip + j, h)),
+                pl.BlockSpec((length, LANES), lambda h, j, z: (0, h)),
+                pl.BlockSpec((length, LANES), lambda h, j, z: (0, h)),
+                pl.BlockSpec((1, block), lambda h, j, z: (0, 2 * chip + j)),
             ],
             out_specs=[
-                pl.BlockSpec((block, share * LANES), lambda h, g, z: (at(g, z), h)),
-                pl.BlockSpec((1, share, block), lambda h, g, z: (h, 0, at(g, z))),
+                pl.BlockSpec((block, share * LANES), lambda h, j, z: (j, h)),
+                pl.BlockSpec((1, share, block), lambda h, j, z: (h, 0, j)),
             ],
         ),
         out_shape=[
-            jax.ShapeDtypeStruct(q.shape, bf16),
-            jax.ShapeDtypeStruct((kv, share, length), f32),
+            jax.ShapeDtypeStruct((2 * block, q.shape[1]), bf16),
+            jax.ShapeDtypeStruct((kv, share, 2 * block), f32),
         ],
         compiler_params=pltpu.CompilerParams(
             vmem_limit_bytes=40 * 2**20, dimension_semantics=("arbitrary", "arbitrary")
@@ -117,6 +128,8 @@
 def attend_back_kernel(
     ring,
     block,
+    chip,
+    final,
     place_ref,
     q_ref,
     k_ref,
@@ -127,21 +140,24 @@
     start_ref,
     cosq_ref,
     sinq_ref,
-    cosk_ref,
-    sink_ref,
-    dq_ref,
-    dk_ref,
-    dv_ref,
-    dk_acc,
-    dv_acc,
+    *refs,
 ):
-    g = pl.program_id(1)
+    if final:
+        cosk_ref, sink_ref = refs[:2]
+    before = refs[2 * final : -5]
+    dq_ref, dk_ref, dv_ref, dk_acc, dv_acc = refs[-5:]
+    j = pl.program_id(1)
+    g = global_block(2 * chip + j, place_ref, ring)
     share = q_ref.shape[1] // LANES
 
-    @pl.when(g == 0)
+    @pl.when(j == 0)
     def _():
-        dk_acc[...] = jnp.zeros_like(dk_acc)
-        dv_acc[...] = jnp.zeros_like(dv_acc)
+        if before:
+            dk_acc[...] = before[0][...]
+            dv_acc[...] = before[1][...]
+        else:
+            dk_acc[...] = jnp.zeros_like(dk_acc)
+            dv_acc[...] = jnp.zeros_like(dv_acc)
 
     start = start_ref[...]
     row = lax.broadcasted_iota(jnp.int32, (block, block), 0)
@@ -179,72 +195,72 @@
         dv_acc[pl.ds(offset, block), :] += dv
         return tuple(out)
 
-    carry = step(g, tuple(jnp.zeros((LANES, block), f32) for _ in range(share)), True)
+    carry = step(g, tuple(jnp.zeros((LANES, block), f32) for _ in range(share)), 8)
     carry = lax.fori_loop(0, g, lambda kb, c: step(kb, c, False), carry)
     for h in range(share):
         u = jnp.transpose(carry[h]) * HEAD_SIZE ** (-0.5)
         turned = u * cosq_ref[...] - pltpu.roll(u, LANES // 2, 1) * sinq_ref[...]
         dq_ref[:, heads[h]] = turned.astype(bf16)
 
-    @pl.when(g == pl.num_programs(1) - 1)
+    @pl.when(j == 1)
     def _():
         def finish(i, _):
             r = pl.ds(pl.multiple_of(i * block, block), block)
-            u = dk_acc[r, :] * math.log(2.0)
-            turned = u * cosk_ref[r, :] - pltpu.roll(u, LANES // 2, 1) * sink_ref[r, :]
-            dk_ref[r, :] = turned.astype(bf16)
-            dv_ref[r, :] = dv_acc[r, :].astype(bf16)
+            u = dk_acc[r, :]
+            if final:
+                u = u * math.log(2.0)
+                u = u * cosk_ref[r, :] - pltpu.roll(u, LANES // 2, 1) * sink_ref[r, :]
+            dk_ref[r, :] = u.astype(dk_ref.dtype)
+            dv_ref[r, :] = dv_acc[r, :].astype(dv_ref.dtype)
             return 0
 
         lax.fori_loop(0, 2 * ring, finish, 0)
 
 
-def attend_back(place, q, k, v, o, do, lse, start, cos, sin, ring, head):
+def attend_back(chip, place, q, k, v, o, do, lse, start, cos, sin, ring, before):
     length = q.shape[0]
     block = length // (2 * ring)
+    kv = k.shape[1] // LANES
     share = q.shape[1] // k.shape[1]
-
-    def at(g, place_ref):
-        return local_block(g, place_ref, ring)
-
-    qspec = pl.BlockSpec((block, share * LANES), lambda h, g, z: (at(g, z), head))
-    kspec = pl.BlockSpec((length, LANES), lambda h, g, z: (0, head))
-    qout = pl.BlockSpec((block, share * LANES), lambda h, g, z: (at(g, z), 0))
-    kout = pl.BlockSpec((length, LANES), lambda h, g, z: (0, 0))
-    tableq = pl.BlockSpec((block, LANES), lambda h, g, z: (at(g, z), 0))
-    tablek = pl.BlockSpec((length, LANES), lambda h, g, z: (0, 0))
+    final = chip == ring - 1
+    kind = bf16 if final else f32
+    qspec = pl.BlockSpec((block, share * LANES), lambda h, j, z: (2 * chip + j, h))
+    own = pl.BlockSpec((block, share * LANES), lambda h, j, z: (j, h))
+    kspec = pl.BlockSpec((length, LANES), lambda h, j, z: (0, h))
+    table = pl.BlockSpec((block, LANES), lambda h, j, z: (2 * chip + j, 0))
+    whole = pl.BlockSpec((length, LANES), lambda h, j, z: (0, 0))
     return pl.pallas_call(
-        functools.partial(attend_back_kernel, ring, block),
+        functools.partial(attend_back_kernel, ring, block, chip, final),
         grid_spec=pltpu.PrefetchScalarGridSpec(
             num_scalar_prefetch=1,
-            grid=(1, 2 * ring),
+            grid=(kv, 2),
             in_specs=[
                 qspec,
                 kspec,
                 kspec,
-                qspec,
-                qspec,
-                pl.BlockSpec((1, share, block), lambda h, g, z: (head, 0, at(g, z))),
-                pl.BlockSpec((1, block), lambda h, g, z: (0, at(g, z))),
-                tableq,
-                tableq,
-                tablek,
-                tablek,
-            ],
-            out_specs=[qout, kout, kout],
+                own,
+                own,
+                pl.BlockSpec((1, share, block), lambda h, j, z: (h, 0, j)),
+                pl.BlockSpec((1, block), lambda h, j, z: (0, 2 * chip + j)),
+                table,
+                table,
+            ]
+            + [whole, whole] * final
+            + [kspec] * len(before),
+            out_specs=[own, kspec, kspec],
             scratch_shapes=[pltpu.VMEM((length, LANES), f32), pltpu.VMEM((length, LANES), f32)],
         ),
         out_shape=[
-            jax.ShapeDtypeStruct((length, share * LANES), bf16),
-            jax.ShapeDtypeStruct((length, LANES), bf16),
-            jax.ShapeDtypeStruct((length, LANES), bf16),
+            jax.ShapeDtypeStruct((2 * block, q.shape[1]), bf16),
+            jax.ShapeDtypeStruct(k.shape, kind),
+            jax.ShapeDtypeStruct(k.shape, kind),
         ],
         compiler_params=pltpu.CompilerParams(
             vmem_limit_bytes=40 * 2**20, dimension_semantics=("arbitrary", "arbitrary")
         ),
         cost_estimate=light,
         name="attend_back",
-    )(place, q, k, v, o, do, lse, start, cos, sin, cos, sin)
+    )(place, q, k, v, o, do, lse, start, cos, sin, *[cos, sin] * final, *before)
 
 
 def pieces_spec(block, width, count):
@@ -309,11 +325,11 @@
         ),
         cost_estimate=light,
         name="project",
-    )(*pair, gain, w, cos, sin, *before)
+    )(*in_hbm(*pair), gain, *in_hbm(w), cos, sin, *in_hbm(*before))
 
 
 def hidden_kernel(
-    chunk, count, a_ref, b_ref, dy_ref, dz_ref, w_ref, hid_ref, dgu_ref, da_ref, mixed_ref
+    chunk, count, a_ref, b_ref, dy_ref, dz_ref, w_ref, hid_ref, dgu_ref, *refs
 ):
     a = picked(count, a_ref, b_ref)
     dy = picked(count, dy_ref, dz_ref)
@@ -330,12 +346,23 @@
         hid_ref[:, at] = (silu * u).astype(bf16)
         dgu_ref[:, at] = (dh * u * (sig + silu * (1.0 - sig))).astype(bf16)
         dgu_ref[:, up] = (dh * silu).astype(bf16)
-    da_ref[...] = lax.dot_general(
+    da = lax.dot_general(
         dgu_ref[...], w_ref[:, : 2 * units], cols_both, preferred_element_type=f32
     ).astype(bf16)
-    mixed_ref[...] = lax.dot_general(
+    mixed = lax.dot_general(
         hid_ref[...], w_ref[:, 2 * units :], cols_both, preferred_element_type=f32
     ).astype(bf16)
+    mine = pl.program_id(0) < count
+
+    @pl.when(mine)
+    def _():
+        refs[0][...] = da
+        refs[2][...] = mixed
+
+    @pl.when(jnp.logical_not(mine))
+    def _():
+        refs[1][...] = da
+        refs[3][...] = mixed
 
 
 def hidden_pass(a, dy, w):
@@ -343,7 +370,7 @@
     units = w.shape[1] // 3
     block = min(256, rows)
     count = rows // block
-    widths = [units, 2 * units, width, width]
+    widths = [units, 2 * units]
 
     def row(n):
         return pl.BlockSpec((block, n), lambda i: (i, 0))
@@ -354,8 +381,9 @@
         in_specs=pieces_spec(block, width, count)
         + pieces_spec(block, width, count)
         + [pl.BlockSpec(w.shape, lambda i: (0, 0), pipeline_mode=pl.Buffered(1))],
-        out_specs=[row(n) for n in widths],
-        out_shape=[jax.ShapeDtypeStruct((2 * rows, n), bf16) for n in widths],
+        out_specs=[row(n) for n in widths] + 2 * pieces_spec(block, width, count),
+        out_shape=[jax.ShapeDtypeStruct((2 * rows, n), bf16) for n in widths]
+        + [jax.ShapeDtypeStruct((rows, width), bf16)] * 4,
         compiler_params=pltpu.CompilerParams(
             vmem_limit_bytes=40 * 2**20, dimension_semantics=("arbitrary",)
         ),
@@ -364,37 +392,41 @@
     )(*a, *dy, w)
 
 
-def product_kernel(dims, x_ref, w_ref, *refs):
-    p = lax.dot_general(x_ref[...], w_ref[...], dims, preferred_element_type=f32)
+def product_kernel(dims, parts, *refs):
+    x = refs[0][...]
+    if parts > 1:
+        x = jnp.concatenate([ref[...] for ref in refs[:parts]], 1)
+    p = lax.dot_general(x, refs[parts][...], dims, preferred_element_type=f32)
     out_ref = refs[-1]
-    for ref in refs[:-1]:
+    for ref in refs[parts + 1 : -1]:
         p = p + ref[...].astype(f32)
     out_ref[...] = p.astype(out_ref.dtype)
 
 
-def product(x, w, dims, kind=bf16, rows=None, columns=(0, 1), add=None):
-    first, last = (0, x.shape[0]) if rows is None else (rows.start, rows.stop)
-    block = min(256, last - first)
-    wide = w.shape[1] // columns[1]
+def product(parts, rows, w, dims, kind=bf16, columns=None, add=None):
+    block = min(256, rows)
+    columns = columns or (0, w.shape[1])
+    wide = columns[1]
     out = w.shape[0] if dims == cols_both else wide
     row = pl.BlockSpec((block, out), lambda i: (i, 0))
     extra = [] if add is None else [add]
     return pl.pallas_call(
-        functools.partial(product_kernel, dims),
-        grid=((last - first) // block,),
+        functools.partial(product_kernel, dims, len(parts)),
+        grid=(rows // block,),
         in_specs=[
-            pl.BlockSpec((block, x.shape[1]), lambda i: (first // block + i, 0)),
-            pl.BlockSpec((w.shape[0], wide), lambda i: (0, columns[0])),
+            pl.BlockSpec((block, x.shape[1]), lambda i, first=first: (first // block + i, 0))
+            for x, first in parts
         ]
+        + [pl.BlockSpec((w.shape[0], wide), lambda i: (0, columns[0]))]
         + [row] * len(extra),
         out_specs=row,
-        out_shape=jax.ShapeDtypeStruct((last - first, out), kind),
+        out_shape=jax.ShapeDtypeStruct((rows, out), kind),
         compiler_params=pltpu.CompilerParams(
             vmem_limit_bytes=40 * 2**20, dimension_semantics=("arbitrary",)
         ),
         cost_estimate=light,
         name="product",
-    )(x, w, *extra)
+    )(*[x for x, _ in parts], *in_hbm(w), *extra)
 
 
 def wgrad_kernel(counts, *refs):
@@ -532,10 +564,6 @@
     return lax.ppermute(a, ("c", "zh"), cross_pairs)
 
 
-def relay(a):
-    return jnp.where(stays(), a, cross(a))
-
-
 def other_core(a):
     return lax.ppermute(a, "c", swap_two)
 
@@ -579,15 +607,28 @@
 
 
 def sum_rows(grad):
-    return lax.psum_scatter(grad.astype(bf16), "d", scatter_dimension=0, tiled=True)
-
-
-def after(first, then):
-    return lax.optimization_barrier((first, then))[1]
-
-
-def together(a, b):
-    return lax.optimization_barrier((a, b))
+    return lax.psum_scatter(grad, "d", scatter_dimension=0, tiled=True)
+
+
+def together(*items):
+    return lax.optimization_barrier(items)
+
+
+def mark_kernel(*refs):
+    refs[-1][...] = jnp.zeros_like(refs[-1])
+
+
+def mark(arrays, before, long):
+    whole = pl.BlockSpec(before.shape, lambda: (0, 0))
+    cost = pl.CostEstimate(flops=1 + long * 10**9, bytes_accessed=1, transcendentals=0)
+    return pl.pallas_call(
+        mark_kernel,
+        in_specs=[pl.BlockSpec(memory_space=pl.ANY)] * len(arrays) + [whole],
+        out_specs=whole,
+        out_shape=jax.ShapeDtypeStruct(before.shape, before.dtype),
+        cost_estimate=cost,
+        name="mark",
+    )(*arrays, before)
 
 
 def dot(a, b):
@@ -627,22 +668,27 @@
     steps = range(ring)
     core = lax.axis_index("c")
     column = lax.axis_index("zl")
-    place = jnp.stack([core, column]).astype(jnp.int32)
+    place = jnp.stack([core, column, lax.axis_index("zh")]).astype(jnp.int32)
     rows = tokens.shape[0]
     length = 2 * ring * rows
+    marks = [jnp.zeros((8, LANES), f32)]
+
+    def order(first, then, long=0):
+        marks[0], then = together(mark(first, marks[0], long), then)
+        return then
 
     def swap_chips(own):
         return [from_neighbour(own, k, ring) for k in steps[1:]]
 
     def join_cores(partial, kind=bf16):
-        theirs = other_core(partial(slice(rows, 2 * rows), bf16))
-        return partial(slice(0, rows), kind, theirs)
+        theirs = other_core(partial(rows, bf16, None))
+        return partial(0, kind, theirs)
 
     def join(mine, theirs):
         return row_pass(add_rows, "join", [(mine, 0), (theirs, 0)], [], [bf16])[0]
 
-    def chip_slice(k, r):
-        return slice(2 * rows * k + r.start, 2 * rows * k + r.stop)
+    def split_cores(partial):
+        return [partial(0, bf16, None), other_core(partial(rows, bf16, None))]
 
     def send_chips(joined):
         return [
@@ -658,6 +704,14 @@
                     base = (2 * c + zh) * ring
                     out += [(base + i, base + (i - k) % ring) for i in steps]
         return out
+
+    def cross_tokens(a):
+        pairs = []
+        for c, zh in ((0, 1), (1, 0)):
+            pairs += [
+                ((2 * c + zh) * ring + i, (2 * zh + c) * ring + ring - 1 - i) for i in steps
+            ]
+        return lax.ppermute(a, ("c", "zh", "zl"), pairs)
 
     def early_neighbours(original):
         return [
@@ -684,30 +738,22 @@
         ],
         1,
     )
-    places = jnp.where(stays(), positions, other_core(positions)).reshape(2, ring, rows)
-    attn_shard = after(places, attn_shard)
+    other_positions = other_core(positions)
     attn_pair = spread_pair(attn_shard)
+    cot_early = early_neighbours(cotangent)
+    attn_pair, cot_early, tokens, other_positions = together(
+        attn_pair, cot_early, tokens, other_positions
+    )
+    places = jnp.where(stays(), positions, other_positions).reshape(2 * ring, rows)
     attn_rows = arrange(*attn_pair)
-    tokens = after(attn_rows, tokens)
     attn_full = gather_rows(attn_rows)
-    stream_raw = cross(tokens)
+    stream_raw = cross_tokens(tokens)
     tokens_early = early_neighbours(tokens)
 
-    ordered = [
-        lax.dynamic_index_in_dim(
-            lax.dynamic_index_in_dim(places, (core + j) % 2, 0, keepdims=False),
-            (column + k) % ring,
-            0,
-            keepdims=False,
-        )
-        for k in steps
-        for j in range(2)
-    ]
-    firsts = [
-        ((core + j) % 2 * ring + (column + k) % ring) * rows for k in steps for j in range(2)
-    ]
+    blocks = [global_block(l, place, ring) for l in range(2 * ring)]
+    ordered = [lax.dynamic_index_in_dim(places, g, 0, keepdims=False) for g in blocks]
     start = jnp.concatenate(
-        [f + jnp.arange(rows, dtype=jnp.int32) - o for f, o in zip(firsts, ordered)]
+        [g * rows + jnp.arange(rows, dtype=jnp.int32) - o for g, o in zip(blocks, ordered)]
     )[None, :]
     spots = jnp.concatenate(ordered).astype(f32)
     inverse = rope_base ** (-(2.0 / HEAD_SIZE) * jnp.arange(half, dtype=f32))
@@ -717,82 +763,86 @@
     cos = jnp.concatenate([cos_half, gap, cos_half, gap], 1)
     sin = jnp.concatenate([-sin_half, gap, sin_half, gap], 1)
 
-    stream_raw, tokens_early = after((cos, sin, start), (stream_raw, tokens_early))
-    ff_cols = after((stream_raw, tokens_early), jnp.concatenate([w_gate, w_up, w_down], 1))
+    ff_cols = jnp.concatenate([w_gate, w_up, w_down], 1)
+    cos, sin, start, stream_raw, tokens_early, ff_cols = together(
+        cos, sin, start, stream_raw, tokens_early, ff_cols
+    )
     stream_own = jnp.where(stays(), tokens, stream_raw)
     tokens_late = late_neighbours(stream_raw)
     ff_pair = spread_pair(ff_cols)
 
-    out_columns = ((qw + 2 * kw) // qw, (qw + 2 * kw) // qw + 1)
+    out_columns = ((qw + 2 * kw) // qw, qw)
+    qkv_columns = (0, qw + 2 * kw)
     gain_first = attn_full[:, half].astype(f32)[None, :]
     gain_second = attn_full[:, half + 1].astype(f32)[None, :]
 
     projected = project(
         (stream_own, other_core(stream_own)), gain_first, attn_full, cos, sin, qw, kw, 0, ()
     )
-    (tokens_late, ff_pair), projected = together((tokens_late, ff_pair), projected)
+    tokens_late, ff_pair, projected, cot_sent = together(
+        tokens_late, ff_pair, projected, cotangent
+    )
     others = [(x, other_core(x)) for x in choose(tokens_early, tokens_late)]
-    others, ff_pair = together(others, ff_pair)
     ff_rows = arrange(*ff_pair)
     ff_full = gather_rows(ff_rows)
-    cot_sent = after(others, cotangent)
-    cot_raw = cross(cot_sent)
-    cot_early = early_neighbours(cot_sent)
+    cot_raw = cross_tokens(cot_sent)
+    others, projected = order([others[0][1], ff_rows], (others, projected), 8)
     for k, pair in enumerate(others, 1):
         projected = project(pair, gain_first, attn_full, cos, sin, qw, kw, k, projected)
     normed_first, q, k, v = projected
-    o, lse = attend(place, q, k, v, start, ring)
-    o, (cot_raw, cot_early) = together(o, (cot_raw, cot_early))
-
-    def out_product(k):
-        return lambda r, kind, add=None: product(
-            o, attn_full, cols_both, kind, chip_slice(k, r), out_columns, add
+
+    def out_product(o):
+        return lambda first, kind, add: product(
+            [(o, first)], rows, attn_full, cols_both, kind, out_columns, add
         )
 
     def whole_rows(*arrays):
         return [(a, 0) for a in arrays]
 
-    sent = send_chips([join_cores(out_product(k)) for k in steps[1:]])
-    joined = join_cores(out_product(0))
-    cot_own = after(joined, jnp.where(stays(), cotangent, cot_raw))
-    sent = after((joined, cot_own), sent)
+    attended = [attend(i, place, q, k, v, start, ring) for i in steps[1:]]
+    attended, cot_raw = together(attended, cot_raw)
+    joined = [join_cores(out_product(o)) for o, _ in attended]
+    sent = send_chips(joined)
+    q, k, v = order(joined, (q, k, v), 8)
+    attended.insert(0, attend(0, place, q, k, v, start, ring))
+    out_own = split_cores(out_product(attended[0][0]))
+    sent, out_own[0] = together(sent, out_own[0])
     middle, normed_second = row_pass(
         norm_forward,
         "norm_forward",
-        whole_rows(stream_own, joined, *sent),
+        whole_rows(stream_own, *out_own, *sent),
         [gain_second],
         [f32, bf16],
     )
-
+    normed_second, cot_raw = together(normed_second, cot_raw)
+    cot_own = jnp.where(stays(), cotangent, cot_raw)
     ff_others = swap_chips(normed_second)
-    cot_late = late_neighbours(after(normed_second, cot_own))
+    cot_late = late_neighbours(cot_raw)
     ff_in = [(normed_second, other_core(normed_second))]
     out_grads = [(cot_own, other_core(cot_own))]
+    ff_in, out_grads = order([normed_second], (ff_in, out_grads), 8)
     hidden = [hidden_pass(ff_in[0], out_grads[0], ff_full)]
-    hidden[0], (ff_others, cot_late) = together(hidden[0], (ff_others, cot_late))
-
-    def halves(array):
-        return [array, other_core(array[rows:])]
-
-    second_own = halves(hidden[0][2])
-    mixed_own = halves(hidden[0][3])
+    hidden, ff_others, cot_late = together(hidden, ff_others, cot_late)
+
+    second_own = [hidden[0][2], other_core(hidden[0][3])]
+    mixed_own = [hidden[0][4], other_core(hidden[0][5])]
     for a, dy in zip(ff_others, choose(cot_early, cot_late)):
-        ff_in.append((a, other_core(a)))
-        out_grads.append((dy, other_core(dy)))
-        hidden.append(hidden_pass(ff_in[-1], out_grads[-1], ff_full))
+        a, dy = (a, other_core(a)), (dy, other_core(dy))
+        ff_in.append(a)
+        out_grads.append(dy)
+        hidden.append(hidden_pass(a, dy, ff_full))
 
     def pieces(pairs, hidden, i):
         return [(a, 0, h[i], j) for pair, h in zip(pairs, hidden) for j, a in enumerate(pair)]
 
-    joined = [join(*halves(h[2])) for h in hidden[1:]]
-    mixed_joined = [join(*halves(h[3])) for h in hidden[1:]]
+    joined = [join(h[2], other_core(h[3])) for h in hidden[1:]]
     sent = send_chips(joined)
-    (mixed_joined, second_own, mixed_own), hidden = after(
-        joined, ((mixed_joined, second_own, mixed_own), hidden)
-    )
-    down_wgrad = wgrad([pieces(out_grads, hidden, 0)], rows)
-    sent = after((mixed_joined, down_wgrad), sent)
-    down_part = sum_rows(after(sent, down_wgrad))
+    mixed_halves = [(h[4], other_core(h[5])) for h in hidden[1:]]
+    hidden, mixed_halves = order(joined, (hidden, mixed_halves), 8)
+    mixed_joined = [join(*pair) for pair in mixed_halves]
+    ff_wgrad = wgrad([pieces(ff_in, hidden, 1), pieces(out_grads, hidden, 0)], rows)
+    sent, mixed_joined, ff_wgrad = order([ff_wgrad], (sent, mixed_joined, ff_wgrad))
+    ff_part = sum_rows(ff_wgrad)
     middle_grad, db = row_pass(
         norm_back,
         "norm_back",
@@ -802,94 +852,99 @@
     )
     branch_others = swap_chips(db)
     branch = [(db, other_core(db))]
-    do = [product(b, attn_full, plain, columns=out_columns) for b in branch[0]]
-    gate_up_wgrad = wgrad([pieces(ff_in, after(do, hidden), 1)], rows)
-    branch_others = after(gate_up_wgrad, branch_others)
-    gate_up_part = sum_rows(after(branch_others, gate_up_wgrad))
-    mixed_joined, down_part = after(branch_others, (mixed_joined, down_part))
+    branch = order([db], branch, 8)
+
+    def heads_grad(pair):
+        return jnp.concatenate(
+            [product([(b, 0)], rows, attn_full, plain, columns=out_columns) for b in pair], 0
+        )
+
+    def queries_back(i, do, before):
+        o, lse = attended[i]
+        return attend_back(i, place, q, k, v, o, do, lse, start, cos, sin, ring, before)
+
+    dq, *dkv = queries_back(0, heads_grad(branch[0]), ())
+    dqs = [dq]
+    branch_others, mixed_joined, dqs, dkv = together(branch_others, mixed_joined, dqs, dkv)
     mixed_sent = send_chips(mixed_joined)
-    down_blocks = send_blocks(down_part)
-    for b in branch_others:
-        branch.append((b, other_core(b)))
-        do += [product(b, attn_full, plain, columns=out_columns) for b in branch[-1]]
-    do = jnp.concatenate(do, 0)
-    heads = []
-    kvheads = kw // LANES
-    for h in range(kvheads):
-        part = attend_back(place, q, k, v, o, do, lse, start, cos, sin, ring, h)
-        if h == 0:
-            (mixed_sent, down_blocks), (part, do) = together(
-                (mixed_sent, down_blocks), (part, do)
-            )
-            mixed = row_pass(
-                add_rows, "mixed", whole_rows(middle, *mixed_own, *mixed_sent), [], [bf16]
-            )[0]
-            mixed_raw = cross(mixed)
-        heads.append(part)
-    mixed_raw, heads = together(mixed_raw, heads)
-    mixed = jnp.where(stays(), mixed, mixed_raw)
-    gate_up_blocks = send_blocks(after(heads, gate_up_part))
-    dqkv = jnp.concatenate([h[i] for i in range(3) for h in heads], 1)
-    grad_down = add_blocks(down_blocks)
-
-    def first_product(k, dqkv):
-        return lambda r, kind, add=None: product(
-            dqkv, w_qkv, cols_both, kind, chip_slice(k, r), add=add
+    branch += order(
+        [branch_others[0]], [(b, other_core(b)) for b in branch_others], True
+    )
+    for i in steps[1:]:
+        dq, *dkv = queries_back(i, heads_grad(branch[i]), tuple(dkv))
+        dqs.append(dq)
+    mixed_sent, dqs, dkv = together(mixed_sent, dqs, dkv)
+    mixed = row_pass(add_rows, "mixed", whole_rows(middle, *mixed_own, *mixed_sent), [], [bf16])[0]
+    mixed_raw = cross_tokens(mixed)
+
+    def first_product(i, dqs, dkv):
+        base = 2 * rows * i
+        return lambda first, kind, add: product(
+            [(dqs[i], first)] + [(d, base + first) for d in dkv],
+            rows,
+            attn_full,
+            cols_both,
+            kind,
+            qkv_columns,
+            add,
         )
 
-    w_qkv = attn_full[:, : qw + 2 * kw]
-    blocks = range(2 * ring)
+    joined = [join_cores(first_product(i, dqs, dkv)) for i in steps[1:]]
+    sent = send_chips(joined)
+    ff_blocks = send_blocks(ff_part)
+    dqs, dkv = order([*joined, mixed, ff_blocks[0]], (dqs, dkv), 8)
+    first_own = split_cores(first_product(0, dqs, dkv))
     attn_wgrad = wgrad(
-        [
-            [(normed_first, i, dqkv, i) for i in blocks],
-            [(b, 0, o, i) for i, b in zip(blocks, sum(branch, ()))],
-        ],
+        [[(normed_first, 2 * i + j, dqs[i], j) for i in steps for j in range(2)]]
+        + [[(normed_first, i, d, i) for i in range(2 * ring)] for d in dkv]
+        + [[(branch[i][j], 0, attended[i][0], j) for i in steps for j in range(2)]],
         rows,
     )
-    attn_part = sum_rows(after(gate_up_part, attn_wgrad))
-    dqkv = after(attn_wgrad, dqkv)
-    joined = [join_cores(first_product(k, dqkv)) for k in steps[1:]]
-    sent = send_chips(joined)
-    dqkv = after(joined, dqkv)
-    first_own = join_cores(first_product(0, dqkv))
-    sent, (first_own, gate_up_blocks) = together(sent, (first_own, gate_up_blocks))
+    attn_part = sum_rows(attn_wgrad)
+    sent, mixed_raw, ff_blocks, first_own[0] = order(
+        [attn_wgrad], (sent, mixed_raw, ff_blocks, first_own[0])
+    )
+
     input_grad = row_pass(
         norm_back,
         "norm_back",
-        whole_rows(middle_grad, stream_own, first_own, *sent),
+        whole_rows(middle_grad, stream_own, *first_own, *sent),
         [gain_first],
         [bf16, bf16],
     )[0]
-    input_raw = cross(input_grad)
+    input_raw = cross_tokens(input_grad)
+    attn_part, mixed_raw, ff_blocks = order([input_grad], (attn_part, mixed_raw, ff_blocks), 400)
     attn_blocks = send_blocks(attn_part)
-
-    def weighed(weights, part):
-        weights = weights[:, : part.shape[1]]
-        return jnp.sum(weights.astype(f32) * part.astype(f32), 1).reshape(2, -1)
+    attn_part = order([attn_part, attn_blocks[0]], attn_part, 8)
+    mixed = jnp.where(stays(), mixed, mixed_raw)
+    grad_ff = add_blocks(ff_blocks)
+    units = w_gate.shape[1]
+    grad_gate, grad_up, grad_down = (grad_ff[:, units * i : units * (i + 1)] for i in range(3))
+
+    def weighed(weights, part, width):
+        product = weights[:, :width].astype(f32) * part[:, :width].astype(f32)
+        return jnp.sum(product, 1).reshape(2, -1)
 
     gain_parts = jnp.stack(
+        [weighed(attn_rows, attn_part, qw + 2 * kw), weighed(ff_rows, ff_part, 2 * units)]
+    )
+    gain_parts = jnp.where(core == 0, gain_parts, gain_parts[:, ::-1])
+    gain_parts = gain_parts[:, 0] + other_core(gain_parts[:, 1]) + marks[0][0, 0]
+    count = 2 * ring
+    gain_grads = sum_steps(
+        gain_parts,
         [
-            weighed(attn_rows, attn_part[:, : qw + 2 * kw]),
-            weighed(ff_rows, gate_up_part),
-        ]
-    )
-    gain_parts = jnp.where(core == 0, gain_parts, gain_parts[:, ::-1])
-    gain_grads = gain_parts[:, 0] + other_core(gain_parts[:, 1])
-    for k in steps[1:]:
-        gain_parts = from_neighbour(gain_grads, k, ring) + (gain_parts if k > 1 else gain_grads)
-    gain_grads = gain_parts if ring > 1 else gain_grads
-    gain_grads = gain_grads + lax.ppermute(gain_grads, "zh", swap_two)
-    (input_raw, attn_blocks), gain_grads = together((input_raw, attn_blocks), gain_grads)
+            lax.ppermute(gain_parts, ("zh", "zl"), [(i, (i + j) % count) for i in range(count)])
+            for j in range(1, count)
+        ],
+    )
+    gain_grads, input_raw, attn_blocks = together(gain_grads, input_raw, attn_blocks)
     input_grad = jnp.where(stays(), input_grad, input_raw).astype(f32)
-    grad_gate_up = add_blocks(gate_up_blocks)
     grad_attn = cut_heads(add_blocks(attn_blocks))
     grad_query = grad_attn[:, :qcols]
     grad_key = grad_attn[:, qcols : qcols + kcols]
     grad_value = grad_attn[:, qcols + kcols : qcols + 2 * kcols]
     grad_output = grad_attn[:, qcols + 2 * kcols :]
-    grad_gate = grad_gate_up[:, : w_gate.shape[1]]
-    grad_up = grad_gate_up[:, w_gate.shape[1] :]
-
     return (
         mixed,
         input_grad,

time: 708 us -> 663 us (0.936)
  the two profiles are of different devices: /device:TPU:0 before, /device:TPU:1 now
where the time goes in v3:
time: 663 us; the launch traced here: 653 us
  Pallas kernels  278 us (42%)
  waiting for transfers between devices  207 us (31%)
  starting transfers between devices  60 us (9%)
  local copies, waits for them, and re-layouts  54.2 us (8%)
  other arithmetic  37.9 us (6%)
  between operations  15.2 us (2%)
    pallas_call x2, Pallas kernels, hidden_pass(): pl.pallas_call(functools.partial(hidden_kernel, min(256, units), count),...  55 us
    ppermute x4, waiting for transfers between devices, cross(): return lax.ppermute(a, ('c', 'zh'), cross_pairs)  54.7 us
    pallas_call x2, Pallas kernels, wgrad(): pl.pallas_call(functools.partial(wgrad_kernel, counts), grid=(first,), in...  48.4 us
    unnamed x172, local copies, waits for them, and re-layouts  47.6 us
    pallas_call x2, Pallas kernels, attend_back(): pl.pallas_call(functools.partial(attend_back_kernel, ring, block, chip, f...  44.5 us
    pallas_call x12, Pallas kernels, product(): pl.pallas_call(functools.partial(product_kernel, dims, len(parts)), grid=...  43.7 us
    pallas_call x6, Pallas kernels, row_pass(): pl.pallas_call(kernel, grid=(rows // block,), in_specs=[pl.BlockSpec((blo...  28.4 us
    ppermute x4, waiting for transfers between devices, send_chips(): lax.ppermute(p.astype(bf16), 'zl', [(i, (i + k) % ring) for i in steps])  28 us
  transfers between devices with their start and end apart: 47, of which 25 were waited for; matrix products, arithmetic and copies ran while one was open for 6% of the time, Pallas kernels for 38%

profile of v3, /device:TPU:1, one launch (start us, length us, event | category | flops | bytes accessed | tf_op | source)
XLA Modules:
  0.0 652.7 jit_solution(14629535688765071808)
XLA Ops:
  13.9 5.6 collective-permute-start
  21.2 23.2 %collective-permute-done = bf16[192,1536]{1,0:T(8,128)(2,1)S(1)} collective-permute-done((bf16[192,1536]{1,0:T(8,128)(2,1)S(1)}, bf16[192,1536]{1,0:T(8,128)(2,1)S(1)}, u32[]{:S(2)}, u32[]{:S(2)}) %collective-permute-start) | collective-permute-done | bytes 589856 | tf_op jit(solution)/shard_map/ppermute | solution.py:564
  49.1 5.5 collective-permute-start.4
  56.6 3.7 fusion.4
  61.6 27.1 %collective-permute-done.4 = bf16[512,1536]{1,0:T(8,128)(2,1)} collective-permute-done((bf16[512,1536]{1,0:T(8,128)(2,1)}, bf16[512,1536]{1,0:T(8,128)(2,1)}, u32[]{:S(2)}, u32[]{:S(2)}) %collective-permute-start.4) | collective-permute-done | bytes 1572896 | tf_op jit(solution)/shard_map/ppermute | solution.py:714
  92.3 3.3 collective-permute-start.6
  95.6 4.5 collective-permute-start.7
  100.2 6.5 all-gather.3.cloned.1.call-done.w_ref.refs_1_.refs_3_
  108.5 7.6 %project.2 = (bf16[2048,1536]{1,0:T(8,128)(2,1)S(1)}, bf16[2048,512]{1,0:T(8,128)(2,1)S(1)}, bf16[2048,256]{1,0:T(8,128)(2,1)S(1)}, bf16[2048,256]{1,0:T(8,128)(2,1)S(1)}) custom-call(bf16[512,1536]{1,0:T(8,128)(2,1)} %broadcast_select_fusion.4.x_ref.refs_0_.refs_1_, bf16[512,1536]{1,0:T(8,128)(2,1)} %collective-permute-done.9.y_ref, ...), custom_call_target="tpu_custom_call" | custom-call | flops 1 | bytes 1 | tf_op jit(solution)/shard_map/project/pallas_call | solution.py:314
  118.8 31.4 %collective-permute-done.7 = bf16[192,3072]{1,0:T(8,128)(2,1)} collective-permute-done((bf16[192,3072]{1,0:T(8,128)(2,1)S(1)}, bf16[192,3072]{1,0:T(8,128)(2,1)}, u32[]{:S(2)}, u32[]{:S(2)}) %collective-permute-start.7) | collective-permute-done | bytes 1179680 | tf_op jit(solution)/shard_map/ppermute | solution.py:564
  158.7 4.4 collective-permute-start.11
  166.2 9.5 %project.3 = (bf16[2048,1536]{1,0:T(8,128)(2,1)}, bf16[2048,512]{1,0:T(8,128)(2,1)}, bf16[2048,256]{1,0:T(8,128)(2,1)}, bf16[2048,256]{1,0:T(8,128)(2,1)}) custom-call(bf16[512,1536]{1,0:T(8,128)(2,1)} %copy-done.58, bf16[512,1536]{1,0:T(8,128)(2,1)} %copy-done.68, ...), custom_call_target="tpu_custom_call", output_to_operand_aliasing={{0}: (6, {}), {1}: (7, {}), {2}: (8, {}), {3}: (9, {})} | custom-call | flops 1 | bytes 1 | tf_op jit(solution)/shard_map/project/pallas_call | solution.py:314
  179.7 13.7 %attend.2 = (bf16[1024,512]{1,0:T(8,128)(2,1)S(1)}, f32[2,2,1024]{2,1,0:T(2,128)S(1)}) custom-call(s32[3]{0:T(128)S(1)} %pad_add_fusion.1.place_ref, bf16[2048,512]{1,0:T(8,128)(2,1)S(1)} %copy-done.2, bf16[2048,256]{1,0:T(8,128)(2,1)S(1)} %copy-done.15, bf16[2048,256]{1,0:T(8,128)(2,1)S(1)} %copy-done.20, s32[1,2048]{1,0:T(1,128)S(1)} %bitcast.24), custom_call_target="tpu_custom_call" | custom-call | flops 1 | bytes 1 | tf_op jit(solution)/shard_map/attend/pallas_call | solution.py:100
  193.5 3.0 product.12
  196.6 3.4 collective-permute-done.12.refs_2_
  200.0 4.0 product.13.refs_0_
  210.3 13.5 %attend.3 = (bf16[1024,512]{1,0:T(8,128)(2,1)S(1)}, f32[2,2,1024]{2,1,0:T(2,128)S(1)}) custom-call(s32[3]{0:T(128)S(1)} %pad_add_fusion.1.place_ref, bf16[2048,512]{1,0:T(8,128)(2,1)S(1)} %copy-done.3, bf16[2048,256]{1,0:T(8,128)(2,1)S(1)} %copy-done.16, bf16[2048,256]{1,0:T(8,128)(2,1)S(1)} %copy-done.21, s32[1,2048]{1,0:T(1,128)S(1)} %bitcast.25), custom_call_target="tpu_custom_call" | custom-call | flops 1 | bytes 1 | tf_op jit(solution)/shard_map/attend/pallas_call | solution.py:100
  223.9 3.0 product.15
  231.8 9.7 %collective-permute-done.13.refs_3_ = bf16[512,1536]{1,0:T(8,128)(2,1)} collective-permute-done((bf16[512,1536]{1,0:T(8,128)(2,1)}, bf16[512,1536]{1,0:T(8,128)(2,1)}, u32[]{:S(2)}, u32[]{:S(2)}) %collective-permute-start.13) | collective-permute-done | bytes 1572896 | tf_op jit(solution)/shard_map/ppermute | solution.py:695
  241.5 5.0 norm_forward.1
  255.6 27.7 %hidden.2 = (bf16[1024,1024]{1,0:T(8,128)(2,1)}, bf16[1024,2048]{1,0:T(8,128)(2,1)}, bf16[512,1536]{1,0:T(8,128)(2,1)S(1)}, bf16[512,1536]{1,0:T(8,128)(2,1)S(1)...) custom-call(bf16[512,1536]{1,0:T(8,128)(2,1)} %get-tuple-element.199.refs_0_.a_ref, ...), custom_call_target="tpu_custom_call" | custom-call | flops 1 | bytes 1 | tf_op jit(solution)/shard_map/hidden/pallas_call | solution.py:378
  285.7 17.5 %collective-permute-done.18 = bf16[512,1536]{1,0:T(8,128)(2,1)} collective-permute-done((bf16[512,1536]{1,0:T(8,128)(2,1)}, bf16[512,1536]{1,0:T(8,128)(2,1)}, u32[]{:S(2)}, u32[]{:S(2)}) %collective-permute-start.18) | collective-permute-done | bytes 1572896 | tf_op jit(solution)/shard_map/ppermute | solution.py:722
  305.4 4.4 collective-permute-done.22.dz_ref.refs_11_
  310.8 27.3 %hidden.3 = (bf16[1024,1024]{1,0:T(8,128)(2,1)}, bf16[1024,2048]{1,0:T(8,128)(2,1)}, bf16[512,1536]{1,0:T(8,128)(2,1)S(1)}, bf16[512,1536]{1,0:T(8,128)(2,1)S(1)...) custom-call(bf16[512,1536]{1,0:T(8,128)(2,1)} %collective-permute-done.17.a_ref.refs_2_, ...), custom_call_target="tpu_custom_call" | custom-call | flops 1 | bytes 1 | tf_op jit(solution)/shard_map/hidden/pallas_call | solution.py:378
  341.0 3.7 collective-permute-done.23.refs_1_
  358.9 27.4 %wgrad.2.refs_0_ = bf16[1536,3072]{1,0:T(8,128)(2,1)} custom-call(bf16[512,1536]{1,0:T(8,128)(2,1)} %get-tuple-element.199.refs_0_.a_ref, bf16[512,1536]{1,0:T(8,128)(2,1)} %collective-permute-done.15.b_ref.refs_1_, bf16[512,1536]{1,0:T(8,128)(2,1)} %collective-permute-done.17.a_ref.refs_2_, bf16[512,1536]{1,0:T(8,128)(2,1)S(1)} %copy-done.36, ...), custom_call_target="tpu_custom_call" | custom-call | flops 1 | bytes 1 | tf_op jit(solution)/shard_map/wgrad/pallas_call | solution.py:474
  388.2 3.4 collective-permute-done.20.refs_3_
  391.5 7.2 %norm_back.2 = (f32[512,1536]{1,0:T(8,128)}, bf16[512,1536]{1,0:T(8,128)(2,1)}) custom-call(bf16[512,1536]{1,0:T(8,128)(2,1)} %broadcast_select_fusion.2.dy_ref.refs_8_.refs_0_, f32[512,1536]{1,0:T(8,128)} %get-tuple-element.193.refs_1_.refs_0_, bf16[512,1536]{1,0:T(8,128)(2,1)} %copy-done.47, bf16[512,1536]{1,0:T(8,128)(2,1)} %collective-permute-done.20.refs_3_, ...), custom_call_target="tpu_custom_call" | custom-call | flops 1 | bytes 1 | tf_op jit(solution)/shard_map/norm_back/pallas_call | solution.py:499
  406.7 3.1 product.17
  411.6 21.1 %attend_back.2 = (bf16[1024,512]{1,0:T(8,128)(2,1)S(1)}, f32[2048,256]{1,0:T(8,128)S(1)}, f32[2048,256]{1,0:T(8,128)S(1)}) custom-call(s32[3]{0:T(128)S(1)} %pad_add_fusion.1.place_ref, bf16[2048,512]{1,0:T(8,128)(2,1)S(1)} %copy-done.3, bf16[2048,256]{1,0:T(8,128)(2,1)S(1)} %copy-done.17, bf16[2048,256]{1,0:T(8,128)(2,1)S(1)} %copy-done.22, ...), custom_call_target="tpu_custom_call" | custom-call | flops 1 | bytes 1 | tf_op jit(solution)/shard_map/attend_back/pallas_call | solution.py:232
  438.5 3.4 collective-permute-done.29.refs_0_.refs_27_
  441.8 3.4 product.18
  449.8 23.4 %attend_back.3 = (bf16[1024,512]{1,0:T(8,128)(2,1)S(1)}, bf16[2048,256]{1,0:T(8,128)(2,1)S(1)}, bf16[2048,256]{1,0:T(8,128)(2,1)S(1)}) custom-call(s32[3]{0:T(128)S(1)} %pad_add_fusion.1.place_ref, bf16[2048,512]{1,0:T(8,128)(2,1)S(1)} %copy-done.4, bf16[2048,256]{1,0:T(8,128)(2,1)S(1)} %copy-done.18, bf16[2048,256]{1,0:T(8,128)(2,1)S(1)} %copy-done.23, ...), custom_call_target="tpu_custom_call" | custom-call | flops 1 | bytes 1 | tf_op jit(solution)/shard_map/attend_back/pallas_call | solution.py:232
  473.4 5.0 product.20
  479.1 4.6 mixed.1.refs_1_
  486.2 5.1 product.21.refs_0_
  491.3 3.2 broadcast_select_fusion.6
  497.0 4.9 product.23
  501.9 5.4 collective-permute-start.33
  513.9 21.0 %wgrad.3.refs_0_ = bf16[1536,1536]{1,0:T(8,128)(2,1)} custom-call(bf16[2048,1536]{1,0:T(8,128)(2,1)} %get-tuple-element.256.refs_0_.refs_1_.refs_2_.refs_3_.refs_8_.refs_9_.refs_10_.refs_11_.refs_16_.refs_17_.refs_18_.refs_19_, ...), custom_call_target="tpu_custom_call" | custom-call | flops 1 | bytes 1 | tf_op jit(solution)/shard_map/wgrad/pallas_call | solution.py:474
  536.3 4.1 product.22.refs_2_
  542.7 18.1 %collective-permute-done.31.refs_4_ = bf16[512,1536]{1,0:T(8,128)(2,1)} collective-permute-done((bf16[512,1536]{1,0:T(8,128)(2,1)}, bf16[512,1536]{1,0:T(8,128)(2,1)}, u32[]{:S(2)}, u32[]{:S(2)}) %collective-permute-start.31) | collective-permute-done | bytes 1572896 | tf_op jit(solution)/shard_map/ppermute | solution.py:695
  562.9 5.8 norm_back.3
  568.7 5.4 collective-permute-start.40
  575.4 15.4 %reduce-scatter.5.cloned.1.call-done.refs_0_ = bf16[384,1536]{1,0:T(8,128)(2,1)} async-done(((bf16[1536,1536]{1,0:T(8,128)(2,1)}), bf16[384,1536]{1,0:T(8,128)(2,1)}) %reduce-scatter.5.cloned.1.call-update) | async-done | bytes 1179664 | tf_op jit(solution)/shard_map/reduce_scatter | solution.py:610
  593.0 4.9 collective-permute-start.41
  613.0 23.1 %collective-permute-done.39 = f32[2,192]{1,0:T(2,128)S(1)} collective-permute-done((f32[2,192]{1,0:T(2,128)S(1)}, f32[2,192]{1,0:T(2,128)S(1)}, u32[]{:S(2)}, u32[]{:S(2)}) %collective-permute-start.39) | collective-permute-done | bytes 1568 | tf_op jit(solution)/shard_map/ppermute | solution.py:937
  641.5 3.3 select_convert_fusion
  (320 shorter events, 147.5 us)
Async XLA Ops:
  7.2 99.5 %all-gather.3.cloned.1.call-start = ((), (), s32[]{:S(2)}) async-start(), calls=%async_computation.2 | async-start | bytes 5898240 | tf_op jit(solution)/shard_map/all_gather | solution.py:592
  7.2 38.8 %collective-permute-start.2 = (bf16[512,1536]{1,0:T(8,128)(2,1)}, bf16[512,1536]{1,0:T(8,128)(2,1)S(1)}, u32[]{:S(2)}, u32[]{:S(2)}) collective-permute-start(bf16[512,1536]{1,0:T(8,128)(2,1)} %param.23), channel_id=1, source_target_pairs={{0,1},{1,0},{6,7},{7,6},{8,9},{9,8},{14,15},{15,14},{16,17},{17,16... | collective-permute-start | bytes 4718600 | tf_op jit(solution)/shard_map/ppermute | solution.py:718
  13.9 30.5 %collective-permute-start = (bf16[192,1536]{1,0:T(8,128)(2,1)S(1)}, bf16[192,1536]{1,0:T(8,128)(2,1)S(1)}, u32[]{:S(2)}, u32[]{:S(2)}) collective-permute-start(bf16[192,1536]{1,0:T(8,128)(2,1)S(1)} %concatenate.46), channel_id=1, source_target_pairs={{2,4},{4,2},{3,5},{5,3},{10,12},{12,10},{11,13},{13,11},{18,20},{2... | collective-permute-start | bytes 1769480 | tf_op jit(solution)/shard_map/ppermute | solution.py:564
  19.5 26.6 %collective-permute-start.1 = (bf16[192,1536]{1,0:T(8,128)(2,1)S(1)}, bf16[192,1536]{1,0:T(8,128)(2,1)S(1)}, u32[]{:S(2)}, u32[]{:S(2)}) collective-permute-start(bf16[192,1536]{1,0:T(8,128)(2,1)S(1)} %concatenate.46), channel_id=1, source_target_pairs={{0,2},{2,6},{4,0},{6,4},{1,3},{3,7},{5,1},{7,5},{8,10},{10,14},{12... | collective-permute-start | bytes 1769480 | tf_op jit(solution)/shard_map/ppermute | solution.py:580
  19.6 1.6 collective-permute-start.3
  48.5 207.1 %all-gather.5.cloned.1.call-start = ((), (), s32[]{:S(2)}) async-start(), calls=%async_computation.3 | async-start | bytes 11796480 | tf_op jit(solution)/shard_map/all_gather | solution.py:592
  49.1 39.6 %collective-permute-start.4 = (bf16[512,1536]{1,0:T(8,128)(2,1)}, bf16[512,1536]{1,0:T(8,128)(2,1)}, u32[]{:S(2)}, u32[]{:S(2)}) collective-permute-start(bf16[512,1536]{1,0:T(8,128)(2,1)} %param.12), channel_id=1, source_target_pairs={{2,5},{3,4},{4,3},{5,2},{10,13},{11,12},{12,11},{13,10},{18,21},{1... | collective-permute-start | bytes 4718600 | tf_op jit(solution)/shard_map/ppermute | solution.py:714
  54.6 34.1 %collective-permute-start.5 = (bf16[512,1536]{1,0:T(8,128)(2,1)}, bf16[512,1536]{1,0:T(8,128)(2,1)}, u32[]{:S(2)}, u32[]{:S(2)}) collective-permute-start(bf16[512,1536]{1,0:T(8,128)(2,1)} %param.12), channel_id=1, source_target_pairs={{0,1},{1,0},{6,7},{7,6},{8,9},{9,8},{14,15},{15,14},{16,17},{17,16... | collective-permute-start | bytes 4718600 | tf_op jit(solution)/shard_map/ppermute | solution.py:718
  61.6 104.7 %copy-start.5 = (f32[2048,128]{1,0:T(8,128)}, f32[2048,128]{1,0:T(8,128)S(1)}, u32[]{:S(2)}) copy-start(f32[2048,128]{1,0:T(8,128)S(1)} %get-tuple-element.158.cos_ref.cosq_ref.refs_0_) | copy-start | bytes 3145732
  91.4 17.1 %collective-permute-start.9 = (bf16[512,1536]{1,0:T(8,128)(2,1)}, bf16[512,1536]{1,0:T(8,128)(2,1)}, u32[]{:S(2)}, u32[]{:S(2)}) collective-permute-start(bf16[512,1536]{1,0:T(8,128)(2,1)} %broadcast_select_fusion.4.x_ref.refs_0_.refs_1_), channel_id=1, source_target_pairs={{0,4},{4,0},{1,5},{5,1},{2,6},{6,2},{3,7},{7,3},{8,12},{12,8},{9,1... | collective-permute-start | bytes 4718600 | tf_op jit(solution)/shard_map/ppermute | solution.py:568
  92.3 59.8 %collective-permute-start.6 = (bf16[512,1536]{1,0:T(8,128)(2,1)}, bf16[512,1536]{1,0:T(8,128)(2,1)}, u32[]{:S(2)}, u32[]{:S(2)}) collective-permute-start(bf16[512,1536]{1,0:T(8,128)(2,1)} %collective-permute-done.4), channel_id=1, source_target_pairs={{2,3},{3,2},{4,5},{5,4},{10,11},{11,10},{12,13},{13,12},{18,19},{1... | collective-permute-start | bytes 4718600 | tf_op jit(solution)/shard_map/ppermute | solution.py:722
  95.6 54.6 %collective-permute-start.7 = (bf16[192,3072]{1,0:T(8,128)(2,1)S(1)}, bf16[192,3072]{1,0:T(8,128)(2,1)}, u32[]{:S(2)}, u32[]{:S(2)}) collective-permute-start(bf16[192,3072]{1,0:T(8,128)(2,1)S(1)} %pad_maximum_fusion.6), channel_id=1, source_target_pairs={{2,4},{4,2},{3,5},{5,3},{10,12},{12,10},{11,13},{13,11},{18,20},{2... | collective-permute-start | bytes 3538952 | tf_op jit(solution)/shard_map/ppermute | solution.py:564
  100.1 52.0 %collective-permute-start.8 = (bf16[192,3072]{1,0:T(8,128)(2,1)S(1)}, bf16[192,3072]{1,0:T(8,128)(2,1)}, u32[]{:S(2)}, u32[]{:S(2)}) collective-permute-start(bf16[192,3072]{1,0:T(8,128)(2,1)S(1)} %pad_maximum_fusion.6), channel_id=1, source_target_pairs={{0,2},{2,6},{4,0},{6,4},{1,3},{3,7},{5,1},{7,5},{8,10},{10,14},{12... | collective-permute-start | bytes 3538952 | tf_op jit(solution)/shard_map/ppermute | solution.py:580
  156.9 334.3 %reduce-scatter.3.cloned.1.call-start = ((), (), s32[]{:S(2)}) async-start(), calls=%async_computation.4 | async-start | bytes 11796480 | tf_op jit(solution)/shard_map/reduce_scatter | solution.py:610
  158.6 4.6 collective-permute-start.10
  158.7 34.8 %collective-permute-start.11 = (bf16[512,1536]{1,0:T(8,128)(2,1)}, bf16[512,1536]{1,0:T(8,128)(2,1)}, u32[]{:S(2)}, u32[]{:S(2)}) collective-permute-start(bf16[512,1536]{1,0:T(8,128)(2,1)} %param.23), channel_id=1, source_target_pairs={{2,5},{3,4},{4,3},{5,2},{10,13},{11,12},{12,11},{13,10},{18,21},{1... | collective-permute-start | bytes 4718600 | tf_op jit(solution)/shard_map/ppermute | solution.py:714
  196.5 3.5 collective-permute-start.12
  204.0 37.5 %collective-permute-start.13 = (bf16[512,1536]{1,0:T(8,128)(2,1)}, bf16[512,1536]{1,0:T(8,128)(2,1)}, u32[]{:S(2)}, u32[]{:S(2)}) collective-permute-start(bf16[512,1536]{1,0:T(8,128)(2,1)} %product.13.refs_0_), channel_id=1, source_target_pairs={{0,1},{1,0},{2,3},{3,2},{4,5},{5,4},{6,7},{7,6},{8,9},{9,8},{10,11... | collective-permute-start | bytes 4718600 | tf_op jit(solution)/shard_map/ppermute | solution.py:695
  226.9 14.6 %collective-permute-start.14 = (bf16[512,1536]{1,0:T(8,128)(2,1)S(1)}, bf16[512,1536]{1,0:T(8,128)(2,1)}, u32[]{:S(2)}, u32[]{:S(2)}) collective-permute-start(bf16[512,1536]{1,0:T(8,128)(2,1)S(1)} %product.15), channel_id=1, source_target_pairs={{0,4},{4,0},{1,5},{5,1},{2,6},{6,2},{3,7},{7,3},{8,12},{12,8},{9,1... | collective-permute-start | bytes 4718600 | tf_op jit(solution)/shard_map/ppermute | solution.py:568
  249.2 5.6 collective-permute-start.16
  249.9 5.6 collective-permute-start.15
  249.9 35.8 %collective-permute-start.17 = (bf16[512,1536]{1,0:T(8,128)(2,1)}, bf16[512,1536]{1,0:T(8,128)(2,1)}, u32[]{:S(2)}, u32[]{:S(2)}) collective-permute-start(bf16[512,1536]{1,0:T(8,128)(2,1)} %get-tuple-element.199.refs_0_.a_ref), channel_id=1, source_target_pairs={{0,1},{1,0},{2,3},{3,2},{4,5},{5,4},{6,7},{7,6},{8,9},{9,8},{10,11... | collective-permute-start | bytes 4718600 | tf_op jit(solution)/shard_map/ppermute | solution.py:572
  251.4 51.8 %collective-permute-start.18 = (bf16[512,1536]{1,0:T(8,128)(2,1)}, bf16[512,1536]{1,0:T(8,128)(2,1)}, u32[]{:S(2)}, u32[]{:S(2)}) collective-permute-start(bf16[512,1536]{1,0:T(8,128)(2,1)} %collective-permute-done.11), channel_id=1, source_target_pairs={{2,3},{3,2},{4,5},{5,4},{10,11},{11,10},{12,13},{13,12},{18,19},{1... | collective-permute-start | bytes 4718600 | tf_op jit(solution)/shard_map/ppermute | solution.py:722
  304.8 4.9 collective-permute-start.22
  304.9 5.9 collective-permute-start.21
  340.5 4.2 collective-permute-start.23
  340.6 11.1 %collective-permute-start.24 = (bf16[512,1536]{1,0:T(8,128)(2,1)}, bf16[512,1536]{1,0:T(8,128)(2,1)}, u32[]{:S(2)}, u32[]{:S(2)}) collective-permute-start(bf16[512,1536]{1,0:T(8,128)(2,1)} %get-tuple-element.223), channel_id=1, source_target_pairs={{0,4},{4,0},{1,5},{5,1},{2,6},{6,2},{3,7},{7,3},{8,12},{12,8},{9,1... | collective-permute-start | bytes 4718600 | tf_op jit(solution)/shard_map/ppermute | solution.py:568
  348.8 38.8 %collective-permute-start.25 = (bf16[512,1536]{1,0:T(8,128)(2,1)}, bf16[512,1536]{1,0:T(8,128)(2,1)}, u32[]{:S(2)}, u32[]{:S(2)}) collective-permute-start(bf16[512,1536]{1,0:T(8,128)(2,1)} %join.2.refs_0_), channel_id=1, source_target_pairs={{0,1},{1,0},{2,3},{3,2},{4,5},{5,4},{6,7},{7,6},{8,9},{9,8},{10,11... | collective-permute-start | bytes 4718600 | tf_op jit(solution)/shard_map/ppermute | solution.py:695
  387.6 203.2 %reduce-scatter.5.cloned.1.call-start = ((), (), s32[]{:S(2)}) async-start(), calls=%async_computation.5 | async-start | bytes 5898240 | tf_op jit(solution)/shard_map/reduce_scatter | solution.py:610
  387.7 3.9 collective-permute-start.20
  398.7 3.9 collective-permute-start.27
  399.3 37.1 %collective-permute-start.26 = (bf16[512,1536]{1,0:T(8,128)(2,1)}, bf16[512,1536]{1,0:T(8,128)(2,1)}, u32[]{:S(2)}, u32[]{:S(2)}) collective-permute-start(bf16[512,1536]{1,0:T(8,128)(2,1)} %get-tuple-element.236.refs_0_.refs_24_), channel_id=1, source_target_pairs={{0,1},{1,0},{2,3},{3,2},{4,5},{5,4},{6,7},{7,6},{8,9},{9,8},{10,11... | collective-permute-start | bytes 4718600 | tf_op jit(solution)/shard_map/ppermute | solution.py:572
  436.4 5.4 collective-permute-start.29
  437.1 36.3 %collective-permute-start.28 = (bf16[512,1536]{1,0:T(8,128)(2,1)}, bf16[512,1536]{1,0:T(8,128)(2,1)}, u32[]{:S(2)}, u32[]{:S(2)}) collective-permute-start(bf16[512,1536]{1,0:T(8,128)(2,1)} %join.3), channel_id=1, source_target_pairs={{0,1},{1,0},{2,3},{3,2},{4,5},{5,4},{6,7},{7,6},{8,9},{9,8},{10,11... | collective-permute-start | bytes 4718600 | tf_op jit(solution)/shard_map/ppermute | solution.py:695
  437.1 42.0 %collective-permute-start.19 = (bf16[512,1536]{1,0:T(8,128)(2,1)}, bf16[512,1536]{1,0:T(8,128)(2,1)}, u32[]{:S(2)}, u32[]{:S(2)}) collective-permute-start(bf16[512,1536]{1,0:T(8,128)(2,1)} %get-tuple-element.210), channel_id=1, source_target_pairs={{0,4},{4,0},{1,5},{5,1},{2,6},{6,2},{3,7},{7,3},{8,12},{12,8},{9,1... | collective-permute-start | bytes 4718600 | tf_op jit(solution)/shard_map/ppermute | solution.py:568
  478.4 7.7 %collective-permute-start.30 = (bf16[512,1536]{1,0:T(8,128)(2,1)}, bf16[512,1536]{1,0:T(8,128)(2,1)}, u32[]{:S(2)}, u32[]{:S(2)}) collective-permute-start(bf16[512,1536]{1,0:T(8,128)(2,1)} %product.20), channel_id=1, source_target_pairs={{0,4},{4,0},{1,5},{5,1},{2,6},{6,2},{3,7},{7,3},{8,12},{12,8},{9,1... | collective-permute-start | bytes 4718600 | tf_op jit(solution)/shard_map/ppermute | solution.py:568
  483.6 59.1 %collective-permute-start.32 = (bf16[512,1536]{1,0:T(8,128)(2,1)}, bf16[512,1536]{1,0:T(8,128)(2,1)}, u32[]{:S(2)}, u32[]{:S(2)}) collective-permute-start(bf16[512,1536]{1,0:T(8,128)(2,1)} %mixed.1.refs_1_), channel_id=1, source_target_pairs={{2,5},{3,4},{4,3},{5,2},{10,13},{11,12},{12,11},{13,10},{18,21},{1... | collective-permute-start | bytes 4718600 | tf_op jit(solution)/shard_map/ppermute | solution.py:714
  491.3 69.5 %collective-permute-start.31 = (bf16[512,1536]{1,0:T(8,128)(2,1)}, bf16[512,1536]{1,0:T(8,128)(2,1)}, u32[]{:S(2)}, u32[]{:S(2)}) collective-permute-start(bf16[512,1536]{1,0:T(8,128)(2,1)} %product.21.refs_0_), channel_id=1, source_target_pairs={{0,1},{1,0},{2,3},{3,2},{4,5},{5,4},{6,7},{7,6},{8,9},{9,8},{10,11... | collective-permute-start | bytes 4718600 | tf_op jit(solution)/shard_map/ppermute | solution.py:695
  501.9 61.0 %collective-permute-start.35 = (bf16[512,1536]{1,0:T(8,128)(2,1)}, bf16[512,1536]{1,0:T(8,128)(2,1)}, u32[]{:S(2)}, u32[]{:S(2)}) collective-permute-start(bf16[512,1536]{1,0:T(8,128)(2,1)} %product.23), channel_id=1, source_target_pairs={{0,4},{4,0},{1,5},{5,1},{2,6},{6,2},{3,7},{7,3},{8,12},{12,8},{9,1... | collective-permute-start | bytes 4718600 | tf_op jit(solution)/shard_map/ppermute | solution.py:568
  501.9 58.9 %collective-permute-start.33 = (bf16[192,3072]{1,0:T(8,128)(2,1)}, bf16[192,3072]{1,0:T(8,128)(2,1)}, u32[]{:S(2)}, u32[]{:S(2)}) collective-permute-start(bf16[192,3072]{1,0:T(8,128)(2,1)} %get-tuple-element.286.refs_2_), channel_id=1, source_target_pairs={{2,4},{4,2},{3,5},{5,3},{10,12},{12,10},{11,13},{13,11},{18,20},{2... | collective-permute-start | bytes 3538952 | tf_op jit(solution)/shard_map/ppermute | solution.py:564
  507.3 55.6 %collective-permute-start.34 = (bf16[192,3072]{1,0:T(8,128)(2,1)}, bf16[192,3072]{1,0:T(8,128)(2,1)}, u32[]{:S(2)}, u32[]{:S(2)}) collective-permute-start(bf16[192,3072]{1,0:T(8,128)(2,1)} %get-tuple-element.307), channel_id=1, source_target_pairs={{2,0},{6,2},{0,4},{4,6},{3,1},{7,3},{1,5},{5,7},{10,8},{14,10},{8,... | collective-permute-start | bytes 3538952 | tf_op jit(solution)/shard_map/ppermute | solution.py:600
  568.7 67.5 %collective-permute-start.40 = (bf16[512,1536]{1,0:T(8,128)(2,1)}, bf16[512,1536]{1,0:T(8,128)(2,1)}, u32[]{:S(2)}, u32[]{:S(2)}) collective-permute-start(bf16[512,1536]{1,0:T(8,128)(2,1)} %get-tuple-element.270.refs_0_), channel_id=1, source_target_pairs={{2,5},{3,4},{4,3},{5,2},{10,13},{11,12},{12,11},{13,10},{18,21},{1... | collective-permute-start | bytes 4718600 | tf_op jit(solution)/shard_map/ppermute | solution.py:714
  593.0 43.2 %collective-permute-start.41 = (bf16[192,1536]{1,0:T(8,128)(2,1)S(1)}, bf16[192,1536]{1,0:T(8,128)(2,1)}, u32[]{:S(2)}, u32[]{:S(2)}) collective-permute-start(bf16[192,1536]{1,0:T(8,128)(2,1)S(1)} %get-tuple-element.283.refs_1_), channel_id=1, source_target_pairs={{2,4},{4,2},{3,5},{5,3},{10,12},{12,10},{11,13},{13,11},{18,20},{2... | collective-permute-start | bytes 1769480 | tf_op jit(solution)/shard_map/ppermute | solution.py:564
  599.9 3.7 collective-permute-start.36
  600.0 36.2 %collective-permute-start.42 = (bf16[192,1536]{1,0:T(8,128)(2,1)}, bf16[192,1536]{1,0:T(8,128)(2,1)S(1)}, u32[]{:S(2)}, u32[]{:S(2)}) collective-permute-start(bf16[192,1536]{1,0:T(8,128)(2,1)} %get-tuple-element.315), channel_id=1, source_target_pairs={{2,0},{6,2},{0,4},{4,6},{3,1},{7,3},{1,5},{5,7},{10,8},{14,10},{8,... | collective-permute-start | bytes 1769480 | tf_op jit(solution)/shard_map/ppermute | solution.py:600
  604.3 6.9 %collective-permute-start.37 = (f32[2,192]{1,0:T(2,128)S(1)}, f32[2,192]{1,0:T(2,128)S(1)}, u32[]{:S(2)}, u32[]{:S(2)}) collective-permute-start(f32[2,192]{1,0:T(2,128)S(1)} %fusion.6), channel_id=1, source_target_pairs={{0,1},{1,2},{2,3},{3,0},{4,5},{5,6},{6,7},{7,4},{8,9},{9,10},{10,1... | collective-permute-start | bytes 4616 | tf_op jit(solution)/shard_map/ppermute | solution.py:937
  608.3 4.7 collective-permute-start.38
  611.1 25.1 %collective-permute-start.39 = (f32[2,192]{1,0:T(2,128)S(1)}, f32[2,192]{1,0:T(2,128)S(1)}, u32[]{:S(2)}, u32[]{:S(2)}) collective-permute-start(f32[2,192]{1,0:T(2,128)S(1)} %fusion.6), channel_id=1, source_target_pairs={{0,3},{1,0},{2,1},{3,2},{4,7},{5,4},{6,5},{7,6},{8,11},{9,8},{10,9... | collective-permute-start | bytes 4616 | tf_op jit(solution)/shard_map/ppermute | solution.py:937
  (79 other events, 574.3 us)
Sparse Core Ops, SparseCore 0:
  48.6 58.0 all-gather.2
  157.1 95.7 all-gather.4
  387.7 94.8 reduce-scatter.2
  535.0 55.7 reduce-scatter.4

commit v4 on v3

--- a/solution.py
+++ b/solution.py
@@ -22,6 +22,8 @@
 plain = (((1,), (0,)), ((), ()))
 f32 = jnp.float32
 light = pl.CostEstimate(flops=1, bytes_accessed=1, transcendentals=0)
+heavy = pl.CostEstimate(flops=8 * 10**9, bytes_accessed=1, transcendentals=0)
+unread = pl.BlockSpec(memory_space=pl.ANY)
 bf16 = jnp.bfloat16
 
 
@@ -46,7 +48,8 @@
     return [pltpu.with_memory_space_constraint(a, pltpu.HBM) for a in arrays]
 
 
-def attend_kernel(ring, block, chip, place_ref, q_ref, k_ref, v_ref, start_ref, o_ref, lse_ref):
+def attend_kernel(ring, block, chip, place_ref, q_ref, k_ref, v_ref, start_ref, *refs):
+    o_ref, lse_ref = refs[-2:]
     g = global_block(2 * chip + pl.program_id(1), place_ref, ring)
     share = q_ref.shape[1] // LANES
     start = start_ref[...]
@@ -84,7 +87,7 @@
         )
         for _ in range(share)
     )
-    carry = step(g, carry, 8)
+    carry = step(g, carry, True)
     carry = lax.fori_loop(0, g, lambda kb, c: step(kb, c, False), carry)
     for h in range(share):
         largest, total, acc = carry[h]
@@ -92,7 +95,7 @@
         lse_ref[0, h : h + 1, :] = largest + jnp.log2(total)
 
 
-def attend(chip, place, q, k, v, start, ring):
+def attend(chip, place, q, k, v, start, ring, first=()):
     length = q.shape[0]
     block = length // (2 * ring)
     kv = k.shape[1] // LANES
@@ -107,7 +110,8 @@
                 pl.BlockSpec((length, LANES), lambda h, j, z: (0, h)),
                 pl.BlockSpec((length, LANES), lambda h, j, z: (0, h)),
                 pl.BlockSpec((1, block), lambda h, j, z: (0, 2 * chip + j)),
-            ],
+            ]
+            + [unread] * len(first),
             out_specs=[
                 pl.BlockSpec((block, share * LANES), lambda h, j, z: (j, h)),
                 pl.BlockSpec((1, share, block), lambda h, j, z: (h, 0, j)),
@@ -120,9 +124,9 @@
         compiler_params=pltpu.CompilerParams(
             vmem_limit_bytes=40 * 2**20, dimension_semantics=("arbitrary", "arbitrary")
         ),
-        cost_estimate=light,
+        cost_estimate=heavy if first else light,
         name="attend",
-    )(place, q, k, v, start)
+    )(place, q, k, v, start, *first)
 
 
 def attend_back_kernel(
@@ -195,7 +199,7 @@
         dv_acc[pl.ds(offset, block), :] += dv
         return tuple(out)
 
-    carry = step(g, tuple(jnp.zeros((LANES, block), f32) for _ in range(share)), 8)
+    carry = step(g, tuple(jnp.zeros((LANES, block), f32) for _ in range(share)), True)
     carry = lax.fori_loop(0, g, lambda kb, c: step(kb, c, False), carry)
     for h in range(share):
         u = jnp.transpose(carry[h]) * HEAD_SIZE ** (-0.5)
@@ -297,7 +301,7 @@
     v_ref[...] = whole[:, qw + kw :].astype(bf16)
 
 
-def project(pair, gain, w, cos, sin, qw, kw, step, before):
+def project(pair, gain, w, cos, sin, qw, kw, step, before, first=()):
     rows, width = pair[0].shape
     length = cos.shape[0]
     block = min(256, rows)
@@ -316,16 +320,16 @@
         grid=(2 * count,),
         in_specs=pieces_spec(block, width, count)
         + [whole(gain.shape), whole((width, qw + 2 * kw)), row(LANES), row(LANES)]
-        + [pl.BlockSpec(memory_space=pl.ANY)] * len(before),
+        + [unread] * (len(before) + len(first)),
         out_specs=[row(n) for n in widths],
         out_shape=[jax.ShapeDtypeStruct((length, n), bf16) for n in widths],
         input_output_aliases={6 + i: i for i in range(len(before))},
         compiler_params=pltpu.CompilerParams(
             vmem_limit_bytes=40 * 2**20, dimension_semantics=("arbitrary",)
         ),
-        cost_estimate=light,
+        cost_estimate=heavy if first else light,
         name="project",
-    )(*in_hbm(*pair), gain, *in_hbm(w), cos, sin, *in_hbm(*before))
+    )(*in_hbm(*pair), gain, *in_hbm(w), cos, sin, *in_hbm(*before), *first)
 
 
 def hidden_kernel(
@@ -387,23 +391,23 @@
         compiler_params=pltpu.CompilerParams(
             vmem_limit_bytes=40 * 2**20, dimension_semantics=("arbitrary",)
         ),
-        cost_estimate=light,
+        cost_estimate=heavy,
         name="hidden",
     )(*a, *dy, w)
 
 
-def product_kernel(dims, parts, *refs):
+def product_kernel(dims, parts, unused, *refs):
     x = refs[0][...]
     if parts > 1:
         x = jnp.concatenate([ref[...] for ref in refs[:parts]], 1)
     p = lax.dot_general(x, refs[parts][...], dims, preferred_element_type=f32)
     out_ref = refs[-1]
-    for ref in refs[parts + 1 : -1]:
+    for ref in refs[parts + 1 + unused : -1]:
         p = p + ref[...].astype(f32)
     out_ref[...] = p.astype(out_ref.dtype)
 
 
-def product(parts, rows, w, dims, kind=bf16, columns=None, add=None):
+def product(parts, rows, w, dims, kind=bf16, columns=None, add=None, cost=light, after=()):
     block = min(256, rows)
     columns = columns or (0, w.shape[1])
     wide = columns[1]
@@ -411,22 +415,23 @@
     row = pl.BlockSpec((block, out), lambda i: (i, 0))
     extra = [] if add is None else [add]
     return pl.pallas_call(
-        functools.partial(product_kernel, dims, len(parts)),
+        functools.partial(product_kernel, dims, len(parts), len(after)),
         grid=(rows // block,),
         in_specs=[
             pl.BlockSpec((block, x.shape[1]), lambda i, first=first: (first // block + i, 0))
             for x, first in parts
         ]
         + [pl.BlockSpec((w.shape[0], wide), lambda i: (0, columns[0]))]
+        + [unread] * len(after)
         + [row] * len(extra),
         out_specs=row,
         out_shape=jax.ShapeDtypeStruct((rows, out), kind),
         compiler_params=pltpu.CompilerParams(
             vmem_limit_bytes=40 * 2**20, dimension_semantics=("arbitrary",)
         ),
-        cost_estimate=light,
+        cost_estimate=cost,
         name="product",
-    )(*[x for x, _ in parts], *in_hbm(w), *extra)
+    )(*[x for x, _ in parts], *in_hbm(w), *after, *extra)
 
 
 def wgrad_kernel(counts, *refs):
@@ -448,11 +453,11 @@
         first += blocks
 
 
-def wgrad(groups, rows):
+def wgrad(groups, rows, first=()):
     width = groups[0][0][0].shape[1]
     block = min([512] + [group[0][2].shape[1] for group in groups])
     counts, specs, args = [], [], []
-    first = 0
+    column = 0
     for group in groups:
         blocks = group[0][2].shape[1] // block
         counts.append((len(group), blocks))
@@ -465,27 +470,27 @@
             args.append(a)
         for _, _, b, at in group:
 
-            def spot(j, at=at, first=first, blocks=blocks):
-                return (at, jnp.clip(j - first, 0, blocks - 1))
+            def spot(j, at=at, column=column, blocks=blocks):
+                return (at, jnp.clip(j - column, 0, blocks - 1))
 
             specs.append(pl.BlockSpec((rows, block), spot))
             args.append(b)
-        first += blocks
+        column += blocks
     return pl.pallas_call(
         functools.partial(wgrad_kernel, counts),
-        grid=(first,),
-        in_specs=specs,
+        grid=(column,),
+        in_specs=specs + [unread] * len(first),
         out_specs=pl.BlockSpec((width, block), lambda j: (0, j)),
-        out_shape=jax.ShapeDtypeStruct((width, first * block), bf16),
+        out_shape=pltpu.HBM((width, column * block), bf16),
         compiler_params=pltpu.CompilerParams(
             vmem_limit_bytes=40 * 2**20, dimension_semantics=("arbitrary",)
         ),
-        cost_estimate=light,
+        cost_estimate=heavy if first else light,
         name="wgrad",
-    )(*args)
-
-
-def row_pass(body, name, inputs, whole, kinds):
+    )(*in_hbm(*args), *first)
+
+
+def row_pass(body, name, inputs, whole, kinds, after=()):
     width = inputs[0][0].shape[1]
     rows = min(a.shape[0] - first for a, first in inputs)
     block = min(256, rows)
@@ -493,7 +498,7 @@
     def kernel(*refs):
         count = len(inputs) + len(whole)
         values = [ref[...].astype(f32) for ref in refs[:count]]
-        for ref, value in zip(refs[count:], body(*values)):
+        for ref, value in zip(refs[count + len(after) :], body(*values)):
             ref[...] = value.astype(ref.dtype)
 
     return pl.pallas_call(
@@ -503,13 +508,14 @@
             pl.BlockSpec((block, width), lambda i, first=first: (first // block + i, 0))
             for _, first in inputs
         ]
-        + [pl.BlockSpec(a.shape, lambda i: (0, 0)) for a in whole],
+        + [pl.BlockSpec(a.shape, lambda i: (0, 0)) for a in whole]
+        + [unread] * len(after),
         out_specs=[pl.BlockSpec((block, width), lambda i: (i, 0)) for _ in kinds],
         out_shape=[jax.ShapeDtypeStruct((rows, width), kind) for kind in kinds],
         compiler_params=pltpu.CompilerParams(dimension_semantics=("arbitrary",)),
         cost_estimate=light,
         name=name,
-    )(*[a for a, _ in inputs], *whole)
+    )(*[a for a, _ in inputs], *whole, *after)
 
 
 def inverse_root(x):
@@ -530,24 +536,64 @@
     *terms, gain = rest
     root = inverse_root(values)
     scaled = sum_steps(terms[0], terms[1:]) * gain
-    out = (
-        residual
-        + root * scaled
-        - values * root**3 * jnp.mean(scaled * values, -1, keepdims=True)
-    )
-    return out, out
-
-
-def pad_heads(w):
+    mean = jnp.mean(scaled * values, -1, keepdims=True)
+    return (residual + root * scaled - values * root**3 * mean,)
+
+
+def pad_kernel(counts, *refs):
+    out_ref = refs[-1]
+    gains = refs[-2][...]
     half = HEAD_SIZE // 2
-    parts = w.reshape(w.shape[0], -1, half)
-    return jnp.pad(parts, ((0, 0), (0, 0), (0, LANES // 2 - half))).reshape(w.shape[0], -1)
-
-
-def cut_heads(w):
+    rows = out_ref.shape[0]
+    at = 0
+    for ref, heads in zip(refs[:-2], counts):
+        w = ref[...]
+        for h in range(heads):
+            gap = jnp.zeros((rows, LANES // 2 - half), bf16)
+            first = w[:, h * HEAD_SIZE : h * HEAD_SIZE + half]
+            second = w[:, h * HEAD_SIZE + half : (h + 1) * HEAD_SIZE]
+            free = gap if at else jnp.concatenate([gains, gap[:, 2:]], 1)
+            out_ref[:, at : at + LANES] = jnp.concatenate([first, free, second, gap], 1)
+            at += LANES
+
+
+def pad_heads(weights, gains):
+    counts = [w.shape[1] // HEAD_SIZE for w in weights]
+    return pl.pallas_call(
+        functools.partial(pad_kernel, counts),
+        out_shape=jax.ShapeDtypeStruct((weights[0].shape[0], sum(counts) * LANES), bf16),
+        cost_estimate=light,
+        name="pad",
+    )(*weights, gains)
+
+
+def cut_kernel(counts, keep_ref, own_ref, crossed_ref, slanted_ref, *out_refs):
     half = HEAD_SIZE // 2
-    parts = w.reshape(w.shape[0], -1, LANES // 2)
-    return parts[:, :, :half].reshape(w.shape[0], -1)
+    kept = keep_ref[0] == 1
+    at = 0
+    for ref, heads in zip(out_refs, counts):
+        parts = []
+        for _ in range(heads):
+            lanes = slice(at, at + LANES)
+            w = jnp.where(kept, own_ref[:, lanes], crossed_ref[:, lanes]).astype(f32)
+            w = w + slanted_ref[:, lanes].astype(f32)
+            parts += [w[:, :half], w[:, LANES // 2 : LANES // 2 + half]]
+            at += LANES
+        ref[...] = jnp.concatenate(parts, 1)
+
+
+def cut_heads(blocks, widths):
+    counts = [width // HEAD_SIZE for width in widths]
+    rows = blocks[0].shape[0]
+    keep = stays().astype(jnp.int32).reshape(1)
+    return pl.pallas_call(
+        functools.partial(cut_kernel, counts),
+        in_specs=[pl.BlockSpec(memory_space=pltpu.SMEM)]
+        + [pl.BlockSpec(memory_space=pltpu.VMEM)] * 3,
+        out_shape=[jax.ShapeDtypeStruct((rows, width), f32) for width in widths],
+        cost_estimate=light,
+        name="cut",
+    )(keep, *blocks)
 
 
 swap_two = [(0, 1), (1, 0)]
@@ -713,6 +759,18 @@
             ]
         return lax.ppermute(a, ("c", "zh", "zl"), pairs)
 
+    def home_pairs(k):
+        pairs = []
+        for c in range(2):
+            for zh in range(2):
+                for i in steps:
+                    at = (i + k) % ring
+                    home = (2 * c + zh) * ring + at
+                    if c != zh:
+                        home = (2 * zh + c) * ring + ring - 1 - at
+                    pairs.append(((2 * c + zh) * ring + i, home))
+        return pairs
+
     def early_neighbours(original):
         return [
             lax.ppermute(original, ("c", "zh", "zl"), pairs_of(True, k)) for k in steps if k
@@ -728,15 +786,8 @@
     qw = qcols // HEAD_SIZE * LANES
     kw = kcols // HEAD_SIZE * LANES
     half = HEAD_SIZE // 2
-    attn_shard = pad_heads(jnp.concatenate([w_query, key_weight, value_weight, w_out], 1))
-    attn_shard = jnp.concatenate(
-        [
-            attn_shard[:, :half],
-            norm1_gain[:, None],
-            norm2_gain[:, None],
-            attn_shard[:, half + 2 :],
-        ],
-        1,
+    attn_shard = pad_heads(
+        [w_query, key_weight, value_weight, w_out], jnp.stack([norm1_gain, norm2_gain], 1)
     )
     other_positions = other_core(positions)
     attn_pair = spread_pair(attn_shard)
@@ -786,9 +837,10 @@
     ff_rows = arrange(*ff_pair)
     ff_full = gather_rows(ff_rows)
     cot_raw = cross_tokens(cot_sent)
-    others, projected = order([others[0][1], ff_rows], (others, projected), 8)
     for k, pair in enumerate(others, 1):
-        projected = project(pair, gain_first, attn_full, cos, sin, qw, kw, k, projected)
+        projected = project(
+            pair, gain_first, attn_full, cos, sin, qw, kw, k, projected, (ff_rows,)
+        )
     normed_first, q, k, v = projected
 
     def out_product(o):
@@ -803,31 +855,34 @@
     attended, cot_raw = together(attended, cot_raw)
     joined = [join_cores(out_product(o)) for o, _ in attended]
     sent = send_chips(joined)
+    cot_late = late_neighbours(cot_raw)
     q, k, v = order(joined, (q, k, v), 8)
     attended.insert(0, attend(0, place, q, k, v, start, ring))
     out_own = split_cores(out_product(attended[0][0]))
-    sent, out_own[0] = together(sent, out_own[0])
+    sent, out_own[0], cot_late = together(sent, out_own[0], cot_late)
     middle, normed_second = row_pass(
         norm_forward,
         "norm_forward",
         whole_rows(stream_own, *out_own, *sent),
         [gain_second],
-        [f32, bf16],
+        [bf16, bf16],
     )
     normed_second, cot_raw = together(normed_second, cot_raw)
     cot_own = jnp.where(stays(), cotangent, cot_raw)
     ff_others = swap_chips(normed_second)
-    cot_late = late_neighbours(cot_raw)
     ff_in = [(normed_second, other_core(normed_second))]
     out_grads = [(cot_own, other_core(cot_own))]
     ff_in, out_grads = order([normed_second], (ff_in, out_grads), 8)
     hidden = [hidden_pass(ff_in[0], out_grads[0], ff_full)]
-    hidden, ff_others, cot_late = together(hidden, ff_others, cot_late)
+    hidden, ff_others = together(hidden, ff_others)
 
     second_own = [hidden[0][2], other_core(hidden[0][3])]
     mixed_own = [hidden[0][4], other_core(hidden[0][5])]
+    mixed_own = row_pass(add_rows, "mixed", whole_rows(middle, *mixed_own), [], [bf16])[0]
+    mixed_raw = cross_tokens(mixed_own)
     for a, dy in zip(ff_others, choose(cot_early, cot_late)):
         a, dy = (a, other_core(a)), (dy, other_core(dy))
+        a, dy, second_own, mixed_own = together(a, dy, second_own, mixed_own)
         ff_in.append(a)
         out_grads.append(dy)
         hidden.append(hidden_pass(a, dy, ff_full))
@@ -835,28 +890,31 @@
     def pieces(pairs, hidden, i):
         return [(a, 0, h[i], j) for pair, h in zip(pairs, hidden) for j, a in enumerate(pair)]
 
+    hidden, mixed_raw = together(hidden, mixed_raw)
     joined = [join(h[2], other_core(h[3])) for h in hidden[1:]]
     sent = send_chips(joined)
     mixed_halves = [(h[4], other_core(h[5])) for h in hidden[1:]]
-    hidden, mixed_halves = order(joined, (hidden, mixed_halves), 8)
     mixed_joined = [join(*pair) for pair in mixed_halves]
-    ff_wgrad = wgrad([pieces(ff_in, hidden, 1), pieces(out_grads, hidden, 0)], rows)
-    sent, mixed_joined, ff_wgrad = order([ff_wgrad], (sent, mixed_joined, ff_wgrad))
+    ff_wgrad = wgrad([pieces(ff_in, hidden, 1), pieces(out_grads, hidden, 0)], rows, joined)
+    sent, mixed_joined, ff_wgrad = together(sent, mixed_joined, ff_wgrad)
     ff_part = sum_rows(ff_wgrad)
-    middle_grad, db = row_pass(
+    db = row_pass(
         norm_back,
         "norm_back",
         whole_rows(cot_own, middle, *second_own, *sent),
         [gain_second],
-        [f32, bf16],
-    )
+        [bf16],
+    )[0]
     branch_others = swap_chips(db)
     branch = [(db, other_core(db))]
-    branch = order([db], branch, 8)
 
     def heads_grad(pair):
         return jnp.concatenate(
-            [product([(b, 0)], rows, attn_full, plain, columns=out_columns) for b in pair], 0
+            [
+                product([(b, 0)], rows, attn_full, plain, columns=out_columns, cost=cost)
+                for b, cost in zip(pair, (heavy, light))
+            ],
+            0,
         )
 
     def queries_back(i, do, before):
@@ -866,18 +924,15 @@
     dq, *dkv = queries_back(0, heads_grad(branch[0]), ())
     dqs = [dq]
     branch_others, mixed_joined, dqs, dkv = together(branch_others, mixed_joined, dqs, dkv)
-    mixed_sent = send_chips(mixed_joined)
-    branch += order(
-        [branch_others[0]], [(b, other_core(b)) for b in branch_others], True
-    )
+    mixed_others = [
+        lax.ppermute(p, ("c", "zh", "zl"), home_pairs(k)) for k, p in zip(steps[1:], mixed_joined)
+    ]
+    branch += [(b, other_core(b)) for b in branch_others]
     for i in steps[1:]:
         dq, *dkv = queries_back(i, heads_grad(branch[i]), tuple(dkv))
         dqs.append(dq)
-    mixed_sent, dqs, dkv = together(mixed_sent, dqs, dkv)
-    mixed = row_pass(add_rows, "mixed", whole_rows(middle, *mixed_own, *mixed_sent), [], [bf16])[0]
-    mixed_raw = cross_tokens(mixed)
-
-    def first_product(i, dqs, dkv):
+    mixed_others, dqs, dkv = together(mixed_others, dqs, dkv)
+    def first_product(i, after=()):
         base = 2 * rows * i
         return lambda first, kind, add: product(
             [(dqs[i], first)] + [(d, base + first) for d in dkv],
@@ -887,39 +942,44 @@
             kind,
             qkv_columns,
             add,
+            after=after,
         )
 
-    joined = [join_cores(first_product(i, dqs, dkv)) for i in steps[1:]]
+    joined = [join_cores(first_product(i)) for i in steps[1:]]
     sent = send_chips(joined)
     ff_blocks = send_blocks(ff_part)
-    dqs, dkv = order([*joined, mixed, ff_blocks[0]], (dqs, dkv), 8)
-    first_own = split_cores(first_product(0, dqs, dkv))
+    first_own = split_cores(first_product(0, joined))
     attn_wgrad = wgrad(
         [[(normed_first, 2 * i + j, dqs[i], j) for i in steps for j in range(2)]]
         + [[(normed_first, i, d, i) for i in range(2 * ring)] for d in dkv]
         + [[(branch[i][j], 0, attended[i][0], j) for i in steps for j in range(2)]],
         rows,
+        (*joined, ff_blocks[0]),
     )
     attn_part = sum_rows(attn_wgrad)
-    sent, mixed_raw, ff_blocks, first_own[0] = order(
-        [attn_wgrad], (sent, mixed_raw, ff_blocks, first_own[0])
-    )
+    sent, ff_blocks, first_own[0] = together(sent, ff_blocks, first_own[0])
 
     input_grad = row_pass(
         norm_back,
         "norm_back",
-        whole_rows(middle_grad, stream_own, *first_own, *sent),
+        whole_rows(db, stream_own, *first_own, *sent),
         [gain_first],
-        [bf16, bf16],
+        [bf16],
+        [attn_wgrad],
     )[0]
     input_raw = cross_tokens(input_grad)
-    attn_part, mixed_raw, ff_blocks = order([input_grad], (attn_part, mixed_raw, ff_blocks), 400)
+    attn_part, ff_blocks, mixed_others = order(
+        [input_grad], (attn_part, ff_blocks, mixed_others), 400
+    )
+    attn_part, input_raw = together(attn_part, input_raw)
     attn_blocks = send_blocks(attn_part)
     attn_part = order([attn_part, attn_blocks[0]], attn_part, 8)
-    mixed = jnp.where(stays(), mixed, mixed_raw)
+    mixed = jnp.where(stays(), mixed_own, mixed_raw)
+    mixed = row_pass(add_rows, "mixed", whole_rows(mixed, *mixed_others), [], [bf16])[0]
     grad_ff = add_blocks(ff_blocks)
     units = w_gate.shape[1]
     grad_gate, grad_up, grad_down = (grad_ff[:, units * i : units * (i + 1)] for i in range(3))
+    input_grad = jnp.where(stays(), input_grad, input_raw).astype(f32)
 
     def weighed(weights, part, width):
         product = weights[:, :width].astype(f32) * part[:, :width].astype(f32)
@@ -938,22 +998,32 @@
             for j in range(1, count)
         ],
     )
-    gain_grads, input_raw, attn_blocks = together(gain_grads, input_raw, attn_blocks)
-    input_grad = jnp.where(stays(), input_grad, input_raw).astype(f32)
-    grad_attn = cut_heads(add_blocks(attn_blocks))
-    grad_query = grad_attn[:, :qcols]
-    grad_key = grad_attn[:, qcols : qcols + kcols]
-    grad_value = grad_attn[:, qcols + kcols : qcols + 2 * kcols]
-    grad_output = grad_attn[:, qcols + 2 * kcols :]
+    gain_first_grad = gain_grads[0] / norm1_gain.astype(f32)
+    gain_second_grad = gain_grads[1] / norm2_gain.astype(f32)
+    mixed, input_grad, gain_first_grad, gain_second_grad, grad_gate, grad_up, grad_down, attn_blocks = (
+        together(
+            mixed,
+            input_grad,
+            gain_first_grad,
+            gain_second_grad,
+            grad_gate,
+            grad_up,
+            grad_down,
+            attn_blocks,
+        )
+    )
+    grad_query, grad_key, grad_value, grad_output = cut_heads(
+        attn_blocks, [qcols, kcols, kcols, qcols]
+    )
     return (
         mixed,
         input_grad,
-        gain_grads[0] / norm1_gain.astype(f32),
+        gain_first_grad,
         grad_query,
         grad_key,
         grad_value,
         grad_output,
-        gain_grads[1] / norm2_gain.astype(f32),
+        gain_second_grad,
         grad_gate,
         grad_up,
         grad_down,

time: 663 us -> 651 us (0.982)
  the two profiles are of different devices: /device:TPU:1 before, /device:TPU:0 now
where the time goes in v4:
time: 651 us; the launch traced here: 641 us
  Pallas kernels  278 us (43%)
  waiting for transfers between devices  162 us (25%)
  starting transfers between devices  111 us (17%)
  local copies, waits for them, and re-layouts  38.1 us (6%)
  other arithmetic  36.3 us (6%)
  between operations  14.9 us (2%)
    ppermute x18, starting transfers between devices, other_core(): return lax.ppermute(a, 'c', swap_two)  55.9 us
    pallas_call x2, Pallas kernels, hidden_pass(): pl.pallas_call(functools.partial(hidden_kernel, min(256, units), count),...  55.3 us
    pallas_call x2, Pallas kernels, wgrad(): pl.pallas_call(functools.partial(wgrad_kernel, counts), grid=(column,), i...  52.2 us
    pallas_call x2, Pallas kernels, attend_back(): pl.pallas_call(functools.partial(attend_back_kernel, ring, block, chip, f...  44.5 us
    pallas_call x12, Pallas kernels, product(): pl.pallas_call(functools.partial(product_kernel, dims, len(parts), len(af...  43 us
    ppermute x2, waiting for transfers between devices, spread_pair(): return (w, cross(w), lax.ppermute(w, ('c', 'zh'), slant_pairs))  32 us
    unnamed x138, local copies, waits for them, and re-layouts  31.3 us
    ppermute x2, waiting for transfers between devices, early_neighbours(): lax.ppermute(original, ('c', 'zh', 'zl'), pairs_of(True, k))  30.1 us
  transfers between devices with their start and end apart: 47, of which 20 were waited for; matrix products, arithmetic and copies ran while one was open for 6% of the time, Pallas kernels for 43%

profile of v4, /device:TPU:0, one launch (start us, length us, event | category | flops | bytes accessed | tf_op | source)
XLA Modules:
  0.0 640.5 jit_solution(706378766383524907)
XLA Ops:
  7.2 4.9 collective-permute-start.2
  20.2 22.8 %collective-permute-done.1 = bf16[192,1536]{1,0:T(8,128)(2,1)S(1)} collective-permute-done((bf16[192,1536]{1,0:T(8,128)(2,1)}, bf16[192,1536]{1,0:T(8,128)(2,1)S(1)}, u32[]{:S(2)}, u32[]{:S(2)}) %collective-permute-start.1) | collective-permute-done | bytes 589856 | tf_op jit(solution)/shard_map/ppermute | solution.py:626
  50.0 4.8 collective-permute-start.5
  55.0 3.7 fusion.4
  59.9 30.1 %collective-permute-done.5 = bf16[512,1536]{1,0:T(8,128)(2,1)} collective-permute-done((bf16[512,1536]{1,0:T(8,128)(2,1)}, bf16[512,1536]{1,0:T(8,128)(2,1)}, u32[]{:S(2)}, u32[]{:S(2)}) %collective-permute-start.5) | collective-permute-done | bytes 1572896 | tf_op jit(solution)/shard_map/ppermute | solution.py:776
  96.3 4.4 collective-permute-start.8
  100.7 5.2 all-gather.3.cloned.1.call-done.w_ref.refs_1_.refs_3_
  107.7 7.6 %project.2 = (bf16[2048,1536]{1,0:T(8,128)(2,1)S(1)}, bf16[2048,512]{1,0:T(8,128)(2,1)S(1)}, bf16[2048,256]{1,0:T(8,128)(2,1)S(1)}, bf16[2048,256]{1,0:T(8,128)(2,1)S(1)}) custom-call(bf16[512,1536]{1,0:T(8,128)(2,1)} %broadcast_select_fusion.4.x_ref.refs_0_.refs_1_, bf16[512,1536]{1,0:T(8,128)(2,1)} %collective-permute-done.9.y_ref, ...), custom_call_target="tpu_custom_call" | custom-call | flops 1 | bytes 1 | tf_op jit(solution)/shard_map/project/pallas_call | solution.py:318
  118.0 9.2 %collective-permute-done.8 = bf16[192,3072]{1,0:T(8,128)(2,1)} collective-permute-done((bf16[192,3072]{1,0:T(8,128)(2,1)S(1)}, bf16[192,3072]{1,0:T(8,128)(2,1)}, u32[]{:S(2)}, u32[]{:S(2)}) %collective-permute-start.8) | collective-permute-done | bytes 1179680 | tf_op jit(solution)/shard_map/ppermute | solution.py:626
  133.5 25.9 %collective-permute-start.10 = (bf16[512,1536]{1,0:T(8,128)(2,1)S(1)}, bf16[512,1536]{1,0:T(8,128)(2,1)S(1)}, u32[]{:S(2)}, u32[]{:S(2)}) collective-permute-start(bf16[512,1536]{1,0:T(8,128)(2,1)S(1)} %broadcast_select_fusion.3.x_ref), channel_id=1, source_target_pairs={{0,4},{4,0},{1,5},{5,1},{2,6},{6,2},{3,7},{7,3},{8,12},{12,8},{9,1... | collective-permute-start | bytes 4718600 | tf_op jit(solution)/shard_map/ppermute | solution.py:614
  163.7 9.5 %project.3 = (bf16[2048,1536]{1,0:T(8,128)(2,1)}, bf16[2048,512]{1,0:T(8,128)(2,1)}, bf16[2048,256]{1,0:T(8,128)(2,1)}, bf16[2048,256]{1,0:T(8,128)(2,1)}) custom-call(bf16[512,1536]{1,0:T(8,128)(2,1)} %copy-done.57, bf16[512,1536]{1,0:T(8,128)(2,1)} %copy-done.67, ...), custom_call_target="tpu_custom_call", output_to_operand_aliasing={{0}: (6, {}), {1}: (7, {}), {2}: (8, {}), {3}: (9, {})} | custom-call | flops 8000000000 | bytes 1 | tf_op jit(solution)/shard_map/project/pallas_call | solution.py:318
  177.2 13.7 %attend.2 = (bf16[1024,512]{1,0:T(8,128)(2,1)S(1)}, f32[2,2,1024]{2,1,0:T(2,128)S(1)}) custom-call(s32[3]{0:T(128)S(1)} %pad_add_fusion.1.place_ref, bf16[2048,512]{1,0:T(8,128)(2,1)S(1)} %copy-done.4, bf16[2048,256]{1,0:T(8,128)(2,1)S(1)} %copy-done.19, bf16[2048,256]{1,0:T(8,128)(2,1)S(1)} %copy-done.23, s32[1,2048]{1,0:T(1,128)S(1)} %bitcast.21), custom_call_target="tpu_custom_call" | custom-call | flops 1 | bytes 1 | tf_op jit(solution)/shard_map/attend/pallas_call | solution.py:103
  190.9 3.1 product.12
  197.4 3.6 product.13.refs_0_
  201.0 5.2 collective-permute-start.13
  210.9 13.6 %attend.3 = (bf16[1024,512]{1,0:T(8,128)(2,1)S(1)}, f32[2,2,1024]{2,1,0:T(2,128)S(1)}) custom-call(s32[3]{0:T(128)S(1)} %pad_add_fusion.1.place_ref, bf16[2048,512]{1,0:T(8,128)(2,1)S(1)} %copy-done.5, bf16[2048,256]{1,0:T(8,128)(2,1)S(1)} %copy-done.20, bf16[2048,256]{1,0:T(8,128)(2,1)S(1)} %copy-done.24, s32[1,2048]{1,0:T(1,128)S(1)} %bitcast.22), custom_call_target="tpu_custom_call" | custom-call | flops 1 | bytes 1 | tf_op jit(solution)/shard_map/attend/pallas_call | solution.py:103
  224.5 3.0 product.15
  232.0 9.8 %collective-permute-done.13.refs_3_ = bf16[512,1536]{1,0:T(8,128)(2,1)} collective-permute-done((bf16[512,1536]{1,0:T(8,128)(2,1)}, bf16[512,1536]{1,0:T(8,128)(2,1)}, u32[]{:S(2)}, u32[]{:S(2)}) %collective-permute-start.13) | collective-permute-done | bytes 1572896 | tf_op jit(solution)/shard_map/ppermute | solution.py:741
  241.9 4.8 norm_forward.1
  246.7 10.7 %collective-permute-start.16 = (bf16[512,1536]{1,0:T(8,128)(2,1)}, bf16[512,1536]{1,0:T(8,128)(2,1)}, u32[]{:S(2)}, u32[]{:S(2)}) collective-permute-start(bf16[512,1536]{1,0:T(8,128)(2,1)} %get-tuple-element.187.refs_0_.a_ref), channel_id=1, source_target_pairs={{0,4},{4,0},{1,5},{5,1},{2,6},{6,2},{3,7},{7,3},{8,12},{12,8},{9,1... | collective-permute-start | bytes 4718600 | tf_op jit(solution)/shard_map/ppermute | solution.py:614
  263.9 27.7 %hidden.2 = (bf16[1024,1024]{1,0:T(8,128)(2,1)}, bf16[1024,2048]{1,0:T(8,128)(2,1)}, bf16[512,1536]{1,0:T(8,128)(2,1)S(1)}, bf16[512,1536]{1,0:T(8,128)(2,1)}, b...) custom-call(bf16[512,1536]{1,0:T(8,128)(2,1)} %get-tuple-element.187.refs_0_.a_ref, ...), custom_call_target="tpu_custom_call" | custom-call | flops 8000000000 | bytes 1 | tf_op jit(solution)/shard_map/hidden/pallas_call | solution.py:382
  291.6 5.7 collective-permute-done.18.a_ref.refs_2_
  302.2 3.5 mixed.2
  305.7 9.0 %collective-permute-start.23 = (bf16[512,1536]{1,0:T(8,128)(2,1)}, bf16[512,1536]{1,0:T(8,128)(2,1)S(1)}, u32[]{:S(2)}, u32[]{:S(2)}) collective-permute-start(bf16[512,1536]{1,0:T(8,128)(2,1)} %mixed.2), channel_id=1, source_target_pairs={{2,5},{3,4},{4,3},{5,2},{10,13},{11,12},{12,11},{13,10},{18,21},{1... | collective-permute-start | bytes 4718600 | tf_op jit(solution)/shard_map/ppermute | solution.py:760
  314.7 27.6 %hidden.3 = (bf16[1024,1024]{1,0:T(8,128)(2,1)}, bf16[1024,2048]{1,0:T(8,128)(2,1)}, bf16[512,1536]{1,0:T(8,128)(2,1)S(1)}, bf16[512,1536]{1,0:T(8,128)(2,1)S(1)...) custom-call(bf16[512,1536]{1,0:T(8,128)(2,1)} %collective-permute-done.18.a_ref.refs_2_, ...), custom_call_target="tpu_custom_call" | custom-call | flops 8000000000 | bytes 1 | tf_op jit(solution)/shard_map/hidden/pallas_call | solution.py:382
  344.6 4.6 collective-permute-start.24
  356.1 2.9 join.3
  360.5 29.0 %wgrad.2 = bf16[1536,3072]{1,0:T(8,128)(2,1)} custom-call(bf16[512,1536]{1,0:T(8,128)(2,1)} %get-tuple-element.187.refs_0_.a_ref, bf16[512,1536]{1,0:T(8,128)(2,1)} %collective-permute-done.16.b_ref.refs_1_, bf16[512,1536]{1,0:T(8,128)(2,1)} %collective-permute-done.18.a_ref.refs_2_, bf16[512,1536]{1,0:T(8,128)(2,1)} %collective-permute-done.19.b_ref.refs_3_, ...), custom_call_target="tpu_custom_call" | custom-call | flops 8000000000 | bytes 1 | tf_op jit(solution)/shard_map/wgrad/pallas_call | solution.py:479
  392.7 5.6 norm_back.2.refs_0_.refs_24_
  409.0 21.1 %attend_back.2 = (bf16[1024,512]{1,0:T(8,128)(2,1)S(1)}, f32[2048,256]{1,0:T(8,128)S(1)}, f32[2048,256]{1,0:T(8,128)S(1)}) custom-call(s32[3]{0:T(128)S(1)} %pad_add_fusion.1.place_ref, bf16[2048,512]{1,0:T(8,128)(2,1)S(1)} %copy-done.5, bf16[2048,256]{1,0:T(8,128)(2,1)S(1)} %copy-done.21, bf16[2048,256]{1,0:T(8,128)(2,1)S(1)} %copy-done.25, ...), custom_call_target="tpu_custom_call" | custom-call | flops 1 | bytes 1 | tf_op jit(solution)/shard_map/attend_back/pallas_call | solution.py:236
  431.4 3.9 collective-permute-done.27.refs_0_.refs_26_
  438.9 3.2 product.19
  443.7 23.4 %attend_back.3 = (bf16[1024,512]{1,0:T(8,128)(2,1)S(1)}, bf16[2048,256]{1,0:T(8,128)(2,1)S(1)}, bf16[2048,256]{1,0:T(8,128)(2,1)S(1)}) custom-call(s32[3]{0:T(128)S(1)} %pad_add_fusion.1.place_ref, bf16[2048,512]{1,0:T(8,128)(2,1)S(1)} %copy-done.6, bf16[2048,256]{1,0:T(8,128)(2,1)S(1)} %copy-done.21, bf16[2048,256]{1,0:T(8,128)(2,1)S(1)} %copy-done.25, ...), custom_call_target="tpu_custom_call" | custom-call | flops 1 | bytes 1 | tf_op jit(solution)/shard_map/attend_back/pallas_call | solution.py:236
  467.1 3.9 collective-permute-done.29.refs_1_
  471.1 5.4 product.20
  478.9 3.4 collective-permute-done.31.refs_4_
  483.5 5.2 product.21.refs_4_.refs_32_
  488.7 4.9 product.23
  494.0 3.3 broadcast_select_fusion.6
  501.4 4.1 product.22.refs_2_
  506.7 23.2 %wgrad.3.refs_6_ = bf16[1536,1536]{1,0:T(8,128)(2,1)} custom-call(bf16[2048,1536]{1,0:T(8,128)(2,1)} %get-tuple-element.251.refs_0_.refs_1_.refs_2_.refs_3_.refs_8_.refs_9_.refs_10_.refs_11_.refs_16_.refs_17_.refs_18_.refs_19_, ...), custom_call_target="tpu_custom_call" | custom-call | flops 8000000000 | bytes 1 | tf_op jit(solution)/shard_map/wgrad/pallas_call | solution.py:479
  534.1 12.9 %collective-permute-done.32.refs_4_ = bf16[512,1536]{1,0:T(8,128)(2,1)} collective-permute-done((bf16[512,1536]{1,0:T(8,128)(2,1)}, bf16[512,1536]{1,0:T(8,128)(2,1)}, u32[]{:S(2)}, u32[]{:S(2)}) %collective-permute-start.32) | collective-permute-done | bytes 1572896 | tf_op jit(solution)/shard_map/ppermute | solution.py:741
  547.1 7.2 %collective-permute-done.34 = bf16[192,3072]{1,0:T(8,128)(2,1)} collective-permute-done((bf16[192,3072]{1,0:T(8,128)(2,1)}, bf16[192,3072]{1,0:T(8,128)(2,1)}, u32[]{:S(2)}, u32[]{:S(2)}) %collective-permute-start.34) | collective-permute-done | bytes 1179680 | tf_op jit(solution)/shard_map/ppermute | solution.py:646
  554.3 5.4 norm_back.3.refs_0_
  562.9 25.7 %reduce-scatter.5.cloned.1.call-done.refs_0_ = bf16[384,1536]{1,0:T(8,128)(2,1)} async-done(((bf16[1536,1536]{1,0:T(8,128)(2,1)}), bf16[384,1536]{1,0:T(8,128)(2,1)}) %reduce-scatter.5.cloned.1.call-update) | async-done | bytes 1179664 | tf_op jit(solution)/shard_map/reduce_scatter | solution.py:656
  593.6 7.5 %collective-permute-start.37 = (f32[2,192]{1,0:T(2,128)S(1)}, f32[2,192]{1,0:T(2,128)S(1)}, u32[]{:S(2)}, u32[]{:S(2)}) collective-permute-start(f32[2,192]{1,0:T(2,128)S(1)} %bitcast.35), channel_id=1, source_target_pairs={{0,4},{4,0},{1,5},{5,1},{2,6},{6,2},{3,7},{7,3},{8,12},{12,8},{9,1... | collective-permute-start | bytes 4616 | tf_op jit(solution)/shard_map/ppermute | solution.py:614
  607.1 4.0 collective-permute-start.40
  617.6 12.6 %collective-permute-done.42.slanted_ref = bf16[192,1536]{1,0:T(8,128)(2,1)S(1)} collective-permute-done((bf16[192,1536]{1,0:T(8,128)(2,1)S(1)}, bf16[192,1536]{1,0:T(8,128)(2,1)S(1)}, u32[]{:S(2)}, u32[]{:S(2)}) %collective-permute-start.42) | collective-permute-done | bytes 589856 | tf_op jit(solution)/shard_map/ppermute | solution.py:646
  (274 shorter events, 134.0 us)
Async XLA Ops:
  7.2 98.8 %all-gather.3.cloned.1.call-start = ((), (), s32[]{:S(2)}) async-start(), calls=%async_computation.2 | async-start | bytes 5898240 | tf_op jit(solution)/shard_map/all_gather | solution.py:638
  7.2 35.9 %collective-permute-start.2 = (bf16[512,1536]{1,0:T(8,128)(2,1)}, bf16[512,1536]{1,0:T(8,128)(2,1)S(1)}, u32[]{:S(2)}, u32[]{:S(2)}) collective-permute-start(bf16[512,1536]{1,0:T(8,128)(2,1)} %param.23), channel_id=1, source_target_pairs={{0,1},{1,0},{6,7},{7,6},{8,9},{9,8},{14,15},{15,14},{16,17},{17,16... | collective-permute-start | bytes 4718600 | tf_op jit(solution)/shard_map/ppermute | solution.py:776
  16.6 3.7 collective-permute-start
  17.3 25.8 %collective-permute-start.1 = (bf16[192,1536]{1,0:T(8,128)(2,1)}, bf16[192,1536]{1,0:T(8,128)(2,1)S(1)}, u32[]{:S(2)}, u32[]{:S(2)}) collective-permute-start(bf16[192,1536]{1,0:T(8,128)(2,1)} %pad.89), channel_id=1, source_target_pairs={{0,2},{2,6},{4,0},{6,4},{1,3},{3,7},{5,1},{7,5},{8,10},{10,14},{12... | collective-permute-start | bytes 1769480 | tf_op jit(solution)/shard_map/ppermute | solution.py:626
  18.4 1.8 collective-permute-start.3
  46.8 217.1 %all-gather.5.cloned.1.call-start = ((), (), s32[]{:S(2)}) async-start(), calls=%async_computation.3 | async-start | bytes 11796480 | tf_op jit(solution)/shard_map/all_gather | solution.py:638
  48.1 11.8 %collective-permute-start.4 = (bf16[512,1536]{1,0:T(8,128)(2,1)}, bf16[512,1536]{1,0:T(8,128)(2,1)}, u32[]{:S(2)}, u32[]{:S(2)}) collective-permute-start(bf16[512,1536]{1,0:T(8,128)(2,1)} %param.12), channel_id=1, source_target_pairs={{2,5},{3,4},{4,3},{5,2},{10,13},{11,12},{12,11},{13,10},{18,21},{1... | collective-permute-start | bytes 4718600 | tf_op jit(solution)/shard_map/ppermute | solution.py:760
  50.0 40.1 %collective-permute-start.5 = (bf16[512,1536]{1,0:T(8,128)(2,1)}, bf16[512,1536]{1,0:T(8,128)(2,1)}, u32[]{:S(2)}, u32[]{:S(2)}) collective-permute-start(bf16[512,1536]{1,0:T(8,128)(2,1)} %param.12), channel_id=1, source_target_pairs={{0,1},{1,0},{6,7},{7,6},{8,9},{9,8},{14,15},{15,14},{16,17},{17,16... | collective-permute-start | bytes 4718600 | tf_op jit(solution)/shard_map/ppermute | solution.py:776
  92.8 15.0 %collective-permute-start.9 = (bf16[512,1536]{1,0:T(8,128)(2,1)}, bf16[512,1536]{1,0:T(8,128)(2,1)}, u32[]{:S(2)}, u32[]{:S(2)}) collective-permute-start(bf16[512,1536]{1,0:T(8,128)(2,1)} %broadcast_select_fusion.4.x_ref.refs_0_.refs_1_), channel_id=1, source_target_pairs={{0,4},{4,0},{1,5},{5,1},{2,6},{6,2},{3,7},{7,3},{8,12},{12,8},{9,1... | collective-permute-start | bytes 4718600 | tf_op jit(solution)/shard_map/ppermute | solution.py:614
  92.8 34.4 %collective-permute-start.6 = (bf16[512,1536]{1,0:T(8,128)(2,1)}, bf16[512,1536]{1,0:T(8,128)(2,1)}, u32[]{:S(2)}, u32[]{:S(2)}) collective-permute-start(bf16[512,1536]{1,0:T(8,128)(2,1)} %collective-permute-done.4), channel_id=1, source_target_pairs={{2,3},{3,2},{4,5},{5,4},{10,11},{11,10},{12,13},{13,12},{18,19},{1... | collective-permute-start | bytes 4718600 | tf_op jit(solution)/shard_map/ppermute | solution.py:780
  94.7 23.3 %collective-permute-start.7 = (bf16[192,3072]{1,0:T(8,128)(2,1)S(1)}, bf16[192,3072]{1,0:T(8,128)(2,1)}, u32[]{:S(2)}, u32[]{:S(2)}) collective-permute-start(bf16[192,3072]{1,0:T(8,128)(2,1)S(1)} %pad_maximum_fusion.6), channel_id=1, source_target_pairs={{2,4},{4,2},{3,5},{5,3},{10,12},{12,10},{11,13},{13,11},{18,20},{2... | collective-permute-start | bytes 3538952 | tf_op jit(solution)/shard_map/ppermute | solution.py:610
  96.3 30.8 %collective-permute-start.8 = (bf16[192,3072]{1,0:T(8,128)(2,1)S(1)}, bf16[192,3072]{1,0:T(8,128)(2,1)}, u32[]{:S(2)}, u32[]{:S(2)}) collective-permute-start(bf16[192,3072]{1,0:T(8,128)(2,1)S(1)} %pad_maximum_fusion.6), channel_id=1, source_target_pairs={{0,2},{2,6},{4,0},{6,4},{1,3},{3,7},{5,1},{7,5},{8,10},{10,14},{12... | collective-permute-start | bytes 3538952 | tf_op jit(solution)/shard_map/ppermute | solution.py:626
  131.7 362.3 %reduce-scatter.3.cloned.1.call-start = ((), (), s32[]{:S(2)}) async-start(), calls=%async_computation.4 | async-start | bytes 11796480 | tf_op jit(solution)/shard_map/reduce_scatter | solution.py:656
  133.5 28.9 %collective-permute-start.10 = (bf16[512,1536]{1,0:T(8,128)(2,1)S(1)}, bf16[512,1536]{1,0:T(8,128)(2,1)S(1)}, u32[]{:S(2)}, u32[]{:S(2)}) collective-permute-start(bf16[512,1536]{1,0:T(8,128)(2,1)S(1)} %broadcast_select_fusion.3.x_ref), channel_id=1, source_target_pairs={{0,4},{4,0},{1,5},{5,1},{2,6},{6,2},{3,7},{7,3},{8,12},{12,8},{9,1... | collective-permute-start | bytes 4718600 | tf_op jit(solution)/shard_map/ppermute | solution.py:614
  159.4 31.5 %collective-permute-start.11 = (bf16[512,1536]{1,0:T(8,128)(2,1)S(1)}, bf16[512,1536]{1,0:T(8,128)(2,1)}, u32[]{:S(2)}, u32[]{:S(2)}) collective-permute-start(bf16[512,1536]{1,0:T(8,128)(2,1)S(1)} %copy-done.52), channel_id=1, source_target_pairs={{2,5},{3,4},{4,3},{5,2},{10,13},{11,12},{12,11},{13,10},{18,21},{1... | collective-permute-start | bytes 4718600 | tf_op jit(solution)/shard_map/ppermute | solution.py:760
  190.9 251.3 %copy-start.7 = (bf16[1024,512]{1,0:T(8,128)(2,1)}, bf16[1024,512]{1,0:T(8,128)(2,1)S(1)}, u32[]{:S(2)}) copy-start(bf16[1024,512]{1,0:T(8,128)(2,1)S(1)} %get-tuple-element.175.refs_0_.o_ref.refs_30_.refs_31_) | copy-start | bytes 3145732
  194.0 3.5 collective-permute-start.12
  194.4 37.6 %collective-permute-start.14 = (bf16[512,1536]{1,0:T(8,128)(2,1)}, bf16[512,1536]{1,0:T(8,128)(2,1)}, u32[]{:S(2)}, u32[]{:S(2)}) collective-permute-start(bf16[512,1536]{1,0:T(8,128)(2,1)} %collective-permute-done.11), channel_id=1, source_target_pairs={{2,3},{3,2},{4,5},{5,4},{10,11},{11,10},{12,13},{13,12},{18,19},{1... | collective-permute-start | bytes 4718600 | tf_op jit(solution)/shard_map/ppermute | solution.py:780
  201.0 40.8 %collective-permute-start.13 = (bf16[512,1536]{1,0:T(8,128)(2,1)}, bf16[512,1536]{1,0:T(8,128)(2,1)}, u32[]{:S(2)}, u32[]{:S(2)}) collective-permute-start(bf16[512,1536]{1,0:T(8,128)(2,1)} %product.13.refs_0_), channel_id=1, source_target_pairs={{0,1},{1,0},{2,3},{3,2},{4,5},{5,4},{6,7},{7,6},{8,9},{9,8},{10,11... | collective-permute-start | bytes 4718600 | tf_op jit(solution)/shard_map/ppermute | solution.py:741
  227.5 14.4 %collective-permute-start.15 = (bf16[512,1536]{1,0:T(8,128)(2,1)S(1)}, bf16[512,1536]{1,0:T(8,128)(2,1)}, u32[]{:S(2)}, u32[]{:S(2)}) collective-permute-start(bf16[512,1536]{1,0:T(8,128)(2,1)S(1)} %product.15), channel_id=1, source_target_pairs={{0,4},{4,0},{1,5},{5,1},{2,6},{6,2},{3,7},{7,3},{8,12},{12,8},{9,1... | collective-permute-start | bytes 4718600 | tf_op jit(solution)/shard_map/ppermute | solution.py:614
  246.7 16.5 %collective-permute-start.16 = (bf16[512,1536]{1,0:T(8,128)(2,1)}, bf16[512,1536]{1,0:T(8,128)(2,1)}, u32[]{:S(2)}, u32[]{:S(2)}) collective-permute-start(bf16[512,1536]{1,0:T(8,128)(2,1)} %get-tuple-element.187.refs_0_.a_ref), channel_id=1, source_target_pairs={{0,4},{4,0},{1,5},{5,1},{2,6},{6,2},{3,7},{7,3},{8,12},{12,8},{9,1... | collective-permute-start | bytes 4718600 | tf_op jit(solution)/shard_map/ppermute | solution.py:614
  260.1 3.8 collective-permute-start.17
  260.2 37.1 %collective-permute-start.18 = (bf16[512,1536]{1,0:T(8,128)(2,1)}, bf16[512,1536]{1,0:T(8,128)(2,1)}, u32[]{:S(2)}, u32[]{:S(2)}) collective-permute-start(bf16[512,1536]{1,0:T(8,128)(2,1)} %get-tuple-element.187.refs_0_.a_ref), channel_id=1, source_target_pairs={{0,1},{1,0},{2,3},{3,2},{4,5},{5,4},{6,7},{7,6},{8,9},{9,8},{10,11... | collective-permute-start | bytes 4718600 | tf_op jit(solution)/shard_map/ppermute | solution.py:618
  297.3 3.8 collective-permute-start.22
  298.6 16.1 %collective-permute-start.20 = (bf16[512,1536]{1,0:T(8,128)(2,1)}, bf16[512,1536]{1,0:T(8,128)(2,1)}, u32[]{:S(2)}, u32[]{:S(2)}) collective-permute-start(bf16[512,1536]{1,0:T(8,128)(2,1)} %broadcast_select_fusion.1.dy_ref.refs_10_), channel_id=1, source_target_pairs={{0,4},{4,0},{1,5},{5,1},{2,6},{6,2},{3,7},{7,3},{8,12},{12,8},{9,1... | collective-permute-start | bytes 4718600 | tf_op jit(solution)/shard_map/ppermute | solution.py:614
  300.5 14.2 %collective-permute-start.19 = (bf16[512,1536]{1,0:T(8,128)(2,1)}, bf16[512,1536]{1,0:T(8,128)(2,1)}, u32[]{:S(2)}, u32[]{:S(2)}) collective-permute-start(bf16[512,1536]{1,0:T(8,128)(2,1)} %collective-permute-done.18.a_ref.refs_2_), channel_id=1, source_target_pairs={{0,4},{4,0},{1,5},{5,1},{2,6},{6,2},{3,7},{7,3},{8,12},{12,8},{9,1... | collective-permute-start | bytes 4718600 | tf_op jit(solution)/shard_map/ppermute | solution.py:614
  300.6 14.1 %collective-permute-start.21 = (bf16[512,1536]{1,0:T(8,128)(2,1)}, bf16[512,1536]{1,0:T(8,128)(2,1)}, u32[]{:S(2)}, u32[]{:S(2)}) collective-permute-start(bf16[512,1536]{1,0:T(8,128)(2,1)} %get-tuple-element.201), channel_id=1, source_target_pairs={{0,4},{4,0},{1,5},{5,1},{2,6},{6,2},{3,7},{7,3},{8,12},{12,8},{9,1... | collective-permute-start | bytes 4718600 | tf_op jit(solution)/shard_map/ppermute | solution.py:614
  305.7 38.9 %collective-permute-start.23 = (bf16[512,1536]{1,0:T(8,128)(2,1)}, bf16[512,1536]{1,0:T(8,128)(2,1)S(1)}, u32[]{:S(2)}, u32[]{:S(2)}) collective-permute-start(bf16[512,1536]{1,0:T(8,128)(2,1)} %mixed.2), channel_id=1, source_target_pairs={{2,5},{3,4},{4,3},{5,2},{10,13},{11,12},{12,11},{13,10},{18,21},{1... | collective-permute-start | bytes 4718600 | tf_op jit(solution)/shard_map/ppermute | solution.py:760
  344.6 7.8 %collective-permute-start.24 = (bf16[512,1536]{1,0:T(8,128)(2,1)S(1)}, bf16[512,1536]{1,0:T(8,128)(2,1)}, u32[]{:S(2)}, u32[]{:S(2)}) collective-permute-start(bf16[512,1536]{1,0:T(8,128)(2,1)S(1)} %get-tuple-element.222), channel_id=1, source_target_pairs={{0,4},{4,0},{1,5},{5,1},{2,6},{6,2},{3,7},{7,3},{8,12},{12,8},{9,1... | collective-permute-start | bytes 4718600 | tf_op jit(solution)/shard_map/ppermute | solution.py:614
  349.2 6.9 %collective-permute-start.26 = (bf16[512,1536]{1,0:T(8,128)(2,1)}, bf16[512,1536]{1,0:T(8,128)(2,1)}, u32[]{:S(2)}, u32[]{:S(2)}) collective-permute-start(bf16[512,1536]{1,0:T(8,128)(2,1)} %get-tuple-element.224), channel_id=1, source_target_pairs={{0,4},{4,0},{1,5},{5,1},{2,6},{6,2},{3,7},{7,3},{8,12},{12,8},{9,1... | collective-permute-start | bytes 4718600 | tf_op jit(solution)/shard_map/ppermute | solution.py:614
  355.3 37.0 %collective-permute-start.25 = (bf16[512,1536]{1,0:T(8,128)(2,1)}, bf16[512,1536]{1,0:T(8,128)(2,1)}, u32[]{:S(2)}, u32[]{:S(2)}) collective-permute-start(bf16[512,1536]{1,0:T(8,128)(2,1)} %join.2.refs_16_), channel_id=1, source_target_pairs={{0,1},{1,0},{2,3},{3,2},{4,5},{5,4},{6,7},{7,6},{8,9},{9,8},{10,11... | collective-permute-start | bytes 4718600 | tf_op jit(solution)/shard_map/ppermute | solution.py:741
  392.3 196.3 %reduce-scatter.5.cloned.1.call-start = ((), (), s32[]{:S(2)}) async-start(), calls=%async_computation.5 | async-start | bytes 5898240 | tf_op jit(solution)/shard_map/reduce_scatter | solution.py:656
  398.3 4.9 collective-permute-start.28
  398.3 37.0 %collective-permute-start.27 = (bf16[512,1536]{1,0:T(8,128)(2,1)}, bf16[512,1536]{1,0:T(8,128)(2,1)S(1)}, u32[]{:S(2)}, u32[]{:S(2)}) collective-permute-start(bf16[512,1536]{1,0:T(8,128)(2,1)} %norm_back.2.refs_0_.refs_24_), channel_id=1, source_target_pairs={{0,1},{1,0},{2,3},{3,2},{4,5},{5,4},{6,7},{7,6},{8,9},{9,8},{10,11... | collective-permute-start | bytes 4718600 | tf_op jit(solution)/shard_map/ppermute | solution.py:618
  435.3 3.5 collective-permute-start.30
  435.3 35.7 %collective-permute-start.29 = (bf16[512,1536]{1,0:T(8,128)(2,1)S(1)}, bf16[512,1536]{1,0:T(8,128)(2,1)S(1)}, u32[]{:S(2)}, u32[]{:S(2)}) collective-permute-start(bf16[512,1536]{1,0:T(8,128)(2,1)S(1)} %copy-done.59), channel_id=1, source_target_pairs={{0,1},{1,0},{2,4},{3,5},{4,2},{5,3},{6,7},{7,6},{8,9},{9,8},{10,12... | collective-permute-start | bytes 4718600 | tf_op jit(solution)/shard_map/ppermute | solution.py:928
  476.4 5.8 collective-permute-start.31
  488.7 58.4 %collective-permute-start.32 = (bf16[512,1536]{1,0:T(8,128)(2,1)}, bf16[512,1536]{1,0:T(8,128)(2,1)}, u32[]{:S(2)}, u32[]{:S(2)}) collective-permute-start(bf16[512,1536]{1,0:T(8,128)(2,1)} %product.21.refs_4_.refs_32_), channel_id=1, source_target_pairs={{0,1},{1,0},{2,3},{3,2},{4,5},{5,4},{6,7},{7,6},{8,9},{9,8},{10,11... | collective-permute-start | bytes 4718600 | tf_op jit(solution)/shard_map/ppermute | solution.py:741
  493.6 60.7 %collective-permute-start.35 = (bf16[512,1536]{1,0:T(8,128)(2,1)}, bf16[512,1536]{1,0:T(8,128)(2,1)}, u32[]{:S(2)}, u32[]{:S(2)}) collective-permute-start(bf16[512,1536]{1,0:T(8,128)(2,1)} %product.23), channel_id=1, source_target_pairs={{0,4},{4,0},{1,5},{5,1},{2,6},{6,2},{3,7},{7,3},{8,12},{12,8},{9,1... | collective-permute-start | bytes 4718600 | tf_op jit(solution)/shard_map/ppermute | solution.py:614
  497.3 49.8 %collective-permute-start.33 = (bf16[192,3072]{1,0:T(8,128)(2,1)}, bf16[192,3072]{1,0:T(8,128)(2,1)}, u32[]{:S(2)}, u32[]{:S(2)}) collective-permute-start(bf16[192,3072]{1,0:T(8,128)(2,1)} %get-tuple-element.264.refs_33_), channel_id=1, source_target_pairs={{2,4},{4,2},{3,5},{5,3},{10,12},{12,10},{11,13},{13,11},{18,20},{2... | collective-permute-start | bytes 3538952 | tf_op jit(solution)/shard_map/ppermute | solution.py:610
  499.0 55.3 %collective-permute-start.34 = (bf16[192,3072]{1,0:T(8,128)(2,1)}, bf16[192,3072]{1,0:T(8,128)(2,1)}, u32[]{:S(2)}, u32[]{:S(2)}) collective-permute-start(bf16[192,3072]{1,0:T(8,128)(2,1)} %get-tuple-element.288), channel_id=1, source_target_pairs={{2,0},{6,2},{0,4},{4,6},{3,1},{7,3},{1,5},{5,7},{10,8},{14,10},{8,... | collective-permute-start | bytes 3538952 | tf_op jit(solution)/shard_map/ppermute | solution.py:646
  559.7 28.9 %collective-permute-start.36 = (bf16[512,1536]{1,0:T(8,128)(2,1)}, bf16[512,1536]{1,0:T(8,128)(2,1)}, u32[]{:S(2)}, u32[]{:S(2)}) collective-permute-start(bf16[512,1536]{1,0:T(8,128)(2,1)} %norm_back.3.refs_0_), channel_id=1, source_target_pairs={{2,5},{3,4},{4,3},{5,2},{10,13},{11,12},{12,11},{13,10},{18,21},{1... | collective-permute-start | bytes 4718600 | tf_op jit(solution)/shard_map/ppermute | solution.py:760
  589.9 27.7 %collective-permute-start.41 = (bf16[192,1536]{1,0:T(8,128)(2,1)S(1)}, bf16[192,1536]{1,0:T(8,128)(2,1)}, u32[]{:S(2)}, u32[]{:S(2)}) collective-permute-start(bf16[192,1536]{1,0:T(8,128)(2,1)S(1)} %get-tuple-element.270.refs_1_.own_ref), channel_id=1, source_target_pairs={{2,4},{4,2},{3,5},{5,3},{10,12},{12,10},{11,13},{13,11},{18,20},{2... | collective-permute-start | bytes 1769480 | tf_op jit(solution)/shard_map/ppermute | solution.py:610
  593.6 12.8 %collective-permute-start.37 = (f32[2,192]{1,0:T(2,128)S(1)}, f32[2,192]{1,0:T(2,128)S(1)}, u32[]{:S(2)}, u32[]{:S(2)}) collective-permute-start(f32[2,192]{1,0:T(2,128)S(1)} %bitcast.35), channel_id=1, source_target_pairs={{0,4},{4,0},{1,5},{5,1},{2,6},{6,2},{3,7},{7,3},{8,12},{12,8},{9,1... | collective-permute-start | bytes 4616 | tf_op jit(solution)/shard_map/ppermute | solution.py:614
  607.1 9.0 %collective-permute-start.40 = (f32[2,192]{1,0:T(2,128)S(1)}, f32[2,192]{1,0:T(2,128)S(1)}, u32[]{:S(2)}, u32[]{:S(2)}) collective-permute-start(f32[2,192]{1,0:T(2,128)S(1)} %fusion.6), channel_id=1, source_target_pairs={{0,3},{1,0},{2,1},{3,2},{4,7},{5,4},{6,5},{7,6},{8,11},{9,8},{10,9... | collective-permute-start | bytes 4616 | tf_op jit(solution)/shard_map/ppermute | solution.py:997
  611.1 5.0 collective-permute-start.39
  611.1 5.4 collective-permute-start.38
  613.2 17.1 %collective-permute-start.42 = (bf16[192,1536]{1,0:T(8,128)(2,1)S(1)}, bf16[192,1536]{1,0:T(8,128)(2,1)S(1)}, u32[]{:S(2)}, u32[]{:S(2)}) collective-permute-start(bf16[192,1536]{1,0:T(8,128)(2,1)S(1)} %get-tuple-element.292), channel_id=1, source_target_pairs={{2,0},{6,2},{0,4},{4,6},{3,1},{7,3},{1,5},{5,7},{10,8},{14,10},{8,... | collective-permute-start | bytes 1769480 | tf_op jit(solution)/shard_map/ppermute | solution.py:646
  (67 other events, 667.8 us)
Sparse Core Ops, SparseCore 0:
  46.9 58.9 all-gather.2
  131.8 120.3 all-gather.4
  392.4 93.5 reduce-scatter.2
  530.1 58.4 reduce-scatter.4

commit v5 on v4

--- a/solution.py
+++ b/solution.py
@@ -957,7 +957,7 @@
         (*joined, ff_blocks[0]),
     )
     attn_part = sum_rows(attn_wgrad)
-    sent, ff_blocks, first_own[0] = together(sent, ff_blocks, first_own[0])
+    sent, first_own[0], wgrad_there = together(sent, first_own[0], attn_wgrad)
 
     input_grad = row_pass(
         norm_back,
@@ -965,11 +965,11 @@
         whole_rows(db, stream_own, *first_own, *sent),
         [gain_first],
         [bf16],
-        [attn_wgrad],
+        [wgrad_there],
     )[0]
     input_raw = cross_tokens(input_grad)
     attn_part, ff_blocks, mixed_others = order(
-        [input_grad], (attn_part, ff_blocks, mixed_others), 400
+        [input_grad, *ff_blocks[1:]], (attn_part, ff_blocks, mixed_others), 400
     )
     attn_part, input_raw = together(attn_part, input_raw)
     attn_blocks = send_blocks(attn_part)

time: 651 us -> 646 us (level)
    ppermute x2, waiting for transfers between devices: 19.9 us -> 12.9 us  [send_blocks(): lax.ppermute(jnp.where(first, lower, upper), ('c', 'zh'), slant_back)]
  transfers between devices with their start and end apart: 47 -> 47, of which waited for: 20 -> 18; matrix products, arithmetic and copies ran while one was open for 6% -> 6% of each run, Pallas kernels for 43% -> 43%
where the time goes in v5:
time: 646 us; the launch traced here: 636 us
  Pallas kernels  278 us (43%)
  waiting for transfers between devices  164 us (25%)
  starting transfers between devices  106 us (16%)
  local copies, waits for them, and re-layouts  36.5 us (6%)
  other arithmetic  36.3 us (6%)
  between operations  14.9 us (2%)
    pallas_call x2, Pallas kernels, hidden_pass(): pl.pallas_call(functools.partial(hidden_kernel, min(256, units), count),...  55.3 us
    pallas_call x2, Pallas kernels, wgrad(): pl.pallas_call(functools.partial(wgrad_kernel, counts), grid=(column,), i...  52.2 us
    ppermute x18, starting transfers between devices, other_core(): return lax.ppermute(a, 'c', swap_two)  52.1 us
    pallas_call x2, Pallas kernels, attend_back(): pl.pallas_call(functools.partial(attend_back_kernel, ring, block, chip, f...  44.5 us
    pallas_call x12, Pallas kernels, product(): pl.pallas_call(functools.partial(product_kernel, dims, len(parts), len(af...  43 us
    ppermute x2, waiting for transfers between devices, spread_pair(): return (w, cross(w), lax.ppermute(w, ('c', 'zh'), slant_pairs))  32 us
    ppermute x2, waiting for transfers between devices, early_neighbours(): lax.ppermute(original, ('c', 'zh', 'zl'), pairs_of(True, k))  30.1 us
    reduce_scatter x2, waiting for transfers between devices, sum_rows(): return lax.psum_scatter(grad, 'd', scatter_dimension=0, tiled=True)  30 us
  transfers between devices with their start and end apart: 47, of which 18 were waited for; matrix products, arithmetic and copies ran while one was open for 6% of the time, Pallas kernels for 43%

profile of v5, /device:TPU:0, one launch (start us, length us, event | category | flops | bytes accessed | tf_op | source)
XLA Modules:
  0.0 635.6 jit_solution(17535436432395910427)
XLA Ops:
  7.2 4.9 collective-permute-start.2
  20.2 22.8 %collective-permute-done.1 = bf16[192,1536]{1,0:T(8,128)(2,1)S(1)} collective-permute-done((bf16[192,1536]{1,0:T(8,128)(2,1)}, bf16[192,1536]{1,0:T(8,128)(2,1)S(1)}, u32[]{:S(2)}, u32[]{:S(2)}) %collective-permute-start.1) | collective-permute-done | bytes 589856 | tf_op jit(solution)/shard_map/ppermute | solution.py:626
  50.0 4.8 collective-permute-start.5
  55.0 3.7 fusion.4
  59.9 30.1 %collective-permute-done.5 = bf16[512,1536]{1,0:T(8,128)(2,1)} collective-permute-done((bf16[512,1536]{1,0:T(8,128)(2,1)}, bf16[512,1536]{1,0:T(8,128)(2,1)}, u32[]{:S(2)}, u32[]{:S(2)}) %collective-permute-start.5) | collective-permute-done | bytes 1572896 | tf_op jit(solution)/shard_map/ppermute | solution.py:776
  96.3 4.4 collective-permute-start.8
  100.7 5.2 all-gather.3.cloned.1.call-done.w_ref.refs_1_.refs_3_
  107.7 7.6 %project.2 = (bf16[2048,1536]{1,0:T(8,128)(2,1)S(1)}, bf16[2048,512]{1,0:T(8,128)(2,1)S(1)}, bf16[2048,256]{1,0:T(8,128)(2,1)S(1)}, bf16[2048,256]{1,0:T(8,128)(2,1)S(1)}) custom-call(bf16[512,1536]{1,0:T(8,128)(2,1)} %broadcast_select_fusion.4.x_ref.refs_0_.refs_1_, bf16[512,1536]{1,0:T(8,128)(2,1)} %collective-permute-done.9.y_ref, ...), custom_call_target="tpu_custom_call" | custom-call | flops 1 | bytes 1 | tf_op jit(solution)/shard_map/project/pallas_call | solution.py:318
  118.0 9.2 %collective-permute-done.8 = bf16[192,3072]{1,0:T(8,128)(2,1)} collective-permute-done((bf16[192,3072]{1,0:T(8,128)(2,1)S(1)}, bf16[192,3072]{1,0:T(8,128)(2,1)}, u32[]{:S(2)}, u32[]{:S(2)}) %collective-permute-start.8) | collective-permute-done | bytes 1179680 | tf_op jit(solution)/shard_map/ppermute | solution.py:626
  133.5 25.9 %collective-permute-start.10 = (bf16[512,1536]{1,0:T(8,128)(2,1)S(1)}, bf16[512,1536]{1,0:T(8,128)(2,1)S(1)}, u32[]{:S(2)}, u32[]{:S(2)}) collective-permute-start(bf16[512,1536]{1,0:T(8,128)(2,1)S(1)} %broadcast_select_fusion.3.x_ref), channel_id=1, source_target_pairs={{0,4},{4,0},{1,5},{5,1},{2,6},{6,2},{3,7},{7,3},{8,12},{12,8},{9,1... | collective-permute-start | bytes 4718600 | tf_op jit(solution)/shard_map/ppermute | solution.py:614
  163.7 9.5 %project.3 = (bf16[2048,1536]{1,0:T(8,128)(2,1)}, bf16[2048,512]{1,0:T(8,128)(2,1)}, bf16[2048,256]{1,0:T(8,128)(2,1)}, bf16[2048,256]{1,0:T(8,128)(2,1)}) custom-call(bf16[512,1536]{1,0:T(8,128)(2,1)} %copy-done.57, bf16[512,1536]{1,0:T(8,128)(2,1)} %copy-done.67, ...), custom_call_target="tpu_custom_call", output_to_operand_aliasing={{0}: (6, {}), {1}: (7, {}), {2}: (8, {}), {3}: (9, {})} | custom-call | flops 8000000000 | bytes 1 | tf_op jit(solution)/shard_map/project/pallas_call | solution.py:318
  177.2 13.7 %attend.2 = (bf16[1024,512]{1,0:T(8,128)(2,1)S(1)}, f32[2,2,1024]{2,1,0:T(2,128)S(1)}) custom-call(s32[3]{0:T(128)S(1)} %pad_add_fusion.1.place_ref, bf16[2048,512]{1,0:T(8,128)(2,1)S(1)} %copy-done.4, bf16[2048,256]{1,0:T(8,128)(2,1)S(1)} %copy-done.19, bf16[2048,256]{1,0:T(8,128)(2,1)S(1)} %copy-done.23, s32[1,2048]{1,0:T(1,128)S(1)} %bitcast.21), custom_call_target="tpu_custom_call" | custom-call | flops 1 | bytes 1 | tf_op jit(solution)/shard_map/attend/pallas_call | solution.py:103
  190.9 3.1 product.12
  197.4 3.6 product.13.refs_0_
  201.0 5.2 collective-permute-start.13
  210.9 13.6 %attend.3 = (bf16[1024,512]{1,0:T(8,128)(2,1)S(1)}, f32[2,2,1024]{2,1,0:T(2,128)S(1)}) custom-call(s32[3]{0:T(128)S(1)} %pad_add_fusion.1.place_ref, bf16[2048,512]{1,0:T(8,128)(2,1)S(1)} %copy-done.5, bf16[2048,256]{1,0:T(8,128)(2,1)S(1)} %copy-done.20, bf16[2048,256]{1,0:T(8,128)(2,1)S(1)} %copy-done.24, s32[1,2048]{1,0:T(1,128)S(1)} %bitcast.22), custom_call_target="tpu_custom_call" | custom-call | flops 1 | bytes 1 | tf_op jit(solution)/shard_map/attend/pallas_call | solution.py:103
  224.5 3.0 product.15
  232.0 9.8 %collective-permute-done.13.refs_3_ = bf16[512,1536]{1,0:T(8,128)(2,1)} collective-permute-done((bf16[512,1536]{1,0:T(8,128)(2,1)}, bf16[512,1536]{1,0:T(8,128)(2,1)}, u32[]{:S(2)}, u32[]{:S(2)}) %collective-permute-start.13) | collective-permute-done | bytes 1572896 | tf_op jit(solution)/shard_map/ppermute | solution.py:741
  241.9 4.8 norm_forward.1
  246.7 10.7 %collective-permute-start.16 = (bf16[512,1536]{1,0:T(8,128)(2,1)}, bf16[512,1536]{1,0:T(8,128)(2,1)}, u32[]{:S(2)}, u32[]{:S(2)}) collective-permute-start(bf16[512,1536]{1,0:T(8,128)(2,1)} %get-tuple-element.185.refs_0_.a_ref), channel_id=1, source_target_pairs={{0,4},{4,0},{1,5},{5,1},{2,6},{6,2},{3,7},{7,3},{8,12},{12,8},{9,1... | collective-permute-start | bytes 4718600 | tf_op jit(solution)/shard_map/ppermute | solution.py:614
  263.9 27.7 %hidden.2 = (bf16[1024,1024]{1,0:T(8,128)(2,1)}, bf16[1024,2048]{1,0:T(8,128)(2,1)}, bf16[512,1536]{1,0:T(8,128)(2,1)S(1)}, bf16[512,1536]{1,0:T(8,128)(2,1)}, b...) custom-call(bf16[512,1536]{1,0:T(8,128)(2,1)} %get-tuple-element.185.refs_0_.a_ref, ...), custom_call_target="tpu_custom_call" | custom-call | flops 8000000000 | bytes 1 | tf_op jit(solution)/shard_map/hidden/pallas_call | solution.py:382
  291.6 5.7 collective-permute-done.18.a_ref.refs_2_
  302.2 3.5 mixed.2
  305.7 9.0 %collective-permute-start.23 = (bf16[512,1536]{1,0:T(8,128)(2,1)}, bf16[512,1536]{1,0:T(8,128)(2,1)S(1)}, u32[]{:S(2)}, u32[]{:S(2)}) collective-permute-start(bf16[512,1536]{1,0:T(8,128)(2,1)} %mixed.2), channel_id=1, source_target_pairs={{2,5},{3,4},{4,3},{5,2},{10,13},{11,12},{12,11},{13,10},{18,21},{1... | collective-permute-start | bytes 4718600 | tf_op jit(solution)/shard_map/ppermute | solution.py:760
  314.7 27.6 %hidden.3 = (bf16[1024,1024]{1,0:T(8,128)(2,1)}, bf16[1024,2048]{1,0:T(8,128)(2,1)}, bf16[512,1536]{1,0:T(8,128)(2,1)S(1)}, bf16[512,1536]{1,0:T(8,128)(2,1)S(1)...) custom-call(bf16[512,1536]{1,0:T(8,128)(2,1)} %collective-permute-done.18.a_ref.refs_2_, ...), custom_call_target="tpu_custom_call" | custom-call | flops 8000000000 | bytes 1 | tf_op jit(solution)/shard_map/hidden/pallas_call | solution.py:382
  344.6 4.6 collective-permute-start.24
  352.3 2.9 join.2.refs_16_
  356.1 2.9 join.3
  360.5 29.0 %wgrad.2 = bf16[1536,3072]{1,0:T(8,128)(2,1)} custom-call(bf16[512,1536]{1,0:T(8,128)(2,1)} %get-tuple-element.185.refs_0_.a_ref, bf16[512,1536]{1,0:T(8,128)(2,1)} %collective-permute-done.16.b_ref.refs_1_, bf16[512,1536]{1,0:T(8,128)(2,1)} %collective-permute-done.18.a_ref.refs_2_, bf16[512,1536]{1,0:T(8,128)(2,1)} %collective-permute-done.19.b_ref.refs_3_, ...), custom_call_target="tpu_custom_call" | custom-call | flops 8000000000 | bytes 1 | tf_op jit(solution)/shard_map/wgrad/pallas_call | solution.py:479
  392.7 5.6 norm_back.2.refs_0_.refs_24_
  409.0 21.1 %attend_back.2 = (bf16[1024,512]{1,0:T(8,128)(2,1)S(1)}, f32[2048,256]{1,0:T(8,128)S(1)}, f32[2048,256]{1,0:T(8,128)S(1)}) custom-call(s32[3]{0:T(128)S(1)} %pad_add_fusion.1.place_ref, bf16[2048,512]{1,0:T(8,128)(2,1)S(1)} %copy-done.5, bf16[2048,256]{1,0:T(8,128)(2,1)S(1)} %copy-done.21, bf16[2048,256]{1,0:T(8,128)(2,1)S(1)} %copy-done.25, ...), custom_call_target="tpu_custom_call" | custom-call | flops 1 | bytes 1 | tf_op jit(solution)/shard_map/attend_back/pallas_call | solution.py:236
  431.4 3.9 collective-permute-done.27.refs_0_.refs_26_
  438.9 3.2 product.19
  443.7 23.4 %attend_back.3 = (bf16[1024,512]{1,0:T(8,128)(2,1)S(1)}, bf16[2048,256]{1,0:T(8,128)(2,1)S(1)}, bf16[2048,256]{1,0:T(8,128)(2,1)S(1)}) custom-call(s32[3]{0:T(128)S(1)} %pad_add_fusion.1.place_ref, bf16[2048,512]{1,0:T(8,128)(2,1)S(1)} %copy-done.6, bf16[2048,256]{1,0:T(8,128)(2,1)S(1)} %copy-done.21, bf16[2048,256]{1,0:T(8,128)(2,1)S(1)} %copy-done.25, ...), custom_call_target="tpu_custom_call" | custom-call | flops 1 | bytes 1 | tf_op jit(solution)/shard_map/attend_back/pallas_call | solution.py:236
  467.1 3.9 collective-permute-done.29.refs_1_
  471.1 5.4 product.20
  478.9 3.4 collective-permute-done.31.refs_4_
  483.5 5.2 product.21.refs_4_.refs_32_
  488.7 4.8 product.23
  493.9 3.3 broadcast_select_fusion.6
  501.3 4.1 product.22.refs_2_
  506.7 23.2 %wgrad.3.refs_6_ = bf16[1536,1536]{1,0:T(8,128)(2,1)} custom-call(bf16[2048,1536]{1,0:T(8,128)(2,1)} %get-tuple-element.246.refs_0_.refs_1_.refs_2_.refs_3_.refs_8_.refs_9_.refs_10_.refs_11_.refs_16_.refs_17_.refs_18_.refs_19_, ...), custom_call_target="tpu_custom_call" | custom-call | flops 8000000000 | bytes 1 | tf_op jit(solution)/shard_map/wgrad/pallas_call | solution.py:479
  529.9 17.1 %collective-permute-done.32.refs_4_ = bf16[512,1536]{1,0:T(8,128)(2,1)} collective-permute-done((bf16[512,1536]{1,0:T(8,128)(2,1)}, bf16[512,1536]{1,0:T(8,128)(2,1)}, u32[]{:S(2)}, u32[]{:S(2)}) %collective-permute-start.32) | collective-permute-done | bytes 1572896 | tf_op jit(solution)/shard_map/ppermute | solution.py:741
  547.1 5.6 norm_back.3.refs_0_
  558.5 30.0 %reduce-scatter.5.cloned.1.call-done.refs_0_ = bf16[384,1536]{1,0:T(8,128)(2,1)} async-done(((bf16[1536,1536]{1,0:T(8,128)(2,1)}), bf16[384,1536]{1,0:T(8,128)(2,1)}) %reduce-scatter.5.cloned.1.call-update) | async-done | bytes 1179664 | tf_op jit(solution)/shard_map/reduce_scatter | solution.py:656
  593.6 3.7 collective-permute-start.37
  608.2 2.9 mixed.3
  612.4 12.9 %collective-permute-done.42.slanted_ref = bf16[192,1536]{1,0:T(8,128)(2,1)S(1)} collective-permute-done((bf16[192,1536]{1,0:T(8,128)(2,1)S(1)}, bf16[192,1536]{1,0:T(8,128)(2,1)S(1)}, u32[]{:S(2)}, u32[]{:S(2)}) %collective-permute-start.42) | collective-permute-done | bytes 589856 | tf_op jit(solution)/shard_map/ppermute | solution.py:646
  (274 shorter events, 129.2 us)
Async XLA Ops:
  7.2 98.8 %all-gather.3.cloned.1.call-start = ((), (), s32[]{:S(2)}) async-start(), calls=%async_computation.2 | async-start | bytes 5898240 | tf_op jit(solution)/shard_map/all_gather | solution.py:638
  7.2 35.9 %collective-permute-start.2 = (bf16[512,1536]{1,0:T(8,128)(2,1)}, bf16[512,1536]{1,0:T(8,128)(2,1)S(1)}, u32[]{:S(2)}, u32[]{:S(2)}) collective-permute-start(bf16[512,1536]{1,0:T(8,128)(2,1)} %param.23), channel_id=1, source_target_pairs={{0,1},{1,0},{6,7},{7,6},{8,9},{9,8},{14,15},{15,14},{16,17},{17,16... | collective-permute-start | bytes 4718600 | tf_op jit(solution)/shard_map/ppermute | solution.py:776
  16.6 3.7 collective-permute-start
  17.3 25.8 %collective-permute-start.1 = (bf16[192,1536]{1,0:T(8,128)(2,1)}, bf16[192,1536]{1,0:T(8,128)(2,1)S(1)}, u32[]{:S(2)}, u32[]{:S(2)}) collective-permute-start(bf16[192,1536]{1,0:T(8,128)(2,1)} %pad.89), channel_id=1, source_target_pairs={{0,2},{2,6},{4,0},{6,4},{1,3},{3,7},{5,1},{7,5},{8,10},{10,14},{12... | collective-permute-start | bytes 1769480 | tf_op jit(solution)/shard_map/ppermute | solution.py:626
  18.4 1.8 collective-permute-start.3
  46.8 217.1 %all-gather.5.cloned.1.call-start = ((), (), s32[]{:S(2)}) async-start(), calls=%async_computation.3 | async-start | bytes 11796480 | tf_op jit(solution)/shard_map/all_gather | solution.py:638
  48.1 11.8 %collective-permute-start.4 = (bf16[512,1536]{1,0:T(8,128)(2,1)}, bf16[512,1536]{1,0:T(8,128)(2,1)}, u32[]{:S(2)}, u32[]{:S(2)}) collective-permute-start(bf16[512,1536]{1,0:T(8,128)(2,1)} %param.12), channel_id=1, source_target_pairs={{2,5},{3,4},{4,3},{5,2},{10,13},{11,12},{12,11},{13,10},{18,21},{1... | collective-permute-start | bytes 4718600 | tf_op jit(solution)/shard_map/ppermute | solution.py:760
  50.0 40.1 %collective-permute-start.5 = (bf16[512,1536]{1,0:T(8,128)(2,1)}, bf16[512,1536]{1,0:T(8,128)(2,1)}, u32[]{:S(2)}, u32[]{:S(2)}) collective-permute-start(bf16[512,1536]{1,0:T(8,128)(2,1)} %param.12), channel_id=1, source_target_pairs={{0,1},{1,0},{6,7},{7,6},{8,9},{9,8},{14,15},{15,14},{16,17},{17,16... | collective-permute-start | bytes 4718600 | tf_op jit(solution)/shard_map/ppermute | solution.py:776
  92.8 15.0 %collective-permute-start.9 = (bf16[512,1536]{1,0:T(8,128)(2,1)}, bf16[512,1536]{1,0:T(8,128)(2,1)}, u32[]{:S(2)}, u32[]{:S(2)}) collective-permute-start(bf16[512,1536]{1,0:T(8,128)(2,1)} %broadcast_select_fusion.4.x_ref.refs_0_.refs_1_), channel_id=1, source_target_pairs={{0,4},{4,0},{1,5},{5,1},{2,6},{6,2},{3,7},{7,3},{8,12},{12,8},{9,1... | collective-permute-start | bytes 4718600 | tf_op jit(solution)/shard_map/ppermute | solution.py:614
  92.8 34.4 %collective-permute-start.6 = (bf16[512,1536]{1,0:T(8,128)(2,1)}, bf16[512,1536]{1,0:T(8,128)(2,1)}, u32[]{:S(2)}, u32[]{:S(2)}) collective-permute-start(bf16[512,1536]{1,0:T(8,128)(2,1)} %collective-permute-done.4), channel_id=1, source_target_pairs={{2,3},{3,2},{4,5},{5,4},{10,11},{11,10},{12,13},{13,12},{18,19},{1... | collective-permute-start | bytes 4718600 | tf_op jit(solution)/shard_map/ppermute | solution.py:780
  94.7 23.3 %collective-permute-start.7 = (bf16[192,3072]{1,0:T(8,128)(2,1)S(1)}, bf16[192,3072]{1,0:T(8,128)(2,1)}, u32[]{:S(2)}, u32[]{:S(2)}) collective-permute-start(bf16[192,3072]{1,0:T(8,128)(2,1)S(1)} %pad_maximum_fusion.6), channel_id=1, source_target_pairs={{2,4},{4,2},{3,5},{5,3},{10,12},{12,10},{11,13},{13,11},{18,20},{2... | collective-permute-start | bytes 3538952 | tf_op jit(solution)/shard_map/ppermute | solution.py:610
  96.3 30.8 %collective-permute-start.8 = (bf16[192,3072]{1,0:T(8,128)(2,1)S(1)}, bf16[192,3072]{1,0:T(8,128)(2,1)}, u32[]{:S(2)}, u32[]{:S(2)}) collective-permute-start(bf16[192,3072]{1,0:T(8,128)(2,1)S(1)} %pad_maximum_fusion.6), channel_id=1, source_target_pairs={{0,2},{2,6},{4,0},{6,4},{1,3},{3,7},{5,1},{7,5},{8,10},{10,14},{12... | collective-permute-start | bytes 3538952 | tf_op jit(solution)/shard_map/ppermute | solution.py:626
  131.7 362.3 %reduce-scatter.3.cloned.1.call-start = ((), (), s32[]{:S(2)}) async-start(), calls=%async_computation.4 | async-start | bytes 11796480 | tf_op jit(solution)/shard_map/reduce_scatter | solution.py:656
  133.5 28.9 %collective-permute-start.10 = (bf16[512,1536]{1,0:T(8,128)(2,1)S(1)}, bf16[512,1536]{1,0:T(8,128)(2,1)S(1)}, u32[]{:S(2)}, u32[]{:S(2)}) collective-permute-start(bf16[512,1536]{1,0:T(8,128)(2,1)S(1)} %broadcast_select_fusion.3.x_ref), channel_id=1, source_target_pairs={{0,4},{4,0},{1,5},{5,1},{2,6},{6,2},{3,7},{7,3},{8,12},{12,8},{9,1... | collective-permute-start | bytes 4718600 | tf_op jit(solution)/shard_map/ppermute | solution.py:614
  159.4 31.5 %collective-permute-start.11 = (bf16[512,1536]{1,0:T(8,128)(2,1)S(1)}, bf16[512,1536]{1,0:T(8,128)(2,1)}, u32[]{:S(2)}, u32[]{:S(2)}) collective-permute-start(bf16[512,1536]{1,0:T(8,128)(2,1)S(1)} %copy-done.52), channel_id=1, source_target_pairs={{2,5},{3,4},{4,3},{5,2},{10,13},{11,12},{12,11},{13,10},{18,21},{1... | collective-permute-start | bytes 4718600 | tf_op jit(solution)/shard_map/ppermute | solution.py:760
  190.9 251.3 %copy-start.7 = (bf16[1024,512]{1,0:T(8,128)(2,1)}, bf16[1024,512]{1,0:T(8,128)(2,1)S(1)}, u32[]{:S(2)}) copy-start(bf16[1024,512]{1,0:T(8,128)(2,1)S(1)} %get-tuple-element.173.refs_0_.o_ref.refs_30_.refs_31_) | copy-start | bytes 3145732
  194.0 3.5 collective-permute-start.12
  194.4 37.6 %collective-permute-start.14 = (bf16[512,1536]{1,0:T(8,128)(2,1)}, bf16[512,1536]{1,0:T(8,128)(2,1)}, u32[]{:S(2)}, u32[]{:S(2)}) collective-permute-start(bf16[512,1536]{1,0:T(8,128)(2,1)} %collective-permute-done.11), channel_id=1, source_target_pairs={{2,3},{3,2},{4,5},{5,4},{10,11},{11,10},{12,13},{13,12},{18,19},{1... | collective-permute-start | bytes 4718600 | tf_op jit(solution)/shard_map/ppermute | solution.py:780
  201.0 40.8 %collective-permute-start.13 = (bf16[512,1536]{1,0:T(8,128)(2,1)}, bf16[512,1536]{1,0:T(8,128)(2,1)}, u32[]{:S(2)}, u32[]{:S(2)}) collective-permute-start(bf16[512,1536]{1,0:T(8,128)(2,1)} %product.13.refs_0_), channel_id=1, source_target_pairs={{0,1},{1,0},{2,3},{3,2},{4,5},{5,4},{6,7},{7,6},{8,9},{9,8},{10,11... | collective-permute-start | bytes 4718600 | tf_op jit(solution)/shard_map/ppermute | solution.py:741
  227.5 14.4 %collective-permute-start.15 = (bf16[512,1536]{1,0:T(8,128)(2,1)S(1)}, bf16[512,1536]{1,0:T(8,128)(2,1)}, u32[]{:S(2)}, u32[]{:S(2)}) collective-permute-start(bf16[512,1536]{1,0:T(8,128)(2,1)S(1)} %product.15), channel_id=1, source_target_pairs={{0,4},{4,0},{1,5},{5,1},{2,6},{6,2},{3,7},{7,3},{8,12},{12,8},{9,1... | collective-permute-start | bytes 4718600 | tf_op jit(solution)/shard_map/ppermute | solution.py:614
  246.7 16.5 %collective-permute-start.16 = (bf16[512,1536]{1,0:T(8,128)(2,1)}, bf16[512,1536]{1,0:T(8,128)(2,1)}, u32[]{:S(2)}, u32[]{:S(2)}) collective-permute-start(bf16[512,1536]{1,0:T(8,128)(2,1)} %get-tuple-element.185.refs_0_.a_ref), channel_id=1, source_target_pairs={{0,4},{4,0},{1,5},{5,1},{2,6},{6,2},{3,7},{7,3},{8,12},{12,8},{9,1... | collective-permute-start | bytes 4718600 | tf_op jit(solution)/shard_map/ppermute | solution.py:614
  260.1 3.8 collective-permute-start.17
  260.2 37.1 %collective-permute-start.18 = (bf16[512,1536]{1,0:T(8,128)(2,1)}, bf16[512,1536]{1,0:T(8,128)(2,1)}, u32[]{:S(2)}, u32[]{:S(2)}) collective-permute-start(bf16[512,1536]{1,0:T(8,128)(2,1)} %get-tuple-element.185.refs_0_.a_ref), channel_id=1, source_target_pairs={{0,1},{1,0},{2,3},{3,2},{4,5},{5,4},{6,7},{7,6},{8,9},{9,8},{10,11... | collective-permute-start | bytes 4718600 | tf_op jit(solution)/shard_map/ppermute | solution.py:618
  297.3 3.8 collective-permute-start.22
  298.6 16.1 %collective-permute-start.20 = (bf16[512,1536]{1,0:T(8,128)(2,1)}, bf16[512,1536]{1,0:T(8,128)(2,1)}, u32[]{:S(2)}, u32[]{:S(2)}) collective-permute-start(bf16[512,1536]{1,0:T(8,128)(2,1)} %broadcast_select_fusion.1.dy_ref.refs_10_), channel_id=1, source_target_pairs={{0,4},{4,0},{1,5},{5,1},{2,6},{6,2},{3,7},{7,3},{8,12},{12,8},{9,1... | collective-permute-start | bytes 4718600 | tf_op jit(solution)/shard_map/ppermute | solution.py:614
  300.5 14.2 %collective-permute-start.19 = (bf16[512,1536]{1,0:T(8,128)(2,1)}, bf16[512,1536]{1,0:T(8,128)(2,1)}, u32[]{:S(2)}, u32[]{:S(2)}) collective-permute-start(bf16[512,1536]{1,0:T(8,128)(2,1)} %collective-permute-done.18.a_ref.refs_2_), channel_id=1, source_target_pairs={{0,4},{4,0},{1,5},{5,1},{2,6},{6,2},{3,7},{7,3},{8,12},{12,8},{9,1... | collective-permute-start | bytes 4718600 | tf_op jit(solution)/shard_map/ppermute | solution.py:614
  300.6 14.1 %collective-permute-start.21 = (bf16[512,1536]{1,0:T(8,128)(2,1)}, bf16[512,1536]{1,0:T(8,128)(2,1)}, u32[]{:S(2)}, u32[]{:S(2)}) collective-permute-start(bf16[512,1536]{1,0:T(8,128)(2,1)} %get-tuple-element.199), channel_id=1, source_target_pairs={{0,4},{4,0},{1,5},{5,1},{2,6},{6,2},{3,7},{7,3},{8,12},{12,8},{9,1... | collective-permute-start | bytes 4718600 | tf_op jit(solution)/shard_map/ppermute | solution.py:614
  305.7 38.9 %collective-permute-start.23 = (bf16[512,1536]{1,0:T(8,128)(2,1)}, bf16[512,1536]{1,0:T(8,128)(2,1)S(1)}, u32[]{:S(2)}, u32[]{:S(2)}) collective-permute-start(bf16[512,1536]{1,0:T(8,128)(2,1)} %mixed.2), channel_id=1, source_target_pairs={{2,5},{3,4},{4,3},{5,2},{10,13},{11,12},{12,11},{13,10},{18,21},{1... | collective-permute-start | bytes 4718600 | tf_op jit(solution)/shard_map/ppermute | solution.py:760
  344.6 7.8 %collective-permute-start.24 = (bf16[512,1536]{1,0:T(8,128)(2,1)S(1)}, bf16[512,1536]{1,0:T(8,128)(2,1)}, u32[]{:S(2)}, u32[]{:S(2)}) collective-permute-start(bf16[512,1536]{1,0:T(8,128)(2,1)S(1)} %get-tuple-element.220), channel_id=1, source_target_pairs={{0,4},{4,0},{1,5},{5,1},{2,6},{6,2},{3,7},{7,3},{8,12},{12,8},{9,1... | collective-permute-start | bytes 4718600 | tf_op jit(solution)/shard_map/ppermute | solution.py:614
  349.2 6.9 %collective-permute-start.26 = (bf16[512,1536]{1,0:T(8,128)(2,1)}, bf16[512,1536]{1,0:T(8,128)(2,1)}, u32[]{:S(2)}, u32[]{:S(2)}) collective-permute-start(bf16[512,1536]{1,0:T(8,128)(2,1)} %get-tuple-element.222), channel_id=1, source_target_pairs={{0,4},{4,0},{1,5},{5,1},{2,6},{6,2},{3,7},{7,3},{8,12},{12,8},{9,1... | collective-permute-start | bytes 4718600 | tf_op jit(solution)/shard_map/ppermute | solution.py:614
  355.3 37.0 %collective-permute-start.25 = (bf16[512,1536]{1,0:T(8,128)(2,1)}, bf16[512,1536]{1,0:T(8,128)(2,1)}, u32[]{:S(2)}, u32[]{:S(2)}) collective-permute-start(bf16[512,1536]{1,0:T(8,128)(2,1)} %join.2.refs_16_), channel_id=1, source_target_pairs={{0,1},{1,0},{2,3},{3,2},{4,5},{5,4},{6,7},{7,6},{8,9},{9,8},{10,11... | collective-permute-start | bytes 4718600 | tf_op jit(solution)/shard_map/ppermute | solution.py:741
  392.3 196.2 %reduce-scatter.5.cloned.1.call-start = ((), (), s32[]{:S(2)}) async-start(), calls=%async_computation.5 | async-start | bytes 5898240 | tf_op jit(solution)/shard_map/reduce_scatter | solution.py:656
  398.3 4.9 collective-permute-start.28
  398.3 37.0 %collective-permute-start.27 = (bf16[512,1536]{1,0:T(8,128)(2,1)}, bf16[512,1536]{1,0:T(8,128)(2,1)S(1)}, u32[]{:S(2)}, u32[]{:S(2)}) collective-permute-start(bf16[512,1536]{1,0:T(8,128)(2,1)} %norm_back.2.refs_0_.refs_24_), channel_id=1, source_target_pairs={{0,1},{1,0},{2,3},{3,2},{4,5},{5,4},{6,7},{7,6},{8,9},{9,8},{10,11... | collective-permute-start | bytes 4718600 | tf_op jit(solution)/shard_map/ppermute | solution.py:618
  435.3 3.5 collective-permute-start.30
  435.3 35.7 %collective-permute-start.29 = (bf16[512,1536]{1,0:T(8,128)(2,1)S(1)}, bf16[512,1536]{1,0:T(8,128)(2,1)S(1)}, u32[]{:S(2)}, u32[]{:S(2)}) collective-permute-start(bf16[512,1536]{1,0:T(8,128)(2,1)S(1)} %copy-done.59), channel_id=1, source_target_pairs={{0,1},{1,0},{2,4},{3,5},{4,2},{5,3},{6,7},{7,6},{8,9},{9,8},{10,12... | collective-permute-start | bytes 4718600 | tf_op jit(solution)/shard_map/ppermute | solution.py:928
  476.4 5.8 collective-permute-start.31
  488.7 58.4 %collective-permute-start.32 = (bf16[512,1536]{1,0:T(8,128)(2,1)}, bf16[512,1536]{1,0:T(8,128)(2,1)}, u32[]{:S(2)}, u32[]{:S(2)}) collective-permute-start(bf16[512,1536]{1,0:T(8,128)(2,1)} %product.21.refs_4_.refs_32_), channel_id=1, source_target_pairs={{0,1},{1,0},{2,3},{3,2},{4,5},{5,4},{6,7},{7,6},{8,9},{9,8},{10,11... | collective-permute-start | bytes 4718600 | tf_op jit(solution)/shard_map/ppermute | solution.py:741
  493.5 53.5 %collective-permute-start.33 = (bf16[512,1536]{1,0:T(8,128)(2,1)}, bf16[512,1536]{1,0:T(8,128)(2,1)}, u32[]{:S(2)}, u32[]{:S(2)}) collective-permute-start(bf16[512,1536]{1,0:T(8,128)(2,1)} %product.23), channel_id=1, source_target_pairs={{0,4},{4,0},{1,5},{5,1},{2,6},{6,2},{3,7},{7,3},{8,12},{12,8},{9,1... | collective-permute-start | bytes 4718600 | tf_op jit(solution)/shard_map/ppermute | solution.py:614
  497.3 59.9 %collective-permute-start.34 = (bf16[192,3072]{1,0:T(8,128)(2,1)}, bf16[192,3072]{1,0:T(8,128)(2,1)}, u32[]{:S(2)}, u32[]{:S(2)}) collective-permute-start(bf16[192,3072]{1,0:T(8,128)(2,1)} %get-tuple-element.260.refs_33_), channel_id=1, source_target_pairs={{2,4},{4,2},{3,5},{5,3},{10,12},{12,10},{11,13},{13,11},{18,20},{2... | collective-permute-start | bytes 3538952 | tf_op jit(solution)/shard_map/ppermute | solution.py:610
  499.0 58.2 %collective-permute-start.35 = (bf16[192,3072]{1,0:T(8,128)(2,1)}, bf16[192,3072]{1,0:T(8,128)(2,1)}, u32[]{:S(2)}, u32[]{:S(2)}) collective-permute-start(bf16[192,3072]{1,0:T(8,128)(2,1)} %get-tuple-element.284), channel_id=1, source_target_pairs={{2,0},{6,2},{0,4},{4,6},{3,1},{7,3},{1,5},{5,7},{10,8},{14,10},{8,... | collective-permute-start | bytes 3538952 | tf_op jit(solution)/shard_map/ppermute | solution.py:646
  552.7 35.8 %collective-permute-start.36 = (bf16[512,1536]{1,0:T(8,128)(2,1)}, bf16[512,1536]{1,0:T(8,128)(2,1)}, u32[]{:S(2)}, u32[]{:S(2)}) collective-permute-start(bf16[512,1536]{1,0:T(8,128)(2,1)} %norm_back.3.refs_0_), channel_id=1, source_target_pairs={{2,5},{3,4},{4,3},{5,2},{10,13},{11,12},{12,11},{13,10},{18,21},{1... | collective-permute-start | bytes 4718600 | tf_op jit(solution)/shard_map/ppermute | solution.py:760
  589.9 22.5 %collective-permute-start.41 = (bf16[192,1536]{1,0:T(8,128)(2,1)S(1)}, bf16[192,1536]{1,0:T(8,128)(2,1)}, u32[]{:S(2)}, u32[]{:S(2)}) collective-permute-start(bf16[192,1536]{1,0:T(8,128)(2,1)S(1)} %get-tuple-element.266.refs_1_.own_ref), channel_id=1, source_target_pairs={{2,4},{4,2},{3,5},{5,3},{10,12},{12,10},{11,13},{13,11},{18,20},{2... | collective-permute-start | bytes 1769480 | tf_op jit(solution)/shard_map/ppermute | solution.py:610
  593.6 9.0 %collective-permute-start.37 = (f32[2,192]{1,0:T(2,128)S(1)}, f32[2,192]{1,0:T(2,128)S(1)}, u32[]{:S(2)}, u32[]{:S(2)}) collective-permute-start(f32[2,192]{1,0:T(2,128)S(1)} %bitcast.35), channel_id=1, source_target_pairs={{0,4},{4,0},{1,5},{5,1},{2,6},{6,2},{3,7},{7,3},{8,12},{12,8},{9,1... | collective-permute-start | bytes 4616 | tf_op jit(solution)/shard_map/ppermute | solution.py:614
  603.3 7.9 %collective-permute-start.40 = (f32[2,192]{1,0:T(2,128)S(1)}, f32[2,192]{1,0:T(2,128)S(1)}, u32[]{:S(2)}, u32[]{:S(2)}) collective-permute-start(f32[2,192]{1,0:T(2,128)S(1)} %fusion.6), channel_id=1, source_target_pairs={{0,3},{1,0},{2,1},{3,2},{4,7},{5,4},{6,5},{7,6},{8,11},{9,8},{10,9... | collective-permute-start | bytes 4616 | tf_op jit(solution)/shard_map/ppermute | solution.py:997
  605.8 5.3 collective-permute-start.39
  605.8 5.4 collective-permute-start.38
  608.2 17.1 %collective-permute-start.42 = (bf16[192,1536]{1,0:T(8,128)(2,1)S(1)}, bf16[192,1536]{1,0:T(8,128)(2,1)S(1)}, u32[]{:S(2)}, u32[]{:S(2)}) collective-permute-start(bf16[192,1536]{1,0:T(8,128)(2,1)S(1)} %get-tuple-element.288), channel_id=1, source_target_pairs={{2,0},{6,2},{0,4},{4,6},{3,1},{7,3},{1,5},{5,7},{10,8},{14,10},{8,... | collective-permute-start | bytes 1769480 | tf_op jit(solution)/shard_map/ppermute | solution.py:646
  (67 other events, 709.8 us)
Sparse Core Ops, SparseCore 0:
  46.9 58.9 all-gather.2
  131.8 120.3 all-gather.4
  392.4 93.5 reduce-scatter.2
  530.0 58.4 reduce-scatter.4

commit v6 on v5

--- a/solution.py
+++ b/solution.py
@@ -434,33 +434,42 @@
     )(*[x for x, _ in parts], *in_hbm(w), *after, *extra)
 
 
-def wgrad_kernel(counts, *refs):
+def without_gaps(w):
+    half = HEAD_SIZE // 2
+    parts = [w[:, at : at + half] for at in range(0, w.shape[1], LANES // 2)]
+    return jnp.concatenate(parts, 1)
+
+
+def wgrad_kernel(counts, cut, *refs):
     out_ref = refs[-1]
     j = pl.program_id(0)
     first = 0
-    refs = refs[:-1]
-    for pieces, blocks in counts:
-        lefts, rights, refs = refs[:pieces], refs[pieces : 2 * pieces], refs[2 * pieces :]
+    for pieces, parts, blocks in counts:
+        lefts, refs = refs[:pieces], refs[pieces:]
+        rights, refs = refs[: pieces * parts], refs[pieces * parts :]
 
         @pl.when((j >= first) & (j < first + blocks))
         def _():
             total = None
-            for a, b in zip(lefts, rights):
-                p = lax.dot_general(a[...], b[...], rows_both, preferred_element_type=f32)
+            for i, a in enumerate(lefts):
+                b = [ref[...] for ref in rights[parts * i : parts * (i + 1)]]
+                b = b[0] if parts == 1 else jnp.concatenate(b, 1)
+                p = lax.dot_general(a[...], b, rows_both, preferred_element_type=f32)
                 total = p if total is None else total + p
-            out_ref[...] = total.astype(bf16)
+            total = total.astype(bf16)
+            out_ref[...] = without_gaps(total) if cut else total
 
         first += blocks
 
 
-def wgrad(groups, rows, first=()):
+def wgrad(groups, rows, block, first=(), cut=False):
     width = groups[0][0][0].shape[1]
-    block = min([512] + [group[0][2].shape[1] for group in groups])
     counts, specs, args = [], [], []
     column = 0
     for group in groups:
-        blocks = group[0][2].shape[1] // block
-        counts.append((len(group), blocks))
+        parts = len(group[0][2])
+        blocks = sum(b.shape[1] for b in group[0][2]) // block
+        counts.append((len(group), parts, blocks))
         for a, at, _, _ in group:
             specs.append(
                 pl.BlockSpec(
@@ -468,20 +477,22 @@
                 )
             )
             args.append(a)
-        for _, _, b, at in group:
+        for _, _, sides, at in group:
 
             def spot(j, at=at, column=column, blocks=blocks):
                 return (at, jnp.clip(j - column, 0, blocks - 1))
 
-            specs.append(pl.BlockSpec((rows, block), spot))
-            args.append(b)
+            for b in sides:
+                specs.append(pl.BlockSpec((rows, b.shape[1] if parts > 1 else block), spot))
+                args.append(b)
         column += blocks
+    wide = block * 3 // 4 if cut else block
     return pl.pallas_call(
-        functools.partial(wgrad_kernel, counts),
+        functools.partial(wgrad_kernel, counts, cut),
         grid=(column,),
         in_specs=specs + [unread] * len(first),
-        out_specs=pl.BlockSpec((width, block), lambda j: (0, j)),
-        out_shape=pltpu.HBM((width, column * block), bf16),
+        out_specs=pl.BlockSpec((width, wide), lambda j: (0, j)),
+        out_shape=pltpu.HBM((width, column * wide), bf16),
         compiler_params=pltpu.CompilerParams(
             vmem_limit_bytes=40 * 2**20, dimension_semantics=("arbitrary",)
         ),
@@ -567,33 +578,42 @@
     )(*weights, gains)
 
 
-def cut_kernel(counts, keep_ref, own_ref, crossed_ref, slanted_ref, *out_refs):
-    half = HEAD_SIZE // 2
+def cut_kernel(widths, padded, keep_ref, own_ref, crossed_ref, slanted_ref, *out_refs):
     kept = keep_ref[0] == 1
     at = 0
-    for ref, heads in zip(out_refs, counts):
-        parts = []
-        for _ in range(heads):
-            lanes = slice(at, at + LANES)
-            w = jnp.where(kept, own_ref[:, lanes], crossed_ref[:, lanes]).astype(f32)
-            w = w + slanted_ref[:, lanes].astype(f32)
-            parts += [w[:, :half], w[:, LANES // 2 : LANES // 2 + half]]
-            at += LANES
-        ref[...] = jnp.concatenate(parts, 1)
+    for ref, width in zip(out_refs, widths):
+        wide = width // HEAD_SIZE * LANES if padded else width
+        lanes = slice(at, at + wide)
+        w = jnp.where(kept, own_ref[:, lanes], crossed_ref[:, lanes]).astype(f32)
+        w = w + slanted_ref[:, lanes].astype(f32)
+        ref[...] = without_gaps(w) if padded else w
+        at += wide
 
 
 def cut_heads(blocks, widths):
-    counts = [width // HEAD_SIZE for width in widths]
-    rows = blocks[0].shape[0]
+    rows, columns = blocks[0].shape
     keep = stays().astype(jnp.int32).reshape(1)
     return pl.pallas_call(
-        functools.partial(cut_kernel, counts),
+        functools.partial(cut_kernel, widths, columns != sum(widths)),
         in_specs=[pl.BlockSpec(memory_space=pltpu.SMEM)]
         + [pl.BlockSpec(memory_space=pltpu.VMEM)] * 3,
         out_shape=[jax.ShapeDtypeStruct((rows, width), f32) for width in widths],
         cost_estimate=light,
         name="cut",
     )(keep, *blocks)
+
+
+def cut_rows_kernel(in_ref, out_ref):
+    out_ref[...] = without_gaps(in_ref[...])
+
+
+def cut_rows(w):
+    return pl.pallas_call(
+        cut_rows_kernel,
+        out_shape=jax.ShapeDtypeStruct((w.shape[0], w.shape[1] * 3 // 4), w.dtype),
+        cost_estimate=light,
+        name="cut_rows",
+    )(w)
 
 
 swap_two = [(0, 1), (1, 0)]
@@ -798,6 +818,8 @@
     places = jnp.where(stays(), positions, other_positions).reshape(2 * ring, rows)
     attn_rows = arrange(*attn_pair)
     attn_full = gather_rows(attn_rows)
+    cut = qw * 3 // 4 % LANES == 0
+    attn_kept = cut_rows(attn_rows) if cut else attn_rows
     stream_raw = cross_tokens(tokens)
     tokens_early = early_neighbours(tokens)
 
@@ -815,8 +837,8 @@
     sin = jnp.concatenate([-sin_half, gap, sin_half, gap], 1)
 
     ff_cols = jnp.concatenate([w_gate, w_up, w_down], 1)
-    cos, sin, start, stream_raw, tokens_early, ff_cols = together(
-        cos, sin, start, stream_raw, tokens_early, ff_cols
+    cos, sin, start, stream_raw, tokens_early, ff_cols, attn_kept = together(
+        cos, sin, start, stream_raw, tokens_early, ff_cols, attn_kept
     )
     stream_own = jnp.where(stays(), tokens, stream_raw)
     tokens_late = late_neighbours(stream_raw)
@@ -888,14 +910,19 @@
         hidden.append(hidden_pass(a, dy, ff_full))
 
     def pieces(pairs, hidden, i):
-        return [(a, 0, h[i], j) for pair, h in zip(pairs, hidden) for j, a in enumerate(pair)]
+        return [(a, 0, (h[i],), j) for pair, h in zip(pairs, hidden) for j, a in enumerate(pair)]
 
     hidden, mixed_raw = together(hidden, mixed_raw)
     joined = [join(h[2], other_core(h[3])) for h in hidden[1:]]
     sent = send_chips(joined)
     mixed_halves = [(h[4], other_core(h[5])) for h in hidden[1:]]
     mixed_joined = [join(*pair) for pair in mixed_halves]
-    ff_wgrad = wgrad([pieces(ff_in, hidden, 1), pieces(out_grads, hidden, 0)], rows, joined)
+    ff_wgrad = wgrad(
+        [pieces(ff_in, hidden, 1), pieces(out_grads, hidden, 0)],
+        rows,
+        min(512, w_down.shape[1]),
+        joined,
+    )
     sent, mixed_joined, ff_wgrad = together(sent, mixed_joined, ff_wgrad)
     ff_part = sum_rows(ff_wgrad)
     db = row_pass(
@@ -950,11 +977,15 @@
     ff_blocks = send_blocks(ff_part)
     first_own = split_cores(first_product(0, joined))
     attn_wgrad = wgrad(
-        [[(normed_first, 2 * i + j, dqs[i], j) for i in steps for j in range(2)]]
-        + [[(normed_first, i, d, i) for i in range(2 * ring)] for d in dkv]
-        + [[(branch[i][j], 0, attended[i][0], j) for i in steps for j in range(2)]],
+        [
+            [(normed_first, 2 * i + j, (dqs[i],), j) for i in steps for j in range(2)],
+            [(normed_first, i, tuple(dkv), i) for i in range(2 * ring)],
+            [(branch[i][j], 0, (attended[i][0],), j) for i in steps for j in range(2)],
+        ],
         rows,
+        qw,
         (*joined, ff_blocks[0]),
+        cut,
     )
     attn_part = sum_rows(attn_wgrad)
     sent, first_own[0], wgrad_there = together(sent, first_own[0], attn_wgrad)
@@ -986,7 +1017,7 @@
         return jnp.sum(product, 1).reshape(2, -1)
 
     gain_parts = jnp.stack(
-        [weighed(attn_rows, attn_part, qw + 2 * kw), weighed(ff_rows, ff_part, 2 * units)]
+        [weighed(attn_kept, attn_part, qcols + 2 * kcols if cut else qw + 2 * kw), weighed(ff_rows, ff_part, 2 * units)]
     )
     gain_parts = jnp.where(core == 0, gain_parts, gain_parts[:, ::-1])
     gain_parts = gain_parts[:, 0] + other_core(gain_parts[:, 1]) + marks[0][0, 0]

time: 646 us -> 641 us (level)
  waiting for transfers between devices: 164 us -> 148 us
  starting transfers between devices: 106 us -> 118 us
    ppermute x18, starting transfers between devices: 52.1 us -> 64.5 us  [other_core(): return lax.ppermute(a, 'c', swap_two)]
    reduce_scatter x2, waiting for transfers between devices: 30 us -> 18.2 us  [sum_rows(): return lax.psum_scatter(grad, 'd', scatter_dimension=0, tiled=True)]
    unnamed x138 -> x134, local copies, waits for them, and re-layouts: 29.7 us -> 28.3 us
    pallas_call x3 -> x4, Pallas kernels: 54.9 us -> 55.6 us  [the longest x2 50.3 us: wgrad(): pl.pallas_call(functools.partial(wgrad_kernel, counts, cut), grid=(column...]
  transfers between devices with their start and end apart: 47 -> 47, of which waited for: 18 -> 19; matrix products, arithmetic and copies ran while one was open for 6% -> 6% of each run, Pallas kernels for 43% -> 44%
where the time goes in v6:
time: 641 us; the launch traced here: 631 us
  Pallas kernels  279 us (44%)
  waiting for transfers between devices  148 us (23%)
  starting transfers between devices  118 us (18%)
  other arithmetic  36.1 us (6%)
  local copies, waits for them, and re-layouts  35.1 us (5%)
  between operations  14.9 us (2%)
    ppermute x18, starting transfers between devices, other_core(): return lax.ppermute(a, 'c', swap_two)  64.5 us
    pallas_call x2, Pallas kernels, hidden_pass(): pl.pallas_call(functools.partial(hidden_kernel, min(256, units), count),...  55.3 us
    pallas_call x2, Pallas kernels, wgrad(): pl.pallas_call(functools.partial(wgrad_kernel, counts, cut), grid=(column...  50.3 us
    pallas_call x2, Pallas kernels, attend_back(): pl.pallas_call(functools.partial(attend_back_kernel, ring, block, chip, f...  44.5 us
    pallas_call x12, Pallas kernels, product(): pl.pallas_call(functools.partial(product_kernel, dims, len(parts), len(af...  43 us
    ppermute x2, waiting for transfers between devices, spread_pair(): return (w, cross(w), lax.ppermute(w, ('c', 'zh'), slant_pairs))  32.1 us
    ppermute x3, waiting for transfers between devices, send_chips(): lax.ppermute(p.astype(bf16), 'zl', [(i, (i + k) % ring) for i in steps])  31.7 us
    unnamed x134, local copies, waits for them, and re-layouts  28.3 us
  transfers between devices with their start and end apart: 47, of which 19 were waited for; matrix products, arithmetic and copies ran while one was open for 6% of the time, Pallas kernels for 44%

profile of v6, /device:TPU:0, one launch (start us, length us, event | category | flops | bytes accessed | tf_op | source)
XLA Modules:
  0.0 630.6 jit_solution(7052366344622796271)
XLA Ops:
  7.2 4.9 collective-permute-start.2
  20.2 22.8 %collective-permute-done.1 = bf16[192,1536]{1,0:T(8,128)(2,1)S(1)} collective-permute-done((bf16[192,1536]{1,0:T(8,128)(2,1)}, bf16[192,1536]{1,0:T(8,128)(2,1)S(1)}, u32[]{:S(2)}, u32[]{:S(2)}) %collective-permute-start.1) | collective-permute-done | bytes 589856 | tf_op jit(solution)/shard_map/ppermute | solution.py:646
  49.0 4.8 collective-permute-start.5
  53.8 3.0 cut_rows.1
  56.9 3.7 fusion.3
  61.9 27.4 %collective-permute-done.5 = bf16[512,1536]{1,0:T(8,128)(2,1)} collective-permute-done((bf16[512,1536]{1,0:T(8,128)(2,1)}, bf16[512,1536]{1,0:T(8,128)(2,1)}, u32[]{:S(2)}, u32[]{:S(2)}) %collective-permute-start.5) | collective-permute-done | bytes 1572896 | tf_op jit(solution)/shard_map/ppermute | solution.py:796
  95.5 4.4 collective-permute-start.8
  99.9 5.3 all-gather.3.cloned.1.call-done.w_ref.refs_1_.refs_3_
  106.9 7.6 %project.2 = (bf16[2048,1536]{1,0:T(8,128)(2,1)S(1)}, bf16[2048,512]{1,0:T(8,128)(2,1)S(1)}, bf16[2048,256]{1,0:T(8,128)(2,1)S(1)}, bf16[2048,256]{1,0:T(8,128)(2,1)S(1)}) custom-call(bf16[512,1536]{1,0:T(8,128)(2,1)} %broadcast_select_fusion.4.x_ref.refs_0_.refs_1_, bf16[512,1536]{1,0:T(8,128)(2,1)} %collective-permute-done.9.y_ref, ...), custom_call_target="tpu_custom_call" | custom-call | flops 1 | bytes 1 | tf_op jit(solution)/shard_map/project/pallas_call | solution.py:318
  117.2 9.2 %collective-permute-done.8 = bf16[192,3072]{1,0:T(8,128)(2,1)} collective-permute-done((bf16[192,3072]{1,0:T(8,128)(2,1)S(1)}, bf16[192,3072]{1,0:T(8,128)(2,1)}, u32[]{:S(2)}, u32[]{:S(2)}) %collective-permute-start.8) | collective-permute-done | bytes 1179680 | tf_op jit(solution)/shard_map/ppermute | solution.py:646
  132.7 25.9 %collective-permute-start.10 = (bf16[512,1536]{1,0:T(8,128)(2,1)S(1)}, bf16[512,1536]{1,0:T(8,128)(2,1)S(1)}, u32[]{:S(2)}, u32[]{:S(2)}) collective-permute-start(bf16[512,1536]{1,0:T(8,128)(2,1)S(1)} %broadcast_select_fusion.3.x_ref), channel_id=1, source_target_pairs={{0,4},{4,0},{1,5},{5,1},{2,6},{6,2},{3,7},{7,3},{8,12},{12,8},{9,1... | collective-permute-start | bytes 4718600 | tf_op jit(solution)/shard_map/ppermute | solution.py:634
  162.9 9.5 %project.3 = (bf16[2048,1536]{1,0:T(8,128)(2,1)}, bf16[2048,512]{1,0:T(8,128)(2,1)}, bf16[2048,256]{1,0:T(8,128)(2,1)}, bf16[2048,256]{1,0:T(8,128)(2,1)}) custom-call(bf16[512,1536]{1,0:T(8,128)(2,1)} %copy-done.54, bf16[512,1536]{1,0:T(8,128)(2,1)} %copy-done.65, ...), custom_call_target="tpu_custom_call", output_to_operand_aliasing={{0}: (6, {}), {1}: (7, {}), {2}: (8, {}), {3}: (9, {})} | custom-call | flops 8000000000 | bytes 1 | tf_op jit(solution)/shard_map/project/pallas_call | solution.py:318
  176.4 13.7 %attend.2 = (bf16[1024,512]{1,0:T(8,128)(2,1)S(1)}, f32[2,2,1024]{2,1,0:T(2,128)S(1)}) custom-call(s32[3]{0:T(128)S(1)} %pad_add_fusion.1.place_ref, bf16[2048,512]{1,0:T(8,128)(2,1)S(1)} %copy-done.4, bf16[2048,256]{1,0:T(8,128)(2,1)S(1)} %copy-done.19, bf16[2048,256]{1,0:T(8,128)(2,1)S(1)} %copy-done.23, s32[1,2048]{1,0:T(1,128)S(1)} %bitcast.21), custom_call_target="tpu_custom_call" | custom-call | flops 1 | bytes 1 | tf_op jit(solution)/shard_map/attend/pallas_call | solution.py:103
  190.2 3.1 product.12
  196.7 3.6 product.13.refs_0_
  200.3 5.2 collective-permute-start.13
  210.1 13.6 %attend.3 = (bf16[1024,512]{1,0:T(8,128)(2,1)S(1)}, f32[2,2,1024]{2,1,0:T(2,128)S(1)}) custom-call(s32[3]{0:T(128)S(1)} %pad_add_fusion.1.place_ref, bf16[2048,512]{1,0:T(8,128)(2,1)S(1)} %copy-done.5, bf16[2048,256]{1,0:T(8,128)(2,1)S(1)} %copy-done.20, bf16[2048,256]{1,0:T(8,128)(2,1)S(1)} %copy-done.24, s32[1,2048]{1,0:T(1,128)S(1)} %bitcast.22), custom_call_target="tpu_custom_call" | custom-call | flops 1 | bytes 1 | tf_op jit(solution)/shard_map/attend/pallas_call | solution.py:103
  223.7 3.0 product.15
  231.2 9.9 %collective-permute-done.13.refs_3_ = bf16[512,1536]{1,0:T(8,128)(2,1)} collective-permute-done((bf16[512,1536]{1,0:T(8,128)(2,1)}, bf16[512,1536]{1,0:T(8,128)(2,1)}, u32[]{:S(2)}, u32[]{:S(2)}) %collective-permute-start.13) | collective-permute-done | bytes 1572896 | tf_op jit(solution)/shard_map/ppermute | solution.py:761
  241.1 4.8 norm_forward.1
  245.9 10.7 %collective-permute-start.16 = (bf16[512,1536]{1,0:T(8,128)(2,1)}, bf16[512,1536]{1,0:T(8,128)(2,1)}, u32[]{:S(2)}, u32[]{:S(2)}) collective-permute-start(bf16[512,1536]{1,0:T(8,128)(2,1)} %get-tuple-element.186.refs_0_.a_ref), channel_id=1, source_target_pairs={{0,4},{4,0},{1,5},{5,1},{2,6},{6,2},{3,7},{7,3},{8,12},{12,8},{9,1... | collective-permute-start | bytes 4718600 | tf_op jit(solution)/shard_map/ppermute | solution.py:634
  263.1 27.7 %hidden.2 = (bf16[1024,1024]{1,0:T(8,128)(2,1)}, bf16[1024,2048]{1,0:T(8,128)(2,1)}, bf16[512,1536]{1,0:T(8,128)(2,1)S(1)}, bf16[512,1536]{1,0:T(8,128)(2,1)}, b...) custom-call(bf16[512,1536]{1,0:T(8,128)(2,1)} %get-tuple-element.186.refs_0_.a_ref, ...), custom_call_target="tpu_custom_call" | custom-call | flops 8000000000 | bytes 1 | tf_op jit(solution)/shard_map/hidden/pallas_call | solution.py:382
  290.8 5.7 collective-permute-done.18.a_ref.refs_2_
  301.4 3.5 mixed.2
  304.9 9.0 %collective-permute-start.23 = (bf16[512,1536]{1,0:T(8,128)(2,1)}, bf16[512,1536]{1,0:T(8,128)(2,1)S(1)}, u32[]{:S(2)}, u32[]{:S(2)}) collective-permute-start(bf16[512,1536]{1,0:T(8,128)(2,1)} %mixed.2), channel_id=1, source_target_pairs={{2,5},{3,4},{4,3},{5,2},{10,13},{11,12},{12,11},{13,10},{18,21},{1... | collective-permute-start | bytes 4718600 | tf_op jit(solution)/shard_map/ppermute | solution.py:780
  313.9 27.6 %hidden.3 = (bf16[1024,1024]{1,0:T(8,128)(2,1)}, bf16[1024,2048]{1,0:T(8,128)(2,1)}, bf16[512,1536]{1,0:T(8,128)(2,1)S(1)}, bf16[512,1536]{1,0:T(8,128)(2,1)S(1)...) custom-call(bf16[512,1536]{1,0:T(8,128)(2,1)} %collective-permute-done.18.a_ref.refs_2_, ...), custom_call_target="tpu_custom_call" | custom-call | flops 8000000000 | bytes 1 | tf_op jit(solution)/shard_map/hidden/pallas_call | solution.py:382
  343.8 4.6 collective-permute-start.24
  355.3 2.9 join.3
  359.6 28.9 %wgrad.2 = bf16[1536,3072]{1,0:T(8,128)(2,1)} custom-call(bf16[512,1536]{1,0:T(8,128)(2,1)} %get-tuple-element.186.refs_0_.a_ref, bf16[512,1536]{1,0:T(8,128)(2,1)} %collective-permute-done.16.b_ref.refs_1_, bf16[512,1536]{1,0:T(8,128)(2,1)} %collective-permute-done.18.a_ref.refs_2_, bf16[512,1536]{1,0:T(8,128)(2,1)} %collective-permute-done.19.b_ref.refs_3_, ...), custom_call_target="tpu_custom_call" | custom-call | flops 8000000000 | bytes 1 | tf_op jit(solution)/shard_map/wgrad/pallas_call | solution.py:490
  391.9 5.6 norm_back.2.refs_0_.refs_20_
  408.2 21.1 %attend_back.2 = (bf16[1024,512]{1,0:T(8,128)(2,1)S(1)}, f32[2048,256]{1,0:T(8,128)S(1)}, f32[2048,256]{1,0:T(8,128)S(1)}) custom-call(s32[3]{0:T(128)S(1)} %pad_add_fusion.1.place_ref, bf16[2048,512]{1,0:T(8,128)(2,1)S(1)} %copy-done.5, bf16[2048,256]{1,0:T(8,128)(2,1)S(1)} %copy-done.21, bf16[2048,256]{1,0:T(8,128)(2,1)S(1)} %copy-done.25, ...), custom_call_target="tpu_custom_call" | custom-call | flops 1 | bytes 1 | tf_op jit(solution)/shard_map/attend_back/pallas_call | solution.py:236
  430.6 4.0 collective-permute-done.27.refs_0_.refs_22_
  438.1 3.2 product.19
  442.8 23.4 %attend_back.3 = (bf16[1024,512]{1,0:T(8,128)(2,1)S(1)}, bf16[2048,256]{1,0:T(8,128)(2,1)S(1)}, bf16[2048,256]{1,0:T(8,128)(2,1)S(1)}) custom-call(s32[3]{0:T(128)S(1)} %pad_add_fusion.1.place_ref, bf16[2048,512]{1,0:T(8,128)(2,1)S(1)} %copy-done.6, bf16[2048,256]{1,0:T(8,128)(2,1)S(1)} %copy-done.21, bf16[2048,256]{1,0:T(8,128)(2,1)S(1)} %copy-done.25, ...), custom_call_target="tpu_custom_call" | custom-call | flops 1 | bytes 1 | tf_op jit(solution)/shard_map/attend_back/pallas_call | solution.py:236
  466.3 4.0 collective-permute-done.29.refs_1_
  470.2 5.4 product.20
  478.1 3.4 collective-permute-done.31.refs_4_
  482.7 5.2 product.21.refs_4_.refs_28_
  487.9 4.8 product.23
  493.1 3.4 broadcast_select_fusion.6
  500.6 4.1 product.22.refs_2_
  505.8 21.4 %wgrad.3.refs_6_ = bf16[1536,1152]{1,0:T(8,128)(2,1)} custom-call(bf16[2048,1536]{1,0:T(8,128)(2,1)} %get-tuple-element.247.refs_0_.refs_1_.refs_2_.refs_3_.refs_8_.refs_9_.refs_10_.refs_11_, bf16[2048,1536]{1,0:T(8,128)(2,1)} %get-tuple-element.247.refs_0_.refs_1_.refs_2_.refs_3_.refs_8_.refs_9_.refs_10_.refs_11_, ...), custom_call_target="tpu_custom_call" | custom-call | flops 8000000000 | bytes 1 | tf_op jit(solution)/shard_map/wgrad/pallas_call | solution.py:490
  527.3 19.0 %collective-permute-done.32.refs_4_ = bf16[512,1536]{1,0:T(8,128)(2,1)} collective-permute-done((bf16[512,1536]{1,0:T(8,128)(2,1)}, bf16[512,1536]{1,0:T(8,128)(2,1)}, u32[]{:S(2)}, u32[]{:S(2)}) %collective-permute-start.32) | collective-permute-done | bytes 1572896 | tf_op jit(solution)/shard_map/ppermute | solution.py:761
  546.3 5.6 norm_back.3.refs_0_
  557.8 18.2 %reduce-scatter.5.cloned.1.call-done.refs_0_ = bf16[384,1152]{1,0:T(8,128)(2,1)} async-done(((bf16[1536,1152]{1,0:T(8,128)(2,1)}), bf16[384,1152]{1,0:T(8,128)(2,1)}) %reduce-scatter.5.cloned.1.call-update) | async-done | bytes 884752 | tf_op jit(solution)/shard_map/reduce_scatter | solution.py:676
  579.8 16.1 %collective-permute-start.37 = (f32[2,192]{1,0:T(2,128)S(1)}, f32[2,192]{1,0:T(2,128)S(1)}, u32[]{:S(2)}, u32[]{:S(2)}) collective-permute-start(f32[2,192]{1,0:T(2,128)S(1)} %bitcast.35), channel_id=1, source_target_pairs={{0,4},{4,0},{1,5},{5,1},{2,6},{6,2},{3,7},{7,3},{8,12},{12,8},{9,1... | collective-permute-start | bytes 4616 | tf_op jit(solution)/shard_map/ppermute | solution.py:634
  606.8 2.9 mixed.3
  611.0 9.7 %collective-permute-done.42.slanted_ref = bf16[192,1152]{1,0:T(8,128)(2,1)S(1)} collective-permute-done((bf16[192,1152]{1,0:T(8,128)(2,1)S(1)}, bf16[192,1152]{1,0:T(8,128)(2,1)S(1)}, u32[]{:S(2)}, u32[]{:S(2)}) %collective-permute-start.42) | collective-permute-done | bytes 442400 | tf_op jit(solution)/shard_map/ppermute | solution.py:666
  (271 shorter events, 129.5 us)
Async XLA Ops:
  7.2 98.0 %all-gather.3.cloned.1.call-start = ((), (), s32[]{:S(2)}) async-start(), calls=%async_computation.2 | async-start | bytes 5898240 | tf_op jit(solution)/shard_map/all_gather | solution.py:658
  7.2 35.9 %collective-permute-start.2 = (bf16[512,1536]{1,0:T(8,128)(2,1)}, bf16[512,1536]{1,0:T(8,128)(2,1)S(1)}, u32[]{:S(2)}, u32[]{:S(2)}) collective-permute-start(bf16[512,1536]{1,0:T(8,128)(2,1)} %param.23), channel_id=1, source_target_pairs={{0,1},{1,0},{6,7},{7,6},{8,9},{9,8},{14,15},{15,14},{16,17},{17,16... | collective-permute-start | bytes 4718600 | tf_op jit(solution)/shard_map/ppermute | solution.py:796
  16.6 3.7 collective-permute-start
  17.3 25.8 %collective-permute-start.1 = (bf16[192,1536]{1,0:T(8,128)(2,1)}, bf16[192,1536]{1,0:T(8,128)(2,1)S(1)}, u32[]{:S(2)}, u32[]{:S(2)}) collective-permute-start(bf16[192,1536]{1,0:T(8,128)(2,1)} %pad.81), channel_id=1, source_target_pairs={{0,2},{2,6},{4,0},{6,4},{1,3},{3,7},{5,1},{7,5},{8,10},{10,14},{12... | collective-permute-start | bytes 1769480 | tf_op jit(solution)/shard_map/ppermute | solution.py:646
  18.4 1.8 collective-permute-start.3
  45.8 217.3 %all-gather.5.cloned.1.call-start = ((), (), s32[]{:S(2)}) async-start(), calls=%async_computation.3 | async-start | bytes 11796480 | tf_op jit(solution)/shard_map/all_gather | solution.py:658
  47.1 14.7 %collective-permute-start.4 = (bf16[512,1536]{1,0:T(8,128)(2,1)}, bf16[512,1536]{1,0:T(8,128)(2,1)}, u32[]{:S(2)}, u32[]{:S(2)}) collective-permute-start(bf16[512,1536]{1,0:T(8,128)(2,1)} %param.12), channel_id=1, source_target_pairs={{2,5},{3,4},{4,3},{5,2},{10,13},{11,12},{12,11},{13,10},{18,21},{1... | collective-permute-start | bytes 4718600 | tf_op jit(solution)/shard_map/ppermute | solution.py:780
  49.0 40.3 %collective-permute-start.5 = (bf16[512,1536]{1,0:T(8,128)(2,1)}, bf16[512,1536]{1,0:T(8,128)(2,1)}, u32[]{:S(2)}, u32[]{:S(2)}) collective-permute-start(bf16[512,1536]{1,0:T(8,128)(2,1)} %param.12), channel_id=1, source_target_pairs={{0,1},{1,0},{6,7},{7,6},{8,9},{9,8},{14,15},{15,14},{16,17},{17,16... | collective-permute-start | bytes 4718600 | tf_op jit(solution)/shard_map/ppermute | solution.py:796
  92.0 14.9 %collective-permute-start.9 = (bf16[512,1536]{1,0:T(8,128)(2,1)}, bf16[512,1536]{1,0:T(8,128)(2,1)}, u32[]{:S(2)}, u32[]{:S(2)}) collective-permute-start(bf16[512,1536]{1,0:T(8,128)(2,1)} %broadcast_select_fusion.4.x_ref.refs_0_.refs_1_), channel_id=1, source_target_pairs={{0,4},{4,0},{1,5},{5,1},{2,6},{6,2},{3,7},{7,3},{8,12},{12,8},{9,1... | collective-permute-start | bytes 4718600 | tf_op jit(solution)/shard_map/ppermute | solution.py:634
  92.0 34.4 %collective-permute-start.6 = (bf16[512,1536]{1,0:T(8,128)(2,1)}, bf16[512,1536]{1,0:T(8,128)(2,1)}, u32[]{:S(2)}, u32[]{:S(2)}) collective-permute-start(bf16[512,1536]{1,0:T(8,128)(2,1)} %collective-permute-done.4), channel_id=1, source_target_pairs={{2,3},{3,2},{4,5},{5,4},{10,11},{11,10},{12,13},{13,12},{18,19},{1... | collective-permute-start | bytes 4718600 | tf_op jit(solution)/shard_map/ppermute | solution.py:800
  93.9 23.3 %collective-permute-start.7 = (bf16[192,3072]{1,0:T(8,128)(2,1)S(1)}, bf16[192,3072]{1,0:T(8,128)(2,1)}, u32[]{:S(2)}, u32[]{:S(2)}) collective-permute-start(bf16[192,3072]{1,0:T(8,128)(2,1)S(1)} %pad_maximum_fusion.5), channel_id=1, source_target_pairs={{2,4},{4,2},{3,5},{5,3},{10,12},{12,10},{11,13},{13,11},{18,20},{2... | collective-permute-start | bytes 3538952 | tf_op jit(solution)/shard_map/ppermute | solution.py:630
  95.5 30.8 %collective-permute-start.8 = (bf16[192,3072]{1,0:T(8,128)(2,1)S(1)}, bf16[192,3072]{1,0:T(8,128)(2,1)}, u32[]{:S(2)}, u32[]{:S(2)}) collective-permute-start(bf16[192,3072]{1,0:T(8,128)(2,1)S(1)} %pad_maximum_fusion.5), channel_id=1, source_target_pairs={{0,2},{2,6},{4,0},{6,4},{1,3},{3,7},{5,1},{7,5},{8,10},{10,14},{12... | collective-permute-start | bytes 3538952 | tf_op jit(solution)/shard_map/ppermute | solution.py:646
  130.9 362.3 %reduce-scatter.3.cloned.1.call-start = ((), (), s32[]{:S(2)}) async-start(), calls=%async_computation.4 | async-start | bytes 11796480 | tf_op jit(solution)/shard_map/reduce_scatter | solution.py:676
  132.7 28.9 %collective-permute-start.10 = (bf16[512,1536]{1,0:T(8,128)(2,1)S(1)}, bf16[512,1536]{1,0:T(8,128)(2,1)S(1)}, u32[]{:S(2)}, u32[]{:S(2)}) collective-permute-start(bf16[512,1536]{1,0:T(8,128)(2,1)S(1)} %broadcast_select_fusion.3.x_ref), channel_id=1, source_target_pairs={{0,4},{4,0},{1,5},{5,1},{2,6},{6,2},{3,7},{7,3},{8,12},{12,8},{9,1... | collective-permute-start | bytes 4718600 | tf_op jit(solution)/shard_map/ppermute | solution.py:634
  158.6 31.6 %collective-permute-start.11 = (bf16[512,1536]{1,0:T(8,128)(2,1)S(1)}, bf16[512,1536]{1,0:T(8,128)(2,1)}, u32[]{:S(2)}, u32[]{:S(2)}) collective-permute-start(bf16[512,1536]{1,0:T(8,128)(2,1)S(1)} %copy-done.49), channel_id=1, source_target_pairs={{2,5},{3,4},{4,3},{5,2},{10,13},{11,12},{12,11},{13,10},{18,21},{1... | collective-permute-start | bytes 4718600 | tf_op jit(solution)/shard_map/ppermute | solution.py:780
  190.1 251.2 %copy-start.7 = (bf16[1024,512]{1,0:T(8,128)(2,1)}, bf16[1024,512]{1,0:T(8,128)(2,1)S(1)}, u32[]{:S(2)}) copy-start(bf16[1024,512]{1,0:T(8,128)(2,1)S(1)} %get-tuple-element.174.refs_0_.o_ref.refs_26_.refs_27_) | copy-start | bytes 3145732
  193.2 3.5 collective-permute-start.12
  193.7 37.5 %collective-permute-start.14 = (bf16[512,1536]{1,0:T(8,128)(2,1)}, bf16[512,1536]{1,0:T(8,128)(2,1)}, u32[]{:S(2)}, u32[]{:S(2)}) collective-permute-start(bf16[512,1536]{1,0:T(8,128)(2,1)} %collective-permute-done.11), channel_id=1, source_target_pairs={{2,3},{3,2},{4,5},{5,4},{10,11},{11,10},{12,13},{13,12},{18,19},{1... | collective-permute-start | bytes 4718600 | tf_op jit(solution)/shard_map/ppermute | solution.py:800
  200.3 40.8 %collective-permute-start.13 = (bf16[512,1536]{1,0:T(8,128)(2,1)}, bf16[512,1536]{1,0:T(8,128)(2,1)}, u32[]{:S(2)}, u32[]{:S(2)}) collective-permute-start(bf16[512,1536]{1,0:T(8,128)(2,1)} %product.13.refs_0_), channel_id=1, source_target_pairs={{0,1},{1,0},{2,3},{3,2},{4,5},{5,4},{6,7},{7,6},{8,9},{9,8},{10,11... | collective-permute-start | bytes 4718600 | tf_op jit(solution)/shard_map/ppermute | solution.py:761
  226.7 14.3 %collective-permute-start.15 = (bf16[512,1536]{1,0:T(8,128)(2,1)S(1)}, bf16[512,1536]{1,0:T(8,128)(2,1)}, u32[]{:S(2)}, u32[]{:S(2)}) collective-permute-start(bf16[512,1536]{1,0:T(8,128)(2,1)S(1)} %product.15), channel_id=1, source_target_pairs={{0,4},{4,0},{1,5},{5,1},{2,6},{6,2},{3,7},{7,3},{8,12},{12,8},{9,1... | collective-permute-start | bytes 4718600 | tf_op jit(solution)/shard_map/ppermute | solution.py:634
  245.9 16.5 %collective-permute-start.16 = (bf16[512,1536]{1,0:T(8,128)(2,1)}, bf16[512,1536]{1,0:T(8,128)(2,1)}, u32[]{:S(2)}, u32[]{:S(2)}) collective-permute-start(bf16[512,1536]{1,0:T(8,128)(2,1)} %get-tuple-element.186.refs_0_.a_ref), channel_id=1, source_target_pairs={{0,4},{4,0},{1,5},{5,1},{2,6},{6,2},{3,7},{7,3},{8,12},{12,8},{9,1... | collective-permute-start | bytes 4718600 | tf_op jit(solution)/shard_map/ppermute | solution.py:634
  259.3 3.8 collective-permute-start.17
  259.4 37.1 %collective-permute-start.18 = (bf16[512,1536]{1,0:T(8,128)(2,1)}, bf16[512,1536]{1,0:T(8,128)(2,1)}, u32[]{:S(2)}, u32[]{:S(2)}) collective-permute-start(bf16[512,1536]{1,0:T(8,128)(2,1)} %get-tuple-element.186.refs_0_.a_ref), channel_id=1, source_target_pairs={{0,1},{1,0},{2,3},{3,2},{4,5},{5,4},{6,7},{7,6},{8,9},{9,8},{10,11... | collective-permute-start | bytes 4718600 | tf_op jit(solution)/shard_map/ppermute | solution.py:638
  296.5 3.8 collective-permute-start.22
  297.8 16.1 %collective-permute-start.20 = (bf16[512,1536]{1,0:T(8,128)(2,1)}, bf16[512,1536]{1,0:T(8,128)(2,1)}, u32[]{:S(2)}, u32[]{:S(2)}) collective-permute-start(bf16[512,1536]{1,0:T(8,128)(2,1)} %broadcast_select_fusion.1.dy_ref.refs_10_), channel_id=1, source_target_pairs={{0,4},{4,0},{1,5},{5,1},{2,6},{6,2},{3,7},{7,3},{8,12},{12,8},{9,1... | collective-permute-start | bytes 4718600 | tf_op jit(solution)/shard_map/ppermute | solution.py:634
  299.7 14.2 %collective-permute-start.19 = (bf16[512,1536]{1,0:T(8,128)(2,1)}, bf16[512,1536]{1,0:T(8,128)(2,1)}, u32[]{:S(2)}, u32[]{:S(2)}) collective-permute-start(bf16[512,1536]{1,0:T(8,128)(2,1)} %collective-permute-done.18.a_ref.refs_2_), channel_id=1, source_target_pairs={{0,4},{4,0},{1,5},{5,1},{2,6},{6,2},{3,7},{7,3},{8,12},{12,8},{9,1... | collective-permute-start | bytes 4718600 | tf_op jit(solution)/shard_map/ppermute | solution.py:634
  299.8 14.1 %collective-permute-start.21 = (bf16[512,1536]{1,0:T(8,128)(2,1)}, bf16[512,1536]{1,0:T(8,128)(2,1)}, u32[]{:S(2)}, u32[]{:S(2)}) collective-permute-start(bf16[512,1536]{1,0:T(8,128)(2,1)} %get-tuple-element.200), channel_id=1, source_target_pairs={{0,4},{4,0},{1,5},{5,1},{2,6},{6,2},{3,7},{7,3},{8,12},{12,8},{9,1... | collective-permute-start | bytes 4718600 | tf_op jit(solution)/shard_map/ppermute | solution.py:634
  304.9 38.9 %collective-permute-start.23 = (bf16[512,1536]{1,0:T(8,128)(2,1)}, bf16[512,1536]{1,0:T(8,128)(2,1)S(1)}, u32[]{:S(2)}, u32[]{:S(2)}) collective-permute-start(bf16[512,1536]{1,0:T(8,128)(2,1)} %mixed.2), channel_id=1, source_target_pairs={{2,5},{3,4},{4,3},{5,2},{10,13},{11,12},{12,11},{13,10},{18,21},{1... | collective-permute-start | bytes 4718600 | tf_op jit(solution)/shard_map/ppermute | solution.py:780
  343.8 7.8 %collective-permute-start.24 = (bf16[512,1536]{1,0:T(8,128)(2,1)S(1)}, bf16[512,1536]{1,0:T(8,128)(2,1)}, u32[]{:S(2)}, u32[]{:S(2)}) collective-permute-start(bf16[512,1536]{1,0:T(8,128)(2,1)S(1)} %get-tuple-element.221), channel_id=1, source_target_pairs={{0,4},{4,0},{1,5},{5,1},{2,6},{6,2},{3,7},{7,3},{8,12},{12,8},{9,1... | collective-permute-start | bytes 4718600 | tf_op jit(solution)/shard_map/ppermute | solution.py:634
  348.4 6.9 %collective-permute-start.26 = (bf16[512,1536]{1,0:T(8,128)(2,1)}, bf16[512,1536]{1,0:T(8,128)(2,1)}, u32[]{:S(2)}, u32[]{:S(2)}) collective-permute-start(bf16[512,1536]{1,0:T(8,128)(2,1)} %get-tuple-element.223), channel_id=1, source_target_pairs={{0,4},{4,0},{1,5},{5,1},{2,6},{6,2},{3,7},{7,3},{8,12},{12,8},{9,1... | collective-permute-start | bytes 4718600 | tf_op jit(solution)/shard_map/ppermute | solution.py:634
  354.4 37.0 %collective-permute-start.25 = (bf16[512,1536]{1,0:T(8,128)(2,1)}, bf16[512,1536]{1,0:T(8,128)(2,1)}, u32[]{:S(2)}, u32[]{:S(2)}) collective-permute-start(bf16[512,1536]{1,0:T(8,128)(2,1)} %join.2.refs_16_), channel_id=1, source_target_pairs={{0,1},{1,0},{2,3},{3,2},{4,5},{5,4},{6,7},{7,6},{8,9},{9,8},{10,11... | collective-permute-start | bytes 4718600 | tf_op jit(solution)/shard_map/ppermute | solution.py:761
  391.5 184.5 %reduce-scatter.5.cloned.1.call-start = ((), (), s32[]{:S(2)}) async-start(), calls=%async_computation.5 | async-start | bytes 4423680 | tf_op jit(solution)/shard_map/reduce_scatter | solution.py:676
  397.5 4.9 collective-permute-start.28
  397.5 37.0 %collective-permute-start.27 = (bf16[512,1536]{1,0:T(8,128)(2,1)}, bf16[512,1536]{1,0:T(8,128)(2,1)S(1)}, u32[]{:S(2)}, u32[]{:S(2)}) collective-permute-start(bf16[512,1536]{1,0:T(8,128)(2,1)} %norm_back.2.refs_0_.refs_20_), channel_id=1, source_target_pairs={{0,1},{1,0},{2,3},{3,2},{4,5},{5,4},{6,7},{7,6},{8,9},{9,8},{10,11... | collective-permute-start | bytes 4718600 | tf_op jit(solution)/shard_map/ppermute | solution.py:638
  434.5 3.5 collective-permute-start.30
  434.5 35.7 %collective-permute-start.29 = (bf16[512,1536]{1,0:T(8,128)(2,1)S(1)}, bf16[512,1536]{1,0:T(8,128)(2,1)S(1)}, u32[]{:S(2)}, u32[]{:S(2)}) collective-permute-start(bf16[512,1536]{1,0:T(8,128)(2,1)S(1)} %copy-done.56), channel_id=1, source_target_pairs={{0,1},{1,0},{2,4},{3,5},{4,2},{5,3},{6,7},{7,6},{8,9},{9,8},{10,12... | collective-permute-start | bytes 4718600 | tf_op jit(solution)/shard_map/ppermute | solution.py:955
  475.6 5.8 collective-permute-start.31
  487.9 58.4 %collective-permute-start.32 = (bf16[512,1536]{1,0:T(8,128)(2,1)}, bf16[512,1536]{1,0:T(8,128)(2,1)}, u32[]{:S(2)}, u32[]{:S(2)}) collective-permute-start(bf16[512,1536]{1,0:T(8,128)(2,1)} %product.21.refs_4_.refs_28_), channel_id=1, source_target_pairs={{0,1},{1,0},{2,3},{3,2},{4,5},{5,4},{6,7},{7,6},{8,9},{9,8},{10,11... | collective-permute-start | bytes 4718600 | tf_op jit(solution)/shard_map/ppermute | solution.py:761
  492.7 53.5 %collective-permute-start.33 = (bf16[512,1536]{1,0:T(8,128)(2,1)}, bf16[512,1536]{1,0:T(8,128)(2,1)}, u32[]{:S(2)}, u32[]{:S(2)}) collective-permute-start(bf16[512,1536]{1,0:T(8,128)(2,1)} %product.23), channel_id=1, source_target_pairs={{0,4},{4,0},{1,5},{5,1},{2,6},{6,2},{3,7},{7,3},{8,12},{12,8},{9,1... | collective-permute-start | bytes 4718600 | tf_op jit(solution)/shard_map/ppermute | solution.py:634
  496.5 60.0 %collective-permute-start.34 = (bf16[192,3072]{1,0:T(8,128)(2,1)}, bf16[192,3072]{1,0:T(8,128)(2,1)}, u32[]{:S(2)}, u32[]{:S(2)}) collective-permute-start(bf16[192,3072]{1,0:T(8,128)(2,1)} %get-tuple-element.262.refs_29_), channel_id=1, source_target_pairs={{2,4},{4,2},{3,5},{5,3},{10,12},{12,10},{11,13},{13,11},{18,20},{2... | collective-permute-start | bytes 3538952 | tf_op jit(solution)/shard_map/ppermute | solution.py:630
  498.3 58.2 %collective-permute-start.35 = (bf16[192,3072]{1,0:T(8,128)(2,1)}, bf16[192,3072]{1,0:T(8,128)(2,1)}, u32[]{:S(2)}, u32[]{:S(2)}) collective-permute-start(bf16[192,3072]{1,0:T(8,128)(2,1)} %get-tuple-element.286), channel_id=1, source_target_pairs={{2,0},{6,2},{0,4},{4,6},{3,1},{7,3},{1,5},{5,7},{10,8},{14,10},{8,... | collective-permute-start | bytes 3538952 | tf_op jit(solution)/shard_map/ppermute | solution.py:666
  551.8 24.1 %collective-permute-start.36 = (bf16[512,1536]{1,0:T(8,128)(2,1)}, bf16[512,1536]{1,0:T(8,128)(2,1)}, u32[]{:S(2)}, u32[]{:S(2)}) collective-permute-start(bf16[512,1536]{1,0:T(8,128)(2,1)} %norm_back.3.refs_0_), channel_id=1, source_target_pairs={{2,5},{3,4},{4,3},{5,2},{10,13},{11,12},{12,11},{13,10},{18,21},{1... | collective-permute-start | bytes 4718600 | tf_op jit(solution)/shard_map/ppermute | solution.py:780
  577.2 33.8 %collective-permute-start.41 = (bf16[192,1152]{1,0:T(8,128)(2,1)S(1)}, bf16[192,1152]{1,0:T(8,128)(2,1)S(1)}, u32[]{:S(2)}, u32[]{:S(2)}) collective-permute-start(bf16[192,1152]{1,0:T(8,128)(2,1)S(1)} %get-tuple-element.268.refs_1_.own_ref), channel_id=1, source_target_pairs={{2,4},{4,2},{3,5},{5,3},{10,12},{12,10},{11,13},{13,11},{18,20},{2... | collective-permute-start | bytes 1327112 | tf_op jit(solution)/shard_map/ppermute | solution.py:630
  579.8 21.4 %collective-permute-start.37 = (f32[2,192]{1,0:T(2,128)S(1)}, f32[2,192]{1,0:T(2,128)S(1)}, u32[]{:S(2)}, u32[]{:S(2)}) collective-permute-start(f32[2,192]{1,0:T(2,128)S(1)} %bitcast.35), channel_id=1, source_target_pairs={{0,4},{4,0},{1,5},{5,1},{2,6},{6,2},{3,7},{7,3},{8,12},{12,8},{9,1... | collective-permute-start | bytes 4616 | tf_op jit(solution)/shard_map/ppermute | solution.py:634
  601.9 7.9 %collective-permute-start.40 = (f32[2,192]{1,0:T(2,128)S(1)}, f32[2,192]{1,0:T(2,128)S(1)}, u32[]{:S(2)}, u32[]{:S(2)}) collective-permute-start(f32[2,192]{1,0:T(2,128)S(1)} %fusion.5), channel_id=1, source_target_pairs={{0,3},{1,0},{2,1},{3,2},{4,7},{5,4},{6,5},{7,6},{8,11},{9,8},{10,9... | collective-permute-start | bytes 4616 | tf_op jit(solution)/shard_map/ppermute | solution.py:1028
  604.5 5.3 collective-permute-start.39
  604.5 5.4 collective-permute-start.38
  606.8 13.9 %collective-permute-start.42 = (bf16[192,1152]{1,0:T(8,128)(2,1)S(1)}, bf16[192,1152]{1,0:T(8,128)(2,1)S(1)}, u32[]{:S(2)}, u32[]{:S(2)}) collective-permute-start(bf16[192,1152]{1,0:T(8,128)(2,1)S(1)} %get-tuple-element.292), channel_id=1, source_target_pairs={{2,0},{6,2},{0,4},{4,6},{3,1},{7,3},{1,5},{5,7},{10,8},{14,10},{8,... | collective-permute-start | bytes 1327112 | tf_op jit(solution)/shard_map/ppermute | solution.py:666
  (65 other events, 726.0 us)
Sparse Core Ops, SparseCore 0:
  45.9 59.2 all-gather.2
  131.0 120.5 all-gather.4
  391.6 93.5 reduce-scatter.2
  527.4 48.5 reduce-scatter.4

commit v7 on v6

--- a/solution.py
+++ b/solution.py
@@ -177,13 +177,11 @@
         for h in heads
     ]
 
-    def step(kb, carry, diagonal):
+    def step(kb, carry):
         offset = pl.multiple_of(local_block(kb, place_ref, ring) * block, block)
         keys = k_ref[pl.ds(offset, block), :]
         values = v_ref[pl.ds(offset, block), :]
         shown = row >= start - kb * block
-        if diagonal:
-            shown = shown & (row <= col)
         out = []
         dk = jnp.zeros((block, LANES), f32)
         dv = jnp.zeros((block, LANES), f32)
@@ -199,8 +197,31 @@
         dv_acc[pl.ds(offset, block), :] += dv
         return tuple(out)
 
-    carry = step(g, tuple(jnp.zeros((LANES, block), f32) for _ in range(share)), True)
-    carry = lax.fori_loop(0, g, lambda kb, c: step(kb, c, False), carry)
+    half = block // 2
+    offset = pl.multiple_of(local_block(g, place_ref, ring) * block, block)
+    found = [[] for _ in range(share)]
+    for part in range(2):
+        seen, lanes = (part + 1) * half, slice(part * half, (part + 1) * half)
+        keys = k_ref[pl.ds(offset, seen), :]
+        values = v_ref[pl.ds(offset, seen), :]
+        shown = (row[:seen, :half] >= start[:, lanes] - g * block) & (
+            row[:seen, :half] <= col[:seen, lanes]
+        )
+        dk = jnp.zeros((seen, LANES), f32)
+        dv = jnp.zeros((seen, LANES), f32)
+        for h in range(share):
+            q, do = queries[h][lanes], grads[h][lanes]
+            s = lax.dot_general(keys, q, cols_both, preferred_element_type=f32)
+            p = jnp.where(shown, jnp.exp2(s - lses[h][:, lanes]), 0.0)
+            dp = lax.dot_general(values, do, cols_both, preferred_element_type=f32)
+            ds = (p * (dp - inner[h][:, lanes])).astype(bf16)
+            dv += jnp.dot(p.astype(bf16), do, preferred_element_type=f32)
+            dk += jnp.dot(ds, q, preferred_element_type=f32)
+            found[h].append(lax.dot_general(keys, ds, rows_both, preferred_element_type=f32))
+        dk_acc[pl.ds(offset, seen), :] += dk
+        dv_acc[pl.ds(offset, seen), :] += dv
+    carry = tuple(jnp.concatenate(found[h], 1) for h in range(share))
+    carry = lax.fori_loop(0, g, step, carry)
     for h in range(share):
         u = jnp.transpose(carry[h]) * HEAD_SIZE ** (-0.5)
         turned = u * cosq_ref[...] - pltpu.roll(u, LANES // 2, 1) * sinq_ref[...]
@@ -796,6 +817,14 @@
             lax.ppermute(original, ("c", "zh", "zl"), pairs_of(True, k)) for k in steps if k
         ]
 
+    def first_moves(original):
+        pairs = [(a, b) for a, b in home_pairs(0) if a != b] + pairs_of(True, 1)
+        moved = lax.ppermute(original, ("c", "zh", "zl"), pairs)
+        rest = [
+            lax.ppermute(original, ("c", "zh", "zl"), pairs_of(True, k)) for k in steps[2:]
+        ]
+        return moved, [moved] + rest
+
     def late_neighbours(moved):
         return [lax.ppermute(moved, ("c", "zh", "zl"), pairs_of(False, k)) for k in steps[1:]]
 
@@ -819,9 +848,7 @@
     attn_rows = arrange(*attn_pair)
     attn_full = gather_rows(attn_rows)
     cut = qw * 3 // 4 % LANES == 0
-    attn_kept = cut_rows(attn_rows) if cut else attn_rows
-    stream_raw = cross_tokens(tokens)
-    tokens_early = early_neighbours(tokens)
+    stream_raw, tokens_early = first_moves(tokens)
 
     blocks = [global_block(l, place, ring) for l in range(2 * ring)]
     ordered = [lax.dynamic_index_in_dim(places, g, 0, keepdims=False) for g in blocks]
@@ -837,9 +864,10 @@
     sin = jnp.concatenate([-sin_half, gap, sin_half, gap], 1)
 
     ff_cols = jnp.concatenate([w_gate, w_up, w_down], 1)
-    cos, sin, start, stream_raw, tokens_early, ff_cols, attn_kept = together(
-        cos, sin, start, stream_raw, tokens_early, ff_cols, attn_kept
-    )
+    cos, sin, start, stream_raw, tokens_early, ff_cols, attn_rows = together(
+        cos, sin, start, stream_raw, tokens_early, ff_cols, attn_rows
+    )
+    attn_kept = cut_rows(attn_rows) if cut else attn_rows
     stream_own = jnp.where(stays(), tokens, stream_raw)
     tokens_late = late_neighbours(stream_raw)
     ff_pair = spread_pair(ff_cols)
@@ -852,8 +880,8 @@
     projected = project(
         (stream_own, other_core(stream_own)), gain_first, attn_full, cos, sin, qw, kw, 0, ()
     )
-    tokens_late, ff_pair, projected, cot_sent = together(
-        tokens_late, ff_pair, projected, cotangent
+    tokens_late, ff_pair, projected, cot_sent, attn_kept = together(
+        tokens_late, ff_pair, projected, cotangent, attn_kept
     )
     others = [(x, other_core(x)) for x in choose(tokens_early, tokens_late)]
     ff_rows = arrange(*ff_pair)

time: 641 us -> 636 us (level)
    ppermute x0 -> x1, waiting for transfers between devices: none -> 30.5 us  [first_moves(): moved = lax.ppermute(original, ('c', 'zh', 'zl'), pairs)]
    ppermute x2 -> x1, waiting for transfers between devices: 27.4 us -> 0.01 us  [early_neighbours(): lax.ppermute(original, ('c', 'zh', 'zl'), pairs_of(True, k))]
    ppermute x4 -> x3, starting transfers between devices: 15 us -> 13.2 us  [cross_tokens(): return lax.ppermute(a, ('c', 'zh', 'zl'), pairs)]
  transfers between devices with their start and end apart: 47 -> 46, of which waited for: 19 -> 18; matrix products, arithmetic and copies ran while one was open for 6% -> 6% of each run, Pallas kernels for 44% -> 44%
where the time goes in v7:
time: 636 us; the launch traced here: 628 us
  Pallas kernels  276 us (43%)
  waiting for transfers between devices  150 us (24%)
  starting transfers between devices  116 us (18%)
  other arithmetic  36.2 us (6%)
  local copies, waits for them, and re-layouts  35.2 us (6%)
  between operations  14.9 us (2%)
    ppermute x18, starting transfers between devices, other_core(): return lax.ppermute(a, 'c', swap_two)  65.1 us
    pallas_call x2, Pallas kernels, hidden_pass(): pl.pallas_call(functools.partial(hidden_kernel, min(256, units), count),...  55.3 us
    pallas_call x2, Pallas kernels, wgrad(): pl.pallas_call(functools.partial(wgrad_kernel, counts, cut), grid=(column...  50.3 us
    pallas_call x12, Pallas kernels, product(): pl.pallas_call(functools.partial(product_kernel, dims, len(parts), len(af...  42.9 us
    pallas_call x2, Pallas kernels, attend_back(): pl.pallas_call(functools.partial(attend_back_kernel, ring, block, chip, f...  42.4 us
    ppermute x3, waiting for transfers between devices, send_chips(): lax.ppermute(p.astype(bf16), 'zl', [(i, (i + k) % ring) for i in steps])  31.2 us
    ppermute x1, waiting for transfers between devices, first_moves(): moved = lax.ppermute(original, ('c', 'zh', 'zl'), pairs)  30.5 us
    ppermute x2, waiting for transfers between devices, spread_pair(): return (w, cross(w), lax.ppermute(w, ('c', 'zh'), slant_pairs))  28.8 us
  transfers between devices with their start and end apart: 46, of which 18 were waited for; matrix products, arithmetic and copies ran while one was open for 6% of the time, Pallas kernels for 44%

profile of v7, /device:TPU:0, one launch (start us, length us, event | category | flops | bytes accessed | tf_op | source)
XLA Modules:
  0.0 628.2 jit_solution(8924930525485112887)
XLA Ops:
  7.2 4.9 collective-permute-start.2
  20.2 22.8 %collective-permute-done.1 = bf16[192,1536]{1,0:T(8,128)(2,1)S(1)} collective-permute-done((bf16[192,1536]{1,0:T(8,128)(2,1)}, bf16[192,1536]{1,0:T(8,128)(2,1)S(1)}, u32[]{:S(2)}, u32[]{:S(2)}) %collective-permute-start.1) | collective-permute-done | bytes 589856 | tf_op jit(solution)/shard_map/ppermute | solution.py:667
  47.2 3.0 collective-permute-start.4
  50.2 3.7 fusion.3
  55.2 30.5 %collective-permute-done.4 = bf16[512,1536]{1,0:T(8,128)(2,1)} collective-permute-done((bf16[512,1536]{1,0:T(8,128)(2,1)}, bf16[512,1536]{1,0:T(8,128)(2,1)}, u32[]{:S(2)}, u32[]{:S(2)}) %collective-permute-start.4) | collective-permute-done | bytes 1572896 | tf_op jit(solution)/shard_map/ppermute | solution.py:822
  92.1 4.6 collective-permute-start.7
  99.5 5.6 all-gather.3.cloned.1.call-done.w_ref.refs_1_.refs_3_
  106.9 7.6 %project.2 = (bf16[2048,1536]{1,0:T(8,128)(2,1)S(1)}, bf16[2048,512]{1,0:T(8,128)(2,1)S(1)}, bf16[2048,256]{1,0:T(8,128)(2,1)S(1)}, bf16[2048,256]{1,0:T(8,128)(2,1)S(1)}) custom-call(bf16[512,1536]{1,0:T(8,128)(2,1)} %broadcast_select_fusion.4.x_ref.refs_0_.refs_1_, bf16[512,1536]{1,0:T(8,128)(2,1)} %collective-permute-done.8.y_ref, ...), custom_call_target="tpu_custom_call" | custom-call | flops 1 | bytes 1 | tf_op jit(solution)/shard_map/project/pallas_call | solution.py:339
  117.2 6.0 collective-permute-done.7
  129.5 25.9 %collective-permute-start.9 = (bf16[512,1536]{1,0:T(8,128)(2,1)S(1)}, bf16[512,1536]{1,0:T(8,128)(2,1)S(1)}, u32[]{:S(2)}, u32[]{:S(2)}) collective-permute-start(bf16[512,1536]{1,0:T(8,128)(2,1)S(1)} %broadcast_select_fusion.3.x_ref), channel_id=1, source_target_pairs={{0,4},{4,0},{1,5},{5,1},{2,6},{6,2},{3,7},{7,3},{8,12},{12,8},{9,1... | collective-permute-start | bytes 4718600 | tf_op jit(solution)/shard_map/ppermute | solution.py:655
  159.7 9.7 %project.3 = (bf16[2048,1536]{1,0:T(8,128)(2,1)}, bf16[2048,512]{1,0:T(8,128)(2,1)}, bf16[2048,256]{1,0:T(8,128)(2,1)}, bf16[2048,256]{1,0:T(8,128)(2,1)}) custom-call(bf16[512,1536]{1,0:T(8,128)(2,1)} %copy-done.54, bf16[512,1536]{1,0:T(8,128)(2,1)} %copy-done.65, ...), custom_call_target="tpu_custom_call", output_to_operand_aliasing={{0}: (6, {}), {1}: (7, {}), {2}: (8, {}), {3}: (9, {})} | custom-call | flops 8000000000 | bytes 1 | tf_op jit(solution)/shard_map/project/pallas_call | solution.py:339
  173.5 13.7 %attend.2 = (bf16[1024,512]{1,0:T(8,128)(2,1)S(1)}, f32[2,2,1024]{2,1,0:T(2,128)S(1)}) custom-call(s32[3]{0:T(128)S(1)} %pad_add_fusion.1.place_ref, bf16[2048,512]{1,0:T(8,128)(2,1)S(1)} %copy-done.4, bf16[2048,256]{1,0:T(8,128)(2,1)S(1)} %copy-done.19, bf16[2048,256]{1,0:T(8,128)(2,1)S(1)} %copy-done.23, s32[1,2048]{1,0:T(1,128)S(1)} %bitcast.21), custom_call_target="tpu_custom_call" | custom-call | flops 1 | bytes 1 | tf_op jit(solution)/shard_map/attend/pallas_call | solution.py:103
  187.2 3.1 product.12
  194.6 3.6 product.13.refs_0_
  198.2 5.0 collective-permute-start.12
  207.8 13.6 %attend.3 = (bf16[1024,512]{1,0:T(8,128)(2,1)S(1)}, f32[2,2,1024]{2,1,0:T(2,128)S(1)}) custom-call(s32[3]{0:T(128)S(1)} %pad_add_fusion.1.place_ref, bf16[2048,512]{1,0:T(8,128)(2,1)S(1)} %copy-done.5, bf16[2048,256]{1,0:T(8,128)(2,1)S(1)} %copy-done.20, bf16[2048,256]{1,0:T(8,128)(2,1)S(1)} %copy-done.24, s32[1,2048]{1,0:T(1,128)S(1)} %bitcast.22), custom_call_target="tpu_custom_call" | custom-call | flops 1 | bytes 1 | tf_op jit(solution)/shard_map/attend/pallas_call | solution.py:103
  221.4 3.0 product.15
  228.9 9.8 %collective-permute-done.12.refs_3_ = bf16[512,1536]{1,0:T(8,128)(2,1)} collective-permute-done((bf16[512,1536]{1,0:T(8,128)(2,1)}, bf16[512,1536]{1,0:T(8,128)(2,1)}, u32[]{:S(2)}, u32[]{:S(2)}) %collective-permute-start.12) | collective-permute-done | bytes 1572896 | tf_op jit(solution)/shard_map/ppermute | solution.py:782
  238.8 4.8 norm_forward.1
  243.6 10.8 %collective-permute-start.15 = (bf16[512,1536]{1,0:T(8,128)(2,1)}, bf16[512,1536]{1,0:T(8,128)(2,1)}, u32[]{:S(2)}, u32[]{:S(2)}) collective-permute-start(bf16[512,1536]{1,0:T(8,128)(2,1)} %get-tuple-element.188.refs_0_.a_ref), channel_id=1, source_target_pairs={{0,4},{4,0},{1,5},{5,1},{2,6},{6,2},{3,7},{7,3},{8,12},{12,8},{9,1... | collective-permute-start | bytes 4718600 | tf_op jit(solution)/shard_map/ppermute | solution.py:655
  260.9 27.7 %hidden.2 = (bf16[1024,1024]{1,0:T(8,128)(2,1)}, bf16[1024,2048]{1,0:T(8,128)(2,1)}, bf16[512,1536]{1,0:T(8,128)(2,1)S(1)}, bf16[512,1536]{1,0:T(8,128)(2,1)}, b...) custom-call(bf16[512,1536]{1,0:T(8,128)(2,1)} %get-tuple-element.188.refs_0_.a_ref, ...), custom_call_target="tpu_custom_call" | custom-call | flops 8000000000 | bytes 1 | tf_op jit(solution)/shard_map/hidden/pallas_call | solution.py:403
  288.6 5.7 collective-permute-done.17.a_ref.refs_2_
  299.2 3.5 mixed.2
  302.7 9.0 %collective-permute-start.22 = (bf16[512,1536]{1,0:T(8,128)(2,1)}, bf16[512,1536]{1,0:T(8,128)(2,1)S(1)}, u32[]{:S(2)}, u32[]{:S(2)}) collective-permute-start(bf16[512,1536]{1,0:T(8,128)(2,1)} %mixed.2), channel_id=1, source_target_pairs={{2,5},{3,4},{4,3},{5,2},{10,13},{11,12},{12,11},{13,10},{18,21},{1... | collective-permute-start | bytes 4718600 | tf_op jit(solution)/shard_map/ppermute | solution.py:801
  311.7 27.6 %hidden.3 = (bf16[1024,1024]{1,0:T(8,128)(2,1)}, bf16[1024,2048]{1,0:T(8,128)(2,1)}, bf16[512,1536]{1,0:T(8,128)(2,1)S(1)}, bf16[512,1536]{1,0:T(8,128)(2,1)S(1)...) custom-call(bf16[512,1536]{1,0:T(8,128)(2,1)} %collective-permute-done.17.a_ref.refs_2_, ...), custom_call_target="tpu_custom_call" | custom-call | flops 8000000000 | bytes 1 | tf_op jit(solution)/shard_map/hidden/pallas_call | solution.py:403
  341.6 3.6 collective-permute-start.23
  348.4 2.9 join.2.refs_16_
  352.1 2.9 join.3
  356.5 29.0 %wgrad.2 = bf16[1536,3072]{1,0:T(8,128)(2,1)} custom-call(bf16[512,1536]{1,0:T(8,128)(2,1)} %get-tuple-element.188.refs_0_.a_ref, bf16[512,1536]{1,0:T(8,128)(2,1)} %collective-permute-done.15.b_ref.refs_1_, bf16[512,1536]{1,0:T(8,128)(2,1)} %collective-permute-done.17.a_ref.refs_2_, bf16[512,1536]{1,0:T(8,128)(2,1)} %collective-permute-done.18.b_ref.refs_3_, ...), custom_call_target="tpu_custom_call" | custom-call | flops 8000000000 | bytes 1 | tf_op jit(solution)/shard_map/wgrad/pallas_call | solution.py:511
  388.7 5.6 norm_back.2.refs_0_.refs_20_
  405.0 20.0 %attend_back.2 = (bf16[1024,512]{1,0:T(8,128)(2,1)S(1)}, f32[2048,256]{1,0:T(8,128)S(1)}, f32[2048,256]{1,0:T(8,128)S(1)}) custom-call(s32[3]{0:T(128)S(1)} %pad_add_fusion.1.place_ref, bf16[2048,512]{1,0:T(8,128)(2,1)S(1)} %copy-done.5, bf16[2048,256]{1,0:T(8,128)(2,1)S(1)} %copy-done.21, bf16[2048,256]{1,0:T(8,128)(2,1)S(1)} %copy-done.25, ...), custom_call_target="tpu_custom_call" | custom-call | flops 1 | bytes 1 | tf_op jit(solution)/shard_map/attend_back/pallas_call | solution.py:257
  426.3 5.0 collective-permute-done.26.refs_0_.refs_22_
  434.9 3.2 product.19
  439.8 22.3 %attend_back.3 = (bf16[1024,512]{1,0:T(8,128)(2,1)S(1)}, bf16[2048,256]{1,0:T(8,128)(2,1)S(1)}, bf16[2048,256]{1,0:T(8,128)(2,1)S(1)}) custom-call(s32[3]{0:T(128)S(1)} %pad_add_fusion.1.place_ref, bf16[2048,512]{1,0:T(8,128)(2,1)S(1)} %copy-done.6, bf16[2048,256]{1,0:T(8,128)(2,1)S(1)} %copy-done.21, bf16[2048,256]{1,0:T(8,128)(2,1)S(1)} %copy-done.25, ...), custom_call_target="tpu_custom_call" | custom-call | flops 1 | bytes 1 | tf_op jit(solution)/shard_map/attend_back/pallas_call | solution.py:257
  462.1 5.1 collective-permute-done.28.refs_1_
  467.2 5.4 product.20
  474.9 3.4 collective-permute-done.30.refs_4_
  479.6 5.3 product.21.refs_4_.refs_28_
  484.9 4.8 product.23
  490.1 3.4 broadcast_select_fusion.6
  498.2 3.9 product.22.refs_2_
  503.3 21.3 %wgrad.3.refs_6_ = bf16[1536,1152]{1,0:T(8,128)(2,1)} custom-call(bf16[2048,1536]{1,0:T(8,128)(2,1)} %get-tuple-element.249.refs_0_.refs_1_.refs_2_.refs_3_.refs_8_.refs_9_.refs_10_.refs_11_, bf16[2048,1536]{1,0:T(8,128)(2,1)} %get-tuple-element.249.refs_0_.refs_1_.refs_2_.refs_3_.refs_8_.refs_9_.refs_10_.refs_11_, ...), custom_call_target="tpu_custom_call" | custom-call | flops 8000000000 | bytes 1 | tf_op jit(solution)/shard_map/wgrad/pallas_call | solution.py:511
  524.7 18.5 %collective-permute-done.31.refs_4_ = bf16[512,1536]{1,0:T(8,128)(2,1)} collective-permute-done((bf16[512,1536]{1,0:T(8,128)(2,1)}, bf16[512,1536]{1,0:T(8,128)(2,1)}, u32[]{:S(2)}, u32[]{:S(2)}) %collective-permute-start.31) | collective-permute-done | bytes 1572896 | tf_op jit(solution)/shard_map/ppermute | solution.py:782
  543.2 5.6 norm_back.3.refs_0_
  554.8 18.0 %reduce-scatter.5.cloned.1.call-done.refs_0_ = bf16[384,1152]{1,0:T(8,128)(2,1)} async-done(((bf16[1536,1152]{1,0:T(8,128)(2,1)}), bf16[384,1152]{1,0:T(8,128)(2,1)}) %reduce-scatter.5.cloned.1.call-update) | async-done | bytes 884752 | tf_op jit(solution)/shard_map/reduce_scatter | solution.py:697
  576.7 16.9 %collective-permute-start.36 = (f32[2,192]{1,0:T(2,128)S(1)}, f32[2,192]{1,0:T(2,128)S(1)}, u32[]{:S(2)}, u32[]{:S(2)}) collective-permute-start(f32[2,192]{1,0:T(2,128)S(1)} %bitcast.35), channel_id=1, source_target_pairs={{0,4},{4,0},{1,5},{5,1},{2,6},{6,2},{3,7},{7,3},{8,12},{12,8},{9,1... | collective-permute-start | bytes 4616 | tf_op jit(solution)/shard_map/ppermute | solution.py:655
  604.4 2.9 mixed.3
  608.6 9.8 %collective-permute-done.41.slanted_ref = bf16[192,1152]{1,0:T(8,128)(2,1)S(1)} collective-permute-done((bf16[192,1152]{1,0:T(8,128)(2,1)S(1)}, bf16[192,1152]{1,0:T(8,128)(2,1)S(1)}, u32[]{:S(2)}, u32[]{:S(2)}) %collective-permute-start.41) | collective-permute-done | bytes 442400 | tf_op jit(solution)/shard_map/ppermute | solution.py:687
  (269 shorter events, 129.0 us)
Async XLA Ops:
  7.2 98.0 %all-gather.3.cloned.1.call-start = ((), (), s32[]{:S(2)}) async-start(), calls=%async_computation.2 | async-start | bytes 5898240 | tf_op jit(solution)/shard_map/all_gather | solution.py:679
  7.2 35.9 %collective-permute-start.2 = (bf16[512,1536]{1,0:T(8,128)(2,1)}, bf16[512,1536]{1,0:T(8,128)(2,1)S(1)}, u32[]{:S(2)}, u32[]{:S(2)}) collective-permute-start(bf16[512,1536]{1,0:T(8,128)(2,1)} %param.23), channel_id=1, source_target_pairs={{0,1},{1,0},{6,7},{7,6},{8,9},{9,8},{14,15},{15,14},{16,17},{17,16... | collective-permute-start | bytes 4718600 | tf_op jit(solution)/shard_map/ppermute | solution.py:817
  16.6 3.7 collective-permute-start
  17.3 25.8 %collective-permute-start.1 = (bf16[192,1536]{1,0:T(8,128)(2,1)}, bf16[192,1536]{1,0:T(8,128)(2,1)S(1)}, u32[]{:S(2)}, u32[]{:S(2)}) collective-permute-start(bf16[192,1536]{1,0:T(8,128)(2,1)} %pad.81), channel_id=1, source_target_pairs={{0,2},{2,6},{4,0},{6,4},{1,3},{3,7},{5,1},{7,5},{8,10},{10,14},{12... | collective-permute-start | bytes 1769480 | tf_op jit(solution)/shard_map/ppermute | solution.py:667
  18.4 1.8 collective-permute-start.3
  45.8 215.2 %all-gather.5.cloned.1.call-start = ((), (), s32[]{:S(2)}) async-start(), calls=%async_computation.3 | async-start | bytes 11796480 | tf_op jit(solution)/shard_map/all_gather | solution.py:679
  47.2 38.6 %collective-permute-start.4 = (bf16[512,1536]{1,0:T(8,128)(2,1)}, bf16[512,1536]{1,0:T(8,128)(2,1)}, u32[]{:S(2)}, u32[]{:S(2)}) collective-permute-start(bf16[512,1536]{1,0:T(8,128)(2,1)} %param.12), channel_id=1, source_target_pairs={{2,5},{3,4},{4,3},{5,2},{0,1},{1,0},{6,7},{7,6},{10,13},{11,12},{1... | collective-permute-start | bytes 4718600 | tf_op jit(solution)/shard_map/ppermute | solution.py:822
  55.2 103.3 %copy-start.10 = (f32[2048,128]{1,0:T(8,128)}, f32[2048,128]{1,0:T(8,128)S(1)}, u32[]{:S(2)}) copy-start(f32[2048,128]{1,0:T(8,128)S(1)} %get-tuple-element.155.sin_ref.sinq_ref.refs_1_) | copy-start | bytes 3145732
  88.4 18.5 %collective-permute-start.8 = (bf16[512,1536]{1,0:T(8,128)(2,1)}, bf16[512,1536]{1,0:T(8,128)(2,1)}, u32[]{:S(2)}, u32[]{:S(2)}) collective-permute-start(bf16[512,1536]{1,0:T(8,128)(2,1)} %broadcast_select_fusion.4.x_ref.refs_0_.refs_1_), channel_id=1, source_target_pairs={{0,4},{4,0},{1,5},{5,1},{2,6},{6,2},{3,7},{7,3},{8,12},{12,8},{9,1... | collective-permute-start | bytes 4718600 | tf_op jit(solution)/shard_map/ppermute | solution.py:655
  88.5 34.7 %collective-permute-start.5 = (bf16[512,1536]{1,0:T(8,128)(2,1)}, bf16[512,1536]{1,0:T(8,128)(2,1)}, u32[]{:S(2)}, u32[]{:S(2)}) collective-permute-start(bf16[512,1536]{1,0:T(8,128)(2,1)} %collective-permute-done.4), channel_id=1, source_target_pairs={{2,3},{3,2},{4,5},{5,4},{10,11},{11,10},{12,13},{13,12},{18,19},{1... | collective-permute-start | bytes 4718600 | tf_op jit(solution)/shard_map/ppermute | solution.py:829
  90.4 26.9 %collective-permute-start.6 = (bf16[192,3072]{1,0:T(8,128)(2,1)S(1)}, bf16[192,3072]{1,0:T(8,128)(2,1)}, u32[]{:S(2)}, u32[]{:S(2)}) collective-permute-start(bf16[192,3072]{1,0:T(8,128)(2,1)S(1)} %pad_maximum_fusion.5), channel_id=1, source_target_pairs={{2,4},{4,2},{3,5},{5,3},{10,12},{12,10},{11,13},{13,11},{18,20},{2... | collective-permute-start | bytes 3538952 | tf_op jit(solution)/shard_map/ppermute | solution.py:651
  92.1 31.1 %collective-permute-start.7 = (bf16[192,3072]{1,0:T(8,128)(2,1)S(1)}, bf16[192,3072]{1,0:T(8,128)(2,1)}, u32[]{:S(2)}, u32[]{:S(2)}) collective-permute-start(bf16[192,3072]{1,0:T(8,128)(2,1)S(1)} %pad_maximum_fusion.5), channel_id=1, source_target_pairs={{0,2},{2,6},{4,0},{6,4},{1,3},{3,7},{5,1},{7,5},{8,10},{10,14},{12... | collective-permute-start | bytes 3538952 | tf_op jit(solution)/shard_map/ppermute | solution.py:667
  127.7 362.5 %reduce-scatter.3.cloned.1.call-start = ((), (), s32[]{:S(2)}) async-start(), calls=%async_computation.4 | async-start | bytes 11796480 | tf_op jit(solution)/shard_map/reduce_scatter | solution.py:697
  129.5 29.0 %collective-permute-start.9 = (bf16[512,1536]{1,0:T(8,128)(2,1)S(1)}, bf16[512,1536]{1,0:T(8,128)(2,1)S(1)}, u32[]{:S(2)}, u32[]{:S(2)}) collective-permute-start(bf16[512,1536]{1,0:T(8,128)(2,1)S(1)} %broadcast_select_fusion.3.x_ref), channel_id=1, source_target_pairs={{0,4},{4,0},{1,5},{5,1},{2,6},{6,2},{3,7},{7,3},{8,12},{12,8},{9,1... | collective-permute-start | bytes 4718600 | tf_op jit(solution)/shard_map/ppermute | solution.py:655
  155.4 31.8 %collective-permute-start.10 = (bf16[512,1536]{1,0:T(8,128)(2,1)S(1)}, bf16[512,1536]{1,0:T(8,128)(2,1)}, u32[]{:S(2)}, u32[]{:S(2)}) collective-permute-start(bf16[512,1536]{1,0:T(8,128)(2,1)S(1)} %copy-done.49), channel_id=1, source_target_pairs={{2,5},{3,4},{4,3},{5,2},{10,13},{11,12},{12,11},{13,10},{18,21},{1... | collective-permute-start | bytes 4718600 | tf_op jit(solution)/shard_map/ppermute | solution.py:801
  187.2 251.0 %copy-start.7 = (bf16[1024,512]{1,0:T(8,128)(2,1)}, bf16[1024,512]{1,0:T(8,128)(2,1)S(1)}, u32[]{:S(2)}) copy-start(bf16[1024,512]{1,0:T(8,128)(2,1)S(1)} %get-tuple-element.176.refs_0_.o_ref.refs_26_.refs_27_) | copy-start | bytes 3145732
  190.3 4.3 collective-permute-start.11
  191.5 37.4 %collective-permute-start.13 = (bf16[512,1536]{1,0:T(8,128)(2,1)}, bf16[512,1536]{1,0:T(8,128)(2,1)}, u32[]{:S(2)}, u32[]{:S(2)}) collective-permute-start(bf16[512,1536]{1,0:T(8,128)(2,1)} %collective-permute-done.10), channel_id=1, source_target_pairs={{2,3},{3,2},{4,5},{5,4},{10,11},{11,10},{12,13},{13,12},{18,19},{1... | collective-permute-start | bytes 4718600 | tf_op jit(solution)/shard_map/ppermute | solution.py:829
  198.2 40.6 %collective-permute-start.12 = (bf16[512,1536]{1,0:T(8,128)(2,1)}, bf16[512,1536]{1,0:T(8,128)(2,1)}, u32[]{:S(2)}, u32[]{:S(2)}) collective-permute-start(bf16[512,1536]{1,0:T(8,128)(2,1)} %product.13.refs_0_), channel_id=1, source_target_pairs={{0,1},{1,0},{2,3},{3,2},{4,5},{5,4},{6,7},{7,6},{8,9},{9,8},{10,11... | collective-permute-start | bytes 4718600 | tf_op jit(solution)/shard_map/ppermute | solution.py:782
  224.4 14.3 %collective-permute-start.14 = (bf16[512,1536]{1,0:T(8,128)(2,1)S(1)}, bf16[512,1536]{1,0:T(8,128)(2,1)}, u32[]{:S(2)}, u32[]{:S(2)}) collective-permute-start(bf16[512,1536]{1,0:T(8,128)(2,1)S(1)} %product.15), channel_id=1, source_target_pairs={{0,4},{4,0},{1,5},{5,1},{2,6},{6,2},{3,7},{7,3},{8,12},{12,8},{9,1... | collective-permute-start | bytes 4718600 | tf_op jit(solution)/shard_map/ppermute | solution.py:655
  243.6 16.5 %collective-permute-start.15 = (bf16[512,1536]{1,0:T(8,128)(2,1)}, bf16[512,1536]{1,0:T(8,128)(2,1)}, u32[]{:S(2)}, u32[]{:S(2)}) collective-permute-start(bf16[512,1536]{1,0:T(8,128)(2,1)} %get-tuple-element.188.refs_0_.a_ref), channel_id=1, source_target_pairs={{0,4},{4,0},{1,5},{5,1},{2,6},{6,2},{3,7},{7,3},{8,12},{12,8},{9,1... | collective-permute-start | bytes 4718600 | tf_op jit(solution)/shard_map/ppermute | solution.py:655
  257.2 3.8 collective-permute-start.16
  257.2 37.1 %collective-permute-start.17 = (bf16[512,1536]{1,0:T(8,128)(2,1)}, bf16[512,1536]{1,0:T(8,128)(2,1)}, u32[]{:S(2)}, u32[]{:S(2)}) collective-permute-start(bf16[512,1536]{1,0:T(8,128)(2,1)} %get-tuple-element.188.refs_0_.a_ref), channel_id=1, source_target_pairs={{0,1},{1,0},{2,3},{3,2},{4,5},{5,4},{6,7},{7,6},{8,9},{9,8},{10,11... | collective-permute-start | bytes 4718600 | tf_op jit(solution)/shard_map/ppermute | solution.py:659
  294.3 3.8 collective-permute-start.21
  295.6 16.1 %collective-permute-start.19 = (bf16[512,1536]{1,0:T(8,128)(2,1)}, bf16[512,1536]{1,0:T(8,128)(2,1)}, u32[]{:S(2)}, u32[]{:S(2)}) collective-permute-start(bf16[512,1536]{1,0:T(8,128)(2,1)} %broadcast_select_fusion.1.dy_ref.refs_10_), channel_id=1, source_target_pairs={{0,4},{4,0},{1,5},{5,1},{2,6},{6,2},{3,7},{7,3},{8,12},{12,8},{9,1... | collective-permute-start | bytes 4718600 | tf_op jit(solution)/shard_map/ppermute | solution.py:655
  297.6 14.2 %collective-permute-start.18 = (bf16[512,1536]{1,0:T(8,128)(2,1)}, bf16[512,1536]{1,0:T(8,128)(2,1)}, u32[]{:S(2)}, u32[]{:S(2)}) collective-permute-start(bf16[512,1536]{1,0:T(8,128)(2,1)} %collective-permute-done.17.a_ref.refs_2_), channel_id=1, source_target_pairs={{0,4},{4,0},{1,5},{5,1},{2,6},{6,2},{3,7},{7,3},{8,12},{12,8},{9,1... | collective-permute-start | bytes 4718600 | tf_op jit(solution)/shard_map/ppermute | solution.py:655
  297.6 14.1 %collective-permute-start.20 = (bf16[512,1536]{1,0:T(8,128)(2,1)}, bf16[512,1536]{1,0:T(8,128)(2,1)}, u32[]{:S(2)}, u32[]{:S(2)}) collective-permute-start(bf16[512,1536]{1,0:T(8,128)(2,1)} %get-tuple-element.202), channel_id=1, source_target_pairs={{0,4},{4,0},{1,5},{5,1},{2,6},{6,2},{3,7},{7,3},{8,12},{12,8},{9,1... | collective-permute-start | bytes 4718600 | tf_op jit(solution)/shard_map/ppermute | solution.py:655
  302.7 38.9 %collective-permute-start.22 = (bf16[512,1536]{1,0:T(8,128)(2,1)}, bf16[512,1536]{1,0:T(8,128)(2,1)S(1)}, u32[]{:S(2)}, u32[]{:S(2)}) collective-permute-start(bf16[512,1536]{1,0:T(8,128)(2,1)} %mixed.2), channel_id=1, source_target_pairs={{2,5},{3,4},{4,3},{5,2},{10,13},{11,12},{12,11},{13,10},{18,21},{1... | collective-permute-start | bytes 4718600 | tf_op jit(solution)/shard_map/ppermute | solution.py:801
  341.6 6.8 %collective-permute-start.23 = (bf16[512,1536]{1,0:T(8,128)(2,1)S(1)}, bf16[512,1536]{1,0:T(8,128)(2,1)}, u32[]{:S(2)}, u32[]{:S(2)}) collective-permute-start(bf16[512,1536]{1,0:T(8,128)(2,1)S(1)} %get-tuple-element.223), channel_id=1, source_target_pairs={{0,4},{4,0},{1,5},{5,1},{2,6},{6,2},{3,7},{7,3},{8,12},{12,8},{9,1... | collective-permute-start | bytes 4718600 | tf_op jit(solution)/shard_map/ppermute | solution.py:655
  345.2 6.9 %collective-permute-start.25 = (bf16[512,1536]{1,0:T(8,128)(2,1)}, bf16[512,1536]{1,0:T(8,128)(2,1)}, u32[]{:S(2)}, u32[]{:S(2)}) collective-permute-start(bf16[512,1536]{1,0:T(8,128)(2,1)} %get-tuple-element.225), channel_id=1, source_target_pairs={{0,4},{4,0},{1,5},{5,1},{2,6},{6,2},{3,7},{7,3},{8,12},{12,8},{9,1... | collective-permute-start | bytes 4718600 | tf_op jit(solution)/shard_map/ppermute | solution.py:655
  351.3 37.0 %collective-permute-start.24 = (bf16[512,1536]{1,0:T(8,128)(2,1)}, bf16[512,1536]{1,0:T(8,128)(2,1)}, u32[]{:S(2)}, u32[]{:S(2)}) collective-permute-start(bf16[512,1536]{1,0:T(8,128)(2,1)} %join.2.refs_16_), channel_id=1, source_target_pairs={{0,1},{1,0},{2,3},{3,2},{4,5},{5,4},{6,7},{7,6},{8,9},{9,8},{10,11... | collective-permute-start | bytes 4718600 | tf_op jit(solution)/shard_map/ppermute | solution.py:782
  388.3 184.5 %reduce-scatter.5.cloned.1.call-start = ((), (), s32[]{:S(2)}) async-start(), calls=%async_computation.5 | async-start | bytes 4423680 | tf_op jit(solution)/shard_map/reduce_scatter | solution.py:697
  394.3 4.9 collective-permute-start.27
  394.3 37.0 %collective-permute-start.26 = (bf16[512,1536]{1,0:T(8,128)(2,1)}, bf16[512,1536]{1,0:T(8,128)(2,1)S(1)}, u32[]{:S(2)}, u32[]{:S(2)}) collective-permute-start(bf16[512,1536]{1,0:T(8,128)(2,1)} %norm_back.2.refs_0_.refs_20_), channel_id=1, source_target_pairs={{0,1},{1,0},{2,3},{3,2},{4,5},{5,4},{6,7},{7,6},{8,9},{9,8},{10,11... | collective-permute-start | bytes 4718600 | tf_op jit(solution)/shard_map/ppermute | solution.py:659
  431.4 3.5 collective-permute-start.29
  431.4 35.8 %collective-permute-start.28 = (bf16[512,1536]{1,0:T(8,128)(2,1)S(1)}, bf16[512,1536]{1,0:T(8,128)(2,1)S(1)}, u32[]{:S(2)}, u32[]{:S(2)}) collective-permute-start(bf16[512,1536]{1,0:T(8,128)(2,1)S(1)} %copy-done.56), channel_id=1, source_target_pairs={{0,1},{1,0},{2,4},{3,5},{4,2},{5,3},{6,7},{7,6},{8,9},{9,8},{10,12... | collective-permute-start | bytes 4718600 | tf_op jit(solution)/shard_map/ppermute | solution.py:983
  472.6 5.7 collective-permute-start.30
  484.9 58.3 %collective-permute-start.31 = (bf16[512,1536]{1,0:T(8,128)(2,1)}, bf16[512,1536]{1,0:T(8,128)(2,1)}, u32[]{:S(2)}, u32[]{:S(2)}) collective-permute-start(bf16[512,1536]{1,0:T(8,128)(2,1)} %product.21.refs_4_.refs_28_), channel_id=1, source_target_pairs={{0,1},{1,0},{2,3},{3,2},{4,5},{5,4},{6,7},{7,6},{8,9},{9,8},{10,11... | collective-permute-start | bytes 4718600 | tf_op jit(solution)/shard_map/ppermute | solution.py:782
  489.7 53.5 %collective-permute-start.32 = (bf16[512,1536]{1,0:T(8,128)(2,1)}, bf16[512,1536]{1,0:T(8,128)(2,1)}, u32[]{:S(2)}, u32[]{:S(2)}) collective-permute-start(bf16[512,1536]{1,0:T(8,128)(2,1)} %product.23), channel_id=1, source_target_pairs={{0,4},{4,0},{1,5},{5,1},{2,6},{6,2},{3,7},{7,3},{8,12},{12,8},{9,1... | collective-permute-start | bytes 4718600 | tf_op jit(solution)/shard_map/ppermute | solution.py:655
  493.5 60.0 %collective-permute-start.33 = (bf16[192,3072]{1,0:T(8,128)(2,1)}, bf16[192,3072]{1,0:T(8,128)(2,1)}, u32[]{:S(2)}, u32[]{:S(2)}) collective-permute-start(bf16[192,3072]{1,0:T(8,128)(2,1)} %get-tuple-element.264.refs_29_), channel_id=1, source_target_pairs={{2,4},{4,2},{3,5},{5,3},{10,12},{12,10},{11,13},{13,11},{18,20},{2... | collective-permute-start | bytes 3538952 | tf_op jit(solution)/shard_map/ppermute | solution.py:651
  495.3 58.2 %collective-permute-start.34 = (bf16[192,3072]{1,0:T(8,128)(2,1)}, bf16[192,3072]{1,0:T(8,128)(2,1)}, u32[]{:S(2)}, u32[]{:S(2)}) collective-permute-start(bf16[192,3072]{1,0:T(8,128)(2,1)} %get-tuple-element.288), channel_id=1, source_target_pairs={{2,0},{6,2},{0,4},{4,6},{3,1},{7,3},{1,5},{5,7},{10,8},{14,10},{8,... | collective-permute-start | bytes 3538952 | tf_op jit(solution)/shard_map/ppermute | solution.py:687
  548.8 24.0 %collective-permute-start.35 = (bf16[512,1536]{1,0:T(8,128)(2,1)}, bf16[512,1536]{1,0:T(8,128)(2,1)}, u32[]{:S(2)}, u32[]{:S(2)}) collective-permute-start(bf16[512,1536]{1,0:T(8,128)(2,1)} %norm_back.3.refs_0_), channel_id=1, source_target_pairs={{2,5},{3,4},{4,3},{5,2},{10,13},{11,12},{12,11},{13,10},{18,21},{1... | collective-permute-start | bytes 4718600 | tf_op jit(solution)/shard_map/ppermute | solution.py:801
  574.1 34.5 %collective-permute-start.40 = (bf16[192,1152]{1,0:T(8,128)(2,1)S(1)}, bf16[192,1152]{1,0:T(8,128)(2,1)S(1)}, u32[]{:S(2)}, u32[]{:S(2)}) collective-permute-start(bf16[192,1152]{1,0:T(8,128)(2,1)S(1)} %get-tuple-element.270.refs_1_.own_ref), channel_id=1, source_target_pairs={{2,4},{4,2},{3,5},{5,3},{10,12},{12,10},{11,13},{13,11},{18,20},{2... | collective-permute-start | bytes 1327112 | tf_op jit(solution)/shard_map/ppermute | solution.py:651
  576.7 22.2 %collective-permute-start.36 = (f32[2,192]{1,0:T(2,128)S(1)}, f32[2,192]{1,0:T(2,128)S(1)}, u32[]{:S(2)}, u32[]{:S(2)}) collective-permute-start(f32[2,192]{1,0:T(2,128)S(1)} %bitcast.35), channel_id=1, source_target_pairs={{0,4},{4,0},{1,5},{5,1},{2,6},{6,2},{3,7},{7,3},{8,12},{12,8},{9,1... | collective-permute-start | bytes 4616 | tf_op jit(solution)/shard_map/ppermute | solution.py:655
  599.5 7.9 %collective-permute-start.39 = (f32[2,192]{1,0:T(2,128)S(1)}, f32[2,192]{1,0:T(2,128)S(1)}, u32[]{:S(2)}, u32[]{:S(2)}) collective-permute-start(f32[2,192]{1,0:T(2,128)S(1)} %fusion.5), channel_id=1, source_target_pairs={{0,3},{1,0},{2,1},{3,2},{4,7},{5,4},{6,5},{7,6},{8,11},{9,8},{10,9... | collective-permute-start | bytes 4616 | tf_op jit(solution)/shard_map/ppermute | solution.py:1056
  601.9 5.5 collective-permute-start.38
  601.9 5.5 collective-permute-start.37
  604.4 13.9 %collective-permute-start.41 = (bf16[192,1152]{1,0:T(8,128)(2,1)S(1)}, bf16[192,1152]{1,0:T(8,128)(2,1)S(1)}, u32[]{:S(2)}, u32[]{:S(2)}) collective-permute-start(bf16[192,1152]{1,0:T(8,128)(2,1)S(1)} %get-tuple-element.294), channel_id=1, source_target_pairs={{2,0},{6,2},{0,4},{4,6},{3,1},{7,3},{1,5},{5,7},{10,8},{14,10},{8,... | collective-permute-start | bytes 1327112 | tf_op jit(solution)/shard_map/ppermute | solution.py:687
  (64 other events, 614.5 us)
Sparse Core Ops, SparseCore 0:
  45.9 59.2 all-gather.2
  127.8 121.8 all-gather.4
  388.4 93.7 reduce-scatter.2
  524.8 47.9 reduce-scatter.4

commit v8 on v7

--- a/solution.py
+++ b/solution.py
@@ -525,7 +525,7 @@
 def row_pass(body, name, inputs, whole, kinds, after=()):
     width = inputs[0][0].shape[1]
     rows = min(a.shape[0] - first for a, first in inputs)
-    block = min(256, rows)
+    block = min(512, rows) if body is add_rows else min(256, rows)
 
     def kernel(*refs):
         count = len(inputs) + len(whole)
@@ -544,7 +544,9 @@
         + [unread] * len(after),
         out_specs=[pl.BlockSpec((block, width), lambda i: (i, 0)) for _ in kinds],
         out_shape=[jax.ShapeDtypeStruct((rows, width), kind) for kind in kinds],
-        compiler_params=pltpu.CompilerParams(dimension_semantics=("arbitrary",)),
+        compiler_params=pltpu.CompilerParams(
+            vmem_limit_bytes=40 * 2**20, dimension_semantics=("arbitrary",)
+        ),
         cost_estimate=light,
         name=name,
     )(*[a for a, _ in inputs], *whole, *after)

time: 636 us -> 632 us (level)
  Pallas kernels: 276 us -> 264 us
  waiting for transfers between devices: 150 us -> 161 us
    pallas_call x7, Pallas kernels: 28.2 us -> 16.1 us  [row_pass(): pl.pallas_call(kernel, grid=(rows // block,), in_specs=[pl.BlockSpec((blo...]
    unnamed x134 -> x158, local copies, waits for them, and re-layouts: 28.4 us -> 28.3 us
  transfers between devices with their start and end apart: 46 -> 46, of which waited for: 18 -> 23; matrix products, arithmetic and copies ran while one was open for 6% -> 5% of each run, Pallas kernels for 44% -> 42%
where the time goes in v8:
time: 632 us; the launch traced here: 624 us
  Pallas kernels  264 us (42%)
  waiting for transfers between devices  161 us (25%)
  starting transfers between devices  116 us (18%)
  local copies, waits for them, and re-layouts  34.6 us (5%)
  other arithmetic  32.5 us (5%)
  between operations  15.1 us (2%)
    ppermute x18, starting transfers between devices, other_core(): return lax.ppermute(a, 'c', swap_two)  68.7 us
    pallas_call x2, Pallas kernels, hidden_pass(): pl.pallas_call(functools.partial(hidden_kernel, min(256, units), count),...  55.5 us
    pallas_call x2, Pallas kernels, wgrad(): pl.pallas_call(functools.partial(wgrad_kernel, counts, cut), grid=(column...  50.3 us
    pallas_call x12, Pallas kernels, product(): pl.pallas_call(functools.partial(product_kernel, dims, len(parts), len(af...  43 us
    pallas_call x2, Pallas kernels, attend_back(): pl.pallas_call(functools.partial(attend_back_kernel, ring, block, chip, f...  42.3 us
    ppermute x3, waiting for transfers between devices, send_chips(): lax.ppermute(p.astype(bf16), 'zl', [(i, (i + k) % ring) for i in steps])  36.8 us
    ppermute x1, waiting for transfers between devices, first_moves(): moved = lax.ppermute(original, ('c', 'zh', 'zl'), pairs)  30.5 us
    unnamed x158, local copies, waits for them, and re-layouts  28.3 us
  transfers between devices with their start and end apart: 46, of which 23 were waited for; matrix products, arithmetic and copies ran while one was open for 5% of the time, Pallas kernels for 42%

profile of v8, /device:TPU:0, one launch (start us, length us, event | category | flops | bytes accessed | tf_op | source)
XLA Modules:
  0.0 623.6 jit_solution(13892653641991755884)
XLA Ops:
  7.2 4.9 collective-permute-start.2
  20.2 22.8 %collective-permute-done.1 = bf16[192,1536]{1,0:T(8,128)(2,1)S(1)} collective-permute-done((bf16[192,1536]{1,0:T(8,128)(2,1)}, bf16[192,1536]{1,0:T(8,128)(2,1)S(1)}, u32[]{:S(2)}, u32[]{:S(2)}) %collective-permute-start.1) | collective-permute-done | bytes 589856 | tf_op jit(solution)/shard_map/ppermute | solution.py:669
  46.6 3.0 collective-permute-start.4
  49.6 3.7 fusion.3
  54.6 30.5 %collective-permute-done.4 = bf16[512,1536]{1,0:T(8,128)(2,1)} collective-permute-done((bf16[512,1536]{1,0:T(8,128)(2,1)}, bf16[512,1536]{1,0:T(8,128)(2,1)}, u32[]{:S(2)}, u32[]{:S(2)}) %collective-permute-start.4) | collective-permute-done | bytes 1572896 | tf_op jit(solution)/shard_map/ppermute | solution.py:824
  91.3 4.8 collective-permute-start.7
  96.1 2.8 cut_rows.1
  98.9 6.2 %all-gather.3.cloned.1.call-done.w_ref.refs_1_.refs_3_ = bf16[1536,1536]{1,0:T(8,128)(2,1)} async-done(((bf16[384,1536]{1,0:T(8,128)(2,1)}), bf16[1536,1536]{1,0:T(8,128)(2,1)}) %all-gather.3.cloned.1.call-update) | async-done | bytes 4718608 | tf_op jit(solution)/shard_map/all_gather | solution.py:681
  106.9 7.6 %project.2 = (bf16[2048,1536]{1,0:T(8,128)(2,1)S(1)}, bf16[2048,512]{1,0:T(8,128)(2,1)S(1)}, bf16[2048,256]{1,0:T(8,128)(2,1)S(1)}, bf16[2048,256]{1,0:T(8,128)(2,1)S(1)}) custom-call(bf16[512,1536]{1,0:T(8,128)(2,1)} %broadcast_select_fusion.4.x_ref.refs_0_.refs_1_, bf16[512,1536]{1,0:T(8,128)(2,1)} %collective-permute-done.8.y_ref, ...), custom_call_target="tpu_custom_call" | custom-call | flops 1 | bytes 1 | tf_op jit(solution)/shard_map/project/pallas_call | solution.py:339
  117.1 5.5 collective-permute-done.7
  128.9 25.9 %collective-permute-start.9 = (bf16[512,1536]{1,0:T(8,128)(2,1)S(1)}, bf16[512,1536]{1,0:T(8,128)(2,1)S(1)}, u32[]{:S(2)}, u32[]{:S(2)}) collective-permute-start(bf16[512,1536]{1,0:T(8,128)(2,1)S(1)} %broadcast_select_fusion.3.x_ref), channel_id=1, source_target_pairs={{0,4},{4,0},{1,5},{5,1},{2,6},{6,2},{3,7},{7,3},{8,12},{12,8},{9,1... | collective-permute-start | bytes 4718600 | tf_op jit(solution)/shard_map/ppermute | solution.py:657
  159.1 9.7 %project.3 = (bf16[2048,1536]{1,0:T(8,128)(2,1)}, bf16[2048,512]{1,0:T(8,128)(2,1)}, bf16[2048,256]{1,0:T(8,128)(2,1)}, bf16[2048,256]{1,0:T(8,128)(2,1)}) custom-call(bf16[512,1536]{1,0:T(8,128)(2,1)} %copy-done.67, bf16[512,1536]{1,0:T(8,128)(2,1)} %copy-done.77, ...), custom_call_target="tpu_custom_call", output_to_operand_aliasing={{0}: (6, {}), {1}: (7, {}), {2}: (8, {}), {3}: (9, {})} | custom-call | flops 8000000000 | bytes 1 | tf_op jit(solution)/shard_map/project/pallas_call | solution.py:339
  172.8 13.7 %attend.2 = (bf16[1024,512]{1,0:T(8,128)(2,1)S(1)}, f32[2,2,1024]{2,1,0:T(2,128)S(1)}) custom-call(s32[3]{0:T(128)S(1)} %pad_add_fusion.1.place_ref, bf16[2048,512]{1,0:T(8,128)(2,1)S(1)} %copy-done.4, bf16[2048,256]{1,0:T(8,128)(2,1)S(1)} %copy-done.20, bf16[2048,256]{1,0:T(8,128)(2,1)S(1)} %copy-done.24, s32[1,2048]{1,0:T(1,128)S(1)} %bitcast.21), custom_call_target="tpu_custom_call" | custom-call | flops 1 | bytes 1 | tf_op jit(solution)/shard_map/attend/pallas_call | solution.py:103
  186.6 3.1 product.12
  193.9 3.7 product.13.refs_0_
  197.6 5.1 collective-permute-start.12
  207.3 13.6 %attend.3 = (bf16[1024,512]{1,0:T(8,128)(2,1)S(1)}, f32[2,2,1024]{2,1,0:T(2,128)S(1)}) custom-call(s32[3]{0:T(128)S(1)} %pad_add_fusion.1.place_ref, bf16[2048,512]{1,0:T(8,128)(2,1)S(1)} %copy-done.5, bf16[2048,256]{1,0:T(8,128)(2,1)S(1)} %copy-done.21, bf16[2048,256]{1,0:T(8,128)(2,1)S(1)} %copy-done.25, s32[1,2048]{1,0:T(1,128)S(1)} %bitcast.22), custom_call_target="tpu_custom_call" | custom-call | flops 1 | bytes 1 | tf_op jit(solution)/shard_map/attend/pallas_call | solution.py:103
  220.9 3.0 product.15
  226.7 11.5 %collective-permute-done.12.refs_3_ = bf16[512,1536]{1,0:T(8,128)(2,1)} collective-permute-done((bf16[512,1536]{1,0:T(8,128)(2,1)}, bf16[512,1536]{1,0:T(8,128)(2,1)}, u32[]{:S(2)}, u32[]{:S(2)}) %collective-permute-start.12) | collective-permute-done | bytes 1572896 | tf_op jit(solution)/shard_map/ppermute | solution.py:784
  238.3 3.9 norm_forward.1
  242.2 10.8 %collective-permute-start.15 = (bf16[512,1536]{1,0:T(8,128)(2,1)}, bf16[512,1536]{1,0:T(8,128)(2,1)}, u32[]{:S(2)}, u32[]{:S(2)}) collective-permute-start(bf16[512,1536]{1,0:T(8,128)(2,1)} %get-tuple-element.188.refs_0_.a_ref), channel_id=1, source_target_pairs={{0,4},{4,0},{1,5},{5,1},{2,6},{6,2},{3,7},{7,3},{8,12},{12,8},{9,1... | collective-permute-start | bytes 4718600 | tf_op jit(solution)/shard_map/ppermute | solution.py:657
  259.6 27.4 %hidden.2 = (bf16[1024,1024]{1,0:T(8,128)(2,1)}, bf16[1024,2048]{1,0:T(8,128)(2,1)}, bf16[512,1536]{1,0:T(8,128)(2,1)S(1)}, bf16[512,1536]{1,0:T(8,128)(2,1)S(1)...) custom-call(bf16[512,1536]{1,0:T(8,128)(2,1)} %get-tuple-element.188.refs_0_.a_ref, ...), custom_call_target="tpu_custom_call" | custom-call | flops 8000000000 | bytes 1 | tf_op jit(solution)/shard_map/hidden/pallas_call | solution.py:403
  287.0 5.9 collective-permute-done.17.a_ref.refs_2_
  296.8 9.2 %collective-permute-start.22 = (bf16[512,1536]{1,0:T(8,128)(2,1)S(1)}, bf16[512,1536]{1,0:T(8,128)(2,1)S(1)}, u32[]{:S(2)}, u32[]{:S(2)}) collective-permute-start(bf16[512,1536]{1,0:T(8,128)(2,1)S(1)} %mixed.2), channel_id=1, source_target_pairs={{2,5},{3,4},{4,3},{5,2},{10,13},{11,12},{12,11},{13,10},{18,21},{1... | collective-permute-start | bytes 4718600 | tf_op jit(solution)/shard_map/ppermute | solution.py:803
  306.1 28.1 %hidden.3 = (bf16[1024,1024]{1,0:T(8,128)(2,1)}, bf16[1024,2048]{1,0:T(8,128)(2,1)}, bf16[512,1536]{1,0:T(8,128)(2,1)S(1)}, bf16[512,1536]{1,0:T(8,128)(2,1)S(1)...) custom-call(bf16[512,1536]{1,0:T(8,128)(2,1)} %collective-permute-done.17.a_ref.refs_2_, ...), custom_call_target="tpu_custom_call" | custom-call | flops 8000000000 | bytes 1 | tf_op jit(solution)/shard_map/hidden/pallas_call | solution.py:403
  334.3 4.5 collective-permute-start.23
  338.9 3.0 collective-permute-done.23.refs_1_
  345.8 28.9 %wgrad.2 = bf16[1536,3072]{1,0:T(8,128)(2,1)} custom-call(bf16[512,1536]{1,0:T(8,128)(2,1)} %get-tuple-element.188.refs_0_.a_ref, bf16[512,1536]{1,0:T(8,128)(2,1)} %collective-permute-done.15.b_ref.refs_1_, bf16[512,1536]{1,0:T(8,128)(2,1)} %collective-permute-done.17.a_ref.refs_2_, bf16[512,1536]{1,0:T(8,128)(2,1)} %copy-done.43, ...), custom_call_target="tpu_custom_call" | custom-call | flops 8000000000 | bytes 1 | tf_op jit(solution)/shard_map/wgrad/pallas_call | solution.py:511
  374.7 5.6 collective-permute-done.24.refs_4_
  385.0 3.7 norm_back.2.refs_0_.refs_20_
  392.2 3.2 product.17
  397.1 20.0 %attend_back.2 = (bf16[1024,512]{1,0:T(8,128)(2,1)S(1)}, f32[2048,256]{1,0:T(8,128)S(1)}, f32[2048,256]{1,0:T(8,128)S(1)}) custom-call(s32[3]{0:T(128)S(1)} %pad_add_fusion.1.place_ref, bf16[2048,512]{1,0:T(8,128)(2,1)S(1)} %copy-done.5, bf16[2048,256]{1,0:T(8,128)(2,1)S(1)} %copy-done.22, bf16[2048,256]{1,0:T(8,128)(2,1)S(1)} %copy-done.26, ...), custom_call_target="tpu_custom_call" | custom-call | flops 1 | bytes 1 | tf_op jit(solution)/shard_map/attend_back/pallas_call | solution.py:257
  417.1 8.5 %collective-permute-done.26.refs_0_.refs_22_ = bf16[512,1536]{1,0:T(8,128)(2,1)S(1)} collective-permute-done((bf16[512,1536]{1,0:T(8,128)(2,1)S(1)}, bf16[512,1536]{1,0:T(8,128)(2,1)S(1)}, u32[]{:S(2)}, u32[]{:S(2)}) %collective-permute-start.26) | collective-permute-done | bytes 1572896 | tf_op jit(solution)/shard_map/ppermute | solution.py:661
  434.4 22.3 %attend_back.3 = (bf16[1024,512]{1,0:T(8,128)(2,1)S(1)}, bf16[2048,256]{1,0:T(8,128)(2,1)S(1)}, bf16[2048,256]{1,0:T(8,128)(2,1)S(1)}) custom-call(s32[3]{0:T(128)S(1)} %pad_add_fusion.1.place_ref, bf16[2048,512]{1,0:T(8,128)(2,1)S(1)} %copy-done.6, bf16[2048,256]{1,0:T(8,128)(2,1)S(1)} %copy-done.22, bf16[2048,256]{1,0:T(8,128)(2,1)S(1)} %copy-done.26, ...), custom_call_target="tpu_custom_call" | custom-call | flops 1 | bytes 1 | tf_op jit(solution)/shard_map/attend_back/pallas_call | solution.py:257
  456.8 4.1 collective-permute-done.28.refs_1_
  461.0 5.4 product.20
  469.2 3.4 collective-permute-done.30.refs_4_
  473.8 5.3 product.21.refs_4_.refs_28_
  479.1 4.8 product.23
  484.3 3.4 broadcast_select_fusion.6
  491.4 3.9 product.22.refs_2_
  496.5 21.3 %wgrad.3.refs_6_ = bf16[1536,1152]{1,0:T(8,128)(2,1)} custom-call(bf16[2048,1536]{1,0:T(8,128)(2,1)} %get-tuple-element.249.refs_0_.refs_1_.refs_2_.refs_3_.refs_8_.refs_9_.refs_10_.refs_11_, bf16[2048,1536]{1,0:T(8,128)(2,1)} %get-tuple-element.249.refs_0_.refs_1_.refs_2_.refs_3_.refs_8_.refs_9_.refs_10_.refs_11_, ...), custom_call_target="tpu_custom_call" | custom-call | flops 8000000000 | bytes 1 | tf_op jit(solution)/shard_map/wgrad/pallas_call | solution.py:511
  517.9 19.6 %collective-permute-done.31.refs_4_ = bf16[512,1536]{1,0:T(8,128)(2,1)} collective-permute-done((bf16[512,1536]{1,0:T(8,128)(2,1)}, bf16[512,1536]{1,0:T(8,128)(2,1)}, u32[]{:S(2)}, u32[]{:S(2)}) %collective-permute-start.31) | collective-permute-done | bytes 1572896 | tf_op jit(solution)/shard_map/ppermute | solution.py:784
  540.4 4.6 norm_back.3.refs_0_
  549.6 17.2 %reduce-scatter.5.cloned.1.call-done.refs_0_ = bf16[384,1152]{1,0:T(8,128)(2,1)} async-done(((bf16[1536,1152]{1,0:T(8,128)(2,1)}), bf16[384,1152]{1,0:T(8,128)(2,1)}) %reduce-scatter.5.cloned.1.call-update) | async-done | bytes 884752 | tf_op jit(solution)/shard_map/reduce_scatter | solution.py:699
  570.7 18.1 %collective-permute-start.36 = (f32[2,192]{1,0:T(2,128)S(1)}, f32[2,192]{1,0:T(2,128)S(1)}, u32[]{:S(2)}, u32[]{:S(2)}) collective-permute-start(f32[2,192]{1,0:T(2,128)S(1)} %bitcast.35), channel_id=1, source_target_pairs={{0,4},{4,0},{1,5},{5,1},{2,6},{6,2},{3,7},{7,3},{8,12},{12,8},{9,1... | collective-permute-start | bytes 4616 | tf_op jit(solution)/shard_map/ppermute | solution.py:657
  591.0 3.3 select_convert_fusion
  604.3 9.5 %collective-permute-done.41.slanted_ref = bf16[192,1152]{1,0:T(8,128)(2,1)S(1)} collective-permute-done((bf16[192,1152]{1,0:T(8,128)(2,1)S(1)}, bf16[192,1152]{1,0:T(8,128)(2,1)S(1)}, u32[]{:S(2)}, u32[]{:S(2)}) %collective-permute-start.41) | collective-permute-done | bytes 442400 | tf_op jit(solution)/shard_map/ppermute | solution.py:689
  (293 shorter events, 118.5 us)
Async XLA Ops:
  7.2 98.0 %all-gather.3.cloned.1.call-start = ((), (), s32[]{:S(2)}) async-start(), calls=%async_computation.2 | async-start | bytes 5898240 | tf_op jit(solution)/shard_map/all_gather | solution.py:681
  7.2 35.9 %collective-permute-start.2 = (bf16[512,1536]{1,0:T(8,128)(2,1)}, bf16[512,1536]{1,0:T(8,128)(2,1)S(1)}, u32[]{:S(2)}, u32[]{:S(2)}) collective-permute-start(bf16[512,1536]{1,0:T(8,128)(2,1)} %param.23), channel_id=1, source_target_pairs={{0,1},{1,0},{6,7},{7,6},{8,9},{9,8},{14,15},{15,14},{16,17},{17,16... | collective-permute-start | bytes 4718600 | tf_op jit(solution)/shard_map/ppermute | solution.py:819
  16.6 3.7 collective-permute-start
  17.3 25.8 %collective-permute-start.1 = (bf16[192,1536]{1,0:T(8,128)(2,1)}, bf16[192,1536]{1,0:T(8,128)(2,1)S(1)}, u32[]{:S(2)}, u32[]{:S(2)}) collective-permute-start(bf16[192,1536]{1,0:T(8,128)(2,1)} %pad.81), channel_id=1, source_target_pairs={{0,2},{2,6},{4,0},{6,4},{1,3},{3,7},{5,1},{7,5},{8,10},{10,14},{12... | collective-permute-start | bytes 1769480 | tf_op jit(solution)/shard_map/ppermute | solution.py:669
  18.4 1.8 collective-permute-start.3
  45.8 213.8 %all-gather.5.cloned.1.call-start = ((), (), s32[]{:S(2)}) async-start(), calls=%async_computation.3 | async-start | bytes 11796480 | tf_op jit(solution)/shard_map/all_gather | solution.py:681
  46.6 38.6 %collective-permute-start.4 = (bf16[512,1536]{1,0:T(8,128)(2,1)}, bf16[512,1536]{1,0:T(8,128)(2,1)}, u32[]{:S(2)}, u32[]{:S(2)}) collective-permute-start(bf16[512,1536]{1,0:T(8,128)(2,1)} %param.12), channel_id=1, source_target_pairs={{2,5},{3,4},{4,3},{5,2},{0,1},{1,0},{6,7},{7,6},{10,13},{11,12},{1... | collective-permute-start | bytes 4718600 | tf_op jit(solution)/shard_map/ppermute | solution.py:824
  54.6 103.3 %copy-start.11 = (f32[2048,128]{1,0:T(8,128)}, f32[2048,128]{1,0:T(8,128)S(1)}, u32[]{:S(2)}) copy-start(f32[2048,128]{1,0:T(8,128)S(1)} %get-tuple-element.155.sin_ref.sinq_ref.refs_1_) | copy-start | bytes 3145732
  87.8 19.1 %collective-permute-start.8 = (bf16[512,1536]{1,0:T(8,128)(2,1)}, bf16[512,1536]{1,0:T(8,128)(2,1)}, u32[]{:S(2)}, u32[]{:S(2)}) collective-permute-start(bf16[512,1536]{1,0:T(8,128)(2,1)} %broadcast_select_fusion.4.x_ref.refs_0_.refs_1_), channel_id=1, source_target_pairs={{0,4},{4,0},{1,5},{5,1},{2,6},{6,2},{3,7},{7,3},{8,12},{12,8},{9,1... | collective-permute-start | bytes 4718600 | tf_op jit(solution)/shard_map/ppermute | solution.py:657
  87.8 34.7 %collective-permute-start.5 = (bf16[512,1536]{1,0:T(8,128)(2,1)}, bf16[512,1536]{1,0:T(8,128)(2,1)}, u32[]{:S(2)}, u32[]{:S(2)}) collective-permute-start(bf16[512,1536]{1,0:T(8,128)(2,1)} %collective-permute-done.4), channel_id=1, source_target_pairs={{2,3},{3,2},{4,5},{5,4},{10,11},{11,10},{12,13},{13,12},{18,19},{1... | collective-permute-start | bytes 4718600 | tf_op jit(solution)/shard_map/ppermute | solution.py:831
  89.7 27.5 %collective-permute-start.6 = (bf16[192,3072]{1,0:T(8,128)(2,1)S(1)}, bf16[192,3072]{1,0:T(8,128)(2,1)}, u32[]{:S(2)}, u32[]{:S(2)}) collective-permute-start(bf16[192,3072]{1,0:T(8,128)(2,1)S(1)} %pad_maximum_fusion.5), channel_id=1, source_target_pairs={{2,4},{4,2},{3,5},{5,3},{10,12},{12,10},{11,13},{13,11},{18,20},{2... | collective-permute-start | bytes 3538952 | tf_op jit(solution)/shard_map/ppermute | solution.py:653
  91.3 31.2 %collective-permute-start.7 = (bf16[192,3072]{1,0:T(8,128)(2,1)S(1)}, bf16[192,3072]{1,0:T(8,128)(2,1)}, u32[]{:S(2)}, u32[]{:S(2)}) collective-permute-start(bf16[192,3072]{1,0:T(8,128)(2,1)S(1)} %pad_maximum_fusion.5), channel_id=1, source_target_pairs={{0,2},{2,6},{4,0},{6,4},{1,3},{3,7},{5,1},{7,5},{8,10},{10,14},{12... | collective-permute-start | bytes 3538952 | tf_op jit(solution)/shard_map/ppermute | solution.py:669
  127.1 357.3 %reduce-scatter.3.cloned.1.call-start = ((), (), s32[]{:S(2)}) async-start(), calls=%async_computation.4 | async-start | bytes 11796480 | tf_op jit(solution)/shard_map/reduce_scatter | solution.py:699
  128.9 29.0 %collective-permute-start.9 = (bf16[512,1536]{1,0:T(8,128)(2,1)S(1)}, bf16[512,1536]{1,0:T(8,128)(2,1)S(1)}, u32[]{:S(2)}, u32[]{:S(2)}) collective-permute-start(bf16[512,1536]{1,0:T(8,128)(2,1)S(1)} %broadcast_select_fusion.3.x_ref), channel_id=1, source_target_pairs={{0,4},{4,0},{1,5},{5,1},{2,6},{6,2},{3,7},{7,3},{8,12},{12,8},{9,1... | collective-permute-start | bytes 4718600 | tf_op jit(solution)/shard_map/ppermute | solution.py:657
  154.8 31.7 %collective-permute-start.10 = (bf16[512,1536]{1,0:T(8,128)(2,1)S(1)}, bf16[512,1536]{1,0:T(8,128)(2,1)}, u32[]{:S(2)}, u32[]{:S(2)}) collective-permute-start(bf16[512,1536]{1,0:T(8,128)(2,1)S(1)} %copy-done.61), channel_id=1, source_target_pairs={{2,5},{3,4},{4,3},{5,2},{10,13},{11,12},{12,11},{13,10},{18,21},{1... | collective-permute-start | bytes 4718600 | tf_op jit(solution)/shard_map/ppermute | solution.py:803
  186.5 246.3 %copy-start.8 = (bf16[1024,512]{1,0:T(8,128)(2,1)}, bf16[1024,512]{1,0:T(8,128)(2,1)S(1)}, u32[]{:S(2)}) copy-start(bf16[1024,512]{1,0:T(8,128)(2,1)S(1)} %get-tuple-element.176.refs_0_.o_ref.refs_26_.refs_27_) | copy-start | bytes 3145732
  189.6 4.3 collective-permute-start.11
  190.9 35.8 %collective-permute-start.13 = (bf16[512,1536]{1,0:T(8,128)(2,1)}, bf16[512,1536]{1,0:T(8,128)(2,1)}, u32[]{:S(2)}, u32[]{:S(2)}) collective-permute-start(bf16[512,1536]{1,0:T(8,128)(2,1)} %collective-permute-done.10), channel_id=1, source_target_pairs={{2,3},{3,2},{4,5},{5,4},{10,11},{11,10},{12,13},{13,12},{18,19},{1... | collective-permute-start | bytes 4718600 | tf_op jit(solution)/shard_map/ppermute | solution.py:831
  197.6 40.7 %collective-permute-start.12 = (bf16[512,1536]{1,0:T(8,128)(2,1)}, bf16[512,1536]{1,0:T(8,128)(2,1)}, u32[]{:S(2)}, u32[]{:S(2)}) collective-permute-start(bf16[512,1536]{1,0:T(8,128)(2,1)} %product.13.refs_0_), channel_id=1, source_target_pairs={{0,1},{1,0},{2,3},{3,2},{4,5},{5,4},{6,7},{7,6},{8,9},{9,8},{10,11... | collective-permute-start | bytes 4718600 | tf_op jit(solution)/shard_map/ppermute | solution.py:784
  223.9 14.3 %collective-permute-start.14 = (bf16[512,1536]{1,0:T(8,128)(2,1)S(1)}, bf16[512,1536]{1,0:T(8,128)(2,1)S(1)}, u32[]{:S(2)}, u32[]{:S(2)}) collective-permute-start(bf16[512,1536]{1,0:T(8,128)(2,1)S(1)} %product.15), channel_id=1, source_target_pairs={{0,4},{4,0},{1,5},{5,1},{2,6},{6,2},{3,7},{7,3},{8,12},{12,8},{9,1... | collective-permute-start | bytes 4718600 | tf_op jit(solution)/shard_map/ppermute | solution.py:657
  242.2 17.0 %collective-permute-start.15 = (bf16[512,1536]{1,0:T(8,128)(2,1)}, bf16[512,1536]{1,0:T(8,128)(2,1)}, u32[]{:S(2)}, u32[]{:S(2)}) collective-permute-start(bf16[512,1536]{1,0:T(8,128)(2,1)} %get-tuple-element.188.refs_0_.a_ref), channel_id=1, source_target_pairs={{0,4},{4,0},{1,5},{5,1},{2,6},{6,2},{3,7},{7,3},{8,12},{12,8},{9,1... | collective-permute-start | bytes 4718600 | tf_op jit(solution)/shard_map/ppermute | solution.py:657
  254.2 5.4 collective-permute-start.16
  256.2 36.6 %collective-permute-start.17 = (bf16[512,1536]{1,0:T(8,128)(2,1)}, bf16[512,1536]{1,0:T(8,128)(2,1)}, u32[]{:S(2)}, u32[]{:S(2)}) collective-permute-start(bf16[512,1536]{1,0:T(8,128)(2,1)} %get-tuple-element.188.refs_0_.a_ref), channel_id=1, source_target_pairs={{0,1},{1,0},{2,3},{3,2},{4,5},{5,4},{6,7},{7,6},{8,9},{9,8},{10,11... | collective-permute-start | bytes 4718600 | tf_op jit(solution)/shard_map/ppermute | solution.py:661
  292.8 3.4 collective-permute-start.21
  293.1 13.0 %collective-permute-start.19 = (bf16[512,1536]{1,0:T(8,128)(2,1)S(1)}, bf16[512,1536]{1,0:T(8,128)(2,1)S(1)}, u32[]{:S(2)}, u32[]{:S(2)}) collective-permute-start(bf16[512,1536]{1,0:T(8,128)(2,1)S(1)} %broadcast_select_fusion.1.dy_ref.refs_10_), channel_id=1, source_target_pairs={{0,4},{4,0},{1,5},{5,1},{2,6},{6,2},{3,7},{7,3},{8,12},{12,8},{9,1... | collective-permute-start | bytes 4718600 | tf_op jit(solution)/shard_map/ppermute | solution.py:657
  295.0 11.1 %collective-permute-start.18 = (bf16[512,1536]{1,0:T(8,128)(2,1)}, bf16[512,1536]{1,0:T(8,128)(2,1)S(1)}, u32[]{:S(2)}, u32[]{:S(2)}) collective-permute-start(bf16[512,1536]{1,0:T(8,128)(2,1)} %collective-permute-done.17.a_ref.refs_2_), channel_id=1, source_target_pairs={{0,4},{4,0},{1,5},{5,1},{2,6},{6,2},{3,7},{7,3},{8,12},{12,8},{9,1... | collective-permute-start | bytes 4718600 | tf_op jit(solution)/shard_map/ppermute | solution.py:657
  295.1 11.0 %collective-permute-start.20 = (bf16[512,1536]{1,0:T(8,128)(2,1)S(1)}, bf16[512,1536]{1,0:T(8,128)(2,1)S(1)}, u32[]{:S(2)}, u32[]{:S(2)}) collective-permute-start(bf16[512,1536]{1,0:T(8,128)(2,1)S(1)} %get-tuple-element.202), channel_id=1, source_target_pairs={{0,4},{4,0},{1,5},{5,1},{2,6},{6,2},{3,7},{7,3},{8,12},{12,8},{9,1... | collective-permute-start | bytes 4718600 | tf_op jit(solution)/shard_map/ppermute | solution.py:657
  296.8 37.4 %collective-permute-start.22 = (bf16[512,1536]{1,0:T(8,128)(2,1)S(1)}, bf16[512,1536]{1,0:T(8,128)(2,1)S(1)}, u32[]{:S(2)}, u32[]{:S(2)}) collective-permute-start(bf16[512,1536]{1,0:T(8,128)(2,1)S(1)} %mixed.2), channel_id=1, source_target_pairs={{2,5},{3,4},{4,3},{5,2},{10,13},{11,12},{12,11},{13,10},{18,21},{1... | collective-permute-start | bytes 4718600 | tf_op jit(solution)/shard_map/ppermute | solution.py:803
  334.3 7.6 %collective-permute-start.23 = (bf16[512,1536]{1,0:T(8,128)(2,1)S(1)}, bf16[512,1536]{1,0:T(8,128)(2,1)S(1)}, u32[]{:S(2)}, u32[]{:S(2)}) collective-permute-start(bf16[512,1536]{1,0:T(8,128)(2,1)S(1)} %get-tuple-element.223), channel_id=1, source_target_pairs={{0,4},{4,0},{1,5},{5,1},{2,6},{6,2},{3,7},{7,3},{8,12},{12,8},{9,1... | collective-permute-start | bytes 4718600 | tf_op jit(solution)/shard_map/ppermute | solution.py:657
  338.8 5.4 collective-permute-start.25
  343.3 37.0 %collective-permute-start.24 = (bf16[512,1536]{1,0:T(8,128)(2,1)}, bf16[512,1536]{1,0:T(8,128)(2,1)}, u32[]{:S(2)}, u32[]{:S(2)}) collective-permute-start(bf16[512,1536]{1,0:T(8,128)(2,1)} %join.2.refs_16_), channel_id=1, source_target_pairs={{0,1},{1,0},{2,3},{3,2},{4,5},{5,4},{6,7},{7,6},{8,9},{9,8},{10,11... | collective-permute-start | bytes 4718600 | tf_op jit(solution)/shard_map/ppermute | solution.py:784
  380.4 186.4 %reduce-scatter.5.cloned.1.call-start = ((), (), s32[]{:S(2)}) async-start(), calls=%async_computation.5 | async-start | bytes 4423680 | tf_op jit(solution)/shard_map/reduce_scatter | solution.py:699
  388.7 3.5 collective-permute-start.27
  388.8 36.8 %collective-permute-start.26 = (bf16[512,1536]{1,0:T(8,128)(2,1)S(1)}, bf16[512,1536]{1,0:T(8,128)(2,1)S(1)}, u32[]{:S(2)}, u32[]{:S(2)}) collective-permute-start(bf16[512,1536]{1,0:T(8,128)(2,1)S(1)} %norm_back.2.refs_0_.refs_20_), channel_id=1, source_target_pairs={{0,1},{1,0},{2,3},{3,2},{4,5},{5,4},{6,7},{7,6},{8,9},{9,8},{10,11... | collective-permute-start | bytes 4718600 | tf_op jit(solution)/shard_map/ppermute | solution.py:661
  425.6 3.4 collective-permute-start.29
  425.6 35.3 %collective-permute-start.28 = (bf16[512,1536]{1,0:T(8,128)(2,1)S(1)}, bf16[512,1536]{1,0:T(8,128)(2,1)S(1)}, u32[]{:S(2)}, u32[]{:S(2)}) collective-permute-start(bf16[512,1536]{1,0:T(8,128)(2,1)S(1)} %copy-done.51), channel_id=1, source_target_pairs={{0,1},{1,0},{2,4},{3,5},{4,2},{5,3},{6,7},{7,6},{8,9},{9,8},{10,12... | collective-permute-start | bytes 4718600 | tf_op jit(solution)/shard_map/ppermute | solution.py:985
  466.4 6.1 collective-permute-start.30
  479.1 58.4 %collective-permute-start.31 = (bf16[512,1536]{1,0:T(8,128)(2,1)}, bf16[512,1536]{1,0:T(8,128)(2,1)}, u32[]{:S(2)}, u32[]{:S(2)}) collective-permute-start(bf16[512,1536]{1,0:T(8,128)(2,1)} %product.21.refs_4_.refs_28_), channel_id=1, source_target_pairs={{0,1},{1,0},{2,3},{3,2},{4,5},{5,4},{6,7},{7,6},{8,9},{9,8},{10,11... | collective-permute-start | bytes 4718600 | tf_op jit(solution)/shard_map/ppermute | solution.py:784
  483.9 53.6 %collective-permute-start.32 = (bf16[512,1536]{1,0:T(8,128)(2,1)}, bf16[512,1536]{1,0:T(8,128)(2,1)}, u32[]{:S(2)}, u32[]{:S(2)}) collective-permute-start(bf16[512,1536]{1,0:T(8,128)(2,1)} %product.23), channel_id=1, source_target_pairs={{0,4},{4,0},{1,5},{5,1},{2,6},{6,2},{3,7},{7,3},{8,12},{12,8},{9,1... | collective-permute-start | bytes 4718600 | tf_op jit(solution)/shard_map/ppermute | solution.py:657
  487.7 60.6 %collective-permute-start.33 = (bf16[192,3072]{1,0:T(8,128)(2,1)}, bf16[192,3072]{1,0:T(8,128)(2,1)}, u32[]{:S(2)}, u32[]{:S(2)}) collective-permute-start(bf16[192,3072]{1,0:T(8,128)(2,1)} %get-tuple-element.264.refs_29_), channel_id=1, source_target_pairs={{2,4},{4,2},{3,5},{5,3},{10,12},{12,10},{11,13},{13,11},{18,20},{2... | collective-permute-start | bytes 3538952 | tf_op jit(solution)/shard_map/ppermute | solution.py:653
  489.4 58.9 %collective-permute-start.34 = (bf16[192,3072]{1,0:T(8,128)(2,1)}, bf16[192,3072]{1,0:T(8,128)(2,1)}, u32[]{:S(2)}, u32[]{:S(2)}) collective-permute-start(bf16[192,3072]{1,0:T(8,128)(2,1)} %get-tuple-element.288), channel_id=1, source_target_pairs={{2,0},{6,2},{0,4},{4,6},{3,1},{7,3},{1,5},{5,7},{10,8},{14,10},{8,... | collective-permute-start | bytes 3538952 | tf_op jit(solution)/shard_map/ppermute | solution.py:689
  545.0 21.8 %collective-permute-start.35 = (bf16[512,1536]{1,0:T(8,128)(2,1)}, bf16[512,1536]{1,0:T(8,128)(2,1)}, u32[]{:S(2)}, u32[]{:S(2)}) collective-permute-start(bf16[512,1536]{1,0:T(8,128)(2,1)} %norm_back.3.refs_0_), channel_id=1, source_target_pairs={{2,5},{3,4},{4,3},{5,2},{10,13},{11,12},{12,11},{13,10},{18,21},{1... | collective-permute-start | bytes 4718600 | tf_op jit(solution)/shard_map/ppermute | solution.py:803
  568.1 36.2 %collective-permute-start.40 = (bf16[192,1152]{1,0:T(8,128)(2,1)S(1)}, bf16[192,1152]{1,0:T(8,128)(2,1)S(1)}, u32[]{:S(2)}, u32[]{:S(2)}) collective-permute-start(bf16[192,1152]{1,0:T(8,128)(2,1)S(1)} %get-tuple-element.270.refs_1_.own_ref), channel_id=1, source_target_pairs={{2,4},{4,2},{3,5},{5,3},{10,12},{12,10},{11,13},{13,11},{18,20},{2... | collective-permute-start | bytes 1327112 | tf_op jit(solution)/shard_map/ppermute | solution.py:653
  570.7 24.8 %collective-permute-start.36 = (f32[2,192]{1,0:T(2,128)S(1)}, f32[2,192]{1,0:T(2,128)S(1)}, u32[]{:S(2)}, u32[]{:S(2)}) collective-permute-start(f32[2,192]{1,0:T(2,128)S(1)} %bitcast.35), channel_id=1, source_target_pairs={{0,4},{4,0},{1,5},{5,1},{2,6},{6,2},{3,7},{7,3},{8,12},{12,8},{9,1... | collective-permute-start | bytes 4616 | tf_op jit(solution)/shard_map/ppermute | solution.py:657
  596.1 5.2 collective-permute-start.39
  597.7 4.5 collective-permute-start.38
  597.7 5.4 collective-permute-start.37
  599.8 13.9 %collective-permute-start.41 = (bf16[192,1152]{1,0:T(8,128)(2,1)S(1)}, bf16[192,1152]{1,0:T(8,128)(2,1)S(1)}, u32[]{:S(2)}, u32[]{:S(2)}) collective-permute-start(bf16[192,1152]{1,0:T(8,128)(2,1)S(1)} %get-tuple-element.294), channel_id=1, source_target_pairs={{2,0},{6,2},{0,4},{4,6},{3,1},{7,3},{1,5},{5,7},{10,8},{14,10},{8,... | collective-permute-start | bytes 1327112 | tf_op jit(solution)/shard_map/ppermute | solution.py:689
  (76 other events, 724.8 us)
Sparse Core Ops, SparseCore 0:
  45.9 59.1 all-gather.2
  127.2 121.8 all-gather.4
  380.5 93.5 reduce-scatter.2
  518.0 48.6 reduce-scatter.4
